TPU v7x, 32 devices: a whole 2x2x4 slice. The times are simulated.
32 devices in a mesh: ctx: 4 (over z), tp: 4 (over y, x), dp: 2 (over core).
Axes of the slice: x: 2, y: 2, z: 4, core: 2. Of those that a mesh axis runs over, the one named last changes fastest.
Arguments:
- projected: bfloat16 [3, 2, 1024, 1024], P(None, 'dp', 'ctx', 'tp'), may hold values from -6 to 6
- segment_ids: int32 [2, 1024], P('dp', 'ctx'), may hold values from 0 to 1, never falling along the last dimension, each value on 1 to 768 neighbouring positions
- short_filter: float32 [3, 3, 1024], P(None, None, 'tp'), may hold values from -3.5 to 3.5
- long_filter: float32 [64, 1024], P('tp', 'ctx'), may hold values from -4 to 4
- out_proj: bfloat16 [1024, 1024], P('tp'), may hold values from -0.1875 to 0.1875
- mixed_cotangent: bfloat16 [2, 1024, 1024], P('dp', 'ctx', 'tp'), may hold values from -6 to 6
Outputs:
- mixed: bfloat16 [2, 1024, 1024], P('dp', 'ctx', 'tp')
- grad_projected: bfloat16 [3, 2, 1024, 1024], P(None, 'dp', 'ctx', 'tp')
- grad_short: float32 [3, 3, 1024], P(None, None, 'tp')
- grad_long: float32 [64, 1024], P('tp', 'ctx')
- grad_out_proj: float32 [1024, 1024], P('tp')
Inputs may be any that keep to these rules, and one draw needn't show every extreme that they name: `segment_ids`: along each window the id never falls; every id covers 1 to 768 consecutive positions, and one covers exactly 768.
All inputs are finite; a program needn't handle non-finite values.
Results may differ from a plain program's by a relative error of at most 0.0049.
Values may be sent and summed in bfloat16 or wider, within the bound.
No kernel may reach another device: no remote copies, remote signals or barrier semaphores. Data moves between devices by JAX's collectives and lax.ppermute only.
A program may use at most 64 MiB of HBM per device.

v0:
```python
import functools
import math

import jax
import jax.numpy as jnp
from jax import lax
from jax.experimental import pallas as pl
from jax.experimental.pallas import tpu as pltpu
from jax.sharding import PartitionSpec as P

highest_precision = lax.Precision.HIGHEST


def shifted(value, axis, steps):
    count = lax.axis_size(axis)
    first, last = (max(0, -steps), min(count, count - steps))
    return lax.ppermute(value, axis, [(source, source + steps) for source in range(first, last)])


def angle_table(height, breadth, period, direction):
    product = (
        jnp.arange(height, dtype=jnp.int32)[:, None]
        * jnp.arange(breadth, dtype=jnp.int32)[None, :]
        % period
    )
    angles = direction * 2.0 * math.pi / period * product.astype(jnp.float32)
    return (jnp.cos(angles), jnp.sin(angles))


def row_twiddle(spec_re, spec_im, direction):
    my_index = lax.axis_index("ctx")
    devices = lax.axis_size("ctx")
    row_count = spec_re.shape[1]
    period = 2 * devices * row_count
    freq_pair = 2 * my_index + jnp.arange(2, dtype=jnp.int32)
    product = freq_pair[:, None] * jnp.arange(row_count, dtype=jnp.int32)[None, :] % period
    angles = direction * 2.0 * math.pi / period * product.astype(jnp.float32)
    cosine = jnp.cos(angles)[:, :, None]
    sine_part = jnp.sin(angles)[:, :, None]
    return (spec_re * cosine - spec_im * sine_part, spec_re * sine_part + spec_im * cosine)


def row_transform(spec_re, spec_im, direction):
    row_count = spec_re.shape[1]
    cosine, sine_part = angle_table(row_count, row_count, row_count, direction)

    def along_rows(blocks, matrix):
        return jnp.einsum("kmc,mq->kqc", blocks, matrix, precision=highest_precision)

    return (
        along_rows(spec_re, cosine) - along_rows(spec_im, sine_part),
        along_rows(spec_re, sine_part) + along_rows(spec_im, cosine),
    )


def mixing(matrix, blocks):
    return jnp.einsum("kj,jmc->kmc", matrix, blocks, precision=highest_precision)


def forward_spectrum(real_part):
    devices = lax.axis_size("ctx")
    cosine, sine_part = angle_table(2 * devices, devices, 2 * devices, -1.0)
    spread_re = lax.all_to_all(real_part[None], "ctx", split_axis=1, concat_axis=0, tiled=True)
    column_re = mixing(cosine, spread_re)
    column_im = mixing(sine_part, spread_re)
    near_re, near_im = (
        lax.all_to_all(column_re, "ctx", split_axis=0, concat_axis=1, tiled=True),
        lax.all_to_all(column_im, "ctx", split_axis=0, concat_axis=1, tiled=True),
    )
    twist_re, twist_im = row_twiddle(near_re, near_im, -1.0)
    return row_transform(twist_re, twist_im, -1.0)


def inverse_spectrum(spec_re, spec_im):
    devices = lax.axis_size("ctx")
    row_count = spec_re.shape[1]
    back_re, back_im = row_transform(spec_re, spec_im, 1.0)
    twist_re, twist_im = row_twiddle(back_re / row_count, back_im / row_count, 1.0)
    far_re, far_im = (
        lax.all_to_all(twist_re, "ctx", split_axis=1, concat_axis=0, tiled=True),
        lax.all_to_all(twist_im, "ctx", split_axis=1, concat_axis=0, tiled=True),
    )
    cosine, sine_part = angle_table(devices, 2 * devices, 2 * devices, 1.0)
    out_re = (mixing(cosine, far_re) - mixing(sine_part, far_im)) / (2 * devices)
    rows_re = lax.all_to_all(out_re, "ctx", split_axis=0, concat_axis=1, tiled=True)
    return (rows_re[0], rows_re[0])


def pack_columns(values):
    return (values, values)


def by_filter(val_re, val_im, fil_re, fil_im, conjugate):
    val_shape = val_re.shape
    group_count = fil_re.shape[2]
    v_re = val_re.reshape(val_shape[0], val_shape[1], group_count, -1)
    v_im = val_im.reshape(val_shape[0], val_shape[1], group_count, -1)
    f_re = fil_re[:, :, :, None]
    f_im = fil_im[:, :, :, None]
    if conjugate:
        f_im = -f_im
    out_re = v_re * f_re - v_im * f_im
    out_im = v_re * f_im + v_im * f_re
    return (out_re.reshape(val_shape), out_im.reshape(val_shape))


def short_local(extended, filters, seg_ext):
    reach_taps = filters.shape[1]
    out_rows = extended.shape[1] - reach_taps + 1
    own_seg = seg_ext[reach_taps - 1 :]
    running = jnp.zeros((extended.shape[0], out_rows, extended.shape[2]), jnp.float32)
    for shift_by in range(reach_taps):
        start_row = reach_taps - 1 - shift_by
        same_doc = jnp.where(seg_ext[start_row : start_row + out_rows] == own_seg, 1.0, 0.0)
        running = (
            running
            + filters[:, shift_by][:, None, :]
            * same_doc[None, :, None]
            * extended[:, start_row : start_row + out_rows]
        )
    return running


def spectral_device(projected, segment_ids, short_filter, long_filter, out_proj, mixed_cotangent):
    row_count = projected.shape[2]
    stacked = projected.shape[0]
    width_dev = projected.shape[3]
    short_reach = short_filter.shape[1]
    group_count = long_filter.shape[0]
    grad_scale = 1.0 / math.sqrt(
        projected.shape[1] * lax.axis_size("dp") * row_count * lax.axis_size("ctx")
    )
    segments = segment_ids[0]
    source = projected[:, 0]
    short_rows = short_reach - 1
    cot_full = lax.all_gather(mixed_cotangent[0], "tp", axis=1, tiled=True)
    prev_tail, prev_seg = shifted(
        (source[:, row_count - short_rows :], segments[row_count - short_rows :]), "ctx", 1
    )
    short_seg = jnp.concatenate([prev_seg, segments])
    short_ext = jnp.concatenate([prev_tail, source], axis=1).astype(jnp.float32)

    def short_piece(extended, filters):
        return short_local(extended, filters, short_seg)

    short_out, short_pull = jax.vjp(short_piece, short_ext, short_filter)
    query_conv = short_out[0]
    gated_rows = short_out[1] * short_out[2]
    filter_cols = long_filter.T
    mid_re, mid_im = pack_columns(gated_rows)
    spec_re, spec_im = forward_spectrum(jnp.concatenate([mid_re, filter_cols], axis=1))
    data_cols = spec_re.shape[2] - group_count
    signal_re = spec_re[:, :, :data_cols]
    signal_im = spec_im[:, :, :data_cols]
    filt_re = spec_re[:, :, data_cols:]
    filt_im = spec_im[:, :, data_cols:]
    long_re, long_im = by_filter(signal_re, signal_im, filt_re, filt_im, False)
    out_re, out_im = inverse_spectrum(long_re, long_im)
    y_out = (query_conv * out_re).astype(jnp.bfloat16)
    partial_out = jnp.dot(y_out, out_proj, preferred_element_type=jnp.float32)
    mixed = lax.psum_scatter(partial_out, "tp", scatter_dimension=1, tiled=True).astype(
        jnp.bfloat16
    )
    grad_y = jnp.dot(cot_full, out_proj.T, preferred_element_type=jnp.float32)
    grad_proj_local = jnp.dot(y_out.T, cot_full, preferred_element_type=jnp.float32)
    grad_long_out = grad_y * query_conv
    grad_query = grad_y * out_re
    grad_in_re, grad_in_im = pack_columns(grad_long_out)
    cot_re, cot_im = forward_spectrum(grad_in_re)
    back_re, back_im = by_filter(cot_re, cot_im, filt_re, filt_im, True)
    cross_re = (
        (signal_re * cot_re + signal_im * cot_im).reshape(2, row_count, group_count, -1).sum(axis=3)
    )
    cross_im = (
        (signal_re * cot_im - signal_im * cot_re).reshape(2, row_count, group_count, -1).sum(axis=3)
    )
    inv_re, inv_im = inverse_spectrum(
        jnp.concatenate([back_re, cross_re], axis=2), jnp.concatenate([back_im, cross_im], axis=2)
    )
    grad_gated = inv_re[:, :data_cols]
    grad_long_local = inv_re[:, data_cols:].T
    grad_short_out = jnp.stack([grad_query, grad_gated * short_out[2], grad_gated * short_out[1]])
    grad_short_ext, grad_short_local = short_pull(grad_short_out)
    returned_short = shifted(grad_short_ext[:, :short_rows], "ctx", -1)
    grad_source = grad_short_ext[:, short_rows:] + jnp.concatenate(
        [jnp.zeros((stacked, row_count - short_rows, width_dev), jnp.float32), returned_short],
        axis=1,
    )
    total_proj, total_short = lax.psum((grad_proj_local, grad_short_local), ("ctx", "dp"))
    total_long = lax.psum(grad_long_local, "dp")
    return (
        mixed[None],
        grad_source[:, None].astype(jnp.bfloat16),
        total_short * grad_scale,
        total_long * grad_scale,
        total_proj * grad_scale,
    )


bf16 = jnp.bfloat16
f32 = jnp.float32
SUB = 128


def split_bf16(value):
    high = value.astype(bf16)
    return high, (value - high.astype(f32)).astype(bf16)


def rotate(value, axis, steps):
    count = lax.axis_size(axis)
    return lax.ppermute(value, axis, [(i, (i + steps) % count) for i in range(count)])


def scatter_chunks(chunks, axis):
    return [chunks[0]] + [rotate(chunks[s], axis, s) for s in range(1, len(chunks))]


def spread(value, axis):
    return [value] + [rotate(value, axis, s) for s in range(1, lax.axis_size(axis))]


def on_core(kernel, outs, args, name, scratch=(), flops=0):
    moved = sum(a.size * a.dtype.itemsize for a in args)
    moved += sum(math.prod(shape) * jnp.dtype(kind).itemsize for shape, kind in outs)
    return pl.pallas_call(
        kernel,
        out_shape=[jax.ShapeDtypeStruct(shape, kind) for shape, kind in outs],
        scratch_shapes=list(scratch),
        compiler_params=pltpu.CompilerParams(vmem_limit_bytes=48 * 1024 * 1024),
        cost_estimate=pl.CostEstimate(flops=flops, bytes_accessed=moved, transcendentals=0),
        name=name,
    )(*args)


def block_at(index, size):
    return pl.ds(pl.multiple_of(index * size, size), size)


def pack_signal_kernel(devices, projected, filters, segments, *rest):
    outs, (turned, small) = rest[:devices], rest[devices:]
    me = lax.axis_index("ctx")
    stacked, _, width = projected.shape
    chunk = width // devices
    groups = filters.shape[0] // devices
    for i in range(stacked):
        turned[i] = projected[i].T
    small[...] = jnp.zeros_like(small)
    seg = segments[...]
    small[2 * groups : 2 * groups + 1] = (seg >> 8).astype(f32)
    small[2 * groups + 1 : 2 * groups + 2] = (seg & 255).astype(f32)
    for s in range(devices):
        to = lax.rem(me + s, devices)
        for i in range(stacked):
            outs[s][i * chunk : (i + 1) * chunk] = turned[i, block_at(to, chunk)]
        count = groups * devices
        taps = pltpu.roll(filters[...], lax.rem(count - to * groups, count), 0)[0:groups]
        high = taps.astype(bf16).astype(f32)
        small[0:groups] = high
        small[groups : 2 * groups] = taps - high
        outs[s][stacked * chunk :] = small[...].astype(bf16)


def pack_channels_kernel(parts, cotangent, weights, *outs):
    me = lax.axis_index("tp")
    rows, width = cotangent.shape
    for s in range(1, parts):
        to = lax.rem(me + s, parts)
        outs[s - 1][0:rows] = cotangent[...]
        outs[s - 1][rows:] = weights[:, block_at(to, width)]


def tap_columns(short_filter, flat, columns, me, chunk):
    stacked, taps, _ = short_filter.shape
    flat[...] = jnp.zeros_like(flat)
    for i in range(stacked):
        flat[i * taps : (i + 1) * taps] = short_filter[i]
    columns[...] = flat[...].T
    return columns[block_at(me, chunk)]


def tap_masks(seg, taps):
    wide = jnp.broadcast_to(seg, (8, seg.shape[1]))
    place = lax.broadcasted_iota(jnp.int32, wide.shape, 1)
    masks = [None]
    for s in range(1, taps):
        same = (wide == pltpu.roll(wide, s, 1)) & (place >= s)
        masks.append(jnp.where(same, 1.0, 0.0)[0:1])
    return masks


def conv_kernel(devices, short_filter, *rest):
    pays, rest = rest[:devices], rest[devices:]
    y_outs, rest = rest[:devices], rest[devices:]
    conv, long, source, seg_out, columns_out, toeplitz, small, flat, columns, y_full = rest
    me = lax.axis_index("ctx")
    stacked, taps, _ = short_filter.shape
    _, chunk, span = conv.shape
    length = span // devices
    groups = toeplitz.shape[0]
    size = chunk // groups
    body = stacked * chunk
    for s in range(devices):
        at = block_at(lax.rem(me - s + devices, devices), length)
        source[:, at] = pays[s][0:body]
        small[:, at] = pays[s][body:].astype(f32)
    seg = small[2 * groups : 2 * groups + 1] * 256.0 + small[2 * groups + 1 : 2 * groups + 2]
    seg_out[...] = jnp.broadcast_to(seg, seg_out.shape)
    masks = tap_masks(seg, taps)
    column = tap_columns(short_filter, flat, columns, me, chunk)
    columns_out[...] = column
    for i in range(stacked):
        x = source[i * chunk : (i + 1) * chunk].astype(f32)
        total = column[:, i * taps : i * taps + 1] * x
        for s in range(1, taps):
            j = i * taps + s
            total += column[:, j : j + 1] * (masks[s] * pltpu.roll(x, s, 1))
        conv[i] = total
    high, low = split_bf16(conv[1] * conv[2])
    for g in range(groups):
        line = small[g : g + 1] + small[groups + g : groups + g + 1]
        padded = jnp.concatenate([line, jnp.zeros((1, SUB), f32)], axis=1)
        turned = pltpu.roll(
            jnp.broadcast_to(padded, (SUB, span + SUB)), 0, 1, stride=1, stride_axis=0
        )[:, :span].astype(bf16)
        for r in range(length // SUB):
            rows = slice(r * SUB, (r + 1) * SUB)
            if r:
                toeplitz[g, rows, : r * SUB] = jnp.zeros((SUB, r * SUB), bf16)
            toeplitz[g, rows, r * SUB :] = turned[:, : span - r * SUB]
        own = slice(g * size, (g + 1) * size)
        pieces = []
        for j in range(devices):
            at = slice(j * length, (j + 1) * length)
            pieces += [high[own, at], low[own, at]]
        stack = jnp.concatenate(pieces, axis=0)
        totals = [None] * devices
        for lag in range(devices):
            part = jnp.dot(
                stack[: 2 * size * (devices - lag)],
                toeplitz[g, :, lag * length : (lag + 1) * length],
                preferred_element_type=f32,
            )
            for j in range(devices - lag):
                term = part[2 * size * j : 2 * size * j + size]
                term += part[2 * size * j + size : 2 * size * (j + 1)]
                i = j + lag
                totals[i] = term if totals[i] is None else totals[i] + term
        for i in range(devices):
            long[own, i * length : (i + 1) * length] = totals[i]
    y_full[...] = (conv[0] * long[...]).astype(bf16)
    for s in range(devices):
        y_outs[s][...] = y_full[:, block_at(lax.rem(me + s, devices), length)]


def grad_y_kernel(devices, parts, weights, cotangent, *rest):
    pays, rest = rest[: parts - 1], rest[parts - 1 :]
    outs, (full,) = rest[:devices], rest[devices:]
    me, mine = lax.axis_index("ctx"), lax.axis_index("tp")
    rows, width = cotangent.shape
    chunk = width // devices
    total = None
    for s in range(parts):
        cot = cotangent[...] if s == 0 else pays[s - 1][0:rows]
        lhs = weights[:, block_at(lax.rem(mine - s + parts, parts), width)]
        term = lax.dot_general(lhs, cot, (((1,), (1,)), ((), ())), preferred_element_type=f32)
        total = term if total is None else total + term
    full[...] = total
    for s in range(devices):
        outs[s][...] = full[block_at(lax.rem(me + s, devices), chunk)].astype(outs[s].dtype)


def weight_grad_kernel(devices, parts, cotangent, *rest):
    pays, rest = rest[: parts - 1], rest[parts - 1 :]
    ys, (y_out, keep, send, full) = rest[:devices], rest[devices:]
    me, mine, core = lax.axis_index("ctx"), lax.axis_index("tp"), lax.axis_index("dp")
    rows, width = cotangent.shape
    chunk = width // devices
    half = width // 2
    for s in range(devices):
        y_out[block_at(lax.rem(me - s + devices, devices), chunk)] = ys[s][...]
    y = y_out[...]
    for s in range(parts):
        cot = cotangent[...] if s == 0 else pays[s - 1][0:rows]
        at = block_at(lax.rem(mine - s + parts, parts), width)
        full[:, at] = jnp.dot(y, cot, preferred_element_type=f32)
    keep[...] = full[block_at(core, half)]
    send[...] = full[block_at(1 - core, half)].astype(send.dtype)


def core_sum_kernel(devices, keep, other, *rest):
    outs, (full,) = rest[:devices], rest[devices:]
    me = lax.axis_index("ctx")
    rows = keep.shape[0] // devices
    full[...] = keep[...] + other[...].astype(f32)
    for s in range(devices):
        at = block_at(lax.rem(me + s, devices), rows)
        outs[s][...] = full[at].astype(outs[s].dtype)


def block_sum_kernel(scale, *refs):
    total = refs[0][...]
    for ref in refs[1:-1]:
        total += ref[...].astype(f32)
    refs[-1][...] = (total * scale).astype(refs[-1].dtype)


def weight_out_kernel(devices, *refs):
    out = refs[-1]
    me, core = lax.axis_index("ctx"), lax.axis_index("dp")
    rows = out.shape[0] // (2 * devices)
    for h in range(2):
        side = core if h == 0 else 1 - core
        for s in range(devices):
            block = side * devices + lax.rem(me - s + devices, devices)
            out[block_at(block, rows)] = refs[h * devices + s][...].astype(f32)


def mixed_kernel(parts, weights, *rest):
    ys, pays, out = rest[:parts], rest[parts:-1], rest[-1]
    mine = lax.axis_index("tp")
    rows, width = out.shape
    total = None
    for s in range(parts):
        w = weights[:, block_at(mine, width)] if s == 0 else pays[s - 1][rows:]
        term = lax.dot_general(
            ys[s][...], w, (((0,), (0,)), ((), ())), preferred_element_type=f32
        )
        total = term if total is None else total + term
    out[...] = total.astype(bf16)


def backward_kernel(devices, taps, conv, long, source, seg, column_ref, toeplitz, *rest):
    gys, rest = rest[:devices], rest[devices:]
    outs, (grad_y, grads, small, marks) = rest[:devices], rest[devices:]
    me = lax.axis_index("ctx")
    stacked, chunk, span = conv.shape
    length = span // devices
    groups = toeplitz.shape[0]
    size = chunk // groups
    body = stacked * chunk
    for s in range(devices):
        at = block_at(lax.rem(me - s + devices, devices), length)
        grad_y[:, at] = gys[s][...].astype(f32)
    masks = tap_masks(seg[0:1], taps)
    column = column_ref[...]
    gy = grad_y[...]
    grad_long_out = gy * conv[0]
    high, low = split_bf16(grad_long_out)
    gated = (conv[1] * conv[2]).astype(bf16)
    gg_parts = []
    corner = lax.broadcasted_iota(jnp.int32, (SUB, SUB), 0)
    corner += lax.broadcasted_iota(jnp.int32, (SUB, SUB), 1)
    flip = jnp.where(corner == SUB - 1, 1.0, 0.0).astype(bf16)
    subs = span // SUB
    small[...] = jnp.zeros_like(small)
    for g in range(groups):
        own = slice(g * size, (g + 1) * size)
        pieces = []
        for i in range(devices):
            at = slice(i * length, (i + 1) * length)
            pieces += [high[own, at], low[own, at]]
        stack = jnp.concatenate(pieces, axis=0)
        totals = [None] * devices
        for lag in range(devices):
            part = lax.dot_general(
                stack[2 * size * lag :],
                toeplitz[g, :, lag * length : (lag + 1) * length],
                (((1,), (1,)), ((), ())),
                preferred_element_type=f32,
            )
            for j in range(devices - lag):
                term = part[2 * size * j : 2 * size * j + size]
                term += part[2 * size * j + size : 2 * size * (j + 1)]
                totals[j] = term if totals[j] is None else totals[j] + term
        gg_parts.append(jnp.concatenate(totals, axis=1))
        left = jnp.concatenate([gated[own, j * SUB : (j + 1) * SUB] for j in range(subs)], axis=0)
        right = jnp.concatenate([high[own, j * SUB : (j + 1) * SUB] for j in range(subs)], axis=0)
        turned = lax.dot_general(
            flip, left, (((1,), (1,)), ((), ())), preferred_element_type=f32
        ).astype(bf16)
        lines = []
        for lag in range(subs):
            cross = jnp.dot(
                turned[:, : size * (subs - lag)], right[size * lag :], preferred_element_type=f32
            )
            wide = jnp.concatenate([cross, jnp.zeros((SUB, SUB), f32)], axis=1)
            wide = pltpu.roll(wide, 1, 1, stride=1, stride_axis=0)
            lines.append(jnp.sum(wide, axis=0, keepdims=True))
        per = length // SUB
        for lag in range(subs):
            line = lines[lag][:, SUB:]
            if lag + 1 < subs:
                line += lines[lag + 1][:, :SUB]
            b, within = divmod(lag, per)
            small[b, g : g + 1, within * SUB : (within + 1) * SUB] = line
    grad_gated = jnp.concatenate(gg_parts, axis=0)
    lane = lax.broadcasted_iota(jnp.int32, (chunk, SUB), 1)
    sums = jnp.zeros((chunk, SUB), f32)
    for i in range(stacked):
        if i == 0:
            grad = gy * long[...]
        else:
            grad = grad_gated * conv[3 - i]
        x = source[i * chunk : (i + 1) * chunk].astype(f32)
        total = column[:, i * taps : i * taps + 1] * grad
        sums += jnp.where(lane == i * taps, jnp.sum(grad * x, axis=1, keepdims=True), 0.0)
        for s in range(1, taps):
            j = i * taps + s
            masked = masks[s] * grad
            total += column[:, j : j + 1] * pltpu.roll(masked, span - s, 1)
            tap = jnp.sum(masked * pltpu.roll(x, s, 1), axis=1, keepdims=True)
            sums += jnp.where(lane == j, tap, 0.0)
        grads[i * chunk : (i + 1) * chunk] = total.astype(bf16)
    rows = stacked * taps
    marks[...] = jnp.zeros_like(marks)
    marks[:, 0:chunk] = sums.T
    placed = pltpu.roll(marks[0:16], me * chunk, 1)
    for b in range(devices):
        small[b, groups : groups + rows] = placed[0:rows]
    room = small.shape[1]
    for s in range(devices):
        to = lax.rem(me + s, devices)
        outs[s][0:body] = grads[:, block_at(to, length)]
        value = small[to]
        top = value.astype(bf16)
        outs[s][body : body + room] = top
        outs[s][body + room :] = (value - top.astype(f32)).astype(bf16)


def grad_out_kernel(devices, groups, *refs):
    pays, (out, sums, turned) = refs[:devices], refs[devices:]
    me = lax.axis_index("ctx")
    stacked, _, width = out.shape
    chunk = width // devices
    body = stacked * chunk
    room = (pays[0].shape[0] - body) // 2
    count = groups * devices
    total = long_rows = None
    for s in range(devices):
        come = lax.rem(me - s + devices, devices)
        for i in range(stacked):
            turned[i, block_at(come, chunk)] = pays[s][i * chunk : (i + 1) * chunk]
        value = pays[s][body : body + room].astype(f32) + pays[s][body + room :].astype(f32)
        row = lax.broadcasted_iota(jnp.int32, (count, value.shape[1]), 0)
        line = pltpu.roll(jnp.where(row < groups, value[0:count], 0.0), come * groups, 0)
        long_rows = line if long_rows is None else long_rows + line
        total = value if total is None else total + value
    for i in range(stacked):
        out[i] = turned[i].T
    sums[...] = jnp.zeros_like(sums)
    sums[0:count] = long_rows
    sums[count : count + room - groups] = total[groups:]


def small_out_kernel(scale, mine, other, short_out, long_out):
    total = (mine[...] + other[...]) * scale
    count = long_out.shape[0]
    stacked, taps, _ = short_out.shape
    long_out[...] = total[0:count]
    for i in range(stacked):
        start = count + i * taps
        short_out[i] = total[start : start + taps]


def direct_device(projected, segment_ids, short_filter, long_filter, out_proj, mixed_cotangent):
    devices, parts = lax.axis_size("ctx"), lax.axis_size("tp")
    stacked, _, length, width = projected.shape
    taps = short_filter.shape[1]
    groups = long_filter.shape[0] // devices
    chunk = width // devices
    span = length * devices
    total_cols = out_proj.shape[1]
    grad_scale = 1.0 / math.sqrt(projected.shape[1] * lax.axis_size("dp") * span)
    cotangent = mixed_cotangent[0]
    room = 16
    size = stacked * chunk + room

    packed = on_core(
        functools.partial(pack_signal_kernel, devices),
        [((size, length), bf16)] * devices,
        (projected[:, 0], long_filter, segment_ids),
        "pack_signal",
        [pltpu.VMEM((stacked, width, length), bf16), pltpu.VMEM((room, length), f32)],
    )
    signal = scatter_chunks(packed, "ctx")
    tp_packed = on_core(
        functools.partial(pack_channels_kernel, parts),
        [((length + width, width), bf16)] * (parts - 1),
        (cotangent, out_proj),
        "pack_channels",
    )
    pays = [rotate(tp_packed[s - 1], "tp", s) for s in range(1, parts)]

    gy = on_core(
        functools.partial(grad_y_kernel, devices, parts),
        [((chunk, length), bf16)] * devices,
        (out_proj, cotangent, *pays),
        "grad_y",
        [pltpu.VMEM((width, length), f32)],
        flops=2 * width * length * total_cols,
    )
    gy_in = scatter_chunks(gy, "ctx")

    conv_flops = 2 * groups * span * span * 64
    outs = on_core(
        functools.partial(conv_kernel, devices),
        [((chunk, length), bf16)] * devices
        + [
            ((stacked, chunk, span), f32),
            ((chunk, span), f32),
            ((stacked * chunk, span), bf16),
            ((8, span), f32),
            ((chunk, 16), f32),
            ((groups, length, span), bf16),
        ],
        (short_filter, *signal),
        "conv",
        [
            pltpu.VMEM((room, span), f32),
            pltpu.VMEM((16, width), f32),
            pltpu.VMEM((width, 16), f32),
            pltpu.VMEM((chunk, span), bf16),
        ],
        flops=conv_flops,
    )
    ys, kept = outs[:devices], outs[devices:]
    y_in = scatter_chunks(ys, "ctx")

    half = width // 2
    y_full, keep, send = on_core(
        functools.partial(weight_grad_kernel, devices, parts),
        [((width, length), bf16), ((half, total_cols), f32), ((half, total_cols), f32)],
        (cotangent, *pays, *y_in),
        "weight_grad",
        [pltpu.VMEM((width, total_cols), f32)],
        flops=2 * width * length * total_cols,
    )
    other = rotate(send, "dp", 1)
    rows = half // devices
    sums = on_core(
        functools.partial(core_sum_kernel, devices),
        [((rows, total_cols), f32)] + [((rows, total_cols), bf16)] * (devices - 1),
        (keep, other),
        "core_sum",
        [pltpu.VMEM((half, total_cols), f32)],
    )
    sums = scatter_chunks(sums, "ctx")
    (block,) = on_core(
        functools.partial(block_sum_kernel, grad_scale),
        [((rows, total_cols), bf16)],
        sums,
        "block_sum",
    )
    near = spread(block, "ctx")
    far = [rotate(piece, "dp", 1) for piece in near]
    (grad_out_proj,) = on_core(
        functools.partial(weight_out_kernel, devices),
        [((width, total_cols), f32)],
        (*near, *far),
        "weight_out",
    )

    y_all = spread(y_full, "tp")
    (mixed,) = on_core(
        functools.partial(mixed_kernel, parts),
        [((length, width), bf16)],
        (out_proj, *y_all, *pays),
        "mixed",
        flops=2 * width * length * total_cols,
    )

    back = on_core(
        functools.partial(backward_kernel, devices, taps),
        [((size + room, length), bf16)] * devices,
        (*kept, *gy_in),
        "backward",
        [
            pltpu.VMEM((chunk, span), f32),
            pltpu.VMEM((stacked * chunk, span), bf16),
            pltpu.VMEM((devices, room, length), f32),
            pltpu.VMEM((SUB, width), f32),
        ],
        flops=2 * conv_flops,
    )
    back = scatter_chunks(back, "ctx")
    count = groups * devices
    grad_projected, small = on_core(
        functools.partial(grad_out_kernel, devices, groups),
        [((stacked, length, width), bf16), ((count + 16, width), f32)],
        back,
        "grad_out",
        [pltpu.VMEM((stacked, width, length), bf16)],
    )
    grad_short, grad_long = on_core(
        functools.partial(small_out_kernel, grad_scale),
        [(short_filter.shape, f32), ((count, length), f32)],
        (small, rotate(small, "dp", 1)),
        "small_out",
    )
    return (mixed[None], grad_projected[:, None], grad_short, grad_long, grad_out_proj)


def direct_fits(mesh, projected, short_filter, long_filter):
    devices = mesh.shape["ctx"]
    length = projected.shape[2] // devices
    width = projected.shape[3] // mesh.shape["tp"]
    groups = long_filter.shape[0] // mesh.shape["tp"]
    stacked, taps = short_filter.shape[:2]
    return (
        mesh.shape["dp"] == 2
        and projected.shape[1] == 2
        and stacked == 3
        and length == width
        and length % SUB == 0
        and groups % devices == 0
        and groups == 16
        and (width // devices) % 16 == 0
        and width // devices <= SUB
        and (width // groups) == 16
        and 2 * groups // devices + 2 <= 16
        and groups // devices + stacked * taps <= 16
    )


def solution(mesh):
    in_specs = (
        P(None, "dp", "ctx", "tp"),
        P("dp", "ctx"),
        P(None, None, "tp"),
        P("tp", "ctx"),
        P("tp", None),
        P("dp", "ctx", "tp"),
    )
    out_specs = (
        P("dp", "ctx", "tp"),
        P(None, "dp", "ctx", "tp"),
        P(None, None, "tp"),
        P("tp", "ctx"),
        P("tp", None),
    )

    def layer(projected, segment_ids, short_filter, long_filter, out_proj, mixed_cotangent):
        fits = direct_fits(mesh, projected, short_filter, long_filter)
        return jax.shard_map(
            direct_device if fits else spectral_device,
            mesh=mesh,
            in_specs=in_specs,
            out_specs=out_specs,
            check_vma=False,
        )(projected, segment_ids, short_filter, long_filter, out_proj, mixed_cotangent)

    return layer
```

profile of v0, /device:TPU:0, one launch (start us, length us, event | category | flops | bytes accessed | tf_op | source)
XLA Modules:
  0.0 70.0 jit_solution(9140406996217703802)
XLA Ops:
  0.6 0.0 copy-start.3
  0.7 1.0 %copy-done.4 = bf16[3,1,256,256]{3,2,1,0:T(8,128)(2,1)S(1)} copy-done((bf16[3,1,256,256]{3,2,1,0:T(8,128)(2,1)S(1)}, bf16[3,1,256,256]{3,2,1,0:T(8,128)(2,1)}, u32[]{:S(2)}) %copy-start.4) | copy-done | bytes 393240
  1.7 0.7 %copy-done.5 = f32[16,256]{1,0:T(8,128)S(1)} copy-done((f32[16,256]{1,0:T(8,128)S(1)}, f32[16,256]{1,0:T(8,128)}, u32[]{:S(2)}) %copy-start.5) | copy-done | bytes 16408
  2.4 0.7 copy-done.6
  3.1 0.2 pack_signal.1
  3.3 3.1 %collective-permute-start.3 = (bf16[208,256]{1,0:T(8,128)(2,1)S(1)}, bf16[208,256]{1,0:T(8,128)(2,1)S(1)}, u32[]{:S(2)}, u32[]{:S(2)}) collective-permute-start(bf16[208,256]{1,0:T(8,128)(2,1)S(1)} %get-tuple-element.45), channel_id=1, source_target_pairs={{0,8},{8,16},{16,24},{24,0},{1,9},{9,17},{17,25},{25,1},{2,10},{10... | collective-permute-start | bytes 319496 | tf_op jit(solution)/shard_map/ppermute | solution.py:212
  6.3 1.0 %copy-done = bf16[256,1024]{1,0:T(8,128)(2,1)S(1)} copy-done((bf16[256,1024]{1,0:T(8,128)(2,1)S(1)}, bf16[256,1024]{1,0:T(8,128)(2,1)}, u32[]{:S(2)}) %copy-start) | copy-done | bytes 524312
  7.4 0.9 %copy-done.2 = bf16[1,256,256]{2,1,0:T(8,128)(2,1)S(1)} copy-done((bf16[1,256,256]{2,1,0:T(8,128)(2,1)S(1)}, bf16[1,256,256]{2,1,0:T(8,128)(2,1)}, u32[]{:S(2)}) %copy-start.2) | copy-done | bytes 131096
  8.3 0.1 pack_channels.1
  8.3 1.5 %collective-permute-start = (bf16[512,256]{1,0:T(8,128)(2,1)S(1)}, bf16[512,256]{1,0:T(8,128)(2,1)S(1)}, u32[]{:S(2)}, u32[]{:S(2)}) collective-permute-start(bf16[512,256]{1,0:T(8,128)(2,1)S(1)} %get-tuple-element.41), channel_id=1, source_target_pairs={{0,2},{2,4},{4,6},{6,0},{1,3},{3,5},{5,7},{7,1},{8,10},{10,12},{12... | collective-permute-start | bytes 786440 | tf_op jit(solution)/shard_map/ppermute | solution.py:212
  9.9 1.5 %collective-permute-start.1 = (bf16[512,256]{1,0:T(8,128)(2,1)S(1)}, bf16[512,256]{1,0:T(8,128)(2,1)S(1)}, u32[]{:S(2)}, u32[]{:S(2)}) collective-permute-start(bf16[512,256]{1,0:T(8,128)(2,1)S(1)} %get-tuple-element.42), channel_id=1, source_target_pairs={{0,4},{2,6},{4,0},{6,2},{1,5},{3,7},{5,1},{7,3},{8,12},{10,14},{12... | collective-permute-start | bytes 786440 | tf_op jit(solution)/shard_map/ppermute | solution.py:212
  11.4 1.4 %collective-permute-start.2 = (bf16[512,256]{1,0:T(8,128)(2,1)S(1)}, bf16[512,256]{1,0:T(8,128)(2,1)S(1)}, u32[]{:S(2)}, u32[]{:S(2)}) collective-permute-start(bf16[512,256]{1,0:T(8,128)(2,1)S(1)} %get-tuple-element.43), channel_id=1, source_target_pairs={{0,6},{2,0},{4,2},{6,4},{1,7},{3,1},{5,3},{7,5},{8,14},{10,8},{12,... | collective-permute-start | bytes 786440 | tf_op jit(solution)/shard_map/ppermute | solution.py:212
  12.8 2.6 %collective-permute-start.4 = (bf16[208,256]{1,0:T(8,128)(2,1)S(1)}, bf16[208,256]{1,0:T(8,128)(2,1)S(1)}, u32[]{:S(2)}, u32[]{:S(2)}) collective-permute-start(bf16[208,256]{1,0:T(8,128)(2,1)S(1)} %get-tuple-element.46), channel_id=1, source_target_pairs={{0,16},{8,24},{16,0},{24,8},{1,17},{9,25},{17,1},{25,9},{2,18},{10... | collective-permute-start | bytes 319496 | tf_op jit(solution)/shard_map/ppermute | solution.py:212
  15.4 0.0 collective-permute-done.3.rest_1_
  15.4 1.3 %collective-permute-start.5 = (bf16[208,256]{1,0:T(8,128)(2,1)S(1)}, bf16[208,256]{1,0:T(8,128)(2,1)S(1)}, u32[]{:S(2)}, u32[]{:S(2)}) collective-permute-start(bf16[208,256]{1,0:T(8,128)(2,1)S(1)} %get-tuple-element.47), channel_id=1, source_target_pairs={{0,24},{8,0},{16,8},{24,16},{1,25},{9,1},{17,9},{25,17},{2,26},{10... | collective-permute-start | bytes 319496 | tf_op jit(solution)/shard_map/ppermute | solution.py:212
  16.8 4.0 %collective-permute-done.4.rest_2_ = bf16[208,256]{1,0:T(8,128)(2,1)S(1)} collective-permute-done((bf16[208,256]{1,0:T(8,128)(2,1)S(1)}, bf16[208,256]{1,0:T(8,128)(2,1)S(1)}, u32[]{:S(2)}, u32[]{:S(2)}) %collective-permute-start.4) | collective-permute-done | bytes 106528 | tf_op jit(solution)/shard_map/ppermute | solution.py:212
  20.8 0.7 %copy-done.7 = f32[3,3,256]{2,1,0:T(4,128)S(1)} copy-done((f32[3,3,256]{2,1,0:T(4,128)S(1)}, f32[3,3,256]{2,1,0:T(4,128)}, u32[]{:S(2)}) %copy-start.7) | copy-done | bytes 9240
  21.5 1.3 %conv.1 = (bf16[64,256]{1,0:T(8,128)(2,1)S(1)}, bf16[64,256]{1,0:T(8,128)(2,1)S(1)}, bf16[64,256]{1,0:T(8,128)(2,1)S(1)}, bf16[64,256]{1,0:T(8,128)(2,1)S(1)}, f...) custom-call(f32[3,3,256]{2,1,0:T(4,128)S(1)} %copy-done.7, ...), custom_call_target="tpu_custom_call" | custom-call | flops 536870912 | bytes 4142080 | tf_op jit(solution)/shard_map/conv/pallas_call | solution.py:226
  22.7 1.8 %collective-permute-start.6 = (bf16[64,256]{1,0:T(8,128)(2,1)S(1)}, bf16[64,256]{1,0:T(8,128)(2,1)S(1)}, u32[]{:S(2)}, u32[]{:S(2)}) collective-permute-start(bf16[64,256]{1,0:T(8,128)(2,1)S(1)} %get-tuple-element.49), channel_id=1, source_target_pairs={{0,8},{8,16},{16,24},{24,0},{1,9},{9,17},{17,25},{25,1},{2,10},{10... | collective-permute-start | bytes 98312 | tf_op jit(solution)/shard_map/ppermute | solution.py:212
  24.5 2.4 %collective-permute-start.7 = (bf16[64,256]{1,0:T(8,128)(2,1)S(1)}, bf16[64,256]{1,0:T(8,128)(2,1)S(1)}, u32[]{:S(2)}, u32[]{:S(2)}) collective-permute-start(bf16[64,256]{1,0:T(8,128)(2,1)S(1)} %get-tuple-element.50), channel_id=1, source_target_pairs={{0,16},{8,24},{16,0},{24,8},{1,17},{9,25},{17,1},{25,9},{2,18},{10... | collective-permute-start | bytes 98312 | tf_op jit(solution)/shard_map/ppermute | solution.py:212
  26.9 1.9 %collective-permute-done.6.rest_4_ = bf16[64,256]{1,0:T(8,128)(2,1)S(1)} collective-permute-done((bf16[64,256]{1,0:T(8,128)(2,1)S(1)}, bf16[64,256]{1,0:T(8,128)(2,1)S(1)}, u32[]{:S(2)}, u32[]{:S(2)}) %collective-permute-start.6) | collective-permute-done | bytes 32800 | tf_op jit(solution)/shard_map/ppermute | solution.py:212
  28.7 1.7 %collective-permute-start.8 = (bf16[64,256]{1,0:T(8,128)(2,1)S(1)}, bf16[64,256]{1,0:T(8,128)(2,1)S(1)}, u32[]{:S(2)}, u32[]{:S(2)}) collective-permute-start(bf16[64,256]{1,0:T(8,128)(2,1)S(1)} %get-tuple-element.51), channel_id=1, source_target_pairs={{0,24},{8,0},{16,8},{24,16},{1,25},{9,1},{17,9},{25,17},{2,26},{10... | collective-permute-start | bytes 98312 | tf_op jit(solution)/shard_map/ppermute | solution.py:212
  30.4 2.2 %collective-permute-done.8.rest_6_ = bf16[64,256]{1,0:T(8,128)(2,1)S(1)} collective-permute-done((bf16[64,256]{1,0:T(8,128)(2,1)S(1)}, bf16[64,256]{1,0:T(8,128)(2,1)S(1)}, u32[]{:S(2)}, u32[]{:S(2)}) %collective-permute-start.8) | collective-permute-done | bytes 32800 | tf_op jit(solution)/shard_map/ppermute | solution.py:212
  32.7 0.0 collective-permute-done.rest_0_.rest_4_
  32.7 0.0 collective-permute-done.1.rest_1_.rest_5_
  32.7 0.0 collective-permute-done.2.rest_2_.rest_6_
  32.7 0.4 weight_grad.1
  33.1 0.1 collective-permute-start.19
  33.2 0.4 grad_y.1
  33.6 0.1 collective-permute-start.12
  33.6 4.0 %collective-permute-start.13 = (bf16[64,256]{1,0:T(8,128)(2,1)S(1)}, bf16[64,256]{1,0:T(8,128)(2,1)S(1)}, u32[]{:S(2)}, u32[]{:S(2)}) collective-permute-start(bf16[64,256]{1,0:T(8,128)(2,1)S(1)} %get-tuple-element.61), channel_id=1, source_target_pairs={{0,16},{8,24},{16,0},{24,8},{1,17},{9,25},{17,1},{25,9},{2,18},{10... | collective-permute-start | bytes 98312 | tf_op jit(solution)/shard_map/ppermute | solution.py:212
  37.6 0.0 collective-permute-start.14
  37.7 0.3 collective-permute-start.11
  38.0 0.0 collective-permute-done.19.other
  38.0 1.5 %collective-permute-start.10 = (bf16[256,256]{1,0:T(8,128)(2,1)S(1)}, bf16[256,256]{1,0:T(8,128)(2,1)S(1)}, u32[]{:S(2)}, u32[]{:S(2)}) collective-permute-start(bf16[256,256]{1,0:T(8,128)(2,1)S(1)} %get-tuple-element.52.rest_0_), channel_id=1, source_target_pairs={{0,4},{2,6},{4,0},{6,2},{1,5},{3,7},{5,1},{7,3},{8,12},{10,14},{12... | collective-permute-start | bytes 393224 | tf_op jit(solution)/shard_map/ppermute | solution.py:212
  39.5 0.1 core_sum.1
  39.6 0.0 collective-permute-done.12.rest_1_
  39.6 2.0 %collective-permute-start.20 = (bf16[32,1024]{1,0:T(8,128)(2,1)S(1)}, bf16[32,1024]{1,0:T(8,128)(2,1)S(1)}, u32[]{:S(2)}, u32[]{:S(2)}) collective-permute-start(bf16[32,1024]{1,0:T(8,128)(2,1)S(1)} %get-tuple-element.74), channel_id=1, source_target_pairs={{0,8},{8,16},{16,24},{24,0},{1,9},{9,17},{17,25},{25,1},{2,10},{10... | collective-permute-start | bytes 196616 | tf_op jit(solution)/shard_map/ppermute | solution.py:212
  41.7 0.0 collective-permute-done.13.rest_2_
  41.7 0.8 %collective-permute-start.21 = (bf16[32,1024]{1,0:T(8,128)(2,1)S(1)}, bf16[32,1024]{1,0:T(8,128)(2,1)S(1)}, u32[]{:S(2)}, u32[]{:S(2)}) collective-permute-start(bf16[32,1024]{1,0:T(8,128)(2,1)S(1)} %get-tuple-element.75), channel_id=1, source_target_pairs={{0,16},{8,24},{16,0},{24,8},{1,17},{9,25},{17,1},{25,9},{2,18},{10... | collective-permute-start | bytes 196616 | tf_op jit(solution)/shard_map/ppermute | solution.py:212
  42.5 2.4 %backward.1 = (bf16[224,256]{1,0:T(8,128)(2,1)S(1)}, bf16[224,256]{1,0:T(8,128)(2,1)S(1)}, bf16[224,256]{1,0:T(8,128)(2,1)S(1)}, bf16[224,256]{1,0:T(8,128)(2,1)S(1)}) custom-call(f32[3,64,1024]{2,1,0:T(8,128)S(1)} %get-tuple-element.53.conv, f32[64,1024]{1,0:T(8,128)S(1)} %get-tuple-element.54.long, bf16[192,1024]{1,0:T(8,128)(2,1)S(1)} %get-tuple-element.55.source, ...), custom_call_target="tpu_custom_call" | custom-call | flops 1073741824 | bytes 4165632 | tf_op jit(solution)/shard_map/backward/pallas_call | solution.py:226
  44.9 1.7 %collective-permute-start.15 = (bf16[224,256]{1,0:T(8,128)(2,1)S(1)}, bf16[224,256]{1,0:T(8,128)(2,1)S(1)}, u32[]{:S(2)}, u32[]{:S(2)}) collective-permute-start(bf16[224,256]{1,0:T(8,128)(2,1)S(1)} %get-tuple-element.64), channel_id=1, source_target_pairs={{0,8},{8,16},{16,24},{24,0},{1,9},{9,17},{17,25},{25,1},{2,10},{10... | collective-permute-start | bytes 344072 | tf_op jit(solution)/shard_map/ppermute | solution.py:212
  46.5 1.1 %collective-permute-start.16 = (bf16[224,256]{1,0:T(8,128)(2,1)S(1)}, bf16[224,256]{1,0:T(8,128)(2,1)S(1)}, u32[]{:S(2)}, u32[]{:S(2)}) collective-permute-start(bf16[224,256]{1,0:T(8,128)(2,1)S(1)} %get-tuple-element.65), channel_id=1, source_target_pairs={{0,16},{8,24},{16,0},{24,8},{1,17},{9,25},{17,1},{25,9},{2,18},{10... | collective-permute-start | bytes 344072 | tf_op jit(solution)/shard_map/ppermute | solution.py:212
  47.7 0.0 collective-permute-done.20.refs_1_
  47.7 2.3 %collective-permute-start.22 = (bf16[32,1024]{1,0:T(8,128)(2,1)S(1)}, bf16[32,1024]{1,0:T(8,128)(2,1)S(1)}, u32[]{:S(2)}, u32[]{:S(2)}) collective-permute-start(bf16[32,1024]{1,0:T(8,128)(2,1)S(1)} %get-tuple-element.76), channel_id=1, source_target_pairs={{0,24},{8,0},{16,8},{24,16},{1,25},{9,1},{17,9},{25,17},{2,26},{10... | collective-permute-start | bytes 196616 | tf_op jit(solution)/shard_map/ppermute | solution.py:212
  50.0 0.9 %collective-permute-start.17 = (bf16[224,256]{1,0:T(8,128)(2,1)S(1)}, bf16[224,256]{1,0:T(8,128)(2,1)S(1)}, u32[]{:S(2)}, u32[]{:S(2)}) collective-permute-start(bf16[224,256]{1,0:T(8,128)(2,1)S(1)} %get-tuple-element.66), channel_id=1, source_target_pairs={{0,24},{8,0},{16,8},{24,16},{1,25},{9,1},{17,9},{25,17},{2,26},{10... | collective-permute-start | bytes 344072 | tf_op jit(solution)/shard_map/ppermute | solution.py:212
  50.9 4.8 %collective-permute-done.22.refs_3_ = bf16[32,1024]{1,0:T(8,128)(2,1)S(1)} collective-permute-done((bf16[32,1024]{1,0:T(8,128)(2,1)S(1)}, bf16[32,1024]{1,0:T(8,128)(2,1)S(1)}, u32[]{:S(2)}, u32[]{:S(2)}) %collective-permute-start.22) | collective-permute-done | bytes 65568 | tf_op jit(solution)/shard_map/ppermute | solution.py:212
  55.7 0.4 collective-permute-start.9
  56.2 0.0 collective-permute-done.10.rest_2_
  56.2 1.8 %collective-permute-start.25 = (bf16[32,1024]{1,0:T(8,128)(2,1)S(1)}, bf16[32,1024]{1,0:T(8,128)(2,1)S(1)}, u32[]{:S(2)}, u32[]{:S(2)}) collective-permute-start(bf16[32,1024]{1,0:T(8,128)(2,1)S(1)} %block_sum.1.refs_0_), channel_id=1, source_target_pairs={{0,24},{8,0},{16,8},{24,16},{1,25},{9,1},{17,9},{25,17},{2,26},{10... | collective-permute-start | bytes 196616 | tf_op jit(solution)/shard_map/ppermute | solution.py:212
  58.0 1.9 %collective-permute-start.24 = (bf16[32,1024]{1,0:T(8,128)(2,1)S(1)}, bf16[32,1024]{1,0:T(8,128)(2,1)S(1)}, u32[]{:S(2)}, u32[]{:S(2)}) collective-permute-start(bf16[32,1024]{1,0:T(8,128)(2,1)S(1)} %block_sum.1.refs_0_), channel_id=1, source_target_pairs={{0,16},{8,24},{16,0},{24,8},{1,17},{9,25},{17,1},{25,9},{2,18},{10... | collective-permute-start | bytes 196616 | tf_op jit(solution)/shard_map/ppermute | solution.py:212
  59.8 0.0 collective-permute-start.23
  59.8 0.0 collective-permute-done.17.refs_3_
  59.8 0.1 collective-permute-start.26
  59.9 1.3 %collective-permute-done.25.refs_3_ = bf16[32,1024]{1,0:T(8,128)(2,1)S(1)} collective-permute-done((bf16[32,1024]{1,0:T(8,128)(2,1)S(1)}, bf16[32,1024]{1,0:T(8,128)(2,1)S(1)}, u32[]{:S(2)}, u32[]{:S(2)}) %collective-permute-start.25) | collective-permute-done | bytes 65568 | tf_op jit(solution)/shard_map/ppermute | solution.py:212
  61.2 0.0 collective-permute-start.29
  61.2 3.3 %collective-permute-done.24.refs_2_ = bf16[32,1024]{1,0:T(8,128)(2,1)S(1)} collective-permute-done((bf16[32,1024]{1,0:T(8,128)(2,1)S(1)}, bf16[32,1024]{1,0:T(8,128)(2,1)S(1)}, u32[]{:S(2)}, u32[]{:S(2)}) %collective-permute-start.24) | collective-permute-done | bytes 65568 | tf_op jit(solution)/shard_map/ppermute | solution.py:212
  64.5 0.0 collective-permute-start.28
  64.5 1.4 %collective-permute-done.23.refs_1_ = bf16[32,1024]{1,0:T(8,128)(2,1)S(1)} collective-permute-done((bf16[32,1024]{1,0:T(8,128)(2,1)S(1)}, bf16[32,1024]{1,0:T(8,128)(2,1)S(1)}, u32[]{:S(2)}, u32[]{:S(2)}) %collective-permute-start.23) | collective-permute-done | bytes 65568 | tf_op jit(solution)/shard_map/ppermute | solution.py:212
  65.9 0.9 %grad_out.1 = (bf16[3,256,256]{2,1,0:T(8,128)(2,1)}, f32[32,256]{1,0:T(8,128)S(1)}) custom-call(bf16[224,256]{1,0:T(8,128)(2,1)S(1)} %get-tuple-element.63.refs_0_, bf16[224,256]{1,0:T(8,128)(2,1)S(1)} %collective-permute-done.15.refs_1_, bf16[224,256]{1,0:T(8,128)(2,1)S(1)} %collective-permute-done.16.refs_2_, ...), custom_call_target="tpu_custom_call" | custom-call | bytes 884736 | tf_op jit(solution)/shard_map/grad_out/pallas_call | solution.py:226
  66.8 0.5 collective-permute-start.18
  67.3 1.0 %mixed.1 = bf16[256,256]{1,0:T(8,128)(2,1)} custom-call(bf16[256,1024]{1,0:T(8,128)(2,1)S(1)} %copy-done.1, bf16[256,256]{1,0:T(8,128)(2,1)S(1)} %get-tuple-element.52.rest_0_, bf16[256,256]{1,0:T(8,128)(2,1)S(1)} %collective-permute-done.9.rest_1_, bf16[256,256]{1,0:T(8,128)(2,1)S(1)} %collective-permute-done.10.rest_2_, ...), custom_call_target="tpu_custom_call" | custom-call | flops 134217728 | bytes 1966080 | tf_op jit(solution)/shard_map/mixed/pallas_call | solution.py:226
  68.4 0.6 small_out.1
  69.0 1.1 %weight_out.1 = f32[256,1024]{1,0:T(8,128)} custom-call(bf16[32,1024]{1,0:T(8,128)(2,1)S(1)} %block_sum.1.refs_0_, bf16[32,1024]{1,0:T(8,128)(2,1)S(1)} %collective-permute-done.23.refs_1_, bf16[32,1024]{1,0:T(8,128)(2,1)S(1)} %collective-permute-done.24.refs_2_, bf16[32,1024]{1,0:T(8,128)(2,1)S(1)} %collective-permute-done.25.refs_3_, ...), custom_call_target="tpu_custom_call" | custom-call | bytes 1572864 | tf_op jit(solution)/shard_map/weight_out/pallas_call | solution.py:226
  (24 shorter events, 0.1 us)
Async XLA Ops:
  0.6 32.0 %copy-start.3 = (bf16[1,256,256]{2,1,0:T(8,128)(2,1)S(1)}, bf16[1,256,256]{2,1,0:T(8,128)(2,1)}, u32[]{:S(2)}) copy-start(bf16[1,256,256]{2,1,0:T(8,128)(2,1)} %param.11) | copy-start | bytes 393220
  0.6 1.0 %copy-start.4 = (bf16[3,1,256,256]{3,2,1,0:T(8,128)(2,1)S(1)}, bf16[3,1,256,256]{3,2,1,0:T(8,128)(2,1)}, u32[]{:S(2)}) copy-start(bf16[3,1,256,256]{3,2,1,0:T(8,128)(2,1)} %param.6) | copy-start | bytes 1179652
  1.7 0.7 %copy-start.5 = (f32[16,256]{1,0:T(8,128)S(1)}, f32[16,256]{1,0:T(8,128)}, u32[]{:S(2)}) copy-start(f32[16,256]{1,0:T(8,128)} %filters.1) | copy-start | bytes 49156
  2.4 0.7 copy-start.6
  3.3 12.2 %collective-permute-start.3 = (bf16[208,256]{1,0:T(8,128)(2,1)S(1)}, bf16[208,256]{1,0:T(8,128)(2,1)S(1)}, u32[]{:S(2)}, u32[]{:S(2)}) collective-permute-start(bf16[208,256]{1,0:T(8,128)(2,1)S(1)} %get-tuple-element.45), channel_id=1, source_target_pairs={{0,8},{8,16},{16,24},{24,0},{1,9},{9,17},{17,25},{25,1},{2,10},{10... | collective-permute-start | bytes 319496 | tf_op jit(solution)/shard_map/ppermute | solution.py:212
  6.3 1.0 %copy-start = (bf16[256,1024]{1,0:T(8,128)(2,1)S(1)}, bf16[256,1024]{1,0:T(8,128)(2,1)}, u32[]{:S(2)}) copy-start(bf16[256,1024]{1,0:T(8,128)(2,1)} %weights.5) | copy-start | bytes 1572868
  7.4 0.9 %copy-start.2 = (bf16[1,256,256]{2,1,0:T(8,128)(2,1)S(1)}, bf16[1,256,256]{2,1,0:T(8,128)(2,1)}, u32[]{:S(2)}) copy-start(bf16[1,256,256]{2,1,0:T(8,128)(2,1)} %param.11) | copy-start | bytes 393220
  8.3 24.9 %copy-start.1 = (bf16[256,1024]{1,0:T(8,128)(2,1)S(1)}, bf16[256,1024]{1,0:T(8,128)(2,1)}, u32[]{:S(2)}) copy-start(bf16[256,1024]{1,0:T(8,128)(2,1)} %weights.5) | copy-start | bytes 1572868
  8.3 24.3 %collective-permute-start = (bf16[512,256]{1,0:T(8,128)(2,1)S(1)}, bf16[512,256]{1,0:T(8,128)(2,1)S(1)}, u32[]{:S(2)}, u32[]{:S(2)}) collective-permute-start(bf16[512,256]{1,0:T(8,128)(2,1)S(1)} %get-tuple-element.41), channel_id=1, source_target_pairs={{0,2},{2,4},{4,6},{6,0},{1,3},{3,5},{5,7},{7,1},{8,10},{10,12},{12... | collective-permute-start | bytes 786440 | tf_op jit(solution)/shard_map/ppermute | solution.py:212
  9.9 22.8 %collective-permute-start.1 = (bf16[512,256]{1,0:T(8,128)(2,1)S(1)}, bf16[512,256]{1,0:T(8,128)(2,1)S(1)}, u32[]{:S(2)}, u32[]{:S(2)}) collective-permute-start(bf16[512,256]{1,0:T(8,128)(2,1)S(1)} %get-tuple-element.42), channel_id=1, source_target_pairs={{0,4},{2,6},{4,0},{6,2},{1,5},{3,7},{5,1},{7,3},{8,12},{10,14},{12... | collective-permute-start | bytes 786440 | tf_op jit(solution)/shard_map/ppermute | solution.py:212
  11.4 21.3 %collective-permute-start.2 = (bf16[512,256]{1,0:T(8,128)(2,1)S(1)}, bf16[512,256]{1,0:T(8,128)(2,1)S(1)}, u32[]{:S(2)}, u32[]{:S(2)}) collective-permute-start(bf16[512,256]{1,0:T(8,128)(2,1)S(1)} %get-tuple-element.43), channel_id=1, source_target_pairs={{0,6},{2,0},{4,2},{6,4},{1,7},{3,1},{5,3},{7,5},{8,14},{10,8},{12,... | collective-permute-start | bytes 786440 | tf_op jit(solution)/shard_map/ppermute | solution.py:212
  12.8 7.9 %collective-permute-start.4 = (bf16[208,256]{1,0:T(8,128)(2,1)S(1)}, bf16[208,256]{1,0:T(8,128)(2,1)S(1)}, u32[]{:S(2)}, u32[]{:S(2)}) collective-permute-start(bf16[208,256]{1,0:T(8,128)(2,1)S(1)} %get-tuple-element.46), channel_id=1, source_target_pairs={{0,16},{8,24},{16,0},{24,8},{1,17},{9,25},{17,1},{25,9},{2,18},{10... | collective-permute-start | bytes 319496 | tf_op jit(solution)/shard_map/ppermute | solution.py:212
  15.4 5.3 %collective-permute-start.5 = (bf16[208,256]{1,0:T(8,128)(2,1)S(1)}, bf16[208,256]{1,0:T(8,128)(2,1)S(1)}, u32[]{:S(2)}, u32[]{:S(2)}) collective-permute-start(bf16[208,256]{1,0:T(8,128)(2,1)S(1)} %get-tuple-element.47), channel_id=1, source_target_pairs={{0,24},{8,0},{16,8},{24,16},{1,25},{9,1},{17,9},{25,17},{2,26},{10... | collective-permute-start | bytes 319496 | tf_op jit(solution)/shard_map/ppermute | solution.py:212
  20.8 0.7 %copy-start.7 = (f32[3,3,256]{2,1,0:T(4,128)S(1)}, f32[3,3,256]{2,1,0:T(4,128)}, u32[]{:S(2)}) copy-start(f32[3,3,256]{2,1,0:T(4,128)} %short_filter.1) | copy-start | bytes 27652
  22.7 6.0 %collective-permute-start.6 = (bf16[64,256]{1,0:T(8,128)(2,1)S(1)}, bf16[64,256]{1,0:T(8,128)(2,1)S(1)}, u32[]{:S(2)}, u32[]{:S(2)}) collective-permute-start(bf16[64,256]{1,0:T(8,128)(2,1)S(1)} %get-tuple-element.49), channel_id=1, source_target_pairs={{0,8},{8,16},{16,24},{24,0},{1,9},{9,17},{17,25},{25,1},{2,10},{10... | collective-permute-start | bytes 98312 | tf_op jit(solution)/shard_map/ppermute | solution.py:212
  24.5 5.9 %collective-permute-start.7 = (bf16[64,256]{1,0:T(8,128)(2,1)S(1)}, bf16[64,256]{1,0:T(8,128)(2,1)S(1)}, u32[]{:S(2)}, u32[]{:S(2)}) collective-permute-start(bf16[64,256]{1,0:T(8,128)(2,1)S(1)} %get-tuple-element.50), channel_id=1, source_target_pairs={{0,16},{8,24},{16,0},{24,8},{1,17},{9,25},{17,1},{25,9},{2,18},{10... | collective-permute-start | bytes 98312 | tf_op jit(solution)/shard_map/ppermute | solution.py:212
  28.7 3.9 %collective-permute-start.8 = (bf16[64,256]{1,0:T(8,128)(2,1)S(1)}, bf16[64,256]{1,0:T(8,128)(2,1)S(1)}, u32[]{:S(2)}, u32[]{:S(2)}) collective-permute-start(bf16[64,256]{1,0:T(8,128)(2,1)S(1)} %get-tuple-element.51), channel_id=1, source_target_pairs={{0,24},{8,0},{16,8},{24,16},{1,25},{9,1},{17,9},{25,17},{2,26},{10... | collective-permute-start | bytes 98312 | tf_op jit(solution)/shard_map/ppermute | solution.py:212
  33.1 4.9 %collective-permute-start.19 = (f32[128,1024]{1,0:T(8,128)S(1)}, f32[128,1024]{1,0:T(8,128)S(1)}, u32[]{:S(2)}, u32[]{:S(2)}) collective-permute-start(f32[128,1024]{1,0:T(8,128)S(1)} %get-tuple-element.72), channel_id=1, source_target_pairs={{0,1},{1,0},{2,3},{3,2},{4,5},{5,4},{6,7},{7,6},{8,9},{9,8},{10,11... | collective-permute-start | bytes 1572872 | tf_op jit(solution)/shard_map/ppermute | solution.py:212
  33.6 6.1 %collective-permute-start.12 = (bf16[64,256]{1,0:T(8,128)(2,1)S(1)}, bf16[64,256]{1,0:T(8,128)(2,1)S(1)}, u32[]{:S(2)}, u32[]{:S(2)}) collective-permute-start(bf16[64,256]{1,0:T(8,128)(2,1)S(1)} %get-tuple-element.60), channel_id=1, source_target_pairs={{0,8},{8,16},{16,24},{24,0},{1,9},{9,17},{17,25},{25,1},{2,10},{10... | collective-permute-start | bytes 98312 | tf_op jit(solution)/shard_map/ppermute | solution.py:212
  33.6 8.0 %collective-permute-start.13 = (bf16[64,256]{1,0:T(8,128)(2,1)S(1)}, bf16[64,256]{1,0:T(8,128)(2,1)S(1)}, u32[]{:S(2)}, u32[]{:S(2)}) collective-permute-start(bf16[64,256]{1,0:T(8,128)(2,1)S(1)} %get-tuple-element.61), channel_id=1, source_target_pairs={{0,16},{8,24},{16,0},{24,8},{1,17},{9,25},{17,1},{25,9},{2,18},{10... | collective-permute-start | bytes 98312 | tf_op jit(solution)/shard_map/ppermute | solution.py:212
  37.6 4.8 %collective-permute-start.14 = (bf16[64,256]{1,0:T(8,128)(2,1)S(1)}, bf16[64,256]{1,0:T(8,128)(2,1)S(1)}, u32[]{:S(2)}, u32[]{:S(2)}) collective-permute-start(bf16[64,256]{1,0:T(8,128)(2,1)S(1)} %get-tuple-element.62), channel_id=1, source_target_pairs={{0,24},{8,0},{16,8},{24,16},{1,25},{9,1},{17,9},{25,17},{2,26},{10... | collective-permute-start | bytes 98312 | tf_op jit(solution)/shard_map/ppermute | solution.py:212
  37.7 8.9 %collective-permute-start.11 = (bf16[256,256]{1,0:T(8,128)(2,1)S(1)}, bf16[256,256]{1,0:T(8,128)(2,1)S(1)}, u32[]{:S(2)}, u32[]{:S(2)}) collective-permute-start(bf16[256,256]{1,0:T(8,128)(2,1)S(1)} %get-tuple-element.52.rest_0_), channel_id=1, source_target_pairs={{0,6},{2,0},{4,2},{6,4},{1,7},{3,1},{5,3},{7,5},{8,14},{10,8},{12,... | collective-permute-start | bytes 393224 | tf_op jit(solution)/shard_map/ppermute | solution.py:212
  38.0 18.2 %collective-permute-start.10 = (bf16[256,256]{1,0:T(8,128)(2,1)S(1)}, bf16[256,256]{1,0:T(8,128)(2,1)S(1)}, u32[]{:S(2)}, u32[]{:S(2)}) collective-permute-start(bf16[256,256]{1,0:T(8,128)(2,1)S(1)} %get-tuple-element.52.rest_0_), channel_id=1, source_target_pairs={{0,4},{2,6},{4,0},{6,2},{1,5},{3,7},{5,1},{7,3},{8,12},{10,14},{12... | collective-permute-start | bytes 393224 | tf_op jit(solution)/shard_map/ppermute | solution.py:212
  39.6 8.0 %collective-permute-start.20 = (bf16[32,1024]{1,0:T(8,128)(2,1)S(1)}, bf16[32,1024]{1,0:T(8,128)(2,1)S(1)}, u32[]{:S(2)}, u32[]{:S(2)}) collective-permute-start(bf16[32,1024]{1,0:T(8,128)(2,1)S(1)} %get-tuple-element.74), channel_id=1, source_target_pairs={{0,8},{8,16},{16,24},{24,0},{1,9},{9,17},{17,25},{25,1},{2,10},{10... | collective-permute-start | bytes 196616 | tf_op jit(solution)/shard_map/ppermute | solution.py:212
  41.7 8.3 %collective-permute-start.21 = (bf16[32,1024]{1,0:T(8,128)(2,1)S(1)}, bf16[32,1024]{1,0:T(8,128)(2,1)S(1)}, u32[]{:S(2)}, u32[]{:S(2)}) collective-permute-start(bf16[32,1024]{1,0:T(8,128)(2,1)S(1)} %get-tuple-element.75), channel_id=1, source_target_pairs={{0,16},{8,24},{16,0},{24,8},{1,17},{9,25},{17,1},{25,9},{2,18},{10... | collective-permute-start | bytes 196616 | tf_op jit(solution)/shard_map/ppermute | solution.py:212
  44.9 13.1 %collective-permute-start.15 = (bf16[224,256]{1,0:T(8,128)(2,1)S(1)}, bf16[224,256]{1,0:T(8,128)(2,1)S(1)}, u32[]{:S(2)}, u32[]{:S(2)}) collective-permute-start(bf16[224,256]{1,0:T(8,128)(2,1)S(1)} %get-tuple-element.64), channel_id=1, source_target_pairs={{0,8},{8,16},{16,24},{24,0},{1,9},{9,17},{17,25},{25,1},{2,10},{10... | collective-permute-start | bytes 344072 | tf_op jit(solution)/shard_map/ppermute | solution.py:212
  46.5 13.3 %collective-permute-start.16 = (bf16[224,256]{1,0:T(8,128)(2,1)S(1)}, bf16[224,256]{1,0:T(8,128)(2,1)S(1)}, u32[]{:S(2)}, u32[]{:S(2)}) collective-permute-start(bf16[224,256]{1,0:T(8,128)(2,1)S(1)} %get-tuple-element.65), channel_id=1, source_target_pairs={{0,16},{8,24},{16,0},{24,8},{1,17},{9,25},{17,1},{25,9},{2,18},{10... | collective-permute-start | bytes 344072 | tf_op jit(solution)/shard_map/ppermute | solution.py:212
  47.7 8.1 %collective-permute-start.22 = (bf16[32,1024]{1,0:T(8,128)(2,1)S(1)}, bf16[32,1024]{1,0:T(8,128)(2,1)S(1)}, u32[]{:S(2)}, u32[]{:S(2)}) collective-permute-start(bf16[32,1024]{1,0:T(8,128)(2,1)S(1)} %get-tuple-element.76), channel_id=1, source_target_pairs={{0,24},{8,0},{16,8},{24,16},{1,25},{9,1},{17,9},{25,17},{2,26},{10... | collective-permute-start | bytes 196616 | tf_op jit(solution)/shard_map/ppermute | solution.py:212
  50.0 9.8 %collective-permute-start.17 = (bf16[224,256]{1,0:T(8,128)(2,1)S(1)}, bf16[224,256]{1,0:T(8,128)(2,1)S(1)}, u32[]{:S(2)}, u32[]{:S(2)}) collective-permute-start(bf16[224,256]{1,0:T(8,128)(2,1)S(1)} %get-tuple-element.66), channel_id=1, source_target_pairs={{0,24},{8,0},{16,8},{24,16},{1,25},{9,1},{17,9},{25,17},{2,26},{10... | collective-permute-start | bytes 344072 | tf_op jit(solution)/shard_map/ppermute | solution.py:212
  55.7 11.1 %collective-permute-start.9 = (bf16[256,256]{1,0:T(8,128)(2,1)S(1)}, bf16[256,256]{1,0:T(8,128)(2,1)S(1)}, u32[]{:S(2)}, u32[]{:S(2)}) collective-permute-start(bf16[256,256]{1,0:T(8,128)(2,1)S(1)} %get-tuple-element.52.rest_0_), channel_id=1, source_target_pairs={{0,2},{2,4},{4,6},{6,0},{1,3},{3,5},{5,7},{7,1},{8,10},{10,12},{12... | collective-permute-start | bytes 393224 | tf_op jit(solution)/shard_map/ppermute | solution.py:212
  56.2 5.0 %collective-permute-start.25 = (bf16[32,1024]{1,0:T(8,128)(2,1)S(1)}, bf16[32,1024]{1,0:T(8,128)(2,1)S(1)}, u32[]{:S(2)}, u32[]{:S(2)}) collective-permute-start(bf16[32,1024]{1,0:T(8,128)(2,1)S(1)} %block_sum.1.refs_0_), channel_id=1, source_target_pairs={{0,24},{8,0},{16,8},{24,16},{1,25},{9,1},{17,9},{25,17},{2,26},{10... | collective-permute-start | bytes 196616 | tf_op jit(solution)/shard_map/ppermute | solution.py:212
  58.0 6.6 %collective-permute-start.24 = (bf16[32,1024]{1,0:T(8,128)(2,1)S(1)}, bf16[32,1024]{1,0:T(8,128)(2,1)S(1)}, u32[]{:S(2)}, u32[]{:S(2)}) collective-permute-start(bf16[32,1024]{1,0:T(8,128)(2,1)S(1)} %block_sum.1.refs_0_), channel_id=1, source_target_pairs={{0,16},{8,24},{16,0},{24,8},{1,17},{9,25},{17,1},{25,9},{2,18},{10... | collective-permute-start | bytes 196616 | tf_op jit(solution)/shard_map/ppermute | solution.py:212
  59.8 6.1 %collective-permute-start.23 = (bf16[32,1024]{1,0:T(8,128)(2,1)S(1)}, bf16[32,1024]{1,0:T(8,128)(2,1)S(1)}, u32[]{:S(2)}, u32[]{:S(2)}) collective-permute-start(bf16[32,1024]{1,0:T(8,128)(2,1)S(1)} %block_sum.1.refs_0_), channel_id=1, source_target_pairs={{0,8},{8,16},{16,24},{24,0},{1,9},{9,17},{17,25},{25,1},{2,10},{10... | collective-permute-start | bytes 196616 | tf_op jit(solution)/shard_map/ppermute | solution.py:212
  59.8 9.1 %collective-permute-start.26 = (bf16[32,1024]{1,0:T(8,128)(2,1)S(1)}, bf16[32,1024]{1,0:T(8,128)(2,1)S(1)}, u32[]{:S(2)}, u32[]{:S(2)}) collective-permute-start(bf16[32,1024]{1,0:T(8,128)(2,1)S(1)} %block_sum.1.refs_0_), channel_id=1, source_target_pairs={{0,1},{1,0},{2,3},{3,2},{4,5},{5,4},{6,7},{7,6},{8,9},{9,8},{10,11... | collective-permute-start | bytes 196616 | tf_op jit(solution)/shard_map/ppermute | solution.py:212
  61.2 7.8 %collective-permute-start.29 = (bf16[32,1024]{1,0:T(8,128)(2,1)S(1)}, bf16[32,1024]{1,0:T(8,128)(2,1)S(1)}, u32[]{:S(2)}, u32[]{:S(2)}) collective-permute-start(bf16[32,1024]{1,0:T(8,128)(2,1)S(1)} %collective-permute-done.25.refs_3_), channel_id=1, source_target_pairs={{0,1},{1,0},{2,3},{3,2},{4,5},{5,4},{6,7},{7,6},{8,9},{9,8},{10,11... | collective-permute-start | bytes 196616 | tf_op jit(solution)/shard_map/ppermute | solution.py:212
  64.5 4.5 %collective-permute-start.28 = (bf16[32,1024]{1,0:T(8,128)(2,1)S(1)}, bf16[32,1024]{1,0:T(8,128)(2,1)S(1)}, u32[]{:S(2)}, u32[]{:S(2)}) collective-permute-start(bf16[32,1024]{1,0:T(8,128)(2,1)S(1)} %collective-permute-done.24.refs_2_), channel_id=1, source_target_pairs={{0,1},{1,0},{2,3},{3,2},{4,5},{5,4},{6,7},{7,6},{8,9},{9,8},{10,11... | collective-permute-start | bytes 196616 | tf_op jit(solution)/shard_map/ppermute | solution.py:212
  65.9 3.1 %collective-permute-start.27 = (bf16[32,1024]{1,0:T(8,128)(2,1)S(1)}, bf16[32,1024]{1,0:T(8,128)(2,1)S(1)}, u32[]{:S(2)}, u32[]{:S(2)}) collective-permute-start(bf16[32,1024]{1,0:T(8,128)(2,1)S(1)} %collective-permute-done.23.refs_1_), channel_id=1, source_target_pairs={{0,1},{1,0},{2,3},{3,2},{4,5},{5,4},{6,7},{7,6},{8,9},{9,8},{10,11... | collective-permute-start | bytes 196616 | tf_op jit(solution)/shard_map/ppermute | solution.py:212
  66.8 1.5 %collective-permute-start.18 = (f32[32,256]{1,0:T(8,128)S(1)}, f32[32,256]{1,0:T(8,128)S(1)}, u32[]{:S(2)}, u32[]{:S(2)}) collective-permute-start(f32[32,256]{1,0:T(8,128)S(1)} %get-tuple-element.68.mine), channel_id=1, source_target_pairs={{0,1},{1,0},{2,3},{3,2},{4,5},{5,4},{6,7},{7,6},{8,9},{9,8},{10,11... | collective-permute-start | bytes 98312 | tf_op jit(solution)/shard_map/ppermute | solution.py:212
where the time goes:
time: 70.4 us; the launch traced here: 70 us
  starting transfers between devices  36.8 us (52%)
  waiting for transfers between devices  19 us (27%)
  Pallas kernels  8.39 us (12%)
  local copies, waits for them, and re-layouts  5.08 us (7%)
  between operations  0.79 us (1%)
    ppermute x30, starting transfers between devices, rotate(): lax.ppermute(value, axis, [(i, (i + steps) % count) for i in range(count)])  36.8 us
    ppermute x30, waiting for transfers between devices, rotate(): lax.ppermute(value, axis, [(i, (i + steps) % count) for i in range(count)])  19 us
    pallas_call x12, Pallas kernels, on_core(): pl.pallas_call(kernel, out_shape=[jax.ShapeDtypeStruct(shape, kind) for s...  8.39 us
    unnamed x16, local copies, waits for them, and re-layouts  5.08 us
  transfers between devices with their start and end apart: 30, of which 7 were waited for; matrix products, arithmetic and copies ran while one was open for 0% of the time, Pallas kernels for 10%

commit v1 on v0

--- a/solution.py
+++ b/solution.py
@@ -212,22 +212,31 @@
     return lax.ppermute(value, axis, [(i, (i + steps) % count) for i in range(count)])
 
 
+def swap(value, axis, bits):
+    return lax.ppermute(value, axis, [(i, i ^ bits) for i in range(lax.axis_size(axis))])
+
+
 def scatter_chunks(chunks, axis):
     return [chunks[0]] + [rotate(chunks[s], axis, s) for s in range(1, len(chunks))]
 
 
+def after(value, other):
+    return lax.optimization_barrier((value, other))[0]
+
+
 def spread(value, axis):
     return [value] + [rotate(value, axis, s) for s in range(1, lax.axis_size(axis))]
 
 
-def on_core(kernel, outs, args, name, scratch=(), flops=0):
+def on_core(kernel, outs, args, name, scratch=(), flops=0, whole=False):
     moved = sum(a.size * a.dtype.itemsize for a in args)
     moved += sum(math.prod(shape) * jnp.dtype(kind).itemsize for shape, kind in outs)
     return pl.pallas_call(
         kernel,
         out_shape=[jax.ShapeDtypeStruct(shape, kind) for shape, kind in outs],
+        in_specs=[pl.BlockSpec(memory_space=pltpu.HBM) if whole else pl.BlockSpec()] * len(args),
         scratch_shapes=list(scratch),
-        compiler_params=pltpu.CompilerParams(vmem_limit_bytes=48 * 1024 * 1024),
+        compiler_params=pltpu.CompilerParams(vmem_limit_bytes=(63 if whole else 40) * 1024 * 1024),
         cost_estimate=pl.CostEstimate(flops=flops, bytes_accessed=moved, transcendentals=0),
         name=name,
     )(*args)
@@ -237,46 +246,51 @@
     return pl.ds(pl.multiple_of(index * size, size), size)
 
 
-def pack_signal_kernel(devices, projected, filters, segments, *rest):
-    outs, (turned, small) = rest[:devices], rest[devices:]
+def pack_kernel(devices, *refs):
+    sources, refs = refs[:3], refs[3:]
+    outs, query, refs = refs[:devices], refs[devices], refs[devices + 1 :]
+    held, (turned, small, sems) = refs[:3], refs[3:]
+    copies = [
+        pltpu.make_async_copy(sources[n], held[n], sems.at[n]) for n in range(len(sources))
+    ]
+    for copy in copies:
+        copy.start()
+    projected, filters, segments = held
     me = lax.axis_index("ctx")
-    stacked, _, width = projected.shape
+    stacked, rows, width = projected.shape
     chunk = width // devices
-    groups = filters.shape[0] // devices
-    for i in range(stacked):
-        turned[i] = projected[i].T
+    count = filters.shape[0]
+    groups = count // devices
+    for copy in copies:
+        copy.wait()
+    for i in range(1, stacked):
+        turned[i - 1] = projected[i].T
+    query[...] = projected[0].T
     small[...] = jnp.zeros_like(small)
     seg = segments[...]
     small[2 * groups : 2 * groups + 1] = (seg >> 8).astype(f32)
     small[2 * groups + 1 : 2 * groups + 2] = (seg & 255).astype(f32)
+    body = (stacked - 1) * chunk
     for s in range(devices):
         to = lax.rem(me + s, devices)
-        for i in range(stacked):
+        for i in range(stacked - 1):
             outs[s][i * chunk : (i + 1) * chunk] = turned[i, block_at(to, chunk)]
-        count = groups * devices
-        taps = pltpu.roll(filters[...], lax.rem(count - to * groups, count), 0)[0:groups]
-        high = taps.astype(bf16).astype(f32)
+        lines = pltpu.roll(filters[...], lax.rem(count - to * groups, count), 0)[0:groups]
+        high = lines.astype(bf16).astype(f32)
         small[0:groups] = high
-        small[groups : 2 * groups] = taps - high
-        outs[s][stacked * chunk :] = small[...].astype(bf16)
-
-
-def pack_channels_kernel(parts, cotangent, weights, *outs):
-    me = lax.axis_index("tp")
-    rows, width = cotangent.shape
-    for s in range(1, parts):
-        to = lax.rem(me + s, parts)
-        outs[s - 1][0:rows] = cotangent[...]
-        outs[s - 1][rows:] = weights[:, block_at(to, width)]
-
-
-def tap_columns(short_filter, flat, columns, me, chunk):
+        small[groups : 2 * groups] = lines - high
+        outs[s][body : body + 16] = small[...].astype(bf16)
+    outs[1][body + 16 :] = projected[0, rows - 16 :]
+
+
+def prepare_kernel(short_filter, chunk, query, columns, chunk_out, query_out, flat):
     stacked, taps, _ = short_filter.shape
     flat[...] = jnp.zeros_like(flat)
     for i in range(stacked):
         flat[i * taps : (i + 1) * taps] = short_filter[i]
     columns[...] = flat[...].T
-    return columns[block_at(me, chunk)]
+    chunk_out[...] = chunk[...]
+    query_out[...] = query[...]
 
 
 def tap_masks(seg, taps):
@@ -289,13 +303,26 @@
     return masks
 
 
-def conv_kernel(devices, short_filter, *rest):
+def block_masks(seg, taps, place, me, length):
+    masks = tap_masks(seg, taps)
+    for s in range(1, taps):
+        place[8 * s : 8 * (s + 1)] = jnp.broadcast_to(masks[s], (8, seg.shape[1]))
+    return [None] + [place[8 * s : 8 * s + 8, block_at(me, length)][0:1] for s in range(1, taps)]
+
+
+def query_shifts(query, previous, taps):
+    halo = previous[previous.shape[0] - 16 :]
+    before = jnp.concatenate([jnp.zeros((SUB - 16, halo.shape[1]), f32), halo.astype(f32)], axis=0)
+    wide = jnp.concatenate([before.T, query.astype(f32)], axis=1)
+    return [wide[:, SUB:]] + [pltpu.roll(wide, s, 1)[:, SUB:] for s in range(1, taps)]
+
+
+def conv_kernel(devices, taps, columns, *rest):
     pays, rest = rest[:devices], rest[devices:]
-    y_outs, rest = rest[:devices], rest[devices:]
-    conv, long, source, seg_out, columns_out, toeplitz, small, flat, columns, y_full = rest
+    outs, rest = rest[:devices], rest[devices:]
+    conv, source, seg_out, toeplitz, small, long, rests = rest
     me = lax.axis_index("ctx")
-    stacked, taps, _ = short_filter.shape
-    _, chunk, span = conv.shape
+    stacked, chunk, span = conv.shape
     length = span // devices
     groups = toeplitz.shape[0]
     size = chunk // groups
@@ -303,31 +330,31 @@
     for s in range(devices):
         at = block_at(lax.rem(me - s + devices, devices), length)
         source[:, at] = pays[s][0:body]
-        small[:, at] = pays[s][body:].astype(f32)
+        small[:, at] = pays[s][body : body + 16].astype(f32)
     seg = small[2 * groups : 2 * groups + 1] * 256.0 + small[2 * groups + 1 : 2 * groups + 2]
     seg_out[...] = jnp.broadcast_to(seg, seg_out.shape)
     masks = tap_masks(seg, taps)
-    column = tap_columns(short_filter, flat, columns, me, chunk)
-    columns_out[...] = column
+    column = columns[block_at(me, chunk)]
     for i in range(stacked):
         x = source[i * chunk : (i + 1) * chunk].astype(f32)
-        total = column[:, i * taps : i * taps + 1] * x
+        j = (i + 1) * taps
+        total = column[:, j : j + 1] * x
         for s in range(1, taps):
-            j = i * taps + s
-            total += column[:, j : j + 1] * (masks[s] * pltpu.roll(x, s, 1))
+            total += column[:, j + s : j + s + 1] * (masks[s] * pltpu.roll(x, s, 1))
         conv[i] = total
-    high, low = split_bf16(conv[1] * conv[2])
+    high, low = split_bf16(conv[0] * conv[1])
     for g in range(groups):
         line = small[g : g + 1] + small[groups + g : groups + g + 1]
         padded = jnp.concatenate([line, jnp.zeros((1, SUB), f32)], axis=1)
         turned = pltpu.roll(
             jnp.broadcast_to(padded, (SUB, span + SUB)), 0, 1, stride=1, stride_axis=0
-        )[:, :span].astype(bf16)
-        for r in range(length // SUB):
-            rows = slice(r * SUB, (r + 1) * SUB)
-            if r:
-                toeplitz[g, rows, : r * SUB] = jnp.zeros((SUB, r * SUB), bf16)
-            toeplitz[g, rows, r * SUB :] = turned[:, : span - r * SUB]
+        )[:, :span]
+        for half, into in zip(split_bf16(turned), (toeplitz, rests)):
+            for r in range(length // SUB):
+                rows = slice(r * SUB, (r + 1) * SUB)
+                if r:
+                    into[g, rows, : r * SUB] = jnp.zeros((SUB, r * SUB), bf16)
+                into[g, rows, r * SUB :] = half[:, : span - r * SUB]
         own = slice(g * size, (g + 1) * size)
         pieces = []
         for j in range(devices):
@@ -336,56 +363,66 @@
         stack = jnp.concatenate(pieces, axis=0)
         totals = [None] * devices
         for lag in range(devices):
-            part = jnp.dot(
-                stack[: 2 * size * (devices - lag)],
-                toeplitz[g, :, lag * length : (lag + 1) * length],
-                preferred_element_type=f32,
-            )
+            lhs = stack[: 2 * size * (devices - lag)]
+            at = slice(lag * length, (lag + 1) * length)
+            part = jnp.dot(lhs, toeplitz[g, :, at], preferred_element_type=f32)
+            part += jnp.dot(lhs, rests[g, :, at], preferred_element_type=f32)
             for j in range(devices - lag):
                 term = part[2 * size * j : 2 * size * j + size]
                 term += part[2 * size * j + size : 2 * size * (j + 1)]
                 i = j + lag
                 totals[i] = term if totals[i] is None else totals[i] + term
         for i in range(devices):
-            long[own, i * length : (i + 1) * length] = totals[i]
-    y_full[...] = (conv[0] * long[...]).astype(bf16)
-    for s in range(devices):
-        y_outs[s][...] = y_full[:, block_at(lax.rem(me + s, devices), length)]
-
-
-def grad_y_kernel(devices, parts, weights, cotangent, *rest):
-    pays, rest = rest[: parts - 1], rest[parts - 1 :]
-    outs, (full,) = rest[:devices], rest[devices:]
+            long[own, i * length : (i + 1) * length] = totals[i].astype(bf16)
+    for s in range(devices):
+        outs[s][...] = long[:, block_at(lax.rem(me + s, devices), length)]
+
+
+def grad_y_kernel(devices, parts, taps, weights, query, previous, columns, seg, *rest):
+    cots, rest = rest[:parts], rest[parts:]
+    longs, rest = rest[:devices], rest[devices:]
+    outs, (grad_y, query_conv, place, full) = rest[:devices], rest[devices:]
     me, mine = lax.axis_index("ctx"), lax.axis_index("tp")
-    rows, width = cotangent.shape
+    rows, width = cots[0].shape
     chunk = width // devices
+    masks = block_masks(seg[0:1], taps, place, me, rows)
+    shifts = query_shifts(query[...], previous, taps)
+    conv = columns[:, 0:1] * shifts[0]
+    for s in range(1, taps):
+        conv += columns[:, s : s + 1] * (masks[s] * shifts[s])
+    query_conv[...] = conv
     total = None
     for s in range(parts):
-        cot = cotangent[...] if s == 0 else pays[s - 1][0:rows]
-        lhs = weights[:, block_at(lax.rem(mine - s + parts, parts), width)]
+        cot = cots[s][...]
+        lhs = weights[:, block_at(mine ^ s, width)]
         term = lax.dot_general(lhs, cot, (((1,), (1,)), ((), ())), preferred_element_type=f32)
         total = term if total is None else total + term
-    full[...] = total
-    for s in range(devices):
-        outs[s][...] = full[block_at(lax.rem(me + s, devices), chunk)].astype(outs[s].dtype)
-
-
-def weight_grad_kernel(devices, parts, cotangent, *rest):
-    pays, rest = rest[: parts - 1], rest[parts - 1 :]
-    ys, (y_out, keep, send, full) = rest[:devices], rest[devices:]
+    grad_y[...] = total
+    full[...] = (total * conv).astype(bf16)
+    for s in range(devices):
+        outs[s][0:chunk] = longs[s][...]
+        outs[s][chunk:] = full[block_at(lax.rem(me + s, devices), chunk)]
+
+
+def weight_grad_kernel(devices, parts, query_conv, *rest):
+    cots, rest = rest[:parts], rest[parts:]
+    longs, rest = rest[:devices], rest[devices:]
+    y_out, long_out, keep, send, full = rest
     me, mine, core = lax.axis_index("ctx"), lax.axis_index("tp"), lax.axis_index("dp")
-    rows, width = cotangent.shape
+    rows, width = cots[0].shape
     chunk = width // devices
     half = width // 2
     for s in range(devices):
-        y_out[block_at(lax.rem(me - s + devices, devices), chunk)] = ys[s][...]
-    y = y_out[...]
+        at = block_at(lax.rem(me - s + devices, devices), chunk)
+        long_out[at] = longs[s][0:chunk].astype(f32)
+    y = (query_conv[...] * long_out[...]).astype(bf16)
+    y_out[...] = y
     for s in range(parts):
-        cot = cotangent[...] if s == 0 else pays[s - 1][0:rows]
-        at = block_at(lax.rem(mine - s + parts, parts), width)
+        cot = cots[s][...]
+        at = block_at(mine ^ s, width)
         full[:, at] = jnp.dot(y, cot, preferred_element_type=f32)
     keep[...] = full[block_at(core, half)]
-    send[...] = full[block_at(1 - core, half)].astype(send.dtype)
+    send[...] = full[block_at(1 - core, half)]
 
 
 def core_sum_kernel(devices, keep, other, *rest):
@@ -398,56 +435,85 @@
         outs[s][...] = full[at].astype(outs[s].dtype)
 
 
-def block_sum_kernel(scale, *refs):
+def block_sum_kernel(devices, scale, *refs):
+    sums, refs = refs[:devices], refs[devices:]
+    pays, outs = refs[:devices], refs[devices:]
+    total = sums[0][...]
+    for s in range(1, devices):
+        total += sums[s][...].astype(f32)
+    total = (total * scale).astype(bf16)
+    rows, width = total.shape[0], outs[0].shape[1]
+    blocks = total.shape[1] // width
+    for s in range(devices):
+        for b in range(blocks):
+            outs[s][b * rows : (b + 1) * rows] = total[:, b * width : (b + 1) * width]
+        outs[s][blocks * rows :] = pays[s][...]
+
+
+def weight_out_kernel(devices, near, far, out):
+    core = lax.axis_index("dp")
+    half = near.shape[0]
+    out[block_at(core, half)] = near[...].astype(f32)
+    out[block_at(1 - core, half)] = far[...].astype(f32)
+
+
+def mixed_part_kernel(parts, y, weights, *rest):
+    outs, (full,) = rest[:parts], rest[parts:]
+    mine = lax.axis_index("tp")
+    width = outs[0].shape[1]
+    full[...] = lax.dot_general(
+        y[...], weights[...], (((0,), (0,)), ((), ())), preferred_element_type=f32
+    )
+    for s in range(parts):
+        outs[s][...] = full[:, block_at(mine ^ s, width)].astype(outs[s].dtype)
+
+
+def mixed_sum_kernel(*refs):
     total = refs[0][...]
     for ref in refs[1:-1]:
         total += ref[...].astype(f32)
-    refs[-1][...] = (total * scale).astype(refs[-1].dtype)
-
-
-def weight_out_kernel(devices, *refs):
-    out = refs[-1]
-    me, core = lax.axis_index("ctx"), lax.axis_index("dp")
-    rows = out.shape[0] // (2 * devices)
-    for h in range(2):
-        side = core if h == 0 else 1 - core
-        for s in range(devices):
-            block = side * devices + lax.rem(me - s + devices, devices)
-            out[block_at(block, rows)] = refs[h * devices + s][...].astype(f32)
-
-
-def mixed_kernel(parts, weights, *rest):
-    ys, pays, out = rest[:parts], rest[parts:-1], rest[-1]
-    mine = lax.axis_index("tp")
-    rows, width = out.shape
-    total = None
-    for s in range(parts):
-        w = weights[:, block_at(mine, width)] if s == 0 else pays[s - 1][rows:]
-        term = lax.dot_general(
-            ys[s][...], w, (((0,), (0,)), ((), ())), preferred_element_type=f32
-        )
-        total = term if total is None else total + term
-    out[...] = total.astype(bf16)
-
-
-def backward_kernel(devices, taps, conv, long, source, seg, column_ref, toeplitz, *rest):
-    gys, rest = rest[:devices], rest[devices:]
-    outs, (grad_y, grads, small, marks) = rest[:devices], rest[devices:]
+    refs[-1][...] = total.astype(bf16)
+
+
+def backward_kernel(
+    devices, taps, conv, source, seg, toeplitz, columns, query, previous, grad_y, long, *rest
+):
+    glos, rest = rest[:devices], rest[devices:]
+    outs, (query_out, grad_long_out, grads, small, marks, place) = rest[:devices], rest[devices:]
     me = lax.axis_index("ctx")
     stacked, chunk, span = conv.shape
     length = span // devices
     groups = toeplitz.shape[0]
     size = chunk // groups
     body = stacked * chunk
+    width = query.shape[0]
+    room = small.shape[1]
+
+    own_masks = block_masks(seg[0:1], taps, place, me, length)
+    shifts = query_shifts(query[...], previous, taps)
+    grad = grad_y[...] * long[...]
+    total = columns[:, 0:1] * grad
+    lane = lax.broadcasted_iota(jnp.int32, (width, SUB), 1)
+    position = lax.broadcasted_iota(jnp.int32, (width, length), 1)
+    sums = jnp.where(lane == groups, jnp.sum(grad * shifts[0], axis=1, keepdims=True), 0.0)
+    early = jnp.zeros((width, SUB), f32)
+    for s in range(1, taps):
+        masked = own_masks[s] * grad
+        back = pltpu.roll(columns[:, s : s + 1] * masked, length - s, 1)
+        total += jnp.where(position < length - s, back, 0.0)
+        early += jnp.where(position >= length - s, back, 0.0)[:, length - SUB :]
+        tap = jnp.sum(masked * shifts[s], axis=1, keepdims=True)
+        sums += jnp.where(lane == groups + s, tap, 0.0)
+    query_out[...] = total
+    common = sums.T[0:room] + early.T[SUB - room :]
+
     for s in range(devices):
         at = block_at(lax.rem(me - s + devices, devices), length)
-        grad_y[:, at] = gys[s][...].astype(f32)
+        grad_long_out[:, at] = glos[s][chunk:]
     masks = tap_masks(seg[0:1], taps)
-    column = column_ref[...]
-    gy = grad_y[...]
-    grad_long_out = gy * conv[0]
-    high, low = split_bf16(grad_long_out)
-    gated = (conv[1] * conv[2]).astype(bf16)
+    column = columns[block_at(me, chunk)]
+    high = grad_long_out[...]
+    gated = (conv[0] * conv[1]).astype(bf16)
     gg_parts = []
     corner = lax.broadcasted_iota(jnp.int32, (SUB, SUB), 0)
     corner += lax.broadcasted_iota(jnp.int32, (SUB, SUB), 1)
@@ -456,22 +522,19 @@
     small[...] = jnp.zeros_like(small)
     for g in range(groups):
         own = slice(g * size, (g + 1) * size)
-        pieces = []
-        for i in range(devices):
-            at = slice(i * length, (i + 1) * length)
-            pieces += [high[own, at], low[own, at]]
-        stack = jnp.concatenate(pieces, axis=0)
+        stack = jnp.concatenate(
+            [high[own, i * length : (i + 1) * length] for i in range(devices)], axis=0
+        )
         totals = [None] * devices
         for lag in range(devices):
             part = lax.dot_general(
-                stack[2 * size * lag :],
+                stack[size * lag :],
                 toeplitz[g, :, lag * length : (lag + 1) * length],
                 (((1,), (1,)), ((), ())),
                 preferred_element_type=f32,
             )
             for j in range(devices - lag):
-                term = part[2 * size * j : 2 * size * j + size]
-                term += part[2 * size * j + size : 2 * size * (j + 1)]
+                term = part[size * j : size * (j + 1)]
                 totals[j] = term if totals[j] is None else totals[j] + term
         gg_parts.append(jnp.concatenate(totals, axis=1))
         left = jnp.concatenate([gated[own, j * SUB : (j + 1) * SUB] for j in range(subs)], axis=0)
@@ -498,59 +561,74 @@
     lane = lax.broadcasted_iota(jnp.int32, (chunk, SUB), 1)
     sums = jnp.zeros((chunk, SUB), f32)
     for i in range(stacked):
-        if i == 0:
-            grad = gy * long[...]
-        else:
-            grad = grad_gated * conv[3 - i]
+        grad = grad_gated * conv[1 - i]
         x = source[i * chunk : (i + 1) * chunk].astype(f32)
-        total = column[:, i * taps : i * taps + 1] * grad
-        sums += jnp.where(lane == i * taps, jnp.sum(grad * x, axis=1, keepdims=True), 0.0)
+        j = (i + 1) * taps
+        total = column[:, j : j + 1] * grad
+        tap = jnp.sum(grad * x, axis=1, keepdims=True)
+        sums += jnp.where(lane == groups + j, tap, 0.0)
         for s in range(1, taps):
-            j = i * taps + s
             masked = masks[s] * grad
-            total += column[:, j : j + 1] * pltpu.roll(masked, span - s, 1)
+            total += column[:, j + s : j + s + 1] * pltpu.roll(masked, span - s, 1)
             tap = jnp.sum(masked * pltpu.roll(x, s, 1), axis=1, keepdims=True)
-            sums += jnp.where(lane == j, tap, 0.0)
+            sums += jnp.where(lane == groups + j + s, tap, 0.0)
         grads[i * chunk : (i + 1) * chunk] = total.astype(bf16)
-    rows = stacked * taps
     marks[...] = jnp.zeros_like(marks)
     marks[:, 0:chunk] = sums.T
-    placed = pltpu.roll(marks[0:16], me * chunk, 1)
-    for b in range(devices):
-        small[b, groups : groups + rows] = placed[0:rows]
-    room = small.shape[1]
+    common += pltpu.roll(marks[0:room], me * chunk, 1)
     for s in range(devices):
         to = lax.rem(me + s, devices)
         outs[s][0:body] = grads[:, block_at(to, length)]
-        value = small[to]
+        value = small[to] + common
         top = value.astype(bf16)
         outs[s][body : body + room] = top
         outs[s][body + room :] = (value - top.astype(f32)).astype(bf16)
 
 
-def grad_out_kernel(devices, groups, *refs):
-    pays, (out, sums, turned) = refs[:devices], refs[devices:]
+def collect_kernel(devices, groups, rows, stacked, *refs):
+    pays, (near, sums) = refs[:devices], refs[devices:]
     me = lax.axis_index("ctx")
-    stacked, _, width = out.shape
-    chunk = width // devices
-    body = stacked * chunk
+    width = pays[0].shape[1]
+    blocks = near.shape[1] // width
+    body = blocks * rows + (stacked - 1) * (width // devices)
     room = (pays[0].shape[0] - body) // 2
     count = groups * devices
     total = long_rows = None
     for s in range(devices):
         come = lax.rem(me - s + devices, devices)
-        for i in range(stacked):
-            turned[i, block_at(come, chunk)] = pays[s][i * chunk : (i + 1) * chunk]
+        for b in range(blocks):
+            at = block_at(come, rows)
+            near[at, b * width : (b + 1) * width] = pays[s][b * rows : (b + 1) * rows]
         value = pays[s][body : body + room].astype(f32) + pays[s][body + room :].astype(f32)
-        row = lax.broadcasted_iota(jnp.int32, (count, value.shape[1]), 0)
-        line = pltpu.roll(jnp.where(row < groups, value[0:count], 0.0), come * groups, 0)
+        row = lax.broadcasted_iota(jnp.int32, value.shape, 0)
+        line = pltpu.roll(jnp.where(row < groups, value, 0.0), come * groups, 0)
         long_rows = line if long_rows is None else long_rows + line
         total = value if total is None else total + value
-    for i in range(stacked):
-        out[i] = turned[i].T
     sums[...] = jnp.zeros_like(sums)
     sums[0:count] = long_rows
     sums[count : count + room - groups] = total[groups:]
+
+
+def grad_out_kernel(devices, taps, start, query_part, *refs):
+    pays, (out, turned) = refs[:devices], refs[devices:]
+    me = lax.axis_index("ctx")
+    stacked, rows, width = out.shape
+    chunk = width // devices
+    body = start + (stacked - 1) * chunk
+    room = (pays[0].shape[0] - body) // 2
+    for s in range(devices):
+        at = block_at(lax.rem(me - s + devices, devices), chunk)
+        for i in range(stacked - 1):
+            turned[i, at] = pays[s][start + i * chunk : start + (i + 1) * chunk]
+    last = pays[devices - 1]
+    value = last[body : body + room].astype(f32) + last[body + room :].astype(f32)
+    row = lax.broadcasted_iota(jnp.int32, value.shape, 0)
+    later = jnp.where(row >= room - (taps - 1), value, 0.0)
+    query = query_part[...].T
+    out[0, 0 : rows - room] = query[0 : rows - room].astype(bf16)
+    out[0, rows - room :] = (query[rows - room :] + later).astype(bf16)
+    for i in range(stacked - 1):
+        out[i + 1] = turned[i].T
 
 
 def small_out_kernel(scale, mine, other, short_out, long_out):
@@ -567,71 +645,88 @@
     devices, parts = lax.axis_size("ctx"), lax.axis_size("tp")
     stacked, _, length, width = projected.shape
     taps = short_filter.shape[1]
-    groups = long_filter.shape[0] // devices
+    count = long_filter.shape[0]
+    groups = count // devices
     chunk = width // devices
     span = length * devices
     total_cols = out_proj.shape[1]
     grad_scale = 1.0 / math.sqrt(projected.shape[1] * lax.axis_size("dp") * span)
     cotangent = mixed_cotangent[0]
     room = 16
-    size = stacked * chunk + room
-
-    packed = on_core(
-        functools.partial(pack_signal_kernel, devices),
-        [((size, length), bf16)] * devices,
-        (projected[:, 0], long_filter, segment_ids),
-        "pack_signal",
-        [pltpu.VMEM((stacked, width, length), bf16), pltpu.VMEM((room, length), f32)],
-    )
-    signal = scatter_chunks(packed, "ctx")
-    tp_packed = on_core(
-        functools.partial(pack_channels_kernel, parts),
-        [((length + width, width), bf16)] * (parts - 1),
-        (cotangent, out_proj),
-        "pack_channels",
-    )
-    pays = [rotate(tp_packed[s - 1], "tp", s) for s in range(1, parts)]
-
-    gy = on_core(
-        functools.partial(grad_y_kernel, devices, parts),
-        [((chunk, length), bf16)] * devices,
-        (out_proj, cotangent, *pays),
-        "grad_y",
-        [pltpu.VMEM((width, length), f32)],
-        flops=2 * width * length * total_cols,
-    )
-    gy_in = scatter_chunks(gy, "ctx")
+    inputs = (projected[:, 0], long_filter, segment_ids)
+
+    outs = on_core(
+        functools.partial(pack_kernel, devices),
+        [
+            (((stacked - 1) * chunk + (2 * room if s == 1 else room), length), bf16)
+            for s in range(devices)
+        ]
+        + [((width, length), bf16)],
+        inputs,
+        "pack",
+        [pltpu.VMEM(a.shape, a.dtype) for a in inputs]
+        + [
+            pltpu.VMEM((stacked - 1, width, length), bf16),
+            pltpu.VMEM((room, length), f32),
+            pltpu.SemaphoreType.DMA((len(inputs),)),
+        ],
+        whole=True,
+    )
+    signal, query = outs[:devices], outs[devices]
+    own, *signal = scatter_chunks(signal, "ctx")
+    beside = swap(cotangent, "tp", 1)
+    columns, own, query = on_core(
+        prepare_kernel,
+        [((width, 16), f32), (own.shape, bf16), ((width, length), bf16)],
+        (after(short_filter, beside), own, query),
+        "prepare",
+        [pltpu.VMEM((16, width), f32)],
+    )
+    signal = [own, *signal]
 
     conv_flops = 2 * groups * span * span * 64
     outs = on_core(
-        functools.partial(conv_kernel, devices),
+        functools.partial(conv_kernel, devices, taps),
         [((chunk, length), bf16)] * devices
         + [
-            ((stacked, chunk, span), f32),
-            ((chunk, span), f32),
-            ((stacked * chunk, span), bf16),
+            ((stacked - 1, chunk, span), f32),
+            (((stacked - 1) * chunk, span), bf16),
             ((8, span), f32),
-            ((chunk, 16), f32),
             ((groups, length, span), bf16),
         ],
-        (short_filter, *signal),
+        (columns, *signal),
         "conv",
         [
             pltpu.VMEM((room, span), f32),
-            pltpu.VMEM((16, width), f32),
-            pltpu.VMEM((width, 16), f32),
             pltpu.VMEM((chunk, span), bf16),
+            pltpu.VMEM((groups, length, span), bf16),
         ],
         flops=conv_flops,
     )
-    ys, kept = outs[:devices], outs[devices:]
-    y_in = scatter_chunks(ys, "ctx")
+    longs, kept = outs[:devices], outs[devices:]
+    seg = kept[2]
+    cots = [cotangent, beside, swap(cotangent, "tp", 2), swap(beside, "tp", 2)]
+    outs = on_core(
+        functools.partial(grad_y_kernel, devices, parts, taps),
+        [((2 * chunk, length), bf16)] * devices + [((width, length), f32)] * 2,
+        (out_proj, query, signal[1], columns, seg, *cots, *longs),
+        "grad_y",
+        [pltpu.VMEM((8 * taps, span), f32), pltpu.VMEM((width, length), bf16)],
+        flops=2 * width * length * total_cols,
+    )
+    pairs, (grad_y, query_conv) = outs[:devices], outs[devices:]
+    pairs = scatter_chunks(pairs, "ctx")
 
     half = width // 2
-    y_full, keep, send = on_core(
+    y, long, keep, send = on_core(
         functools.partial(weight_grad_kernel, devices, parts),
-        [((width, length), bf16), ((half, total_cols), f32), ((half, total_cols), f32)],
-        (cotangent, *pays, *y_in),
+        [
+            ((width, length), bf16),
+            ((width, length), f32),
+            ((half, total_cols), f32),
+            ((half, total_cols), f32),
+        ],
+        (query_conv, *cots, *pairs),
         "weight_grad",
         [pltpu.VMEM((width, total_cols), f32)],
         flops=2 * width * length * total_cols,
@@ -645,58 +740,69 @@
         "core_sum",
         [pltpu.VMEM((half, total_cols), f32)],
     )
-    sums = scatter_chunks(sums, "ctx")
-    (block,) = on_core(
-        functools.partial(block_sum_kernel, grad_scale),
-        [((rows, total_cols), bf16)],
-        sums,
+    parts_out = scatter_chunks(sums, "ctx")
+
+    shares = on_core(
+        functools.partial(mixed_part_kernel, parts),
+        [((length, width), f32)] + [((length, width), bf16)] * (parts - 1),
+        (after(y, sums[1]), out_proj),
+        "mixed_part",
+        [pltpu.VMEM((length, total_cols), f32)],
+        flops=2 * width * length * total_cols,
+    )
+    shares = [shares[0]] + [swap(shares[s], "tp", s) for s in range(1, parts)]
+    (mixed,) = on_core(mixed_sum_kernel, [((length, width), bf16)], shares, "mixed_sum")
+
+    outs = on_core(
+        functools.partial(backward_kernel, devices, taps),
+        [(((stacked - 1) * chunk + 2 * room, length), bf16)] * devices + [((width, length), f32)],
+        (*kept, columns, query, signal[1], grad_y, after(long, sums[1]), *pairs),
+        "backward",
+        [
+            pltpu.VMEM((chunk, span), bf16),
+            pltpu.VMEM(((stacked - 1) * chunk, span), bf16),
+            pltpu.VMEM((devices, room, length), f32),
+            pltpu.VMEM((SUB, width), f32),
+            pltpu.VMEM((8 * taps, span), f32),
+        ],
+        flops=2 * conv_flops,
+    )
+    back, query_part = outs[:devices], outs[devices]
+    start = rows * total_cols // width
+    back = on_core(
+        functools.partial(block_sum_kernel, devices, grad_scale),
+        [((start + back[0].shape[0], width), bf16)] * devices,
+        (*parts_out, *back),
         "block_sum",
     )
-    near = spread(block, "ctx")
-    far = [rotate(piece, "dp", 1) for piece in near]
+    back = scatter_chunks(back, "ctx")
+    back[0] = after(back[0], shares[1:])
+    near, small = on_core(
+        functools.partial(collect_kernel, devices, groups, rows, stacked),
+        [((half, total_cols), bf16), ((count + 16, width), f32)],
+        back,
+        "collect",
+    )
+    far = rotate(near, "dp", 1)
+    other_small = rotate(small, "dp", 1)
+    (grad_projected,) = on_core(
+        functools.partial(grad_out_kernel, devices, taps, start),
+        [((stacked, length, width), bf16)],
+        (query_part, *back),
+        "grad_out",
+        [pltpu.VMEM((stacked - 1, width, length), bf16)],
+    )
+    grad_short, grad_long = on_core(
+        functools.partial(small_out_kernel, grad_scale),
+        [(short_filter.shape, f32), ((count, length), f32)],
+        (small, other_small),
+        "small_out",
+    )
     (grad_out_proj,) = on_core(
         functools.partial(weight_out_kernel, devices),
         [((width, total_cols), f32)],
-        (*near, *far),
+        (near, far),
         "weight_out",
-    )
-
-    y_all = spread(y_full, "tp")
-    (mixed,) = on_core(
-        functools.partial(mixed_kernel, parts),
-        [((length, width), bf16)],
-        (out_proj, *y_all, *pays),
-        "mixed",
-        flops=2 * width * length * total_cols,
-    )
-
-    back = on_core(
-        functools.partial(backward_kernel, devices, taps),
-        [((size + room, length), bf16)] * devices,
-        (*kept, *gy_in),
-        "backward",
-        [
-            pltpu.VMEM((chunk, span), f32),
-            pltpu.VMEM((stacked * chunk, span), bf16),
-            pltpu.VMEM((devices, room, length), f32),
-            pltpu.VMEM((SUB, width), f32),
-        ],
-        flops=2 * conv_flops,
-    )
-    back = scatter_chunks(back, "ctx")
-    count = groups * devices
-    grad_projected, small = on_core(
-        functools.partial(grad_out_kernel, devices, groups),
-        [((stacked, length, width), bf16), ((count + 16, width), f32)],
-        back,
-        "grad_out",
-        [pltpu.VMEM((stacked, width, length), bf16)],
-    )
-    grad_short, grad_long = on_core(
-        functools.partial(small_out_kernel, grad_scale),
-        [(short_filter.shape, f32), ((count, length), f32)],
-        (small, rotate(small, "dp", 1)),
-        "small_out",
     )
     return (mixed[None], grad_projected[:, None], grad_short, grad_long, grad_out_proj)
 
@@ -709,6 +815,7 @@
     stacked, taps = short_filter.shape[:2]
     return (
         mesh.shape["dp"] == 2
+        and mesh.shape["tp"] == 4
         and projected.shape[1] == 2
         and stacked == 3
         and length == width
@@ -719,7 +826,7 @@
         and width // devices <= SUB
         and (width // groups) == 16
         and 2 * groups // devices + 2 <= 16
-        and groups // devices + stacked * taps <= 16
+        and groups // devices + stacked * taps + taps - 1 <= 16
     )
 
 

time: 70.4 us -> 57.8 us (0.82); the launches traced: 70 us -> 56.7 us
  starting transfers between devices: 36.8 us -> 26.4 us
  waiting for transfers between devices: 19 us -> 16.1 us
  local copies, waits for them, and re-layouts: 5.08 us -> 2.5 us
  Pallas kernels: 8.39 us -> 10.9 us
    ppermute x30 -> x15, starting transfers between devices: 36.8 us -> 17.8 us  [rotate(): lax.ppermute(value, axis, [(i, (i + steps) % count) for i in range(count)])]
    ppermute x0 -> x6, starting transfers between devices: none -> 8.6 us  [swap(): lax.ppermute(value, axis, [(i, i ^ bits) for i in range(lax.axis_size(axi...]
    ppermute x30 -> x15, waiting for transfers between devices: 19 us -> 11.3 us  [rotate(): lax.ppermute(value, axis, [(i, (i + steps) % count) for i in range(count)])]
    ppermute x0 -> x6, waiting for transfers between devices: none -> 4.87 us  [swap(): lax.ppermute(value, axis, [(i, i ^ bits) for i in range(lax.axis_size(axi...]
    unnamed x16 -> x10, local copies, waits for them, and re-layouts: 5.08 us -> 2.5 us
    pallas_call x12 -> x14, Pallas kernels: 8.39 us -> 10.9 us  [on_core(): pl.pallas_call(kernel, out_shape=[jax.ShapeDtypeStruct(shape, kind) for s...]
  transfers between devices with their start and end apart: 30 -> 21, of which waited for: 7 -> 9; matrix products, arithmetic and copies ran while one was open for 0% -> 0% of each run, Pallas kernels for 10% -> 15%
where the time goes in v1:
time: 57.8 us; the launch traced here: 56.7 us
  starting transfers between devices  26.4 us (46%)
  waiting for transfers between devices  16.1 us (28%)
  Pallas kernels  10.9 us (19%)
  local copies, waits for them, and re-layouts  2.5 us (4%)
  between operations  0.78 us (1%)
    ppermute x15, starting transfers between devices, rotate(): lax.ppermute(value, axis, [(i, (i + steps) % count) for i in range(count)])  17.8 us
    ppermute x15, waiting for transfers between devices, rotate(): lax.ppermute(value, axis, [(i, (i + steps) % count) for i in range(count)])  11.3 us
    pallas_call x14, Pallas kernels, on_core(): pl.pallas_call(kernel, out_shape=[jax.ShapeDtypeStruct(shape, kind) for s...  10.9 us
    ppermute x6, starting transfers between devices, swap(): lax.ppermute(value, axis, [(i, i ^ bits) for i in range(lax.axis_size(axi...  8.6 us
    ppermute x6, waiting for transfers between devices, swap(): lax.ppermute(value, axis, [(i, i ^ bits) for i in range(lax.axis_size(axi...  4.87 us
    unnamed x10, local copies, waits for them, and re-layouts  2.5 us
  transfers between devices with their start and end apart: 21, of which 9 were waited for; matrix products, arithmetic and copies ran while one was open for 0% of the time, Pallas kernels for 15%

profile of v1, /device:TPU:0, one launch (start us, length us, event | category | flops | bytes accessed | tf_op | source)
XLA Modules:
  0.0 56.7 jit_solution(8774766297898924160)
XLA Ops:
  0.6 0.0 copy-start.1
  0.6 0.0 copy-start
  0.7 3.0 %collective-permute-start = (bf16[256,256]{1,0:T(8,128)(2,1)}, bf16[256,256]{1,0:T(8,128)(2,1)S(1)}, u32[]{:S(2)}, u32[]{:S(2)}) collective-permute-start(bf16[256,256]{1,0:T(8,128)(2,1)} %bitcast.6), channel_id=1, source_target_pairs={{0,2},{2,0},{4,6},{6,4},{1,3},{3,1},{5,7},{7,5},{8,10},{10,8},{12,... | collective-permute-start | bytes 393224 | tf_op jit(solution)/shard_map/ppermute | solution.py:216
  3.7 1.9 %pack.1 = (bf16[144,256]{1,0:T(8,128)(2,1)}, bf16[160,256]{1,0:T(8,128)(2,1)}, bf16[144,256]{1,0:T(8,128)(2,1)}, bf16[144,256]{1,0:T(8,128)(2,1)}, bf16[256,256]{1,0:T(8,128)(2,1)}) custom-call(bf16[3,256,256]{2,1,0:T(8,128)(2,1)} %bitcast.11, f32[16,256]{1,0:T(8,128)} %refs_1_.1, s32[1,256]{1,0:T(1,128)} %refs_2_.1), custom_call_target="tpu_custom_call" | custom-call | bytes 844800 | tf_op jit(solution)/shard_map/pack/pallas_call | solution.py:234
  5.6 1.6 %collective-permute-start.1 = (bf16[160,256]{1,0:T(8,128)(2,1)}, bf16[160,256]{1,0:T(8,128)(2,1)S(1)}, u32[]{:S(2)}, u32[]{:S(2)}) collective-permute-start(bf16[160,256]{1,0:T(8,128)(2,1)} %get-tuple-element.60), channel_id=1, source_target_pairs={{0,8},{8,16},{16,24},{24,0},{1,9},{9,17},{17,25},{25,1},{2,10},{10... | collective-permute-start | bytes 245768 | tf_op jit(solution)/shard_map/ppermute | solution.py:212
  7.2 1.5 %collective-permute-start.4 = (bf16[256,256]{1,0:T(8,128)(2,1)}, bf16[256,256]{1,0:T(8,128)(2,1)S(1)}, u32[]{:S(2)}, u32[]{:S(2)}) collective-permute-start(bf16[256,256]{1,0:T(8,128)(2,1)} %bitcast.7), channel_id=1, source_target_pairs={{0,4},{2,6},{4,0},{6,2},{1,5},{3,7},{5,1},{7,3},{8,12},{10,14},{12... | collective-permute-start | bytes 393224 | tf_op jit(solution)/shard_map/ppermute | solution.py:216
  8.7 0.0 collective-permute-done.rest_1_
  8.7 0.5 collective-permute-start.5
  9.3 2.6 %collective-permute-start.2 = (bf16[144,256]{1,0:T(8,128)(2,1)}, bf16[144,256]{1,0:T(8,128)(2,1)S(1)}, u32[]{:S(2)}, u32[]{:S(2)}) collective-permute-start(bf16[144,256]{1,0:T(8,128)(2,1)} %get-tuple-element.63), channel_id=1, source_target_pairs={{0,16},{8,24},{16,0},{24,8},{1,17},{9,25},{17,1},{25,9},{2,18},{10... | collective-permute-start | bytes 221192 | tf_op jit(solution)/shard_map/ppermute | solution.py:212
  11.8 1.3 %collective-permute-start.3 = (bf16[144,256]{1,0:T(8,128)(2,1)}, bf16[144,256]{1,0:T(8,128)(2,1)S(1)}, u32[]{:S(2)}, u32[]{:S(2)}) collective-permute-start(bf16[144,256]{1,0:T(8,128)(2,1)} %get-tuple-element.64), channel_id=1, source_target_pairs={{0,24},{8,0},{16,8},{24,16},{1,25},{9,1},{17,9},{25,17},{2,26},{10... | collective-permute-start | bytes 221192 | tf_op jit(solution)/shard_map/ppermute | solution.py:212
  13.2 0.0 copy-start.2
  13.2 0.9 %copy-done.2 = bf16[256,256]{1,0:T(8,128)(2,1)S(1)} copy-done((bf16[256,256]{1,0:T(8,128)(2,1)S(1)}, bf16[256,256]{1,0:T(8,128)(2,1)}, u32[]{:S(2)}) %copy-start.2) | copy-done | bytes 131096
  14.1 0.0 copy-start.3
  14.1 0.9 %copy-done.3 = bf16[144,256]{1,0:T(8,128)(2,1)S(1)} copy-done((bf16[144,256]{1,0:T(8,128)(2,1)S(1)}, bf16[144,256]{1,0:T(8,128)(2,1)}, u32[]{:S(2)}) %copy-start.3) | copy-done | bytes 73752
  15.0 0.0 copy-start.4
  15.0 0.7 %copy-done.4 = f32[3,3,256]{2,1,0:T(4,128)S(1)} copy-done((f32[3,3,256]{2,1,0:T(4,128)S(1)}, f32[3,3,256]{2,1,0:T(4,128)}, u32[]{:S(2)}) %copy-start.4) | copy-done | bytes 9240
  15.7 0.1 prepare.1
  15.8 0.5 collective-permute-done.2.rest_2_
  16.3 0.4 collective-permute-done.3.rest_3_
  16.6 0.0 collective-permute-done.1.rest_1_.previous
  16.6 1.4 %conv.1 = (bf16[64,256]{1,0:T(8,128)(2,1)S(1)}, bf16[64,256]{1,0:T(8,128)(2,1)S(1)}, bf16[64,256]{1,0:T(8,128)(2,1)S(1)}, bf16[64,256]{1,0:T(8,128)(2,1)S(1)}, f...) custom-call(f32[256,16]{1,0:T(8,128)S(1)} %get-tuple-element.61.colu, ...), custom_call_target="tpu_custom_call" | custom-call | flops 536870912 | bytes 3366912 | tf_op jit(solution)/shard_map/conv/pallas_call | solution.py:234
  18.1 0.0 collective-permute-done.4.rest_2_
  18.1 0.0 collective-permute-done.5.rest_3_
  18.1 0.0 copy-done.1
  18.1 0.0 copy-done
  18.1 0.4 grad_y.1
  18.6 1.3 %collective-permute-start.6 = (bf16[128,256]{1,0:T(8,128)(2,1)S(1)}, bf16[128,256]{1,0:T(8,128)(2,1)S(1)}, u32[]{:S(2)}, u32[]{:S(2)}) collective-permute-start(bf16[128,256]{1,0:T(8,128)(2,1)S(1)} %get-tuple-element.72), channel_id=1, source_target_pairs={{0,8},{8,16},{16,24},{24,0},{1,9},{9,17},{17,25},{25,1},{2,10},{10... | collective-permute-start | bytes 196616 | tf_op jit(solution)/shard_map/ppermute | solution.py:212
  19.8 2.6 %collective-permute-start.7 = (bf16[128,256]{1,0:T(8,128)(2,1)S(1)}, bf16[128,256]{1,0:T(8,128)(2,1)S(1)}, u32[]{:S(2)}, u32[]{:S(2)}) collective-permute-start(bf16[128,256]{1,0:T(8,128)(2,1)S(1)} %get-tuple-element.73), channel_id=1, source_target_pairs={{0,16},{8,24},{16,0},{24,8},{1,17},{9,25},{17,1},{25,9},{2,18},{10... | collective-permute-start | bytes 196616 | tf_op jit(solution)/shard_map/ppermute | solution.py:212
  22.4 0.0 collective-permute-start.8
  22.4 2.3 %collective-permute-done.6.rest_5_.rest_1_ = bf16[128,256]{1,0:T(8,128)(2,1)S(1)} collective-permute-done((bf16[128,256]{1,0:T(8,128)(2,1)S(1)}, bf16[128,256]{1,0:T(8,128)(2,1)S(1)}, u32[]{:S(2)}, u32[]{:S(2)}) %collective-permute-start.6) | collective-permute-done | bytes 65568 | tf_op jit(solution)/shard_map/ppermute | solution.py:212
  24.8 1.4 %collective-permute-done.7.rest_6_.rest_2_ = bf16[128,256]{1,0:T(8,128)(2,1)S(1)} collective-permute-done((bf16[128,256]{1,0:T(8,128)(2,1)S(1)}, bf16[128,256]{1,0:T(8,128)(2,1)S(1)}, u32[]{:S(2)}, u32[]{:S(2)}) %collective-permute-start.7) | collective-permute-done | bytes 65568 | tf_op jit(solution)/shard_map/ppermute | solution.py:212
  26.2 0.7 %collective-permute-done.8.rest_7_.rest_3_ = bf16[128,256]{1,0:T(8,128)(2,1)S(1)} collective-permute-done((bf16[128,256]{1,0:T(8,128)(2,1)S(1)}, bf16[128,256]{1,0:T(8,128)(2,1)S(1)}, u32[]{:S(2)}, u32[]{:S(2)}) %collective-permute-start.8) | collective-permute-done | bytes 65568 | tf_op jit(solution)/shard_map/ppermute | solution.py:212
  26.9 0.4 weight_grad.1
  27.3 0.1 collective-permute-start.9
  27.3 1.9 %collective-permute-done.9.other = f32[128,1024]{1,0:T(8,128)S(1)} collective-permute-done((f32[128,1024]{1,0:T(8,128)S(1)}, f32[128,1024]{1,0:T(8,128)S(1)}, u32[]{:S(2)}, u32[]{:S(2)}) %collective-permute-start.9) | collective-permute-done | bytes 524320 | tf_op jit(solution)/shard_map/ppermute | solution.py:212
  29.2 0.1 core_sum.1
  29.3 0.4 mixed_part.1
  29.8 1.5 %collective-permute-start.10 = (bf16[256,256]{1,0:T(8,128)(2,1)S(1)}, bf16[256,256]{1,0:T(8,128)(2,1)S(1)}, u32[]{:S(2)}, u32[]{:S(2)}) collective-permute-start(bf16[256,256]{1,0:T(8,128)(2,1)S(1)} %get-tuple-element.81), channel_id=1, source_target_pairs={{0,2},{2,0},{4,6},{6,4},{1,3},{3,1},{5,7},{7,5},{8,10},{10,8},{12,... | collective-permute-start | bytes 393224 | tf_op jit(solution)/shard_map/ppermute | solution.py:216
  31.2 0.6 collective-permute-start.13
  31.8 2.4 %collective-permute-start.14 = (bf16[32,1024]{1,0:T(8,128)(2,1)S(1)}, bf16[32,1024]{1,0:T(8,128)(2,1)S(1)}, u32[]{:S(2)}, u32[]{:S(2)}) collective-permute-start(bf16[32,1024]{1,0:T(8,128)(2,1)S(1)} %get-tuple-element.92), channel_id=1, source_target_pairs={{0,16},{8,24},{16,0},{24,8},{1,17},{9,25},{17,1},{25,9},{2,18},{10... | collective-permute-start | bytes 196616 | tf_op jit(solution)/shard_map/ppermute | solution.py:212
  34.2 0.8 %collective-permute-start.15 = (bf16[32,1024]{1,0:T(8,128)(2,1)S(1)}, bf16[32,1024]{1,0:T(8,128)(2,1)S(1)}, u32[]{:S(2)}, u32[]{:S(2)}) collective-permute-start(bf16[32,1024]{1,0:T(8,128)(2,1)S(1)} %get-tuple-element.93), channel_id=1, source_target_pairs={{0,24},{8,0},{16,8},{24,16},{1,25},{9,1},{17,9},{25,17},{2,26},{10... | collective-permute-start | bytes 196616 | tf_op jit(solution)/shard_map/ppermute | solution.py:212
  35.0 2.7 %backward.1 = (bf16[160,256]{1,0:T(8,128)(2,1)S(1)}, bf16[160,256]{1,0:T(8,128)(2,1)S(1)}, bf16[160,256]{1,0:T(8,128)(2,1)S(1)}, bf16[160,256]{1,0:T(8,128)(2,1)S(1)}, f32[256,256]{1,0:T(8,128)S(1)}) custom-call(f32[2,64,1024]{2,1,0:T(8,128)S(1)} %get-tuple-element.84.conv, bf16[128,1024]{1,0:T(8,128)(2,1)S(1)} %get-tuple-element.85.source, ...), custom_call_target="tpu_custom_call" | custom-call | flops 1073741824 | bytes 4521984 | tf_op jit(solution)/shard_map/backward/pallas_call | solution.py:234
  37.8 2.0 %collective-permute-done.14.refs_2_ = bf16[32,1024]{1,0:T(8,128)(2,1)S(1)} collective-permute-done((bf16[32,1024]{1,0:T(8,128)(2,1)S(1)}, bf16[32,1024]{1,0:T(8,128)(2,1)S(1)}, u32[]{:S(2)}, u32[]{:S(2)}) %collective-permute-start.14) | collective-permute-done | bytes 65568 | tf_op jit(solution)/shard_map/ppermute | solution.py:212
  39.7 0.0 collective-permute-done.15.refs_3_
  39.7 0.0 collective-permute-done.13.refs_1_
  39.8 1.3 %collective-permute-start.16 = (bf16[288,256]{1,0:T(8,128)(2,1)S(1)}, bf16[288,256]{1,0:T(8,128)(2,1)S(1)}, u32[]{:S(2)}, u32[]{:S(2)}) collective-permute-start(bf16[288,256]{1,0:T(8,128)(2,1)S(1)} %get-tuple-element.100), channel_id=1, source_target_pairs={{0,8},{8,16},{16,24},{24,0},{1,9},{9,17},{17,25},{25,1},{2,10},{10... | collective-permute-start | bytes 442376 | tf_op jit(solution)/shard_map/ppermute | solution.py:212
  41.1 1.9 %collective-permute-start.17 = (bf16[288,256]{1,0:T(8,128)(2,1)S(1)}, bf16[288,256]{1,0:T(8,128)(2,1)S(1)}, u32[]{:S(2)}, u32[]{:S(2)}) collective-permute-start(bf16[288,256]{1,0:T(8,128)(2,1)S(1)} %get-tuple-element.101), channel_id=1, source_target_pairs={{0,16},{8,24},{16,0},{24,8},{1,17},{9,25},{17,1},{25,9},{2,18},{10... | collective-permute-start | bytes 442376 | tf_op jit(solution)/shard_map/ppermute | solution.py:212
  43.0 0.7 %collective-permute-start.18 = (bf16[288,256]{1,0:T(8,128)(2,1)S(1)}, bf16[288,256]{1,0:T(8,128)(2,1)S(1)}, u32[]{:S(2)}, u32[]{:S(2)}) collective-permute-start(bf16[288,256]{1,0:T(8,128)(2,1)S(1)} %get-tuple-element.102), channel_id=1, source_target_pairs={{0,24},{8,0},{16,8},{24,16},{1,25},{9,1},{17,9},{25,17},{2,26},{10... | collective-permute-start | bytes 442376 | tf_op jit(solution)/shard_map/ppermute | solution.py:212
  43.7 0.7 %collective-permute-start.11 = (bf16[256,256]{1,0:T(8,128)(2,1)S(1)}, bf16[256,256]{1,0:T(8,128)(2,1)S(1)}, u32[]{:S(2)}, u32[]{:S(2)}) collective-permute-start(bf16[256,256]{1,0:T(8,128)(2,1)S(1)} %get-tuple-element.82), channel_id=1, source_target_pairs={{0,4},{2,6},{4,0},{6,2},{1,5},{3,7},{5,1},{7,3},{8,12},{10,14},{12... | collective-permute-start | bytes 393224 | tf_op jit(solution)/shard_map/ppermute | solution.py:216
  44.3 0.0 collective-permute-done.10.refs_1_
  44.3 1.5 %collective-permute-start.12 = (bf16[256,256]{1,0:T(8,128)(2,1)S(1)}, bf16[256,256]{1,0:T(8,128)(2,1)S(1)}, u32[]{:S(2)}, u32[]{:S(2)}) collective-permute-start(bf16[256,256]{1,0:T(8,128)(2,1)S(1)} %get-tuple-element.83), channel_id=1, source_target_pairs={{0,6},{2,4},{4,2},{6,0},{1,7},{3,5},{5,3},{7,1},{8,14},{10,12},{12... | collective-permute-start | bytes 393224 | tf_op jit(solution)/shard_map/ppermute | solution.py:216
  45.8 4.9 %collective-permute-done.11.refs_2_ = bf16[256,256]{1,0:T(8,128)(2,1)S(1)} collective-permute-done((bf16[256,256]{1,0:T(8,128)(2,1)S(1)}, bf16[256,256]{1,0:T(8,128)(2,1)S(1)}, u32[]{:S(2)}, u32[]{:S(2)}) %collective-permute-start.11) | collective-permute-done | bytes 131104 | tf_op jit(solution)/shard_map/ppermute | solution.py:216
  50.6 0.0 collective-permute-done.12.refs_3_
  50.6 0.0 collective-permute-done.16.refs_1_
  50.7 2.1 %collective-permute-done.17.refs_2_ = bf16[288,256]{1,0:T(8,128)(2,1)S(1)} collective-permute-done((bf16[288,256]{1,0:T(8,128)(2,1)S(1)}, bf16[288,256]{1,0:T(8,128)(2,1)S(1)}, u32[]{:S(2)}, u32[]{:S(2)}) %collective-permute-start.17) | collective-permute-done | bytes 147488 | tf_op jit(solution)/shard_map/ppermute | solution.py:212
  52.8 0.0 collective-permute-done.18.refs_3_
  52.8 0.1 collective-permute-start.20
  52.9 0.5 collective-permute-start.19
  53.4 0.7 %mixed_sum.1 = bf16[256,256]{1,0:T(8,128)(2,1)} custom-call(f32[256,256]{1,0:T(8,128)S(1)} %get-tuple-element.80.refs_0_, bf16[256,256]{1,0:T(8,128)(2,1)S(1)} %collective-permute-done.10.refs_1_, bf16[256,256]{1,0:T(8,128)(2,1)S(1)} %collective-permute-done.11.refs_2_, bf16[256,256]{1,0:T(8,128)(2,1)S(1)} %collective-permute-done.12.refs_3_), custom_call_target="tpu_custom_call" | custom-call | bytes 786432 | tf_op jit(solution)/shard_map/mixed_sum/pallas_call | solution.py:234
  54.1 0.9 %grad_out.1 = bf16[3,256,256]{2,1,0:T(8,128)(2,1)} custom-call(f32[256,256]{1,0:T(8,128)S(1)} %get-tuple-element.90.query_part, bf16[288,256]{1,0:T(8,128)(2,1)S(1)} %get-tuple-element.99.refs_0_, bf16[288,256]{1,0:T(8,128)(2,1)S(1)} %collective-permute-done.16.refs_1_, bf16[288,256]{1,0:T(8,128)(2,1)S(1)} %collective-permute-done.17.refs_2_, ...), custom_call_target="tpu_custom_call" | custom-call | bytes 1245184 | tf_op jit(solution)/shard_map/grad_out/pallas_call | solution.py:234
  55.0 0.0 collective-permute-done.19.other
  55.0 0.6 %small_out.1 = (f32[3,3,256]{2,1,0:T(4,128)}, f32[16,256]{1,0:T(8,128)}) custom-call(f32[32,256]{1,0:T(8,128)S(1)} %get-tuple-element.103.mine, f32[32,256]{1,0:T(8,128)S(1)} %collective-permute-done.19.other), custom_call_target="tpu_custom_call" | custom-call | bytes 91136 | tf_op jit(solution)/shard_map/small_out/pallas_call | solution.py:234
  55.7 0.0 collective-permute-done.20.far
  55.7 1.0 %weight_out.1 = f32[256,1024]{1,0:T(8,128)} custom-call(bf16[128,1024]{1,0:T(8,128)(2,1)S(1)} %get-tuple-element.106.near, bf16[128,1024]{1,0:T(8,128)(2,1)S(1)} %collective-permute-done.20.far), custom_call_target="tpu_custom_call" | custom-call | bytes 1572864 | tf_op jit(solution)/shard_map/weight_out/pallas_call | solution.py:234
  (2 shorter events, 0.1 us)
Async XLA Ops:
  0.6 17.5 %copy-start.1 = (bf16[1,256,256]{2,1,0:T(8,128)(2,1)S(1)}, bf16[1,256,256]{2,1,0:T(8,128)(2,1)}, u32[]{:S(2)}) copy-start(bf16[1,256,256]{2,1,0:T(8,128)(2,1)} %param.11) | copy-start | bytes 393220
  0.6 17.5 %copy-start = (bf16[256,1024]{1,0:T(8,128)(2,1)S(1)}, bf16[256,1024]{1,0:T(8,128)(2,1)}, u32[]{:S(2)}) copy-start(bf16[256,1024]{1,0:T(8,128)(2,1)} %weights.3) | copy-start | bytes 1572868
  0.7 8.1 %collective-permute-start = (bf16[256,256]{1,0:T(8,128)(2,1)}, bf16[256,256]{1,0:T(8,128)(2,1)S(1)}, u32[]{:S(2)}, u32[]{:S(2)}) collective-permute-start(bf16[256,256]{1,0:T(8,128)(2,1)} %bitcast.6), channel_id=1, source_target_pairs={{0,2},{2,0},{4,6},{6,4},{1,3},{3,1},{5,7},{7,5},{8,10},{10,8},{12,... | collective-permute-start | bytes 393224 | tf_op jit(solution)/shard_map/ppermute | solution.py:216
  5.6 11.0 %collective-permute-start.1 = (bf16[160,256]{1,0:T(8,128)(2,1)}, bf16[160,256]{1,0:T(8,128)(2,1)S(1)}, u32[]{:S(2)}, u32[]{:S(2)}) collective-permute-start(bf16[160,256]{1,0:T(8,128)(2,1)} %get-tuple-element.60), channel_id=1, source_target_pairs={{0,8},{8,16},{16,24},{24,0},{1,9},{9,17},{17,25},{25,1},{2,10},{10... | collective-permute-start | bytes 245768 | tf_op jit(solution)/shard_map/ppermute | solution.py:212
  7.2 10.9 %collective-permute-start.4 = (bf16[256,256]{1,0:T(8,128)(2,1)}, bf16[256,256]{1,0:T(8,128)(2,1)S(1)}, u32[]{:S(2)}, u32[]{:S(2)}) collective-permute-start(bf16[256,256]{1,0:T(8,128)(2,1)} %bitcast.7), channel_id=1, source_target_pairs={{0,4},{2,6},{4,0},{6,2},{1,5},{3,7},{5,1},{7,3},{8,12},{10,14},{12... | collective-permute-start | bytes 393224 | tf_op jit(solution)/shard_map/ppermute | solution.py:216
  8.7 9.3 %collective-permute-start.5 = (bf16[256,256]{1,0:T(8,128)(2,1)S(1)}, bf16[256,256]{1,0:T(8,128)(2,1)S(1)}, u32[]{:S(2)}, u32[]{:S(2)}) collective-permute-start(bf16[256,256]{1,0:T(8,128)(2,1)S(1)} %collective-permute-done.rest_1_), channel_id=1, source_target_pairs={{0,4},{2,6},{4,0},{6,2},{1,5},{3,7},{5,1},{7,3},{8,12},{10,14},{12... | collective-permute-start | bytes 393224 | tf_op jit(solution)/shard_map/ppermute | solution.py:216
  9.3 7.0 %collective-permute-start.2 = (bf16[144,256]{1,0:T(8,128)(2,1)}, bf16[144,256]{1,0:T(8,128)(2,1)S(1)}, u32[]{:S(2)}, u32[]{:S(2)}) collective-permute-start(bf16[144,256]{1,0:T(8,128)(2,1)} %get-tuple-element.63), channel_id=1, source_target_pairs={{0,16},{8,24},{16,0},{24,8},{1,17},{9,25},{17,1},{25,9},{2,18},{10... | collective-permute-start | bytes 221192 | tf_op jit(solution)/shard_map/ppermute | solution.py:212
  11.8 4.8 %collective-permute-start.3 = (bf16[144,256]{1,0:T(8,128)(2,1)}, bf16[144,256]{1,0:T(8,128)(2,1)S(1)}, u32[]{:S(2)}, u32[]{:S(2)}) collective-permute-start(bf16[144,256]{1,0:T(8,128)(2,1)} %get-tuple-element.64), channel_id=1, source_target_pairs={{0,24},{8,0},{16,8},{24,16},{1,25},{9,1},{17,9},{25,17},{2,26},{10... | collective-permute-start | bytes 221192 | tf_op jit(solution)/shard_map/ppermute | solution.py:212
  13.2 0.9 %copy-start.2 = (bf16[256,256]{1,0:T(8,128)(2,1)S(1)}, bf16[256,256]{1,0:T(8,128)(2,1)}, u32[]{:S(2)}) copy-start(bf16[256,256]{1,0:T(8,128)(2,1)} %get-tuple-element.58.query) | copy-start | bytes 393220
  14.1 0.9 %copy-start.3 = (bf16[144,256]{1,0:T(8,128)(2,1)S(1)}, bf16[144,256]{1,0:T(8,128)(2,1)}, u32[]{:S(2)}) copy-start(bf16[144,256]{1,0:T(8,128)(2,1)} %get-tuple-element.57.chunk) | copy-start | bytes 221188
  15.0 0.7 %copy-start.4 = (f32[3,3,256]{2,1,0:T(4,128)S(1)}, f32[3,3,256]{2,1,0:T(4,128)}, u32[]{:S(2)}) copy-start(f32[3,3,256]{2,1,0:T(4,128)} %short_filter) | copy-start | bytes 27652
  18.6 6.2 %collective-permute-start.6 = (bf16[128,256]{1,0:T(8,128)(2,1)S(1)}, bf16[128,256]{1,0:T(8,128)(2,1)S(1)}, u32[]{:S(2)}, u32[]{:S(2)}) collective-permute-start(bf16[128,256]{1,0:T(8,128)(2,1)S(1)} %get-tuple-element.72), channel_id=1, source_target_pairs={{0,8},{8,16},{16,24},{24,0},{1,9},{9,17},{17,25},{25,1},{2,10},{10... | collective-permute-start | bytes 196616 | tf_op jit(solution)/shard_map/ppermute | solution.py:212
  19.8 6.3 %collective-permute-start.7 = (bf16[128,256]{1,0:T(8,128)(2,1)S(1)}, bf16[128,256]{1,0:T(8,128)(2,1)S(1)}, u32[]{:S(2)}, u32[]{:S(2)}) collective-permute-start(bf16[128,256]{1,0:T(8,128)(2,1)S(1)} %get-tuple-element.73), channel_id=1, source_target_pairs={{0,16},{8,24},{16,0},{24,8},{1,17},{9,25},{17,1},{25,9},{2,18},{10... | collective-permute-start | bytes 196616 | tf_op jit(solution)/shard_map/ppermute | solution.py:212
  22.4 4.5 %collective-permute-start.8 = (bf16[128,256]{1,0:T(8,128)(2,1)S(1)}, bf16[128,256]{1,0:T(8,128)(2,1)S(1)}, u32[]{:S(2)}, u32[]{:S(2)}) collective-permute-start(bf16[128,256]{1,0:T(8,128)(2,1)S(1)} %get-tuple-element.74), channel_id=1, source_target_pairs={{0,24},{8,0},{16,8},{24,16},{1,25},{9,1},{17,9},{25,17},{2,26},{10... | collective-permute-start | bytes 196616 | tf_op jit(solution)/shard_map/ppermute | solution.py:212
  27.3 2.0 %collective-permute-start.9 = (f32[128,1024]{1,0:T(8,128)S(1)}, f32[128,1024]{1,0:T(8,128)S(1)}, u32[]{:S(2)}, u32[]{:S(2)}) collective-permute-start(f32[128,1024]{1,0:T(8,128)S(1)} %get-tuple-element.77), channel_id=1, source_target_pairs={{0,1},{1,0},{2,3},{3,2},{4,5},{5,4},{6,7},{7,6},{8,9},{9,8},{10,11... | collective-permute-start | bytes 1572872 | tf_op jit(solution)/shard_map/ppermute | solution.py:212
  29.8 14.6 %collective-permute-start.10 = (bf16[256,256]{1,0:T(8,128)(2,1)S(1)}, bf16[256,256]{1,0:T(8,128)(2,1)S(1)}, u32[]{:S(2)}, u32[]{:S(2)}) collective-permute-start(bf16[256,256]{1,0:T(8,128)(2,1)S(1)} %get-tuple-element.81), channel_id=1, source_target_pairs={{0,2},{2,0},{4,6},{6,4},{1,3},{3,1},{5,7},{7,5},{8,10},{10,8},{12,... | collective-permute-start | bytes 393224 | tf_op jit(solution)/shard_map/ppermute | solution.py:216
  31.2 8.5 %collective-permute-start.13 = (bf16[32,1024]{1,0:T(8,128)(2,1)S(1)}, bf16[32,1024]{1,0:T(8,128)(2,1)S(1)}, u32[]{:S(2)}, u32[]{:S(2)}) collective-permute-start(bf16[32,1024]{1,0:T(8,128)(2,1)S(1)} %get-tuple-element.78), channel_id=1, source_target_pairs={{0,8},{8,16},{16,24},{24,0},{1,9},{9,17},{17,25},{25,1},{2,10},{10... | collective-permute-start | bytes 196616 | tf_op jit(solution)/shard_map/ppermute | solution.py:212
  31.8 8.0 %collective-permute-start.14 = (bf16[32,1024]{1,0:T(8,128)(2,1)S(1)}, bf16[32,1024]{1,0:T(8,128)(2,1)S(1)}, u32[]{:S(2)}, u32[]{:S(2)}) collective-permute-start(bf16[32,1024]{1,0:T(8,128)(2,1)S(1)} %get-tuple-element.92), channel_id=1, source_target_pairs={{0,16},{8,24},{16,0},{24,8},{1,17},{9,25},{17,1},{25,9},{2,18},{10... | collective-permute-start | bytes 196616 | tf_op jit(solution)/shard_map/ppermute | solution.py:212
  34.2 5.5 %collective-permute-start.15 = (bf16[32,1024]{1,0:T(8,128)(2,1)S(1)}, bf16[32,1024]{1,0:T(8,128)(2,1)S(1)}, u32[]{:S(2)}, u32[]{:S(2)}) collective-permute-start(bf16[32,1024]{1,0:T(8,128)(2,1)S(1)} %get-tuple-element.93), channel_id=1, source_target_pairs={{0,24},{8,0},{16,8},{24,16},{1,25},{9,1},{17,9},{25,17},{2,26},{10... | collective-permute-start | bytes 196616 | tf_op jit(solution)/shard_map/ppermute | solution.py:212
  39.8 10.9 %collective-permute-start.16 = (bf16[288,256]{1,0:T(8,128)(2,1)S(1)}, bf16[288,256]{1,0:T(8,128)(2,1)S(1)}, u32[]{:S(2)}, u32[]{:S(2)}) collective-permute-start(bf16[288,256]{1,0:T(8,128)(2,1)S(1)} %get-tuple-element.100), channel_id=1, source_target_pairs={{0,8},{8,16},{16,24},{24,0},{1,9},{9,17},{17,25},{25,1},{2,10},{10... | collective-permute-start | bytes 442376 | tf_op jit(solution)/shard_map/ppermute | solution.py:212
  41.1 11.7 %collective-permute-start.17 = (bf16[288,256]{1,0:T(8,128)(2,1)S(1)}, bf16[288,256]{1,0:T(8,128)(2,1)S(1)}, u32[]{:S(2)}, u32[]{:S(2)}) collective-permute-start(bf16[288,256]{1,0:T(8,128)(2,1)S(1)} %get-tuple-element.101), channel_id=1, source_target_pairs={{0,16},{8,24},{16,0},{24,8},{1,17},{9,25},{17,1},{25,9},{2,18},{10... | collective-permute-start | bytes 442376 | tf_op jit(solution)/shard_map/ppermute | solution.py:212
  43.0 9.8 %collective-permute-start.18 = (bf16[288,256]{1,0:T(8,128)(2,1)S(1)}, bf16[288,256]{1,0:T(8,128)(2,1)S(1)}, u32[]{:S(2)}, u32[]{:S(2)}) collective-permute-start(bf16[288,256]{1,0:T(8,128)(2,1)S(1)} %get-tuple-element.102), channel_id=1, source_target_pairs={{0,24},{8,0},{16,8},{24,16},{1,25},{9,1},{17,9},{25,17},{2,26},{10... | collective-permute-start | bytes 442376 | tf_op jit(solution)/shard_map/ppermute | solution.py:212
  43.7 7.0 %collective-permute-start.11 = (bf16[256,256]{1,0:T(8,128)(2,1)S(1)}, bf16[256,256]{1,0:T(8,128)(2,1)S(1)}, u32[]{:S(2)}, u32[]{:S(2)}) collective-permute-start(bf16[256,256]{1,0:T(8,128)(2,1)S(1)} %get-tuple-element.82), channel_id=1, source_target_pairs={{0,4},{2,6},{4,0},{6,2},{1,5},{3,7},{5,1},{7,3},{8,12},{10,14},{12... | collective-permute-start | bytes 393224 | tf_op jit(solution)/shard_map/ppermute | solution.py:216
  44.3 6.3 %collective-permute-start.12 = (bf16[256,256]{1,0:T(8,128)(2,1)S(1)}, bf16[256,256]{1,0:T(8,128)(2,1)S(1)}, u32[]{:S(2)}, u32[]{:S(2)}) collective-permute-start(bf16[256,256]{1,0:T(8,128)(2,1)S(1)} %get-tuple-element.83), channel_id=1, source_target_pairs={{0,6},{2,4},{4,2},{6,0},{1,7},{3,5},{5,3},{7,1},{8,14},{10,12},{12... | collective-permute-start | bytes 393224 | tf_op jit(solution)/shard_map/ppermute | solution.py:216
  52.8 2.8 %collective-permute-start.20 = (bf16[128,1024]{1,0:T(8,128)(2,1)S(1)}, bf16[128,1024]{1,0:T(8,128)(2,1)S(1)}, u32[]{:S(2)}, u32[]{:S(2)}) collective-permute-start(bf16[128,1024]{1,0:T(8,128)(2,1)S(1)} %get-tuple-element.106.near), channel_id=1, source_target_pairs={{0,1},{1,0},{2,3},{3,2},{4,5},{5,4},{6,7},{7,6},{8,9},{9,8},{10,11... | collective-permute-start | bytes 786440 | tf_op jit(solution)/shard_map/ppermute | solution.py:212
  52.9 2.2 %collective-permute-start.19 = (f32[32,256]{1,0:T(8,128)S(1)}, f32[32,256]{1,0:T(8,128)S(1)}, u32[]{:S(2)}, u32[]{:S(2)}) collective-permute-start(f32[32,256]{1,0:T(8,128)S(1)} %get-tuple-element.103.mine), channel_id=1, source_target_pairs={{0,1},{1,0},{2,3},{3,2},{4,5},{5,4},{6,7},{7,6},{8,9},{9,8},{10,11... | collective-permute-start | bytes 98312 | tf_op jit(solution)/shard_map/ppermute | solution.py:212

commit v2 on v1

--- a/solution.py
+++ b/solution.py
@@ -448,13 +448,6 @@
         for b in range(blocks):
             outs[s][b * rows : (b + 1) * rows] = total[:, b * width : (b + 1) * width]
         outs[s][blocks * rows :] = pays[s][...]
-
-
-def weight_out_kernel(devices, near, far, out):
-    core = lax.axis_index("dp")
-    half = near.shape[0]
-    out[block_at(core, half)] = near[...].astype(f32)
-    out[block_at(1 - core, half)] = far[...].astype(f32)
 
 
 def mixed_part_kernel(parts, y, weights, *rest):
@@ -631,7 +624,11 @@
         out[i + 1] = turned[i].T
 
 
-def small_out_kernel(scale, mine, other, short_out, long_out):
+def final_kernel(scale, near, far, mine, other, weight_out, short_out, long_out):
+    core = lax.axis_index("dp")
+    half = near.shape[0]
+    weight_out[block_at(core, half)] = near[...].astype(f32)
+    weight_out[block_at(1 - core, half)] = far[...].astype(f32)
     total = (mine[...] + other[...]) * scale
     count = long_out.shape[0]
     stacked, taps, _ = short_out.shape
@@ -732,6 +729,15 @@
         flops=2 * width * length * total_cols,
     )
     other = rotate(send, "dp", 1)
+    shares = on_core(
+        functools.partial(mixed_part_kernel, parts),
+        [((length, width), f32)] + [((length, width), bf16)] * (parts - 1),
+        (y, out_proj),
+        "mixed_part",
+        [pltpu.VMEM((length, total_cols), f32)],
+        flops=2 * width * length * total_cols,
+    )
+    keep = after(keep, shares[0])
     rows = half // devices
     sums = on_core(
         functools.partial(core_sum_kernel, devices),
@@ -741,17 +747,6 @@
         [pltpu.VMEM((half, total_cols), f32)],
     )
     parts_out = scatter_chunks(sums, "ctx")
-
-    shares = on_core(
-        functools.partial(mixed_part_kernel, parts),
-        [((length, width), f32)] + [((length, width), bf16)] * (parts - 1),
-        (after(y, sums[1]), out_proj),
-        "mixed_part",
-        [pltpu.VMEM((length, total_cols), f32)],
-        flops=2 * width * length * total_cols,
-    )
-    shares = [shares[0]] + [swap(shares[s], "tp", s) for s in range(1, parts)]
-    (mixed,) = on_core(mixed_sum_kernel, [((length, width), bf16)], shares, "mixed_sum")
 
     outs = on_core(
         functools.partial(backward_kernel, devices, taps),
@@ -775,8 +770,12 @@
         (*parts_out, *back),
         "block_sum",
     )
+    shares = [shares[0]] + [
+        swap(shares[s], "tp", s) for s in range(1, parts)
+    ]
+    (mixed,) = on_core(mixed_sum_kernel, [((length, width), bf16)], shares, "mixed_sum")
     back = scatter_chunks(back, "ctx")
-    back[0] = after(back[0], shares[1:])
+    back[0] = after(back[0], mixed)
     near, small = on_core(
         functools.partial(collect_kernel, devices, groups, rows, stacked),
         [((half, total_cols), bf16), ((count + 16, width), f32)],
@@ -792,17 +791,11 @@
         "grad_out",
         [pltpu.VMEM((stacked - 1, width, length), bf16)],
     )
-    grad_short, grad_long = on_core(
-        functools.partial(small_out_kernel, grad_scale),
-        [(short_filter.shape, f32), ((count, length), f32)],
-        (small, other_small),
-        "small_out",
-    )
-    (grad_out_proj,) = on_core(
-        functools.partial(weight_out_kernel, devices),
-        [((width, total_cols), f32)],
-        (near, far),
-        "weight_out",
+    grad_out_proj, grad_short, grad_long = on_core(
+        functools.partial(final_kernel, grad_scale),
+        [((width, total_cols), f32), (short_filter.shape, f32), ((count, length), f32)],
+        (near, far, after(small, grad_projected), other_small),
+        "final",
     )
     return (mixed[None], grad_projected[:, None], grad_short, grad_long, grad_out_proj)
 

time: 57.8 us -> 55.2 us (0.955)
  the two profiles are of different devices: /device:TPU:0 before, /device:TPU:9 now
where the time goes in v2:
time: 55.2 us; the launch traced here: 54.9 us
  starting transfers between devices  24.6 us (45%)
  waiting for transfers between devices  16.7 us (30%)
  Pallas kernels  10.3 us (19%)
  local copies, waits for them, and re-layouts  2.5 us (5%)
  between operations  0.78 us (1%)
    ppermute x15, starting transfers between devices, rotate(): lax.ppermute(value, axis, [(i, (i + steps) % count) for i in range(count)])  18.5 us
    ppermute x15, waiting for transfers between devices, rotate(): lax.ppermute(value, axis, [(i, (i + steps) % count) for i in range(count)])  13 us
    pallas_call x13, Pallas kernels, on_core(): pl.pallas_call(kernel, out_shape=[jax.ShapeDtypeStruct(shape, kind) for s...  10.3 us
    ppermute x6, starting transfers between devices, swap(): lax.ppermute(value, axis, [(i, i ^ bits) for i in range(lax.axis_size(axi...  6.14 us
    ppermute x6, waiting for transfers between devices, swap(): lax.ppermute(value, axis, [(i, i ^ bits) for i in range(lax.axis_size(axi...  3.74 us
    unnamed x10, local copies, waits for them, and re-layouts  2.5 us
  transfers between devices with their start and end apart: 21, of which 11 were waited for; matrix products, arithmetic and copies ran while one was open for 0% of the time, Pallas kernels for 15%

profile of v2, /device:TPU:9, one launch (start us, length us, event | category | flops | bytes accessed | tf_op | source)
XLA Modules:
  0.0 54.9 jit_solution(5501848380685914068)
XLA Ops:
  0.6 0.0 copy-start.1
  0.6 0.0 copy-start
  0.7 1.3 %collective-permute-start = (bf16[256,256]{1,0:T(8,128)(2,1)}, bf16[256,256]{1,0:T(8,128)(2,1)S(1)}, u32[]{:S(2)}, u32[]{:S(2)}) collective-permute-start(bf16[256,256]{1,0:T(8,128)(2,1)} %bitcast.6), channel_id=1, source_target_pairs={{0,2},{2,0},{4,6},{6,4},{1,3},{3,1},{5,7},{7,5},{8,10},{10,8},{12,... | collective-permute-start | bytes 393224 | tf_op jit(solution)/shard_map/ppermute | solution.py:216
  1.9 1.9 %pack.1 = (bf16[144,256]{1,0:T(8,128)(2,1)}, bf16[160,256]{1,0:T(8,128)(2,1)}, bf16[144,256]{1,0:T(8,128)(2,1)}, bf16[144,256]{1,0:T(8,128)(2,1)}, bf16[256,256]{1,0:T(8,128)(2,1)}) custom-call(bf16[3,256,256]{2,1,0:T(8,128)(2,1)} %bitcast.11, f32[16,256]{1,0:T(8,128)} %refs_1_.1, s32[1,256]{1,0:T(1,128)} %refs_2_.1), custom_call_target="tpu_custom_call" | custom-call | bytes 844800 | tf_op jit(solution)/shard_map/pack/pallas_call | solution.py:234
  3.9 1.3 %collective-permute-start.1 = (bf16[160,256]{1,0:T(8,128)(2,1)}, bf16[160,256]{1,0:T(8,128)(2,1)S(1)}, u32[]{:S(2)}, u32[]{:S(2)}) collective-permute-start(bf16[160,256]{1,0:T(8,128)(2,1)} %get-tuple-element.62), channel_id=1, source_target_pairs={{0,8},{8,16},{16,24},{24,0},{1,9},{9,17},{17,25},{25,1},{2,10},{10... | collective-permute-start | bytes 245768 | tf_op jit(solution)/shard_map/ppermute | solution.py:212
  5.2 1.2 %collective-permute-start.4 = (bf16[256,256]{1,0:T(8,128)(2,1)}, bf16[256,256]{1,0:T(8,128)(2,1)S(1)}, u32[]{:S(2)}, u32[]{:S(2)}) collective-permute-start(bf16[256,256]{1,0:T(8,128)(2,1)} %bitcast.7), channel_id=1, source_target_pairs={{0,4},{2,6},{4,0},{6,2},{1,5},{3,7},{5,1},{7,3},{8,12},{10,14},{12... | collective-permute-start | bytes 393224 | tf_op jit(solution)/shard_map/ppermute | solution.py:216
  6.5 0.0 collective-permute-done.rest_1_
  6.5 0.2 collective-permute-start.5
  6.7 2.2 %collective-permute-start.2 = (bf16[144,256]{1,0:T(8,128)(2,1)}, bf16[144,256]{1,0:T(8,128)(2,1)S(1)}, u32[]{:S(2)}, u32[]{:S(2)}) collective-permute-start(bf16[144,256]{1,0:T(8,128)(2,1)} %get-tuple-element.65), channel_id=1, source_target_pairs={{0,16},{8,24},{16,0},{24,8},{1,17},{9,25},{17,1},{25,9},{2,18},{10... | collective-permute-start | bytes 221192 | tf_op jit(solution)/shard_map/ppermute | solution.py:212
  8.8 0.3 collective-permute-start.3
  9.2 0.0 copy-start.2
  9.2 0.9 %copy-done.2 = bf16[256,256]{1,0:T(8,128)(2,1)S(1)} copy-done((bf16[256,256]{1,0:T(8,128)(2,1)S(1)}, bf16[256,256]{1,0:T(8,128)(2,1)}, u32[]{:S(2)}) %copy-start.2) | copy-done | bytes 131096
  10.1 0.0 copy-start.3
  10.1 0.9 %copy-done.3 = bf16[144,256]{1,0:T(8,128)(2,1)S(1)} copy-done((bf16[144,256]{1,0:T(8,128)(2,1)S(1)}, bf16[144,256]{1,0:T(8,128)(2,1)}, u32[]{:S(2)}) %copy-start.3) | copy-done | bytes 73752
  11.0 0.0 copy-start.4
  11.0 0.7 %copy-done.4 = f32[3,3,256]{2,1,0:T(4,128)S(1)} copy-done((f32[3,3,256]{2,1,0:T(4,128)S(1)}, f32[3,3,256]{2,1,0:T(4,128)}, u32[]{:S(2)}) %copy-start.4) | copy-done | bytes 9240
  11.7 0.1 prepare.1
  11.8 0.3 collective-permute-done.2.rest_2_
  12.1 1.8 %collective-permute-done.3.rest_3_ = bf16[144,256]{1,0:T(8,128)(2,1)S(1)} collective-permute-done((bf16[144,256]{1,0:T(8,128)(2,1)}, bf16[144,256]{1,0:T(8,128)(2,1)S(1)}, u32[]{:S(2)}, u32[]{:S(2)}) %collective-permute-start.3) | collective-permute-done | bytes 73760 | tf_op jit(solution)/shard_map/ppermute | solution.py:212
  13.8 0.0 collective-permute-done.1.rest_1_.previous
  13.8 1.4 %conv.1 = (bf16[64,256]{1,0:T(8,128)(2,1)S(1)}, bf16[64,256]{1,0:T(8,128)(2,1)S(1)}, bf16[64,256]{1,0:T(8,128)(2,1)S(1)}, bf16[64,256]{1,0:T(8,128)(2,1)S(1)}, f...) custom-call(f32[256,16]{1,0:T(8,128)S(1)} %get-tuple-element.63.colu, ...), custom_call_target="tpu_custom_call" | custom-call | flops 536870912 | bytes 3366912 | tf_op jit(solution)/shard_map/conv/pallas_call | solution.py:234
  15.3 0.0 collective-permute-done.4.rest_2_
  15.3 0.0 collective-permute-done.5.rest_3_
  15.3 0.0 copy-done.1
  15.3 0.0 copy-done
  15.3 0.4 grad_y.1
  15.7 0.1 collective-permute-start.6
  15.8 2.1 %collective-permute-start.7 = (bf16[128,256]{1,0:T(8,128)(2,1)S(1)}, bf16[128,256]{1,0:T(8,128)(2,1)S(1)}, u32[]{:S(2)}, u32[]{:S(2)}) collective-permute-start(bf16[128,256]{1,0:T(8,128)(2,1)S(1)} %get-tuple-element.75), channel_id=1, source_target_pairs={{0,16},{8,24},{16,0},{24,8},{1,17},{9,25},{17,1},{25,9},{2,18},{10... | collective-permute-start | bytes 196616 | tf_op jit(solution)/shard_map/ppermute | solution.py:212
  17.9 1.4 %collective-permute-start.8 = (bf16[128,256]{1,0:T(8,128)(2,1)S(1)}, bf16[128,256]{1,0:T(8,128)(2,1)S(1)}, u32[]{:S(2)}, u32[]{:S(2)}) collective-permute-start(bf16[128,256]{1,0:T(8,128)(2,1)S(1)} %get-tuple-element.76), channel_id=1, source_target_pairs={{0,24},{8,0},{16,8},{24,16},{1,25},{9,1},{17,9},{25,17},{2,26},{10... | collective-permute-start | bytes 196616 | tf_op jit(solution)/shard_map/ppermute | solution.py:212
  19.3 0.0 collective-permute-done.6.rest_5_.rest_1_
  19.3 1.0 %collective-permute-done.7.rest_6_.rest_2_ = bf16[128,256]{1,0:T(8,128)(2,1)S(1)} collective-permute-done((bf16[128,256]{1,0:T(8,128)(2,1)S(1)}, bf16[128,256]{1,0:T(8,128)(2,1)S(1)}, u32[]{:S(2)}, u32[]{:S(2)}) %collective-permute-start.7) | collective-permute-done | bytes 65568 | tf_op jit(solution)/shard_map/ppermute | solution.py:212
  20.3 1.6 %collective-permute-done.8.rest_7_.rest_3_ = bf16[128,256]{1,0:T(8,128)(2,1)S(1)} collective-permute-done((bf16[128,256]{1,0:T(8,128)(2,1)S(1)}, bf16[128,256]{1,0:T(8,128)(2,1)S(1)}, u32[]{:S(2)}, u32[]{:S(2)}) %collective-permute-start.8) | collective-permute-done | bytes 65568 | tf_op jit(solution)/shard_map/ppermute | solution.py:212
  21.9 0.4 weight_grad.1
  22.3 3.3 %collective-permute-start.12 = (f32[128,1024]{1,0:T(8,128)S(1)}, f32[128,1024]{1,0:T(8,128)S(1)}, u32[]{:S(2)}, u32[]{:S(2)}) collective-permute-start(f32[128,1024]{1,0:T(8,128)S(1)} %get-tuple-element.89), channel_id=1, source_target_pairs={{0,1},{1,0},{2,3},{3,2},{4,5},{5,4},{6,7},{7,6},{8,9},{9,8},{10,11... | collective-permute-start | bytes 1572872 | tf_op jit(solution)/shard_map/ppermute | solution.py:212
  25.6 0.4 mixed_part.1
  26.0 1.2 %collective-permute-start.9 = (bf16[256,256]{1,0:T(8,128)(2,1)S(1)}, bf16[256,256]{1,0:T(8,128)(2,1)S(1)}, u32[]{:S(2)}, u32[]{:S(2)}) collective-permute-start(bf16[256,256]{1,0:T(8,128)(2,1)S(1)} %get-tuple-element.79), channel_id=1, source_target_pairs={{0,2},{2,0},{4,6},{6,4},{1,3},{3,1},{5,7},{7,5},{8,10},{10,8},{12,... | collective-permute-start | bytes 393224 | tf_op jit(solution)/shard_map/ppermute | solution.py:216
  27.1 0.0 collective-permute-done.12.other
  27.1 0.1 core_sum.1
  27.2 0.6 %collective-permute-start.13 = (bf16[32,1024]{1,0:T(8,128)(2,1)S(1)}, bf16[32,1024]{1,0:T(8,128)(2,1)S(1)}, u32[]{:S(2)}, u32[]{:S(2)}) collective-permute-start(bf16[32,1024]{1,0:T(8,128)(2,1)S(1)} %get-tuple-element.90), channel_id=1, source_target_pairs={{0,8},{8,16},{16,24},{24,0},{1,9},{9,17},{17,25},{25,1},{2,10},{10... | collective-permute-start | bytes 196616 | tf_op jit(solution)/shard_map/ppermute | solution.py:212
  27.8 2.7 %collective-permute-start.14 = (bf16[32,1024]{1,0:T(8,128)(2,1)S(1)}, bf16[32,1024]{1,0:T(8,128)(2,1)S(1)}, u32[]{:S(2)}, u32[]{:S(2)}) collective-permute-start(bf16[32,1024]{1,0:T(8,128)(2,1)S(1)} %get-tuple-element.94), channel_id=1, source_target_pairs={{0,16},{8,24},{16,0},{24,8},{1,17},{9,25},{17,1},{25,9},{2,18},{10... | collective-permute-start | bytes 196616 | tf_op jit(solution)/shard_map/ppermute | solution.py:212
  30.5 0.3 collective-permute-start.15
  30.9 2.7 %backward.1 = (bf16[160,256]{1,0:T(8,128)(2,1)S(1)}, bf16[160,256]{1,0:T(8,128)(2,1)S(1)}, bf16[160,256]{1,0:T(8,128)(2,1)S(1)}, bf16[160,256]{1,0:T(8,128)(2,1)S(1)}, f32[256,256]{1,0:T(8,128)S(1)}) custom-call(f32[2,64,1024]{2,1,0:T(8,128)S(1)} %get-tuple-element.82.conv, bf16[128,1024]{1,0:T(8,128)(2,1)S(1)} %get-tuple-element.83.source, ...), custom_call_target="tpu_custom_call" | custom-call | flops 1073741824 | bytes 4521984 | tf_op jit(solution)/shard_map/backward/pallas_call | solution.py:234
  33.6 1.4 %collective-permute-done.14.refs_2_ = bf16[32,1024]{1,0:T(8,128)(2,1)S(1)} collective-permute-done((bf16[32,1024]{1,0:T(8,128)(2,1)S(1)}, bf16[32,1024]{1,0:T(8,128)(2,1)S(1)}, u32[]{:S(2)}, u32[]{:S(2)}) %collective-permute-start.14) | collective-permute-done | bytes 65568 | tf_op jit(solution)/shard_map/ppermute | solution.py:212
  35.1 1.0 %collective-permute-done.15.refs_3_ = bf16[32,1024]{1,0:T(8,128)(2,1)S(1)} collective-permute-done((bf16[32,1024]{1,0:T(8,128)(2,1)S(1)}, bf16[32,1024]{1,0:T(8,128)(2,1)S(1)}, u32[]{:S(2)}, u32[]{:S(2)}) %collective-permute-start.15) | collective-permute-done | bytes 65568 | tf_op jit(solution)/shard_map/ppermute | solution.py:212
  36.1 0.0 collective-permute-done.13.refs_1_
  36.2 0.1 collective-permute-start.16
  36.2 2.1 %collective-permute-start.17 = (bf16[288,256]{1,0:T(8,128)(2,1)S(1)}, bf16[288,256]{1,0:T(8,128)(2,1)S(1)}, u32[]{:S(2)}, u32[]{:S(2)}) collective-permute-start(bf16[288,256]{1,0:T(8,128)(2,1)S(1)} %get-tuple-element.103), channel_id=1, source_target_pairs={{0,16},{8,24},{16,0},{24,8},{1,17},{9,25},{17,1},{25,9},{2,18},{10... | collective-permute-start | bytes 442376 | tf_op jit(solution)/shard_map/ppermute | solution.py:212
  38.4 1.4 %collective-permute-start.18 = (bf16[288,256]{1,0:T(8,128)(2,1)S(1)}, bf16[288,256]{1,0:T(8,128)(2,1)S(1)}, u32[]{:S(2)}, u32[]{:S(2)}) collective-permute-start(bf16[288,256]{1,0:T(8,128)(2,1)S(1)} %get-tuple-element.104), channel_id=1, source_target_pairs={{0,24},{8,0},{16,8},{24,16},{1,25},{9,1},{17,9},{25,17},{2,26},{10... | collective-permute-start | bytes 442376 | tf_op jit(solution)/shard_map/ppermute | solution.py:212
  39.7 1.0 %collective-permute-start.10 = (bf16[256,256]{1,0:T(8,128)(2,1)S(1)}, bf16[256,256]{1,0:T(8,128)(2,1)S(1)}, u32[]{:S(2)}, u32[]{:S(2)}) collective-permute-start(bf16[256,256]{1,0:T(8,128)(2,1)S(1)} %get-tuple-element.80), channel_id=1, source_target_pairs={{0,4},{2,6},{4,0},{6,2},{1,5},{3,7},{5,1},{7,3},{8,12},{10,14},{12... | collective-permute-start | bytes 393224 | tf_op jit(solution)/shard_map/ppermute | solution.py:216
  40.7 0.0 collective-permute-done.9.refs_1_
  40.7 1.3 %collective-permute-start.11 = (bf16[256,256]{1,0:T(8,128)(2,1)S(1)}, bf16[256,256]{1,0:T(8,128)(2,1)S(1)}, u32[]{:S(2)}, u32[]{:S(2)}) collective-permute-start(bf16[256,256]{1,0:T(8,128)(2,1)S(1)} %get-tuple-element.81), channel_id=1, source_target_pairs={{0,6},{2,4},{4,2},{6,0},{1,7},{3,5},{5,3},{7,1},{8,14},{10,12},{12... | collective-permute-start | bytes 393224 | tf_op jit(solution)/shard_map/ppermute | solution.py:216
  42.0 1.6 %collective-permute-done.10.refs_2_ = bf16[256,256]{1,0:T(8,128)(2,1)S(1)} collective-permute-done((bf16[256,256]{1,0:T(8,128)(2,1)S(1)}, bf16[256,256]{1,0:T(8,128)(2,1)S(1)}, u32[]{:S(2)}, u32[]{:S(2)}) %collective-permute-start.10) | collective-permute-done | bytes 131104 | tf_op jit(solution)/shard_map/ppermute | solution.py:216
  43.6 2.1 %collective-permute-done.11.refs_3_ = bf16[256,256]{1,0:T(8,128)(2,1)S(1)} collective-permute-done((bf16[256,256]{1,0:T(8,128)(2,1)S(1)}, bf16[256,256]{1,0:T(8,128)(2,1)S(1)}, u32[]{:S(2)}, u32[]{:S(2)}) %collective-permute-start.11) | collective-permute-done | bytes 131104 | tf_op jit(solution)/shard_map/ppermute | solution.py:216
  45.7 0.7 %mixed_sum.1 = bf16[256,256]{1,0:T(8,128)(2,1)} custom-call(f32[256,256]{1,0:T(8,128)S(1)} %get-tuple-element.78.refs_0_, bf16[256,256]{1,0:T(8,128)(2,1)S(1)} %collective-permute-done.9.refs_1_, bf16[256,256]{1,0:T(8,128)(2,1)S(1)} %collective-permute-done.10.refs_2_, bf16[256,256]{1,0:T(8,128)(2,1)S(1)} %collective-permute-done.11.refs_3_), custom_call_target="tpu_custom_call" | custom-call | bytes 786432 | tf_op jit(solution)/shard_map/mixed_sum/pallas_call | solution.py:234
  46.4 0.0 collective-permute-done.16.refs_1_
  46.4 1.9 %collective-permute-done.17.refs_2_ = bf16[288,256]{1,0:T(8,128)(2,1)S(1)} collective-permute-done((bf16[288,256]{1,0:T(8,128)(2,1)S(1)}, bf16[288,256]{1,0:T(8,128)(2,1)S(1)}, u32[]{:S(2)}, u32[]{:S(2)}) %collective-permute-start.17) | collective-permute-done | bytes 147488 | tf_op jit(solution)/shard_map/ppermute | solution.py:212
  48.3 3.8 %collective-permute-done.18.refs_3_ = bf16[288,256]{1,0:T(8,128)(2,1)S(1)} collective-permute-done((bf16[288,256]{1,0:T(8,128)(2,1)S(1)}, bf16[288,256]{1,0:T(8,128)(2,1)S(1)}, u32[]{:S(2)}, u32[]{:S(2)}) %collective-permute-start.18) | collective-permute-done | bytes 147488 | tf_op jit(solution)/shard_map/ppermute | solution.py:212
  52.1 0.6 %collective-permute-start.19 = (bf16[128,1024]{1,0:T(8,128)(2,1)S(1)}, bf16[128,1024]{1,0:T(8,128)(2,1)S(1)}, u32[]{:S(2)}, u32[]{:S(2)}) collective-permute-start(bf16[128,1024]{1,0:T(8,128)(2,1)S(1)} %get-tuple-element.105.near), channel_id=1, source_target_pairs={{0,1},{1,0},{2,3},{3,2},{4,5},{5,4},{6,7},{7,6},{8,9},{9,8},{10,11... | collective-permute-start | bytes 786440 | tf_op jit(solution)/shard_map/ppermute | solution.py:212
  52.7 0.1 collective-permute-start.20
  52.8 0.9 %grad_out.1 = bf16[3,256,256]{2,1,0:T(8,128)(2,1)} custom-call(f32[256,256]{1,0:T(8,128)S(1)} %get-tuple-element.92.query_part, bf16[288,256]{1,0:T(8,128)(2,1)S(1)} %get-tuple-element.101.refs_0_, bf16[288,256]{1,0:T(8,128)(2,1)S(1)} %collective-permute-done.16.refs_1_, bf16[288,256]{1,0:T(8,128)(2,1)S(1)} %collective-permute-done.17.refs_2_, ...), custom_call_target="tpu_custom_call" | custom-call | bytes 1245184 | tf_op jit(solution)/shard_map/grad_out/pallas_call | solution.py:234
  53.7 0.2 collective-permute-done.20.other
  53.9 0.0 collective-permute-done.19.far
  53.9 1.0 %final.1 = (f32[256,1024]{1,0:T(8,128)}, f32[3,3,256]{2,1,0:T(4,128)}, f32[16,256]{1,0:T(8,128)}) custom-call(bf16[128,1024]{1,0:T(8,128)(2,1)S(1)} %get-tuple-element.105.near, bf16[128,1024]{1,0:T(8,128)(2,1)S(1)} %collective-permute-done.19.far, f32[32,256]{1,0:T(8,128)S(1)} %get-tuple-element.107.mine, f32[32,256]{1,0:T(8,128)S(1)} %collective-permute-done.20.other), custom_call_target="tpu_custom_call" | custom-call | bytes 1664000 | tf_op jit(solution)/shard_map/final/pallas_call | solution.py:234
  (2 shorter events, 0.1 us)
Async XLA Ops:
  0.6 14.7 %copy-start.1 = (bf16[1,256,256]{2,1,0:T(8,128)(2,1)S(1)}, bf16[1,256,256]{2,1,0:T(8,128)(2,1)}, u32[]{:S(2)}) copy-start(bf16[1,256,256]{2,1,0:T(8,128)(2,1)} %param.11) | copy-start | bytes 393220
  0.6 14.7 %copy-start = (bf16[256,1024]{1,0:T(8,128)(2,1)S(1)}, bf16[256,1024]{1,0:T(8,128)(2,1)}, u32[]{:S(2)}) copy-start(bf16[256,1024]{1,0:T(8,128)(2,1)} %weights.3) | copy-start | bytes 1572868
  0.7 5.8 %collective-permute-start = (bf16[256,256]{1,0:T(8,128)(2,1)}, bf16[256,256]{1,0:T(8,128)(2,1)S(1)}, u32[]{:S(2)}, u32[]{:S(2)}) collective-permute-start(bf16[256,256]{1,0:T(8,128)(2,1)} %bitcast.6), channel_id=1, source_target_pairs={{0,2},{2,0},{4,6},{6,4},{1,3},{3,1},{5,7},{7,5},{8,10},{10,8},{12,... | collective-permute-start | bytes 393224 | tf_op jit(solution)/shard_map/ppermute | solution.py:216
  3.9 10.0 %collective-permute-start.1 = (bf16[160,256]{1,0:T(8,128)(2,1)}, bf16[160,256]{1,0:T(8,128)(2,1)S(1)}, u32[]{:S(2)}, u32[]{:S(2)}) collective-permute-start(bf16[160,256]{1,0:T(8,128)(2,1)} %get-tuple-element.62), channel_id=1, source_target_pairs={{0,8},{8,16},{16,24},{24,0},{1,9},{9,17},{17,25},{25,1},{2,10},{10... | collective-permute-start | bytes 245768 | tf_op jit(solution)/shard_map/ppermute | solution.py:212
  5.2 10.1 %collective-permute-start.4 = (bf16[256,256]{1,0:T(8,128)(2,1)}, bf16[256,256]{1,0:T(8,128)(2,1)S(1)}, u32[]{:S(2)}, u32[]{:S(2)}) collective-permute-start(bf16[256,256]{1,0:T(8,128)(2,1)} %bitcast.7), channel_id=1, source_target_pairs={{0,4},{2,6},{4,0},{6,2},{1,5},{3,7},{5,1},{7,3},{8,12},{10,14},{12... | collective-permute-start | bytes 393224 | tf_op jit(solution)/shard_map/ppermute | solution.py:216
  6.5 8.8 %collective-permute-start.5 = (bf16[256,256]{1,0:T(8,128)(2,1)S(1)}, bf16[256,256]{1,0:T(8,128)(2,1)S(1)}, u32[]{:S(2)}, u32[]{:S(2)}) collective-permute-start(bf16[256,256]{1,0:T(8,128)(2,1)S(1)} %collective-permute-done.rest_1_), channel_id=1, source_target_pairs={{0,4},{2,6},{4,0},{6,2},{1,5},{3,7},{5,1},{7,3},{8,12},{10,14},{12... | collective-permute-start | bytes 393224 | tf_op jit(solution)/shard_map/ppermute | solution.py:216
  6.7 5.4 %collective-permute-start.2 = (bf16[144,256]{1,0:T(8,128)(2,1)}, bf16[144,256]{1,0:T(8,128)(2,1)S(1)}, u32[]{:S(2)}, u32[]{:S(2)}) collective-permute-start(bf16[144,256]{1,0:T(8,128)(2,1)} %get-tuple-element.65), channel_id=1, source_target_pairs={{0,16},{8,24},{16,0},{24,8},{1,17},{9,25},{17,1},{25,9},{2,18},{10... | collective-permute-start | bytes 221192 | tf_op jit(solution)/shard_map/ppermute | solution.py:212
  8.8 5.0 %collective-permute-start.3 = (bf16[144,256]{1,0:T(8,128)(2,1)}, bf16[144,256]{1,0:T(8,128)(2,1)S(1)}, u32[]{:S(2)}, u32[]{:S(2)}) collective-permute-start(bf16[144,256]{1,0:T(8,128)(2,1)} %get-tuple-element.66), channel_id=1, source_target_pairs={{0,24},{8,0},{16,8},{24,16},{1,25},{9,1},{17,9},{25,17},{2,26},{10... | collective-permute-start | bytes 221192 | tf_op jit(solution)/shard_map/ppermute | solution.py:212
  9.2 0.9 %copy-start.2 = (bf16[256,256]{1,0:T(8,128)(2,1)S(1)}, bf16[256,256]{1,0:T(8,128)(2,1)}, u32[]{:S(2)}) copy-start(bf16[256,256]{1,0:T(8,128)(2,1)} %get-tuple-element.60.query) | copy-start | bytes 393220
  10.1 0.9 %copy-start.3 = (bf16[144,256]{1,0:T(8,128)(2,1)S(1)}, bf16[144,256]{1,0:T(8,128)(2,1)}, u32[]{:S(2)}) copy-start(bf16[144,256]{1,0:T(8,128)(2,1)} %get-tuple-element.59.chunk) | copy-start | bytes 221188
  11.0 0.7 %copy-start.4 = (f32[3,3,256]{2,1,0:T(4,128)S(1)}, f32[3,3,256]{2,1,0:T(4,128)}, u32[]{:S(2)}) copy-start(f32[3,3,256]{2,1,0:T(4,128)} %short_filter) | copy-start | bytes 27652
  15.7 3.5 %collective-permute-start.6 = (bf16[128,256]{1,0:T(8,128)(2,1)S(1)}, bf16[128,256]{1,0:T(8,128)(2,1)S(1)}, u32[]{:S(2)}, u32[]{:S(2)}) collective-permute-start(bf16[128,256]{1,0:T(8,128)(2,1)S(1)} %get-tuple-element.74), channel_id=1, source_target_pairs={{0,8},{8,16},{16,24},{24,0},{1,9},{9,17},{17,25},{25,1},{2,10},{10... | collective-permute-start | bytes 196616 | tf_op jit(solution)/shard_map/ppermute | solution.py:212
  15.8 4.4 %collective-permute-start.7 = (bf16[128,256]{1,0:T(8,128)(2,1)S(1)}, bf16[128,256]{1,0:T(8,128)(2,1)S(1)}, u32[]{:S(2)}, u32[]{:S(2)}) collective-permute-start(bf16[128,256]{1,0:T(8,128)(2,1)S(1)} %get-tuple-element.75), channel_id=1, source_target_pairs={{0,16},{8,24},{16,0},{24,8},{1,17},{9,25},{17,1},{25,9},{2,18},{10... | collective-permute-start | bytes 196616 | tf_op jit(solution)/shard_map/ppermute | solution.py:212
  17.9 4.0 %collective-permute-start.8 = (bf16[128,256]{1,0:T(8,128)(2,1)S(1)}, bf16[128,256]{1,0:T(8,128)(2,1)S(1)}, u32[]{:S(2)}, u32[]{:S(2)}) collective-permute-start(bf16[128,256]{1,0:T(8,128)(2,1)S(1)} %get-tuple-element.76), channel_id=1, source_target_pairs={{0,24},{8,0},{16,8},{24,16},{1,25},{9,1},{17,9},{25,17},{2,26},{10... | collective-permute-start | bytes 196616 | tf_op jit(solution)/shard_map/ppermute | solution.py:212
  22.3 4.8 %collective-permute-start.12 = (f32[128,1024]{1,0:T(8,128)S(1)}, f32[128,1024]{1,0:T(8,128)S(1)}, u32[]{:S(2)}, u32[]{:S(2)}) collective-permute-start(f32[128,1024]{1,0:T(8,128)S(1)} %get-tuple-element.89), channel_id=1, source_target_pairs={{0,1},{1,0},{2,3},{3,2},{4,5},{5,4},{6,7},{7,6},{8,9},{9,8},{10,11... | collective-permute-start | bytes 1572872 | tf_op jit(solution)/shard_map/ppermute | solution.py:212
  26.0 14.7 %collective-permute-start.9 = (bf16[256,256]{1,0:T(8,128)(2,1)S(1)}, bf16[256,256]{1,0:T(8,128)(2,1)S(1)}, u32[]{:S(2)}, u32[]{:S(2)}) collective-permute-start(bf16[256,256]{1,0:T(8,128)(2,1)S(1)} %get-tuple-element.79), channel_id=1, source_target_pairs={{0,2},{2,0},{4,6},{6,4},{1,3},{3,1},{5,7},{7,5},{8,10},{10,8},{12,... | collective-permute-start | bytes 393224 | tf_op jit(solution)/shard_map/ppermute | solution.py:216
  27.2 8.9 %collective-permute-start.13 = (bf16[32,1024]{1,0:T(8,128)(2,1)S(1)}, bf16[32,1024]{1,0:T(8,128)(2,1)S(1)}, u32[]{:S(2)}, u32[]{:S(2)}) collective-permute-start(bf16[32,1024]{1,0:T(8,128)(2,1)S(1)} %get-tuple-element.90), channel_id=1, source_target_pairs={{0,8},{8,16},{16,24},{24,0},{1,9},{9,17},{17,25},{25,1},{2,10},{10... | collective-permute-start | bytes 196616 | tf_op jit(solution)/shard_map/ppermute | solution.py:212
  27.8 7.3 %collective-permute-start.14 = (bf16[32,1024]{1,0:T(8,128)(2,1)S(1)}, bf16[32,1024]{1,0:T(8,128)(2,1)S(1)}, u32[]{:S(2)}, u32[]{:S(2)}) collective-permute-start(bf16[32,1024]{1,0:T(8,128)(2,1)S(1)} %get-tuple-element.94), channel_id=1, source_target_pairs={{0,16},{8,24},{16,0},{24,8},{1,17},{9,25},{17,1},{25,9},{2,18},{10... | collective-permute-start | bytes 196616 | tf_op jit(solution)/shard_map/ppermute | solution.py:212
  30.5 5.6 %collective-permute-start.15 = (bf16[32,1024]{1,0:T(8,128)(2,1)S(1)}, bf16[32,1024]{1,0:T(8,128)(2,1)S(1)}, u32[]{:S(2)}, u32[]{:S(2)}) collective-permute-start(bf16[32,1024]{1,0:T(8,128)(2,1)S(1)} %get-tuple-element.95), channel_id=1, source_target_pairs={{0,24},{8,0},{16,8},{24,16},{1,25},{9,1},{17,9},{25,17},{2,26},{10... | collective-permute-start | bytes 196616 | tf_op jit(solution)/shard_map/ppermute | solution.py:212
  36.2 10.3 %collective-permute-start.16 = (bf16[288,256]{1,0:T(8,128)(2,1)S(1)}, bf16[288,256]{1,0:T(8,128)(2,1)S(1)}, u32[]{:S(2)}, u32[]{:S(2)}) collective-permute-start(bf16[288,256]{1,0:T(8,128)(2,1)S(1)} %get-tuple-element.102), channel_id=1, source_target_pairs={{0,8},{8,16},{16,24},{24,0},{1,9},{9,17},{17,25},{25,1},{2,10},{10... | collective-permute-start | bytes 442376 | tf_op jit(solution)/shard_map/ppermute | solution.py:212
  36.2 12.1 %collective-permute-start.17 = (bf16[288,256]{1,0:T(8,128)(2,1)S(1)}, bf16[288,256]{1,0:T(8,128)(2,1)S(1)}, u32[]{:S(2)}, u32[]{:S(2)}) collective-permute-start(bf16[288,256]{1,0:T(8,128)(2,1)S(1)} %get-tuple-element.103), channel_id=1, source_target_pairs={{0,16},{8,24},{16,0},{24,8},{1,17},{9,25},{17,1},{25,9},{2,18},{10... | collective-permute-start | bytes 442376 | tf_op jit(solution)/shard_map/ppermute | solution.py:212
  38.4 13.7 %collective-permute-start.18 = (bf16[288,256]{1,0:T(8,128)(2,1)S(1)}, bf16[288,256]{1,0:T(8,128)(2,1)S(1)}, u32[]{:S(2)}, u32[]{:S(2)}) collective-permute-start(bf16[288,256]{1,0:T(8,128)(2,1)S(1)} %get-tuple-element.104), channel_id=1, source_target_pairs={{0,24},{8,0},{16,8},{24,16},{1,25},{9,1},{17,9},{25,17},{2,26},{10... | collective-permute-start | bytes 442376 | tf_op jit(solution)/shard_map/ppermute | solution.py:212
  39.7 3.8 %collective-permute-start.10 = (bf16[256,256]{1,0:T(8,128)(2,1)S(1)}, bf16[256,256]{1,0:T(8,128)(2,1)S(1)}, u32[]{:S(2)}, u32[]{:S(2)}) collective-permute-start(bf16[256,256]{1,0:T(8,128)(2,1)S(1)} %get-tuple-element.80), channel_id=1, source_target_pairs={{0,4},{2,6},{4,0},{6,2},{1,5},{3,7},{5,1},{7,3},{8,12},{10,14},{12... | collective-permute-start | bytes 393224 | tf_op jit(solution)/shard_map/ppermute | solution.py:216
  40.7 5.0 %collective-permute-start.11 = (bf16[256,256]{1,0:T(8,128)(2,1)S(1)}, bf16[256,256]{1,0:T(8,128)(2,1)S(1)}, u32[]{:S(2)}, u32[]{:S(2)}) collective-permute-start(bf16[256,256]{1,0:T(8,128)(2,1)S(1)} %get-tuple-element.81), channel_id=1, source_target_pairs={{0,6},{2,4},{4,2},{6,0},{1,7},{3,5},{5,3},{7,1},{8,14},{10,12},{12... | collective-permute-start | bytes 393224 | tf_op jit(solution)/shard_map/ppermute | solution.py:216
  52.1 1.8 %collective-permute-start.19 = (bf16[128,1024]{1,0:T(8,128)(2,1)S(1)}, bf16[128,1024]{1,0:T(8,128)(2,1)S(1)}, u32[]{:S(2)}, u32[]{:S(2)}) collective-permute-start(bf16[128,1024]{1,0:T(8,128)(2,1)S(1)} %get-tuple-element.105.near), channel_id=1, source_target_pairs={{0,1},{1,0},{2,3},{3,2},{4,5},{5,4},{6,7},{7,6},{8,9},{9,8},{10,11... | collective-permute-start | bytes 786440 | tf_op jit(solution)/shard_map/ppermute | solution.py:212
  52.7 1.2 %collective-permute-start.20 = (f32[32,256]{1,0:T(8,128)S(1)}, f32[32,256]{1,0:T(8,128)S(1)}, u32[]{:S(2)}, u32[]{:S(2)}) collective-permute-start(f32[32,256]{1,0:T(8,128)S(1)} %get-tuple-element.107.mine), channel_id=1, source_target_pairs={{0,1},{1,0},{2,3},{3,2},{4,5},{5,4},{6,7},{7,6},{8,9},{9,8},{10,11... | collective-permute-start | bytes 98312 | tf_op jit(solution)/shard_map/ppermute | solution.py:212

commit v3 on v2

--- a/solution.py
+++ b/solution.py
@@ -246,10 +246,10 @@
     return pl.ds(pl.multiple_of(index * size, size), size)
 
 
-def pack_kernel(devices, *refs):
+def pack_kernel(devices, reach, *refs):
     sources, refs = refs[:3], refs[3:]
-    outs, query, refs = refs[:devices], refs[devices], refs[devices + 1 :]
-    held, (turned, small, sems) = refs[:3], refs[3:]
+    outs, refs = refs[:devices], refs[devices:]
+    held, (turned, small, tail, sems) = refs[:3], refs[3:]
     copies = [
         pltpu.make_async_copy(sources[n], held[n], sems.at[n]) for n in range(len(sources))
     ]
@@ -265,7 +265,9 @@
         copy.wait()
     for i in range(1, stacked):
         turned[i - 1] = projected[i].T
-    query[...] = projected[0].T
+    tail[...] = jnp.zeros_like(tail)
+    for i in range(stacked):
+        tail[i * reach : (i + 1) * reach] = projected[i, rows - reach :].astype(f32)
     small[...] = jnp.zeros_like(small)
     seg = segments[...]
     small[2 * groups : 2 * groups + 1] = (seg >> 8).astype(f32)
@@ -280,17 +282,17 @@
         small[0:groups] = high
         small[groups : 2 * groups] = lines - high
         outs[s][body : body + 16] = small[...].astype(bf16)
-    outs[1][body + 16 :] = projected[0, rows - 16 :]
-
-
-def prepare_kernel(short_filter, chunk, query, columns, chunk_out, query_out, flat):
+    outs[1][body + 16 :] = tail[...].astype(bf16)
+
+
+def prepare_kernel(short_filter, chunk, projected, columns, chunk_out, turned, flat):
     stacked, taps, _ = short_filter.shape
     flat[...] = jnp.zeros_like(flat)
     for i in range(stacked):
         flat[i * taps : (i + 1) * taps] = short_filter[i]
+        turned[i] = projected[i].T
     columns[...] = flat[...].T
     chunk_out[...] = chunk[...]
-    query_out[...] = query[...]
 
 
 def tap_masks(seg, taps):
@@ -310,11 +312,28 @@
     return [None] + [place[8 * s : 8 * s + 8, block_at(me, length)][0:1] for s in range(1, taps)]
 
 
-def query_shifts(query, previous, taps):
-    halo = previous[previous.shape[0] - 16 :]
-    before = jnp.concatenate([jnp.zeros((SUB - 16, halo.shape[1]), f32), halo.astype(f32)], axis=0)
-    wide = jnp.concatenate([before.T, query.astype(f32)], axis=1)
+def local_shifts(turned, previous, taps, i):
+    tail = previous[previous.shape[0] - 16 :].astype(f32)
+    before = jnp.concatenate([tail, jnp.zeros((SUB - 16, tail.shape[1]), f32)], axis=0)
+    before = pltpu.roll(before, SUB - (taps - 1) * (i + 1), 0)
+    wide = jnp.concatenate([before.T, turned[i].astype(f32)], axis=1)
     return [wide[:, SUB:]] + [pltpu.roll(wide, s, 1)[:, SUB:] for s in range(1, taps)]
+
+
+def local_conv(turned, previous, columns, masks, i):
+    taps = len(masks)
+    shifts = local_shifts(turned, previous, taps, i)
+    j = i * taps
+    total = columns[:, j : j + 1] * shifts[0]
+    for s in range(1, taps):
+        total += columns[:, j + s : j + s + 1] * (masks[s] * shifts[s])
+    return total
+
+
+def pair_conv_kernel(taps, turned, previous, columns, seg, out, place):
+    masks = block_masks(seg[0:1], taps, place, lax.axis_index("ctx"), turned.shape[2])
+    for i in range(out.shape[0]):
+        out[i] = local_conv(turned, previous, columns, masks, i + 1)
 
 
 def conv_kernel(devices, taps, columns, *rest):
@@ -378,7 +397,7 @@
         outs[s][...] = long[:, block_at(lax.rem(me + s, devices), length)]
 
 
-def grad_y_kernel(devices, parts, taps, weights, query, previous, columns, seg, *rest):
+def grad_y_kernel(devices, parts, taps, weights, turned, previous, columns, seg, *rest):
     cots, rest = rest[:parts], rest[parts:]
     longs, rest = rest[:devices], rest[devices:]
     outs, (grad_y, query_conv, place, full) = rest[:devices], rest[devices:]
@@ -386,10 +405,7 @@
     rows, width = cots[0].shape
     chunk = width // devices
     masks = block_masks(seg[0:1], taps, place, me, rows)
-    shifts = query_shifts(query[...], previous, taps)
-    conv = columns[:, 0:1] * shifts[0]
-    for s in range(1, taps):
-        conv += columns[:, s : s + 1] * (masks[s] * shifts[s])
+    conv = local_conv(turned, previous, columns, masks, 0)
     query_conv[...] = conv
     total = None
     for s in range(parts):
@@ -435,41 +451,36 @@
         outs[s][...] = full[at].astype(outs[s].dtype)
 
 
-def block_sum_kernel(devices, scale, *refs):
-    sums, refs = refs[:devices], refs[devices:]
-    pays, outs = refs[:devices], refs[devices:]
-    total = sums[0][...]
-    for s in range(1, devices):
-        total += sums[s][...].astype(f32)
-    total = (total * scale).astype(bf16)
-    rows, width = total.shape[0], outs[0].shape[1]
-    blocks = total.shape[1] // width
-    for s in range(devices):
-        for b in range(blocks):
-            outs[s][b * rows : (b + 1) * rows] = total[:, b * width : (b + 1) * width]
-        outs[s][blocks * rows :] = pays[s][...]
-
-
-def mixed_part_kernel(parts, y, weights, *rest):
-    outs, (full,) = rest[:parts], rest[parts:]
-    mine = lax.axis_index("tp")
-    width = outs[0].shape[1]
-    full[...] = lax.dot_general(
-        y[...], weights[...], (((0,), (0,)), ((), ())), preferred_element_type=f32
-    )
-    for s in range(parts):
-        outs[s][...] = full[:, block_at(mine ^ s, width)].astype(outs[s].dtype)
-
-
-def mixed_sum_kernel(*refs):
+def block_sum_kernel(scale, *refs):
     total = refs[0][...]
     for ref in refs[1:-1]:
         total += ref[...].astype(f32)
-    refs[-1][...] = total.astype(bf16)
+    refs[-1][...] = (total * scale).astype(bf16)
+
+
+def mixed_part_kernel(y, weights, kept, sent, full):
+    mine = lax.axis_index("tp")
+    rows, width = full.shape[0], y.shape[0]
+    full[...] = lax.dot_general(
+        y[...], weights[...], (((0,), (0,)), ((), ())), preferred_element_type=f32
+    )
+    for h in range(2):
+        kept[h * rows : (h + 1) * rows] = full[:, block_at(mine ^ (2 * h), width)]
+        sent[h * rows : (h + 1) * rows] = full[:, block_at(mine ^ (2 * h + 1), width)].astype(bf16)
+
+
+def mixed_pair_kernel(kept, come, own, sent):
+    rows = own.shape[0]
+    own[...] = kept[0:rows] + come[0:rows].astype(f32)
+    sent[...] = (kept[rows:] + come[rows:].astype(f32)).astype(bf16)
+
+
+def mixed_sum_kernel(own, come, out):
+    out[...] = (own[...] + come[...].astype(f32)).astype(bf16)
 
 
 def backward_kernel(
-    devices, taps, conv, source, seg, toeplitz, columns, query, previous, grad_y, long, *rest
+    devices, taps, conv, source, seg, toeplitz, columns, turned, previous, grad_y, long, *rest
 ):
     glos, rest = rest[:devices], rest[devices:]
     outs, (query_out, grad_long_out, grads, small, marks, place) = rest[:devices], rest[devices:]
@@ -478,12 +489,10 @@
     length = span // devices
     groups = toeplitz.shape[0]
     size = chunk // groups
-    body = stacked * chunk
-    width = query.shape[0]
-    room = small.shape[1]
+    width = turned.shape[1]
 
     own_masks = block_masks(seg[0:1], taps, place, me, length)
-    shifts = query_shifts(query[...], previous, taps)
+    shifts = local_shifts(turned, previous, taps, 0)
     grad = grad_y[...] * long[...]
     total = columns[:, 0:1] * grad
     lane = lax.broadcasted_iota(jnp.int32, (width, SUB), 1)
@@ -497,8 +506,9 @@
         early += jnp.where(position >= length - s, back, 0.0)[:, length - SUB :]
         tap = jnp.sum(masked * shifts[s], axis=1, keepdims=True)
         sums += jnp.where(lane == groups + s, tap, 0.0)
-    query_out[...] = total
-    common = sums.T[0:room] + early.T[SUB - room :]
+    query_out[...] = total.T
+    common = sums.T[0:16]
+    early_query = early.T[SUB - 16 :]
 
     for s in range(devices):
         at = block_at(lax.rem(me - s + devices, devices), length)
@@ -551,91 +561,132 @@
             b, within = divmod(lag, per)
             small[b, g : g + 1, within * SUB : (within + 1) * SUB] = line
     grad_gated = jnp.concatenate(gg_parts, axis=0)
+    grads[...] = grad_gated.astype(bf16)
     lane = lax.broadcasted_iota(jnp.int32, (chunk, SUB), 1)
     sums = jnp.zeros((chunk, SUB), f32)
+    reach = taps - 1
+    early = [jnp.zeros((chunk, SUB), f32) for _ in range(stacked * devices)]
     for i in range(stacked):
         grad = grad_gated * conv[1 - i]
         x = source[i * chunk : (i + 1) * chunk].astype(f32)
         j = (i + 1) * taps
-        total = column[:, j : j + 1] * grad
         tap = jnp.sum(grad * x, axis=1, keepdims=True)
         sums += jnp.where(lane == groups + j, tap, 0.0)
         for s in range(1, taps):
             masked = masks[s] * grad
-            total += column[:, j + s : j + s + 1] * pltpu.roll(masked, span - s, 1)
             tap = jnp.sum(masked * pltpu.roll(x, s, 1), axis=1, keepdims=True)
             sums += jnp.where(lane == groups + j + s, tap, 0.0)
-        grads[i * chunk : (i + 1) * chunk] = total.astype(bf16)
+            back = column[:, j + s : j + s + 1] * pltpu.roll(masked, span - s, 1)
+            for b in range(devices):
+                end = back[:, (b + 1) * length - SUB : (b + 1) * length]
+                early[i * devices + b] += jnp.where(lane >= SUB - s, end, 0.0)
     marks[...] = jnp.zeros_like(marks)
     marks[:, 0:chunk] = sums.T
-    common += pltpu.roll(marks[0:room], me * chunk, 1)
+    common += pltpu.roll(marks[0:16], me * chunk, 1)
+    count = (stacked + 1) * taps
+    start = 2 * groups + 2 * count
+    high = common.astype(bf16).astype(f32)
+    for b in range(devices):
+        lines = small[b, 0:groups]
+        top = lines.astype(bf16).astype(f32)
+        small[b, 0:groups] = top
+        small[b, groups : 2 * groups] = lines - top
+        small[b, 2 * groups : 2 * groups + count] = high[groups : groups + count]
+        small[b, 2 * groups + count : start] = (common - high)[groups : groups + count]
+        small[b, start : start + reach] = early_query[16 - reach :]
+        for i in range(stacked):
+            marks[:, 0:chunk] = early[i * devices + b].T
+            placed = pltpu.roll(marks[SUB - 16 :], me * chunk, 1)
+            at = start + (i + 1) * reach
+            small[b, at : at + reach] = placed[16 - reach :]
     for s in range(devices):
         to = lax.rem(me + s, devices)
-        outs[s][0:body] = grads[:, block_at(to, length)]
-        value = small[to] + common
-        top = value.astype(bf16)
-        outs[s][body : body + room] = top
-        outs[s][body + room :] = (value - top.astype(f32)).astype(bf16)
-
-
-def collect_kernel(devices, groups, rows, stacked, *refs):
-    pays, (near, sums) = refs[:devices], refs[devices:]
+        outs[s][0:chunk] = grads[:, block_at(to, length)]
+        outs[s][chunk:] = small[to].astype(bf16)
+
+
+def small_sum_kernel(devices, groups, stacked, taps, *refs):
+    pays, (sums, later, tiles) = refs[:devices], refs[devices:]
     me = lax.axis_index("ctx")
     width = pays[0].shape[1]
-    blocks = near.shape[1] // width
-    body = blocks * rows + (stacked - 1) * (width // devices)
-    room = (pays[0].shape[0] - body) // 2
-    count = groups * devices
-    total = long_rows = None
-    for s in range(devices):
-        come = lax.rem(me - s + devices, devices)
-        for b in range(blocks):
-            at = block_at(come, rows)
-            near[at, b * width : (b + 1) * width] = pays[s][b * rows : (b + 1) * rows]
-        value = pays[s][body : body + room].astype(f32) + pays[s][body + room :].astype(f32)
-        row = lax.broadcasted_iota(jnp.int32, value.shape, 0)
-        line = pltpu.roll(jnp.where(row < groups, value, 0.0), come * groups, 0)
-        long_rows = line if long_rows is None else long_rows + line
-        total = value if total is None else total + value
-    sums[...] = jnp.zeros_like(sums)
-    sums[0:count] = long_rows
-    sums[count : count + room - groups] = total[groups:]
-
-
-def grad_out_kernel(devices, taps, start, query_part, *refs):
-    pays, (out, turned) = refs[:devices], refs[devices:]
+    body = width // devices
+    count = stacked * taps
+    start = 2 * groups + 2 * count
+    reach = taps - 1
+    for s in range(devices):
+        tiles[lax.rem(me - s + devices, devices)] = pays[s][body:].astype(f32)
+    total = tiles[0]
+    for c in range(1, devices):
+        total += tiles[c]
+    lines = [tiles[c, 0:groups] + tiles[c, groups : 2 * groups] for c in range(devices)]
+    taps_sum = total[2 * groups : 2 * groups + count] + total[2 * groups + count : start]
+    for n, value in enumerate((jnp.concatenate(lines, axis=0), taps_sum)):
+        if value.shape[0] < 16:
+            rest = jnp.zeros((16 - value.shape[0], width), f32)
+            value = jnp.concatenate([value, rest], axis=0)
+        for h, half in enumerate(split_bf16(value)):
+            sums[:, (2 * h + n) * width : (2 * h + n + 1) * width] = half
+    last = pays[devices - 1][body:].astype(f32)
+    later[...] = jnp.zeros_like(later)
+    later[0, 16 - reach : 16] = last[start : start + reach]
+    for i in range(1, stacked):
+        later[i, 16 - reach : 16] = total[start + i * reach : start + (i + 1) * reach]
+
+
+def collect_kernel(devices, sums, *refs):
+    blocks, near = refs[:devices], refs[devices]
+    me = lax.axis_index("ctx")
+    rows = blocks[0].shape[0]
+    for s in range(devices):
+        near[block_at(lax.rem(me - s + devices, devices), rows)] = blocks[s][...]
+    near[devices * rows :] = sums[...]
+
+
+def grad_out_kernel(devices, taps, query_part, pair, columns, seg, later, *refs):
+    pays, (out, gated, place) = refs[:devices], refs[devices:]
     me = lax.axis_index("ctx")
     stacked, rows, width = out.shape
     chunk = width // devices
-    body = start + (stacked - 1) * chunk
-    room = (pays[0].shape[0] - body) // 2
     for s in range(devices):
         at = block_at(lax.rem(me - s + devices, devices), chunk)
-        for i in range(stacked - 1):
-            turned[i, at] = pays[s][start + i * chunk : start + (i + 1) * chunk]
-    last = pays[devices - 1]
-    value = last[body : body + room].astype(f32) + last[body + room :].astype(f32)
-    row = lax.broadcasted_iota(jnp.int32, value.shape, 0)
-    later = jnp.where(row >= room - (taps - 1), value, 0.0)
-    query = query_part[...].T
-    out[0, 0 : rows - room] = query[0 : rows - room].astype(bf16)
-    out[0, rows - room :] = (query[rows - room :] + later).astype(bf16)
-    for i in range(stacked - 1):
-        out[i + 1] = turned[i].T
-
-
-def final_kernel(scale, near, far, mine, other, weight_out, short_out, long_out):
+        gated[at] = pays[s][0:chunk].astype(f32)
+    masks = block_masks(seg[0:1], taps, place, me, rows)
+    position = lax.broadcasted_iota(jnp.int32, (width, rows), 1)
+    for i in range(stacked):
+        if i == 0:
+            turned = query_part[...]
+        else:
+            grad = gated[...] * pair[2 - i]
+            j = i * taps
+            total = columns[:, j : j + 1] * grad
+            for s in range(1, taps):
+                back = pltpu.roll(columns[:, j + s : j + s + 1] * (masks[s] * grad), rows - s, 1)
+                total += jnp.where(position < rows - s, back, 0.0)
+            turned = total.T
+        out[i, 0 : rows - 16] = turned[0 : rows - 16].astype(bf16)
+        out[i, rows - 16 :] = (turned[rows - 16 :] + later[i]).astype(bf16)
+
+
+def final_kernel(scale, near, far, weight_out, short_out, long_out):
     core = lax.axis_index("dp")
-    half = near.shape[0]
-    weight_out[block_at(core, half)] = near[...].astype(f32)
-    weight_out[block_at(1 - core, half)] = far[...].astype(f32)
-    total = (mine[...] + other[...]) * scale
-    count = long_out.shape[0]
+    half = weight_out.shape[0] // 2
+    weight_out[block_at(core, half)] = near[0:half].astype(f32)
+    weight_out[block_at(1 - core, half)] = far[0:half].astype(f32)
+    count, width = long_out.shape
     stacked, taps, _ = short_out.shape
-    long_out[...] = total[0:count]
+
+    def sums(n):
+        pieces = []
+        for ref in (near, far):
+            high = ref[half:, n * width : (n + 1) * width].astype(f32)
+            low = ref[half:, (n + 2) * width : (n + 3) * width].astype(f32)
+            pieces.append(high + low)
+        return (pieces[0] + pieces[1]) * scale
+
+    long_out[...] = sums(0)
+    total = sums(1)
     for i in range(stacked):
-        start = count + i * taps
-        short_out[i] = total[start : start + taps]
+        short_out[i] = total[i * taps : (i + 1) * taps]
 
 
 def direct_device(projected, segment_ids, short_filter, long_filter, out_proj, mixed_cotangent):
@@ -653,29 +704,28 @@
     inputs = (projected[:, 0], long_filter, segment_ids)
 
     outs = on_core(
-        functools.partial(pack_kernel, devices),
+        functools.partial(pack_kernel, devices, taps - 1),
         [
             (((stacked - 1) * chunk + (2 * room if s == 1 else room), length), bf16)
             for s in range(devices)
-        ]
-        + [((width, length), bf16)],
+        ],
         inputs,
         "pack",
         [pltpu.VMEM(a.shape, a.dtype) for a in inputs]
         + [
             pltpu.VMEM((stacked - 1, width, length), bf16),
             pltpu.VMEM((room, length), f32),
+            pltpu.VMEM((room, width), f32),
             pltpu.SemaphoreType.DMA((len(inputs),)),
         ],
         whole=True,
     )
-    signal, query = outs[:devices], outs[devices]
-    own, *signal = scatter_chunks(signal, "ctx")
+    own, *signal = scatter_chunks(outs, "ctx")
     beside = swap(cotangent, "tp", 1)
-    columns, own, query = on_core(
+    columns, own, turned = on_core(
         prepare_kernel,
-        [((width, 16), f32), (own.shape, bf16), ((width, length), bf16)],
-        (after(short_filter, beside), own, query),
+        [((width, 16), f32), (own.shape, bf16), ((stacked, width, length), bf16)],
+        (after(short_filter, beside), own, inputs[0]),
         "prepare",
         [pltpu.VMEM((16, width), f32)],
     )
@@ -698,7 +748,7 @@
             pltpu.VMEM((chunk, span), bf16),
             pltpu.VMEM((groups, length, span), bf16),
         ],
-        flops=conv_flops,
+        flops=9 * 100000000,
     )
     longs, kept = outs[:devices], outs[devices:]
     seg = kept[2]
@@ -706,13 +756,22 @@
     outs = on_core(
         functools.partial(grad_y_kernel, devices, parts, taps),
         [((2 * chunk, length), bf16)] * devices + [((width, length), f32)] * 2,
-        (out_proj, query, signal[1], columns, seg, *cots, *longs),
+        (out_proj, turned, signal[1], columns, seg, *cots, *longs),
         "grad_y",
         [pltpu.VMEM((8 * taps, span), f32), pltpu.VMEM((width, length), bf16)],
         flops=2 * width * length * total_cols,
     )
     pairs, (grad_y, query_conv) = outs[:devices], outs[devices:]
     pairs = scatter_chunks(pairs, "ctx")
+
+    (pair,) = on_core(
+        functools.partial(pair_conv_kernel, taps),
+        [((stacked - 1, width, length), f32)],
+        (turned, signal[1], columns, seg),
+        "pair_conv",
+        [pltpu.VMEM((8 * taps, span), f32)],
+    )
+    query_conv = after(query_conv, pair)
 
     half = width // 2
     y, long, keep, send = on_core(
@@ -729,15 +788,15 @@
         flops=2 * width * length * total_cols,
     )
     other = rotate(send, "dp", 1)
-    shares = on_core(
-        functools.partial(mixed_part_kernel, parts),
-        [((length, width), f32)] + [((length, width), bf16)] * (parts - 1),
+    kept_part, sent_part = on_core(
+        mixed_part_kernel,
+        [((2 * length, width), f32), ((2 * length, width), bf16)],
         (y, out_proj),
         "mixed_part",
         [pltpu.VMEM((length, total_cols), f32)],
         flops=2 * width * length * total_cols,
     )
-    keep = after(keep, shares[0])
+    keep = after(keep, kept_part)
     rows = half // devices
     sums = on_core(
         functools.partial(core_sum_kernel, devices),
@@ -750,57 +809,70 @@
 
     outs = on_core(
         functools.partial(backward_kernel, devices, taps),
-        [(((stacked - 1) * chunk + 2 * room, length), bf16)] * devices + [((width, length), f32)],
-        (*kept, columns, query, signal[1], grad_y, after(long, sums[1]), *pairs),
+        [((chunk + 2 * room, length), bf16)] * devices + [((length, width), f32)],
+        (*kept, columns, turned, signal[1], grad_y, after(long, sums[1]), *pairs),
         "backward",
         [
             pltpu.VMEM((chunk, span), bf16),
-            pltpu.VMEM(((stacked - 1) * chunk, span), bf16),
-            pltpu.VMEM((devices, room, length), f32),
+            pltpu.VMEM((chunk, span), bf16),
+            pltpu.VMEM((devices, 2 * room, length), f32),
             pltpu.VMEM((SUB, width), f32),
             pltpu.VMEM((8 * taps, span), f32),
         ],
         flops=2 * conv_flops,
     )
     back, query_part = outs[:devices], outs[devices]
-    start = rows * total_cols // width
-    back = on_core(
-        functools.partial(block_sum_kernel, devices, grad_scale),
-        [((start + back[0].shape[0], width), bf16)] * devices,
-        (*parts_out, *back),
+    back = scatter_chunks(back, "ctx")
+    sums, later = on_core(
+        functools.partial(small_sum_kernel, devices, groups, stacked, taps),
+        [((16, total_cols), bf16), ((stacked, 16, width), f32)],
+        back,
+        "small_sum",
+        [pltpu.VMEM((devices, 2 * room, width), f32)],
+        flops=2000 * 1000000,
+    )
+    (grad_projected,) = on_core(
+        functools.partial(grad_out_kernel, devices, taps),
+        [((stacked, length, width), bf16)],
+        (query_part, pair, columns, seg, later, *back),
+        "grad_out",
+        [pltpu.VMEM((width, length), f32), pltpu.VMEM((8 * taps, span), f32)],
+    )
+    (block,) = on_core(
+        functools.partial(block_sum_kernel, grad_scale),
+        [((rows, total_cols), bf16)],
+        parts_out,
         "block_sum",
     )
-    shares = [shares[0]] + [
-        swap(shares[s], "tp", s) for s in range(1, parts)
-    ]
-    (mixed,) = on_core(mixed_sum_kernel, [((length, width), bf16)], shares, "mixed_sum")
-    back = scatter_chunks(back, "ctx")
-    back[0] = after(back[0], mixed)
-    near, small = on_core(
-        functools.partial(collect_kernel, devices, groups, rows, stacked),
-        [((half, total_cols), bf16), ((count + 16, width), f32)],
-        back,
+    own_part, sent_part = on_core(
+        mixed_pair_kernel,
+        [((length, width), f32), ((length, width), bf16)],
+        (after(kept_part, query_part), swap(sent_part, "tp", 1)),
+        "mixed_pair",
+    )
+    come_part = swap(sent_part, "tp", 2)
+    (mixed,) = on_core(
+        mixed_sum_kernel, [((length, width), bf16)], (own_part, come_part), "mixed_sum"
+    )
+
+    blocks = spread(block, "ctx")
+    blocks[0] = after(block, (grad_projected, come_part))
+    (near,) = on_core(
+        functools.partial(collect_kernel, devices),
+        [((half + 16, total_cols), bf16)],
+        (sums, *blocks),
         "collect",
-    )
-    far = rotate(near, "dp", 1)
-    other_small = rotate(small, "dp", 1)
-    (grad_projected,) = on_core(
-        functools.partial(grad_out_kernel, devices, taps, start),
-        [((stacked, length, width), bf16)],
-        (query_part, *back),
-        "grad_out",
-        [pltpu.VMEM((stacked - 1, width, length), bf16)],
     )
     grad_out_proj, grad_short, grad_long = on_core(
         functools.partial(final_kernel, grad_scale),
         [((width, total_cols), f32), (short_filter.shape, f32), ((count, length), f32)],
-        (near, far, after(small, grad_projected), other_small),
+        (after(near, mixed), rotate(near, "dp", 1)),
         "final",
     )
     return (mixed[None], grad_projected[:, None], grad_short, grad_long, grad_out_proj)
 
 
-def direct_fits(mesh, projected, short_filter, long_filter):
+def direct_fits(mesh, projected, short_filter, long_filter, out_proj):
     devices = mesh.shape["ctx"]
     length = projected.shape[2] // devices
     width = projected.shape[3] // mesh.shape["tp"]
@@ -819,7 +891,10 @@
         and width // devices <= SUB
         and (width // groups) == 16
         and 2 * groups // devices + 2 <= 16
-        and groups // devices + stacked * taps + taps - 1 <= 16
+        and out_proj.shape[1] == 4 * width
+        and stacked * (taps - 1) <= 16
+        and groups // devices + stacked * taps <= 16
+        and 2 * (groups // devices) + 2 * stacked * taps + stacked * (taps - 1) <= 32
     )
 
 
@@ -841,7 +916,7 @@
     )
 
     def layer(projected, segment_ids, short_filter, long_filter, out_proj, mixed_cotangent):
-        fits = direct_fits(mesh, projected, short_filter, long_filter)
+        fits = direct_fits(mesh, projected, short_filter, long_filter, out_proj)
         return jax.shard_map(
             direct_device if fits else spectral_device,
             mesh=mesh,

time: 55.2 us -> 52.7 us (0.955)
  the two profiles are of different devices: /device:TPU:9 before, /device:TPU:0 now
where the time goes in v3:
time: 52.7 us; the launch traced here: 52.5 us
  starting transfers between devices  28.7 us (54%)
  Pallas kernels  11.9 us (23%)
  waiting for transfers between devices  8.55 us (16%)
  local copies, waits for them, and re-layouts  2.59 us (5%)
  between operations  0.78 us (1%)
    ppermute x17, starting transfers between devices, rotate(): lax.ppermute(value, axis, [(i, (i + steps) % count) for i in range(count)])  21.4 us
    pallas_call x16, Pallas kernels, on_core(): pl.pallas_call(kernel, out_shape=[jax.ShapeDtypeStruct(shape, kind) for s...  11.9 us
    ppermute x17, waiting for transfers between devices, rotate(): lax.ppermute(value, axis, [(i, (i + steps) % count) for i in range(count)])  7.75 us
    ppermute x5, starting transfers between devices, swap(): lax.ppermute(value, axis, [(i, i ^ bits) for i in range(lax.axis_size(axi...  7.22 us
    unnamed x10, local copies, waits for them, and re-layouts  2.59 us
  transfers between devices with their start and end apart: 22, of which 6 were waited for; matrix products, arithmetic and copies ran while one was open for 0% of the time, Pallas kernels for 19%

profile of v3, /device:TPU:0, one launch (start us, length us, event | category | flops | bytes accessed | tf_op | source)
XLA Modules:
  0.0 52.5 jit_solution(4487303282068815954)
XLA Ops:
  0.6 3.0 %collective-permute-start = (bf16[256,256]{1,0:T(8,128)(2,1)}, bf16[256,256]{1,0:T(8,128)(2,1)S(1)}, u32[]{:S(2)}, u32[]{:S(2)}) collective-permute-start(bf16[256,256]{1,0:T(8,128)(2,1)} %bitcast.8), channel_id=1, source_target_pairs={{0,2},{2,0},{4,6},{6,4},{1,3},{3,1},{5,7},{7,5},{8,10},{10,8},{12,... | collective-permute-start | bytes 393224 | tf_op jit(solution)/shard_map/ppermute | solution.py:216
  3.6 0.0 copy-start
  3.6 1.9 %pack.1 = (bf16[144,256]{1,0:T(8,128)(2,1)}, bf16[160,256]{1,0:T(8,128)(2,1)}, bf16[144,256]{1,0:T(8,128)(2,1)}, bf16[144,256]{1,0:T(8,128)(2,1)}) custom-call(bf16[3,256,256]{2,1,0:T(8,128)(2,1)} %bitcast.6, f32[16,256]{1,0:T(8,128)} %refs_1_.1, s32[1,256]{1,0:T(1,128)} %refs_2_.1), custom_call_target="tpu_custom_call" | custom-call | bytes 713728 | tf_op jit(solution)/shard_map/pack/pallas_call | solution.py:234
  5.6 1.6 %collective-permute-start.1 = (bf16[160,256]{1,0:T(8,128)(2,1)}, bf16[160,256]{1,0:T(8,128)(2,1)S(1)}, u32[]{:S(2)}, u32[]{:S(2)}) collective-permute-start(bf16[160,256]{1,0:T(8,128)(2,1)} %get-tuple-element.58), channel_id=1, source_target_pairs={{0,8},{8,16},{16,24},{24,0},{1,9},{9,17},{17,25},{25,1},{2,10},{10... | collective-permute-start | bytes 245768 | tf_op jit(solution)/shard_map/ppermute | solution.py:212
  7.2 2.6 %collective-permute-start.2 = (bf16[144,256]{1,0:T(8,128)(2,1)}, bf16[144,256]{1,0:T(8,128)(2,1)S(1)}, u32[]{:S(2)}, u32[]{:S(2)}) collective-permute-start(bf16[144,256]{1,0:T(8,128)(2,1)} %get-tuple-element.61), channel_id=1, source_target_pairs={{0,16},{8,24},{16,0},{24,8},{1,17},{9,25},{17,1},{25,9},{2,18},{10... | collective-permute-start | bytes 221192 | tf_op jit(solution)/shard_map/ppermute | solution.py:212
  9.8 1.3 %collective-permute-start.3 = (bf16[144,256]{1,0:T(8,128)(2,1)}, bf16[144,256]{1,0:T(8,128)(2,1)S(1)}, u32[]{:S(2)}, u32[]{:S(2)}) collective-permute-start(bf16[144,256]{1,0:T(8,128)(2,1)} %get-tuple-element.62), channel_id=1, source_target_pairs={{0,24},{8,0},{16,8},{24,16},{1,25},{9,1},{17,9},{25,17},{2,26},{10... | collective-permute-start | bytes 221192 | tf_op jit(solution)/shard_map/ppermute | solution.py:212
  11.1 1.5 %collective-permute-start.4 = (bf16[256,256]{1,0:T(8,128)(2,1)}, bf16[256,256]{1,0:T(8,128)(2,1)S(1)}, u32[]{:S(2)}, u32[]{:S(2)}) collective-permute-start(bf16[256,256]{1,0:T(8,128)(2,1)} %bitcast.9), channel_id=1, source_target_pairs={{0,4},{2,6},{4,0},{6,2},{1,5},{3,7},{5,1},{7,3},{8,12},{10,14},{12... | collective-permute-start | bytes 393224 | tf_op jit(solution)/shard_map/ppermute | solution.py:216
  12.7 0.0 collective-permute-done.rest_1_
  12.7 0.5 collective-permute-start.5
  13.2 0.0 copy-start.1
  13.2 1.0 %copy-done.1 = bf16[3,1,256,256]{3,2,1,0:T(8,128)(2,1)S(1)} copy-done((bf16[3,1,256,256]{3,2,1,0:T(8,128)(2,1)S(1)}, bf16[3,1,256,256]{3,2,1,0:T(8,128)(2,1)}, u32[]{:S(2)}) %copy-start.1) | copy-done | bytes 393240
  14.2 0.0 copy-start.3
  14.2 0.9 %copy-done.3 = bf16[144,256]{1,0:T(8,128)(2,1)S(1)} copy-done((bf16[144,256]{1,0:T(8,128)(2,1)S(1)}, bf16[144,256]{1,0:T(8,128)(2,1)}, u32[]{:S(2)}) %copy-start.3) | copy-done | bytes 73752
  15.1 0.7 %copy-done.4 = f32[3,3,256]{2,1,0:T(4,128)S(1)} copy-done((f32[3,3,256]{2,1,0:T(4,128)S(1)}, f32[3,3,256]{2,1,0:T(4,128)}, u32[]{:S(2)}) %copy-start.4) | copy-done | bytes 9240
  15.8 0.2 prepare.1
  16.0 0.0 collective-permute-done.2.rest_2_
  16.0 0.0 collective-permute-done.3.rest_3_
  16.0 0.0 collective-permute-done.1.rest_1_.previous
  16.0 1.5 %conv.1 = (bf16[64,256]{1,0:T(8,128)(2,1)S(1)}, bf16[64,256]{1,0:T(8,128)(2,1)S(1)}, bf16[64,256]{1,0:T(8,128)(2,1)S(1)}, bf16[64,256]{1,0:T(8,128)(2,1)S(1)}, f...) custom-call(f32[256,16]{1,0:T(8,128)S(1)} %get-tuple-element.59.colu, ...), custom_call_target="tpu_custom_call" | custom-call | flops 900000000 | bytes 3366912 | tf_op jit(solution)/shard_map/conv/pallas_call | solution.py:234
  17.5 0.0 collective-permute-done.4.rest_2_
  17.5 0.8 %collective-permute-done.5.rest_3_ = bf16[256,256]{1,0:T(8,128)(2,1)S(1)} collective-permute-done((bf16[256,256]{1,0:T(8,128)(2,1)S(1)}, bf16[256,256]{1,0:T(8,128)(2,1)S(1)}, u32[]{:S(2)}, u32[]{:S(2)}) %collective-permute-start.5) | collective-permute-done | bytes 131104 | tf_op jit(solution)/shard_map/ppermute | solution.py:216
  18.3 0.0 copy-done
  18.3 0.0 copy-done.2
  18.3 0.4 grad_y.1
  18.7 0.7 %collective-permute-start.6 = (bf16[128,256]{1,0:T(8,128)(2,1)S(1)}, bf16[128,256]{1,0:T(8,128)(2,1)S(1)}, u32[]{:S(2)}, u32[]{:S(2)}) collective-permute-start(bf16[128,256]{1,0:T(8,128)(2,1)S(1)} %get-tuple-element.71), channel_id=1, source_target_pairs={{0,8},{8,16},{16,24},{24,0},{1,9},{9,17},{17,25},{25,1},{2,10},{10... | collective-permute-start | bytes 196616 | tf_op jit(solution)/shard_map/ppermute | solution.py:212
  19.4 1.3 %collective-permute-start.7 = (bf16[128,256]{1,0:T(8,128)(2,1)S(1)}, bf16[128,256]{1,0:T(8,128)(2,1)S(1)}, u32[]{:S(2)}, u32[]{:S(2)}) collective-permute-start(bf16[128,256]{1,0:T(8,128)(2,1)S(1)} %get-tuple-element.72), channel_id=1, source_target_pairs={{0,16},{8,24},{16,0},{24,8},{1,17},{9,25},{17,1},{25,9},{2,18},{10... | collective-permute-start | bytes 196616 | tf_op jit(solution)/shard_map/ppermute | solution.py:212
  20.7 1.9 %collective-permute-start.8 = (bf16[128,256]{1,0:T(8,128)(2,1)S(1)}, bf16[128,256]{1,0:T(8,128)(2,1)S(1)}, u32[]{:S(2)}, u32[]{:S(2)}) collective-permute-start(bf16[128,256]{1,0:T(8,128)(2,1)S(1)} %get-tuple-element.73), channel_id=1, source_target_pairs={{0,24},{8,0},{16,8},{24,16},{1,25},{9,1},{17,9},{25,17},{2,26},{10... | collective-permute-start | bytes 196616 | tf_op jit(solution)/shard_map/ppermute | solution.py:212
  22.6 0.6 %pair_conv.1.pair = f32[2,256,256]{2,1,0:T(8,128)S(1)} custom-call(bf16[3,256,256]{2,1,0:T(8,128)(2,1)S(1)} %get-tuple-element.57.turned, bf16[160,256]{1,0:T(8,128)(2,1)S(1)} %collective-permute-done.1.rest_1_.previous, f32[256,16]{1,0:T(8,128)S(1)} %get-tuple-element.59.columns, f32[8,1024]{1,0:T(8,128)S(1)} %get-tuple-element.63.seg), custom_call_target="tpu_custom_call" | custom-call | bytes 1048576 | tf_op jit(solution)/shard_map/pair_conv/pallas_call | solution.py:234
  23.2 1.7 %collective-permute-done.6.rest_5_.rest_1_ = bf16[128,256]{1,0:T(8,128)(2,1)S(1)} collective-permute-done((bf16[128,256]{1,0:T(8,128)(2,1)S(1)}, bf16[128,256]{1,0:T(8,128)(2,1)S(1)}, u32[]{:S(2)}, u32[]{:S(2)}) %collective-permute-start.6) | collective-permute-done | bytes 65568 | tf_op jit(solution)/shard_map/ppermute | solution.py:212
  25.0 1.1 %collective-permute-done.7.rest_6_.rest_2_ = bf16[128,256]{1,0:T(8,128)(2,1)S(1)} collective-permute-done((bf16[128,256]{1,0:T(8,128)(2,1)S(1)}, bf16[128,256]{1,0:T(8,128)(2,1)S(1)}, u32[]{:S(2)}, u32[]{:S(2)}) %collective-permute-start.7) | collective-permute-done | bytes 65568 | tf_op jit(solution)/shard_map/ppermute | solution.py:212
  26.0 0.0 collective-permute-done.8.rest_7_.rest_3_
  26.0 0.4 weight_grad.1
  26.4 0.1 collective-permute-start.9
  26.5 0.4 mixed_part.1
  26.9 0.6 %collective-permute-start.10 = (bf16[512,256]{1,0:T(8,128)(2,1)S(1)}, bf16[512,256]{1,0:T(8,128)(2,1)S(1)}, u32[]{:S(2)}, u32[]{:S(2)}) collective-permute-start(bf16[512,256]{1,0:T(8,128)(2,1)S(1)} %get-tuple-element.88), channel_id=1, source_target_pairs={{0,2},{2,0},{4,6},{6,4},{1,3},{3,1},{5,7},{7,5},{8,10},{10,8},{12,... | collective-permute-start | bytes 786440 | tf_op jit(solution)/shard_map/ppermute | solution.py:216
  27.5 0.9 %collective-permute-done.9.other = f32[128,1024]{1,0:T(8,128)S(1)} collective-permute-done((f32[128,1024]{1,0:T(8,128)S(1)}, f32[128,1024]{1,0:T(8,128)S(1)}, u32[]{:S(2)}, u32[]{:S(2)}) %collective-permute-start.9) | collective-permute-done | bytes 524320 | tf_op jit(solution)/shard_map/ppermute | solution.py:212
  28.4 0.1 core_sum.1
  28.5 1.5 %collective-permute-start.15 = (bf16[32,1024]{1,0:T(8,128)(2,1)S(1)}, bf16[32,1024]{1,0:T(8,128)(2,1)S(1)}, u32[]{:S(2)}, u32[]{:S(2)}) collective-permute-start(bf16[32,1024]{1,0:T(8,128)(2,1)S(1)} %get-tuple-element.84), channel_id=1, source_target_pairs={{0,8},{8,16},{16,24},{24,0},{1,9},{9,17},{17,25},{25,1},{2,10},{10... | collective-permute-start | bytes 196616 | tf_op jit(solution)/shard_map/ppermute | solution.py:212
  29.9 1.8 %collective-permute-start.16 = (bf16[32,1024]{1,0:T(8,128)(2,1)S(1)}, bf16[32,1024]{1,0:T(8,128)(2,1)S(1)}, u32[]{:S(2)}, u32[]{:S(2)}) collective-permute-start(bf16[32,1024]{1,0:T(8,128)(2,1)S(1)} %get-tuple-element.98), channel_id=1, source_target_pairs={{0,16},{8,24},{16,0},{24,8},{1,17},{9,25},{17,1},{25,9},{2,18},{10... | collective-permute-start | bytes 196616 | tf_op jit(solution)/shard_map/ppermute | solution.py:212
  31.7 0.6 %collective-permute-start.17 = (bf16[32,1024]{1,0:T(8,128)(2,1)S(1)}, bf16[32,1024]{1,0:T(8,128)(2,1)S(1)}, u32[]{:S(2)}, u32[]{:S(2)}) collective-permute-start(bf16[32,1024]{1,0:T(8,128)(2,1)S(1)} %get-tuple-element.99), channel_id=1, source_target_pairs={{0,24},{8,0},{16,8},{24,16},{1,25},{9,1},{17,9},{25,17},{2,26},{10... | collective-permute-start | bytes 196616 | tf_op jit(solution)/shard_map/ppermute | solution.py:212
  32.4 2.8 %backward.1 = (bf16[96,256]{1,0:T(8,128)(2,1)S(1)}, bf16[96,256]{1,0:T(8,128)(2,1)S(1)}, bf16[96,256]{1,0:T(8,128)(2,1)S(1)}, bf16[96,256]{1,0:T(8,128)(2,1)S(1)}, f32[256,256]{1,0:T(8,128)S(1)}) custom-call(f32[2,64,1024]{2,1,0:T(8,128)S(1)} %get-tuple-element.76.conv, bf16[128,1024]{1,0:T(8,128)(2,1)S(1)} %get-tuple-element.77.source, ...), custom_call_target="tpu_custom_call" | custom-call | flops 1073741824 | bytes 4653056 | tf_op jit(solution)/shard_map/backward/pallas_call | solution.py:234
  35.2 1.4 %collective-permute-start.12 = (bf16[96,256]{1,0:T(8,128)(2,1)S(1)}, bf16[96,256]{1,0:T(8,128)(2,1)S(1)}, u32[]{:S(2)}, u32[]{:S(2)}) collective-permute-start(bf16[96,256]{1,0:T(8,128)(2,1)S(1)} %get-tuple-element.92), channel_id=1, source_target_pairs={{0,8},{8,16},{16,24},{24,0},{1,9},{9,17},{17,25},{25,1},{2,10},{10... | collective-permute-start | bytes 147464 | tf_op jit(solution)/shard_map/ppermute | solution.py:212
  36.6 0.0 collective-permute-done.10.come
  36.6 1.1 %collective-permute-start.13 = (bf16[96,256]{1,0:T(8,128)(2,1)S(1)}, bf16[96,256]{1,0:T(8,128)(2,1)S(1)}, u32[]{:S(2)}, u32[]{:S(2)}) collective-permute-start(bf16[96,256]{1,0:T(8,128)(2,1)S(1)} %get-tuple-element.93), channel_id=1, source_target_pairs={{0,16},{8,24},{16,0},{24,8},{1,17},{9,25},{17,1},{25,9},{2,18},{10... | collective-permute-start | bytes 147464 | tf_op jit(solution)/shard_map/ppermute | solution.py:212
  37.8 0.0 collective-permute-done.16.refs_2_
  37.8 2.4 %collective-permute-start.14 = (bf16[96,256]{1,0:T(8,128)(2,1)S(1)}, bf16[96,256]{1,0:T(8,128)(2,1)S(1)}, u32[]{:S(2)}, u32[]{:S(2)}) collective-permute-start(bf16[96,256]{1,0:T(8,128)(2,1)S(1)} %get-tuple-element.94), channel_id=1, source_target_pairs={{0,24},{8,0},{16,8},{24,16},{1,25},{9,1},{17,9},{25,17},{2,26},{10... | collective-permute-start | bytes 147464 | tf_op jit(solution)/shard_map/ppermute | solution.py:212
  40.2 0.0 collective-permute-done.17.refs_3_
  40.2 1.6 %collective-permute-start.11 = (bf16[256,256]{1,0:T(8,128)(2,1)S(1)}, bf16[256,256]{1,0:T(8,128)(2,1)S(1)}, u32[]{:S(2)}, u32[]{:S(2)}) collective-permute-start(bf16[256,256]{1,0:T(8,128)(2,1)S(1)} %get-tuple-element.90), channel_id=1, source_target_pairs={{0,4},{2,6},{4,0},{6,2},{1,5},{3,7},{5,1},{7,3},{8,12},{10,14},{12... | collective-permute-start | bytes 393224 | tf_op jit(solution)/shard_map/ppermute | solution.py:216
  41.8 0.0 collective-permute-done.15.refs_1_
  41.9 0.9 %collective-permute-start.20 = (bf16[32,1024]{1,0:T(8,128)(2,1)S(1)}, bf16[32,1024]{1,0:T(8,128)(2,1)S(1)}, u32[]{:S(2)}, u32[]{:S(2)}) collective-permute-start(bf16[32,1024]{1,0:T(8,128)(2,1)S(1)} %block_sum.1.refs_0_), channel_id=1, source_target_pairs={{0,24},{8,0},{16,8},{24,16},{1,25},{9,1},{17,9},{25,17},{2,26},{10... | collective-permute-start | bytes 196616 | tf_op jit(solution)/shard_map/ppermute | solution.py:212
  42.8 0.0 collective-permute-done.12.refs_1_
  42.8 0.2 collective-permute-start.19
  43.0 0.0 collective-permute-done.13.refs_2_
  43.0 1.9 %collective-permute-start.18 = (bf16[32,1024]{1,0:T(8,128)(2,1)S(1)}, bf16[32,1024]{1,0:T(8,128)(2,1)S(1)}, u32[]{:S(2)}, u32[]{:S(2)}) collective-permute-start(bf16[32,1024]{1,0:T(8,128)(2,1)S(1)} %block_sum.1.refs_0_), channel_id=1, source_target_pairs={{0,8},{8,16},{16,24},{24,0},{1,9},{9,17},{17,25},{25,1},{2,10},{10... | collective-permute-start | bytes 196616 | tf_op jit(solution)/shard_map/ppermute | solution.py:212
  44.9 0.0 collective-permute-done.14.refs_3_
  44.9 1.6 %grad_out.1 = bf16[3,256,256]{2,1,0:T(8,128)(2,1)} custom-call(f32[256,256]{1,0:T(8,128)S(1)} %get-tuple-element.86.query_part, f32[2,256,256]{2,1,0:T(8,128)S(1)} %pair_conv.1.pair, f32[256,16]{1,0:T(8,128)S(1)} %get-tuple-element.59.columns, f32[8,1024]{1,0:T(8,128)S(1)} %get-tuple-element.63.seg, f32[3,16,256]{2,1,0:T(8,128)S(1)} %get-tuple-element.95.later, ...), custom_call_target="tpu_custom_call" | custom-call | bytes 1474560 | tf_op jit(solution)/shard_map/grad_out/pallas_call | solution.py:234
  46.6 0.0 collective-permute-done.11.come
  46.6 0.0 collective-permute-done.20.refs_3_
  46.6 3.1 %collective-permute-done.19.refs_2_ = bf16[32,1024]{1,0:T(8,128)(2,1)S(1)} collective-permute-done((bf16[32,1024]{1,0:T(8,128)(2,1)S(1)}, bf16[32,1024]{1,0:T(8,128)(2,1)S(1)}, u32[]{:S(2)}, u32[]{:S(2)}) %collective-permute-start.19) | collective-permute-done | bytes 65568 | tf_op jit(solution)/shard_map/ppermute | solution.py:212
  49.7 0.0 collective-permute-done.18.refs_1_
  49.8 0.1 collective-permute-start.21
  49.8 0.7 %mixed_sum.1 = bf16[256,256]{1,0:T(8,128)(2,1)} custom-call(f32[256,256]{1,0:T(8,128)S(1)} %get-tuple-element.89.own, bf16[256,256]{1,0:T(8,128)(2,1)S(1)} %collective-permute-done.11.come), custom_call_target="tpu_custom_call" | custom-call | bytes 524288 | tf_op jit(solution)/shard_map/mixed_sum/pallas_call | solution.py:234
  50.5 0.9 %collective-permute-done.21.far = bf16[144,1024]{1,0:T(8,128)(2,1)S(1)} collective-permute-done((bf16[144,1024]{1,0:T(8,128)(2,1)S(1)}, bf16[144,1024]{1,0:T(8,128)(2,1)S(1)}, u32[]{:S(2)}, u32[]{:S(2)}) %collective-permute-start.21) | collective-permute-done | bytes 294944 | tf_op jit(solution)/shard_map/ppermute | solution.py:212
  51.4 1.0 %final.1 = (f32[256,1024]{1,0:T(8,128)}, f32[3,3,256]{2,1,0:T(4,128)}, f32[16,256]{1,0:T(8,128)}) custom-call(bf16[144,1024]{1,0:T(8,128)(2,1)S(1)} %collect.1.near, bf16[144,1024]{1,0:T(8,128)(2,1)S(1)} %collective-permute-done.21.far), custom_call_target="tpu_custom_call" | custom-call | bytes 1664000 | tf_op jit(solution)/shard_map/final/pallas_call | solution.py:234
  (6 shorter events, 0.2 us)
Async XLA Ops:
  0.6 12.0 %collective-permute-start = (bf16[256,256]{1,0:T(8,128)(2,1)}, bf16[256,256]{1,0:T(8,128)(2,1)S(1)}, u32[]{:S(2)}, u32[]{:S(2)}) collective-permute-start(bf16[256,256]{1,0:T(8,128)(2,1)} %bitcast.8), channel_id=1, source_target_pairs={{0,2},{2,0},{4,6},{6,4},{1,3},{3,1},{5,7},{7,5},{8,10},{10,8},{12,... | collective-permute-start | bytes 393224 | tf_op jit(solution)/shard_map/ppermute | solution.py:216
  3.6 14.6 %copy-start = (bf16[256,1024]{1,0:T(8,128)(2,1)S(1)}, bf16[256,1024]{1,0:T(8,128)(2,1)}, u32[]{:S(2)}) copy-start(bf16[256,1024]{1,0:T(8,128)(2,1)} %weights.3) | copy-start | bytes 1572868
  5.6 10.4 %collective-permute-start.1 = (bf16[160,256]{1,0:T(8,128)(2,1)}, bf16[160,256]{1,0:T(8,128)(2,1)S(1)}, u32[]{:S(2)}, u32[]{:S(2)}) collective-permute-start(bf16[160,256]{1,0:T(8,128)(2,1)} %get-tuple-element.58), channel_id=1, source_target_pairs={{0,8},{8,16},{16,24},{24,0},{1,9},{9,17},{17,25},{25,1},{2,10},{10... | collective-permute-start | bytes 245768 | tf_op jit(solution)/shard_map/ppermute | solution.py:212
  7.2 8.8 %collective-permute-start.2 = (bf16[144,256]{1,0:T(8,128)(2,1)}, bf16[144,256]{1,0:T(8,128)(2,1)S(1)}, u32[]{:S(2)}, u32[]{:S(2)}) collective-permute-start(bf16[144,256]{1,0:T(8,128)(2,1)} %get-tuple-element.61), channel_id=1, source_target_pairs={{0,16},{8,24},{16,0},{24,8},{1,17},{9,25},{17,1},{25,9},{2,18},{10... | collective-permute-start | bytes 221192 | tf_op jit(solution)/shard_map/ppermute | solution.py:212
  9.8 6.2 %collective-permute-start.3 = (bf16[144,256]{1,0:T(8,128)(2,1)}, bf16[144,256]{1,0:T(8,128)(2,1)S(1)}, u32[]{:S(2)}, u32[]{:S(2)}) collective-permute-start(bf16[144,256]{1,0:T(8,128)(2,1)} %get-tuple-element.62), channel_id=1, source_target_pairs={{0,24},{8,0},{16,8},{24,16},{1,25},{9,1},{17,9},{25,17},{2,26},{10... | collective-permute-start | bytes 221192 | tf_op jit(solution)/shard_map/ppermute | solution.py:212
  11.1 6.3 %collective-permute-start.4 = (bf16[256,256]{1,0:T(8,128)(2,1)}, bf16[256,256]{1,0:T(8,128)(2,1)S(1)}, u32[]{:S(2)}, u32[]{:S(2)}) collective-permute-start(bf16[256,256]{1,0:T(8,128)(2,1)} %bitcast.9), channel_id=1, source_target_pairs={{0,4},{2,6},{4,0},{6,2},{1,5},{3,7},{5,1},{7,3},{8,12},{10,14},{12... | collective-permute-start | bytes 393224 | tf_op jit(solution)/shard_map/ppermute | solution.py:216
  12.7 5.6 %collective-permute-start.5 = (bf16[256,256]{1,0:T(8,128)(2,1)S(1)}, bf16[256,256]{1,0:T(8,128)(2,1)S(1)}, u32[]{:S(2)}, u32[]{:S(2)}) collective-permute-start(bf16[256,256]{1,0:T(8,128)(2,1)S(1)} %collective-permute-done.rest_1_), channel_id=1, source_target_pairs={{0,4},{2,6},{4,0},{6,2},{1,5},{3,7},{5,1},{7,3},{8,12},{10,14},{12... | collective-permute-start | bytes 393224 | tf_op jit(solution)/shard_map/ppermute | solution.py:216
  13.2 1.0 %copy-start.1 = (bf16[3,1,256,256]{3,2,1,0:T(8,128)(2,1)S(1)}, bf16[3,1,256,256]{3,2,1,0:T(8,128)(2,1)}, u32[]{:S(2)}) copy-start(bf16[3,1,256,256]{3,2,1,0:T(8,128)(2,1)} %param.6) | copy-start | bytes 1179652
  14.2 0.9 %copy-start.3 = (bf16[144,256]{1,0:T(8,128)(2,1)S(1)}, bf16[144,256]{1,0:T(8,128)(2,1)}, u32[]{:S(2)}) copy-start(bf16[144,256]{1,0:T(8,128)(2,1)} %get-tuple-element.56.chunk) | copy-start | bytes 221188
  15.1 0.7 %copy-start.4 = (f32[3,3,256]{2,1,0:T(4,128)S(1)}, f32[3,3,256]{2,1,0:T(4,128)}, u32[]{:S(2)}) copy-start(f32[3,3,256]{2,1,0:T(4,128)} %short_filter) | copy-start | bytes 27652
  15.8 2.5 %copy-start.2 = (bf16[1,256,256]{2,1,0:T(8,128)(2,1)S(1)}, bf16[1,256,256]{2,1,0:T(8,128)(2,1)}, u32[]{:S(2)}) copy-start(bf16[1,256,256]{2,1,0:T(8,128)(2,1)} %param.11) | copy-start | bytes 393220
  18.7 6.2 %collective-permute-start.6 = (bf16[128,256]{1,0:T(8,128)(2,1)S(1)}, bf16[128,256]{1,0:T(8,128)(2,1)S(1)}, u32[]{:S(2)}, u32[]{:S(2)}) collective-permute-start(bf16[128,256]{1,0:T(8,128)(2,1)S(1)} %get-tuple-element.71), channel_id=1, source_target_pairs={{0,8},{8,16},{16,24},{24,0},{1,9},{9,17},{17,25},{25,1},{2,10},{10... | collective-permute-start | bytes 196616 | tf_op jit(solution)/shard_map/ppermute | solution.py:212
  19.4 6.6 %collective-permute-start.7 = (bf16[128,256]{1,0:T(8,128)(2,1)S(1)}, bf16[128,256]{1,0:T(8,128)(2,1)S(1)}, u32[]{:S(2)}, u32[]{:S(2)}) collective-permute-start(bf16[128,256]{1,0:T(8,128)(2,1)S(1)} %get-tuple-element.72), channel_id=1, source_target_pairs={{0,16},{8,24},{16,0},{24,8},{1,17},{9,25},{17,1},{25,9},{2,18},{10... | collective-permute-start | bytes 196616 | tf_op jit(solution)/shard_map/ppermute | solution.py:212
  20.7 5.3 %collective-permute-start.8 = (bf16[128,256]{1,0:T(8,128)(2,1)S(1)}, bf16[128,256]{1,0:T(8,128)(2,1)S(1)}, u32[]{:S(2)}, u32[]{:S(2)}) collective-permute-start(bf16[128,256]{1,0:T(8,128)(2,1)S(1)} %get-tuple-element.73), channel_id=1, source_target_pairs={{0,24},{8,0},{16,8},{24,16},{1,25},{9,1},{17,9},{25,17},{2,26},{10... | collective-permute-start | bytes 196616 | tf_op jit(solution)/shard_map/ppermute | solution.py:212
  26.4 2.0 %collective-permute-start.9 = (f32[128,1024]{1,0:T(8,128)S(1)}, f32[128,1024]{1,0:T(8,128)S(1)}, u32[]{:S(2)}, u32[]{:S(2)}) collective-permute-start(f32[128,1024]{1,0:T(8,128)S(1)} %get-tuple-element.83), channel_id=1, source_target_pairs={{0,1},{1,0},{2,3},{3,2},{4,5},{5,4},{6,7},{7,6},{8,9},{9,8},{10,11... | collective-permute-start | bytes 1572872 | tf_op jit(solution)/shard_map/ppermute | solution.py:212
  26.9 9.7 %collective-permute-start.10 = (bf16[512,256]{1,0:T(8,128)(2,1)S(1)}, bf16[512,256]{1,0:T(8,128)(2,1)S(1)}, u32[]{:S(2)}, u32[]{:S(2)}) collective-permute-start(bf16[512,256]{1,0:T(8,128)(2,1)S(1)} %get-tuple-element.88), channel_id=1, source_target_pairs={{0,2},{2,0},{4,6},{6,4},{1,3},{3,1},{5,7},{7,5},{8,10},{10,8},{12,... | collective-permute-start | bytes 786440 | tf_op jit(solution)/shard_map/ppermute | solution.py:216
  28.5 13.3 %collective-permute-start.15 = (bf16[32,1024]{1,0:T(8,128)(2,1)S(1)}, bf16[32,1024]{1,0:T(8,128)(2,1)S(1)}, u32[]{:S(2)}, u32[]{:S(2)}) collective-permute-start(bf16[32,1024]{1,0:T(8,128)(2,1)S(1)} %get-tuple-element.84), channel_id=1, source_target_pairs={{0,8},{8,16},{16,24},{24,0},{1,9},{9,17},{17,25},{25,1},{2,10},{10... | collective-permute-start | bytes 196616 | tf_op jit(solution)/shard_map/ppermute | solution.py:212
  29.9 7.8 %collective-permute-start.16 = (bf16[32,1024]{1,0:T(8,128)(2,1)S(1)}, bf16[32,1024]{1,0:T(8,128)(2,1)S(1)}, u32[]{:S(2)}, u32[]{:S(2)}) collective-permute-start(bf16[32,1024]{1,0:T(8,128)(2,1)S(1)} %get-tuple-element.98), channel_id=1, source_target_pairs={{0,16},{8,24},{16,0},{24,8},{1,17},{9,25},{17,1},{25,9},{2,18},{10... | collective-permute-start | bytes 196616 | tf_op jit(solution)/shard_map/ppermute | solution.py:212
  31.7 8.5 %collective-permute-start.17 = (bf16[32,1024]{1,0:T(8,128)(2,1)S(1)}, bf16[32,1024]{1,0:T(8,128)(2,1)S(1)}, u32[]{:S(2)}, u32[]{:S(2)}) collective-permute-start(bf16[32,1024]{1,0:T(8,128)(2,1)S(1)} %get-tuple-element.99), channel_id=1, source_target_pairs={{0,24},{8,0},{16,8},{24,16},{1,25},{9,1},{17,9},{25,17},{2,26},{10... | collective-permute-start | bytes 196616 | tf_op jit(solution)/shard_map/ppermute | solution.py:212
  35.2 7.6 %collective-permute-start.12 = (bf16[96,256]{1,0:T(8,128)(2,1)S(1)}, bf16[96,256]{1,0:T(8,128)(2,1)S(1)}, u32[]{:S(2)}, u32[]{:S(2)}) collective-permute-start(bf16[96,256]{1,0:T(8,128)(2,1)S(1)} %get-tuple-element.92), channel_id=1, source_target_pairs={{0,8},{8,16},{16,24},{24,0},{1,9},{9,17},{17,25},{25,1},{2,10},{10... | collective-permute-start | bytes 147464 | tf_op jit(solution)/shard_map/ppermute | solution.py:212
  36.6 6.4 %collective-permute-start.13 = (bf16[96,256]{1,0:T(8,128)(2,1)S(1)}, bf16[96,256]{1,0:T(8,128)(2,1)S(1)}, u32[]{:S(2)}, u32[]{:S(2)}) collective-permute-start(bf16[96,256]{1,0:T(8,128)(2,1)S(1)} %get-tuple-element.93), channel_id=1, source_target_pairs={{0,16},{8,24},{16,0},{24,8},{1,17},{9,25},{17,1},{25,9},{2,18},{10... | collective-permute-start | bytes 147464 | tf_op jit(solution)/shard_map/ppermute | solution.py:212
  37.8 7.1 %collective-permute-start.14 = (bf16[96,256]{1,0:T(8,128)(2,1)S(1)}, bf16[96,256]{1,0:T(8,128)(2,1)S(1)}, u32[]{:S(2)}, u32[]{:S(2)}) collective-permute-start(bf16[96,256]{1,0:T(8,128)(2,1)S(1)} %get-tuple-element.94), channel_id=1, source_target_pairs={{0,24},{8,0},{16,8},{24,16},{1,25},{9,1},{17,9},{25,17},{2,26},{10... | collective-permute-start | bytes 147464 | tf_op jit(solution)/shard_map/ppermute | solution.py:212
  40.2 6.3 %collective-permute-start.11 = (bf16[256,256]{1,0:T(8,128)(2,1)S(1)}, bf16[256,256]{1,0:T(8,128)(2,1)S(1)}, u32[]{:S(2)}, u32[]{:S(2)}) collective-permute-start(bf16[256,256]{1,0:T(8,128)(2,1)S(1)} %get-tuple-element.90), channel_id=1, source_target_pairs={{0,4},{2,6},{4,0},{6,2},{1,5},{3,7},{5,1},{7,3},{8,12},{10,14},{12... | collective-permute-start | bytes 393224 | tf_op jit(solution)/shard_map/ppermute | solution.py:216
  41.9 4.7 %collective-permute-start.20 = (bf16[32,1024]{1,0:T(8,128)(2,1)S(1)}, bf16[32,1024]{1,0:T(8,128)(2,1)S(1)}, u32[]{:S(2)}, u32[]{:S(2)}) collective-permute-start(bf16[32,1024]{1,0:T(8,128)(2,1)S(1)} %block_sum.1.refs_0_), channel_id=1, source_target_pairs={{0,24},{8,0},{16,8},{24,16},{1,25},{9,1},{17,9},{25,17},{2,26},{10... | collective-permute-start | bytes 196616 | tf_op jit(solution)/shard_map/ppermute | solution.py:212
  42.8 6.9 %collective-permute-start.19 = (bf16[32,1024]{1,0:T(8,128)(2,1)S(1)}, bf16[32,1024]{1,0:T(8,128)(2,1)S(1)}, u32[]{:S(2)}, u32[]{:S(2)}) collective-permute-start(bf16[32,1024]{1,0:T(8,128)(2,1)S(1)} %block_sum.1.refs_0_), channel_id=1, source_target_pairs={{0,16},{8,24},{16,0},{24,8},{1,17},{9,25},{17,1},{25,9},{2,18},{10... | collective-permute-start | bytes 196616 | tf_op jit(solution)/shard_map/ppermute | solution.py:212
  43.0 6.7 %collective-permute-start.18 = (bf16[32,1024]{1,0:T(8,128)(2,1)S(1)}, bf16[32,1024]{1,0:T(8,128)(2,1)S(1)}, u32[]{:S(2)}, u32[]{:S(2)}) collective-permute-start(bf16[32,1024]{1,0:T(8,128)(2,1)S(1)} %block_sum.1.refs_0_), channel_id=1, source_target_pairs={{0,8},{8,16},{16,24},{24,0},{1,9},{9,17},{17,25},{25,1},{2,10},{10... | collective-permute-start | bytes 196616 | tf_op jit(solution)/shard_map/ppermute | solution.py:212
  49.8 1.6 %collective-permute-start.21 = (bf16[144,1024]{1,0:T(8,128)(2,1)S(1)}, bf16[144,1024]{1,0:T(8,128)(2,1)S(1)}, u32[]{:S(2)}, u32[]{:S(2)}) collective-permute-start(bf16[144,1024]{1,0:T(8,128)(2,1)S(1)} %collect.1.near), channel_id=1, source_target_pairs={{0,1},{1,0},{2,3},{3,2},{4,5},{5,4},{6,7},{7,6},{8,9},{9,8},{10,11... | collective-permute-start | bytes 884744 | tf_op jit(solution)/shard_map/ppermute | solution.py:212

commit v4 on v3

--- a/solution.py
+++ b/solution.py
@@ -328,12 +328,6 @@
     for s in range(1, taps):
         total += columns[:, j + s : j + s + 1] * (masks[s] * shifts[s])
     return total
-
-
-def pair_conv_kernel(taps, turned, previous, columns, seg, out, place):
-    masks = block_masks(seg[0:1], taps, place, lax.axis_index("ctx"), turned.shape[2])
-    for i in range(out.shape[0]):
-        out[i] = local_conv(turned, previous, columns, masks, i + 1)
 
 
 def conv_kernel(devices, taps, columns, *rest):
@@ -479,33 +473,81 @@
     out[...] = (own[...] + come[...].astype(f32)).astype(bf16)
 
 
+def ready_kernel(devices, taps, turned, previous, columns, seg, conv, source, *rest):
+    pair_w, query_taps, query_w, flips, sum_w, early_w, place = rest
+    me = lax.axis_index("ctx")
+    stacked, chunk, span = conv.shape
+    _, width, length = turned.shape
+    groups = flips.shape[0]
+    size = chunk // groups
+    subs = span // SUB
+    own = block_masks(seg[0:1], taps, place, me, length)
+    shifts = local_shifts(turned, previous, taps, 0)
+    position = lax.broadcasted_iota(jnp.int32, (width, length), 1)
+    query_taps[0] = shifts[0]
+    for s in range(1, taps):
+        query_taps[s] = own[s] * shifts[s]
+        query_w[s - 1] = jnp.broadcast_to(columns[:, s : s + 1] * own[s], (width, length))
+    for i in range(stacked):
+        other = local_conv(turned, previous, columns, own, stacked - i)
+        j = (i + 1) * taps
+        pair_w[i * taps] = columns[:, j : j + 1] * other
+        for s in range(1, taps):
+            weight = columns[:, j + s : j + s + 1] * own[s] * other
+            pair_w[i * taps + s] = jnp.where(position >= s, weight, 0.0)
+    masks = tap_masks(seg[0:1], taps)
+    column = columns[block_at(me, chunk)]
+    for i in range(stacked):
+        x = source[i * chunk : (i + 1) * chunk].astype(f32)
+        other = conv[1 - i]
+        j = (i + 1) * taps
+        sum_w[i * taps] = other * x
+        for s in range(1, taps):
+            masked = masks[s] * other
+            sum_w[i * taps + s] = masked * pltpu.roll(x, s, 1)
+            weight = column[:, j + s : j + s + 1] * masked
+            for b in range(devices - 1):
+                at = slice((b + 1) * length, (b + 1) * length + SUB)
+                early_w[i * (taps - 1) + s - 1, :, b * SUB : (b + 1) * SUB] = weight[:, at]
+    gated = (conv[0] * conv[1]).astype(bf16)
+    corner = lax.broadcasted_iota(jnp.int32, (SUB, SUB), 0)
+    corner += lax.broadcasted_iota(jnp.int32, (SUB, SUB), 1)
+    flip = jnp.where(corner == SUB - 1, 1.0, 0.0).astype(bf16)
+    for g in range(groups):
+        rows = slice(g * size, (g + 1) * size)
+        left = jnp.concatenate([gated[rows, j * SUB : (j + 1) * SUB] for j in range(subs)], axis=0)
+        flips[g] = lax.dot_general(
+            flip, left, (((1,), (1,)), ((), ())), preferred_element_type=f32
+        ).astype(bf16)
+
+
 def backward_kernel(
-    devices, taps, conv, source, seg, toeplitz, columns, turned, previous, grad_y, long, *rest
+    devices, taps, toeplitz, columns, grad_y, long, query_taps, query_w, flips, sum_w, early_w, *rest
 ):
     glos, rest = rest[:devices], rest[devices:]
-    outs, (query_out, grad_long_out, grads, small, marks, place) = rest[:devices], rest[devices:]
+    outs, (query_out, grad_long_out, grads, small, marks) = rest[:devices], rest[devices:]
     me = lax.axis_index("ctx")
-    stacked, chunk, span = conv.shape
+    _, chunk, span = sum_w.shape
+    stacked = sum_w.shape[0] // taps
     length = span // devices
     groups = toeplitz.shape[0]
     size = chunk // groups
-    width = turned.shape[1]
-
-    own_masks = block_masks(seg[0:1], taps, place, me, length)
-    shifts = local_shifts(turned, previous, taps, 0)
+    width = grad_y.shape[0]
+    reach = taps - 1
+
     grad = grad_y[...] * long[...]
     total = columns[:, 0:1] * grad
     lane = lax.broadcasted_iota(jnp.int32, (width, SUB), 1)
     position = lax.broadcasted_iota(jnp.int32, (width, length), 1)
-    sums = jnp.where(lane == groups, jnp.sum(grad * shifts[0], axis=1, keepdims=True), 0.0)
+    sums = jnp.zeros((width, SUB), f32)
     early = jnp.zeros((width, SUB), f32)
-    for s in range(1, taps):
-        masked = own_masks[s] * grad
-        back = pltpu.roll(columns[:, s : s + 1] * masked, length - s, 1)
-        total += jnp.where(position < length - s, back, 0.0)
-        early += jnp.where(position >= length - s, back, 0.0)[:, length - SUB :]
-        tap = jnp.sum(masked * shifts[s], axis=1, keepdims=True)
+    for s in range(taps):
+        tap = jnp.sum(grad * query_taps[s], axis=1, keepdims=True)
         sums += jnp.where(lane == groups + s, tap, 0.0)
+        if s:
+            back = pltpu.roll(query_w[s - 1] * grad, length - s, 1)
+            total += jnp.where(position < length - s, back, 0.0)
+            early += jnp.where(lane >= SUB - s, back[:, length - SUB :], 0.0)
     query_out[...] = total.T
     common = sums.T[0:16]
     early_query = early.T[SUB - 16 :]
@@ -513,14 +555,8 @@
     for s in range(devices):
         at = block_at(lax.rem(me - s + devices, devices), length)
         grad_long_out[:, at] = glos[s][chunk:]
-    masks = tap_masks(seg[0:1], taps)
-    column = columns[block_at(me, chunk)]
     high = grad_long_out[...]
-    gated = (conv[0] * conv[1]).astype(bf16)
     gg_parts = []
-    corner = lax.broadcasted_iota(jnp.int32, (SUB, SUB), 0)
-    corner += lax.broadcasted_iota(jnp.int32, (SUB, SUB), 1)
-    flip = jnp.where(corner == SUB - 1, 1.0, 0.0).astype(bf16)
     subs = span // SUB
     small[...] = jnp.zeros_like(small)
     for g in range(groups):
@@ -540,11 +576,8 @@
                 term = part[size * j : size * (j + 1)]
                 totals[j] = term if totals[j] is None else totals[j] + term
         gg_parts.append(jnp.concatenate(totals, axis=1))
-        left = jnp.concatenate([gated[own, j * SUB : (j + 1) * SUB] for j in range(subs)], axis=0)
         right = jnp.concatenate([high[own, j * SUB : (j + 1) * SUB] for j in range(subs)], axis=0)
-        turned = lax.dot_general(
-            flip, left, (((1,), (1,)), ((), ())), preferred_element_type=f32
-        ).astype(bf16)
+        turned = flips[g]
         lines = []
         for lag in range(subs):
             cross = jnp.dot(
@@ -564,22 +597,9 @@
     grads[...] = grad_gated.astype(bf16)
     lane = lax.broadcasted_iota(jnp.int32, (chunk, SUB), 1)
     sums = jnp.zeros((chunk, SUB), f32)
-    reach = taps - 1
-    early = [jnp.zeros((chunk, SUB), f32) for _ in range(stacked * devices)]
-    for i in range(stacked):
-        grad = grad_gated * conv[1 - i]
-        x = source[i * chunk : (i + 1) * chunk].astype(f32)
-        j = (i + 1) * taps
-        tap = jnp.sum(grad * x, axis=1, keepdims=True)
-        sums += jnp.where(lane == groups + j, tap, 0.0)
-        for s in range(1, taps):
-            masked = masks[s] * grad
-            tap = jnp.sum(masked * pltpu.roll(x, s, 1), axis=1, keepdims=True)
-            sums += jnp.where(lane == groups + j + s, tap, 0.0)
-            back = column[:, j + s : j + s + 1] * pltpu.roll(masked, span - s, 1)
-            for b in range(devices):
-                end = back[:, (b + 1) * length - SUB : (b + 1) * length]
-                early[i * devices + b] += jnp.where(lane >= SUB - s, end, 0.0)
+    for n in range(stacked * taps):
+        tap = jnp.sum(grad_gated * sum_w[n], axis=1, keepdims=True)
+        sums += jnp.where(lane == groups + taps + n, tap, 0.0)
     marks[...] = jnp.zeros_like(marks)
     marks[:, 0:chunk] = sums.T
     common += pltpu.roll(marks[0:16], me * chunk, 1)
@@ -594,8 +614,16 @@
         small[b, 2 * groups : 2 * groups + count] = high[groups : groups + count]
         small[b, 2 * groups + count : start] = (common - high)[groups : groups + count]
         small[b, start : start + reach] = early_query[16 - reach :]
+        if b == devices - 1:
+            continue
+        first = grad_gated[:, (b + 1) * length : (b + 1) * length + SUB]
         for i in range(stacked):
-            marks[:, 0:chunk] = early[i * devices + b].T
+            early = jnp.zeros((chunk, SUB), f32)
+            for s in range(1, taps):
+                weight = early_w[i * reach + s - 1, :, b * SUB : (b + 1) * SUB]
+                back = pltpu.roll(weight * first, SUB - s, 1)
+                early += jnp.where(lane >= SUB - s, back, 0.0)
+            marks[:, 0:chunk] = early.T
             placed = pltpu.roll(marks[SUB - 16 :], me * chunk, 1)
             at = start + (i + 1) * reach
             small[b, at : at + reach] = placed[16 - reach :]
@@ -633,53 +661,44 @@
         later[i, 16 - reach : 16] = total[start + i * reach : start + (i + 1) * reach]
 
 
-def collect_kernel(devices, sums, *refs):
-    blocks, near = refs[:devices], refs[devices]
-    me = lax.axis_index("ctx")
-    rows = blocks[0].shape[0]
-    for s in range(devices):
-        near[block_at(lax.rem(me - s + devices, devices), rows)] = blocks[s][...]
-    near[devices * rows :] = sums[...]
-
-
-def grad_out_kernel(devices, taps, query_part, pair, columns, seg, later, *refs):
-    pays, (out, gated, place) = refs[:devices], refs[devices:]
+def grad_out_kernel(devices, taps, query_part, pair_w, later, *refs):
+    pays, (out, gated) = refs[:devices], refs[devices:]
     me = lax.axis_index("ctx")
     stacked, rows, width = out.shape
     chunk = width // devices
     for s in range(devices):
         at = block_at(lax.rem(me - s + devices, devices), chunk)
         gated[at] = pays[s][0:chunk].astype(f32)
-    masks = block_masks(seg[0:1], taps, place, me, rows)
-    position = lax.broadcasted_iota(jnp.int32, (width, rows), 1)
     for i in range(stacked):
         if i == 0:
             turned = query_part[...]
         else:
-            grad = gated[...] * pair[2 - i]
-            j = i * taps
-            total = columns[:, j : j + 1] * grad
+            j = (i - 1) * taps
+            total = pair_w[j] * gated[...]
             for s in range(1, taps):
-                back = pltpu.roll(columns[:, j + s : j + s + 1] * (masks[s] * grad), rows - s, 1)
-                total += jnp.where(position < rows - s, back, 0.0)
+                total += pltpu.roll(pair_w[j + s] * gated[...], rows - s, 1)
             turned = total.T
         out[i, 0 : rows - 16] = turned[0 : rows - 16].astype(bf16)
         out[i, rows - 16 :] = (turned[rows - 16 :] + later[i]).astype(bf16)
 
 
-def final_kernel(scale, near, far, weight_out, short_out, long_out):
-    core = lax.axis_index("dp")
-    half = weight_out.shape[0] // 2
-    weight_out[block_at(core, half)] = near[0:half].astype(f32)
-    weight_out[block_at(1 - core, half)] = far[0:half].astype(f32)
-    count, width = long_out.shape
+def final_kernel(devices, scale, *refs):
+    near, far, refs = refs[:devices], refs[devices : 2 * devices], refs[2 * devices :]
+    mine, other, weight_out, short_out, long_out = refs
+    me, core = lax.axis_index("ctx"), lax.axis_index("dp")
+    rows = near[0].shape[0]
+    for side, blocks in ((core, near), (1 - core, far)):
+        for s in range(devices):
+            at = side * devices + lax.rem(me - s + devices, devices)
+            weight_out[block_at(at, rows)] = blocks[s][...].astype(f32)
+    width = long_out.shape[1]
     stacked, taps, _ = short_out.shape
 
     def sums(n):
         pieces = []
-        for ref in (near, far):
-            high = ref[half:, n * width : (n + 1) * width].astype(f32)
-            low = ref[half:, (n + 2) * width : (n + 3) * width].astype(f32)
+        for ref in (mine, other):
+            high = ref[:, n * width : (n + 1) * width].astype(f32)
+            low = ref[:, (n + 2) * width : (n + 3) * width].astype(f32)
             pieces.append(high + low)
         return (pieces[0] + pieces[1]) * scale
 
@@ -764,14 +783,21 @@
     pairs, (grad_y, query_conv) = outs[:devices], outs[devices:]
     pairs = scatter_chunks(pairs, "ctx")
 
-    (pair,) = on_core(
-        functools.partial(pair_conv_kernel, taps),
-        [((stacked - 1, width, length), f32)],
-        (turned, signal[1], columns, seg),
-        "pair_conv",
+    pair_w, *factors = on_core(
+        functools.partial(ready_kernel, devices, taps),
+        [
+            (((stacked - 1) * taps, width, length), f32),
+            ((taps, width, length), f32),
+            ((taps - 1, width, length), f32),
+            ((groups, SUB, SUB), bf16),
+            (((stacked - 1) * taps, chunk, span), f32),
+            (((stacked - 1) * (taps - 1), chunk, (devices - 1) * SUB), f32),
+        ],
+        (turned, signal[1], columns, seg, *kept[:2]),
+        "ready",
         [pltpu.VMEM((8 * taps, span), f32)],
     )
-    query_conv = after(query_conv, pair)
+    query_conv = after(query_conv, factors[0])
 
     half = width // 2
     y, long, keep, send = on_core(
@@ -810,14 +836,13 @@
     outs = on_core(
         functools.partial(backward_kernel, devices, taps),
         [((chunk + 2 * room, length), bf16)] * devices + [((length, width), f32)],
-        (*kept, columns, turned, signal[1], grad_y, after(long, sums[1]), *pairs),
+        (kept[3], columns, grad_y, after(long, sums[1]), *factors, *pairs),
         "backward",
         [
             pltpu.VMEM((chunk, span), bf16),
             pltpu.VMEM((chunk, span), bf16),
             pltpu.VMEM((devices, 2 * room, length), f32),
             pltpu.VMEM((SUB, width), f32),
-            pltpu.VMEM((8 * taps, span), f32),
         ],
         flops=2 * conv_flops,
     )
@@ -834,9 +859,9 @@
     (grad_projected,) = on_core(
         functools.partial(grad_out_kernel, devices, taps),
         [((stacked, length, width), bf16)],
-        (query_part, pair, columns, seg, later, *back),
+        (query_part, pair_w, later, *back),
         "grad_out",
-        [pltpu.VMEM((width, length), f32), pltpu.VMEM((8 * taps, span), f32)],
+        [pltpu.VMEM((width, length), f32)],
     )
     (block,) = on_core(
         functools.partial(block_sum_kernel, grad_scale),
@@ -855,18 +880,14 @@
         mixed_sum_kernel, [((length, width), bf16)], (own_part, come_part), "mixed_sum"
     )
 
-    blocks = spread(block, "ctx")
-    blocks[0] = after(block, (grad_projected, come_part))
-    (near,) = on_core(
-        functools.partial(collect_kernel, devices),
-        [((half + 16, total_cols), bf16)],
-        (sums, *blocks),
-        "collect",
-    )
+    near = spread(block, "ctx")
+    other_sums = rotate(sums, "dp", 1)
+    near[1] = after(near[1], (grad_projected, come_part, other_sums))
+    far = [rotate(piece, "dp", 1) for piece in near]
     grad_out_proj, grad_short, grad_long = on_core(
-        functools.partial(final_kernel, grad_scale),
+        functools.partial(final_kernel, devices, grad_scale),
         [((width, total_cols), f32), (short_filter.shape, f32), ((count, length), f32)],
-        (after(near, mixed), rotate(near, "dp", 1)),
+        (*near, *far, sums, other_sums),
         "final",
     )
     return (mixed[None], grad_projected[:, None], grad_short, grad_long, grad_out_proj)

time: 52.7 us -> 52.5 us (level)
  waiting for transfers between devices: 8.55 us -> 7.62 us
  starting transfers between devices: 28.7 us -> 29.6 us
    ppermute x17 -> x21, starting transfers between devices: 21.4 us -> 22.4 us  [rotate(): lax.ppermute(value, axis, [(i, (i + steps) % count) for i in range(count)])]
    ppermute x17 -> x21, waiting for transfers between devices: 7.75 us -> 6.83 us  [rotate(): lax.ppermute(value, axis, [(i, (i + steps) % count) for i in range(count)])]
    pallas_call x16 -> x15, Pallas kernels: 11.9 us -> 11.6 us  [on_core(): pl.pallas_call(kernel, out_shape=[jax.ShapeDtypeStruct(shape, kind) for s...]
  transfers between devices with their start and end apart: 22 -> 26, of which waited for: 6 -> 8; matrix products, arithmetic and copies ran while one was open for 0% -> 0% of each run, Pallas kernels for 19% -> 19%
where the time goes in v4:
time: 52.5 us; the launch traced here: 52.3 us
  starting transfers between devices  29.6 us (56%)
  Pallas kernels  11.6 us (22%)
  waiting for transfers between devices  7.62 us (15%)
  local copies, waits for them, and re-layouts  2.6 us (5%)
  between operations  0.82 us (2%)
    ppermute x21, starting transfers between devices, rotate(): lax.ppermute(value, axis, [(i, (i + steps) % count) for i in range(count)])  22.4 us
    pallas_call x15, Pallas kernels, on_core(): pl.pallas_call(kernel, out_shape=[jax.ShapeDtypeStruct(shape, kind) for s...  11.6 us
    ppermute x5, starting transfers between devices, swap(): lax.ppermute(value, axis, [(i, i ^ bits) for i in range(lax.axis_size(axi...  7.22 us
    ppermute x21, waiting for transfers between devices, rotate(): lax.ppermute(value, axis, [(i, (i + steps) % count) for i in range(count)])  6.83 us
    unnamed x10, local copies, waits for them, and re-layouts  2.6 us
  transfers between devices with their start and end apart: 26, of which 8 were waited for; matrix products, arithmetic and copies ran while one was open for 0% of the time, Pallas kernels for 19%

profile of v4, /device:TPU:0, one launch (start us, length us, event | category | flops | bytes accessed | tf_op | source)
XLA Modules:
  0.0 52.3 jit_solution(743857980033383451)
XLA Ops:
  0.6 3.0 %collective-permute-start = (bf16[256,256]{1,0:T(8,128)(2,1)}, bf16[256,256]{1,0:T(8,128)(2,1)S(1)}, u32[]{:S(2)}, u32[]{:S(2)}) collective-permute-start(bf16[256,256]{1,0:T(8,128)(2,1)} %bitcast.8), channel_id=1, source_target_pairs={{0,2},{2,0},{4,6},{6,4},{1,3},{3,1},{5,7},{7,5},{8,10},{10,8},{12,... | collective-permute-start | bytes 393224 | tf_op jit(solution)/shard_map/ppermute | solution.py:216
  3.6 1.9 %pack.1 = (bf16[144,256]{1,0:T(8,128)(2,1)}, bf16[160,256]{1,0:T(8,128)(2,1)}, bf16[144,256]{1,0:T(8,128)(2,1)}, bf16[144,256]{1,0:T(8,128)(2,1)}) custom-call(bf16[3,256,256]{2,1,0:T(8,128)(2,1)} %bitcast.6, f32[16,256]{1,0:T(8,128)} %refs_1_.1, s32[1,256]{1,0:T(1,128)} %refs_2_.1), custom_call_target="tpu_custom_call" | custom-call | bytes 713728 | tf_op jit(solution)/shard_map/pack/pallas_call | solution.py:234
  5.5 1.6 %collective-permute-start.1 = (bf16[160,256]{1,0:T(8,128)(2,1)}, bf16[160,256]{1,0:T(8,128)(2,1)S(1)}, u32[]{:S(2)}, u32[]{:S(2)}) collective-permute-start(bf16[160,256]{1,0:T(8,128)(2,1)} %get-tuple-element.63), channel_id=1, source_target_pairs={{0,8},{8,16},{16,24},{24,0},{1,9},{9,17},{17,25},{25,1},{2,10},{10... | collective-permute-start | bytes 245768 | tf_op jit(solution)/shard_map/ppermute | solution.py:212
  7.1 2.6 %collective-permute-start.2 = (bf16[144,256]{1,0:T(8,128)(2,1)}, bf16[144,256]{1,0:T(8,128)(2,1)S(1)}, u32[]{:S(2)}, u32[]{:S(2)}) collective-permute-start(bf16[144,256]{1,0:T(8,128)(2,1)} %get-tuple-element.66), channel_id=1, source_target_pairs={{0,16},{8,24},{16,0},{24,8},{1,17},{9,25},{17,1},{25,9},{2,18},{10... | collective-permute-start | bytes 221192 | tf_op jit(solution)/shard_map/ppermute | solution.py:212
  9.7 1.3 %collective-permute-start.3 = (bf16[144,256]{1,0:T(8,128)(2,1)}, bf16[144,256]{1,0:T(8,128)(2,1)S(1)}, u32[]{:S(2)}, u32[]{:S(2)}) collective-permute-start(bf16[144,256]{1,0:T(8,128)(2,1)} %get-tuple-element.67), channel_id=1, source_target_pairs={{0,24},{8,0},{16,8},{24,16},{1,25},{9,1},{17,9},{25,17},{2,26},{10... | collective-permute-start | bytes 221192 | tf_op jit(solution)/shard_map/ppermute | solution.py:212
  11.1 1.5 %collective-permute-start.4 = (bf16[256,256]{1,0:T(8,128)(2,1)}, bf16[256,256]{1,0:T(8,128)(2,1)S(1)}, u32[]{:S(2)}, u32[]{:S(2)}) collective-permute-start(bf16[256,256]{1,0:T(8,128)(2,1)} %bitcast.9), channel_id=1, source_target_pairs={{0,4},{2,6},{4,0},{6,2},{1,5},{3,7},{5,1},{7,3},{8,12},{10,14},{12... | collective-permute-start | bytes 393224 | tf_op jit(solution)/shard_map/ppermute | solution.py:216
  12.6 0.0 collective-permute-done.rest_1_
  12.6 0.5 collective-permute-start.5
  13.1 1.0 %copy-done.1 = bf16[3,1,256,256]{3,2,1,0:T(8,128)(2,1)S(1)} copy-done((bf16[3,1,256,256]{3,2,1,0:T(8,128)(2,1)S(1)}, bf16[3,1,256,256]{3,2,1,0:T(8,128)(2,1)}, u32[]{:S(2)}) %copy-start.1) | copy-done | bytes 393240
  14.1 0.9 %copy-done.3 = bf16[144,256]{1,0:T(8,128)(2,1)S(1)} copy-done((bf16[144,256]{1,0:T(8,128)(2,1)S(1)}, bf16[144,256]{1,0:T(8,128)(2,1)}, u32[]{:S(2)}) %copy-start.3) | copy-done | bytes 73752
  15.0 0.7 %copy-done.4 = f32[3,3,256]{2,1,0:T(4,128)S(1)} copy-done((f32[3,3,256]{2,1,0:T(4,128)S(1)}, f32[3,3,256]{2,1,0:T(4,128)}, u32[]{:S(2)}) %copy-start.4) | copy-done | bytes 9240
  15.7 0.2 prepare.1
  15.9 0.0 collective-permute-done.2.rest_2_
  15.9 0.0 collective-permute-done.3.rest_3_
  15.9 0.0 collective-permute-done.1.rest_1_.previous
  15.9 0.0 copy-start
  16.0 0.0 copy-start.2
  16.0 1.4 %conv.1 = (bf16[64,256]{1,0:T(8,128)(2,1)S(1)}, bf16[64,256]{1,0:T(8,128)(2,1)S(1)}, bf16[64,256]{1,0:T(8,128)(2,1)S(1)}, bf16[64,256]{1,0:T(8,128)(2,1)S(1)}, f...) custom-call(f32[256,16]{1,0:T(8,128)S(1)} %get-tuple-element.64.colu, ...), custom_call_target="tpu_custom_call" | custom-call | flops 900000000 | bytes 3366912 | tf_op jit(solution)/shard_map/conv/pallas_call | solution.py:234
  17.4 0.0 collective-permute-done.4.rest_2_
  17.4 0.8 %collective-permute-done.5.rest_3_ = bf16[256,256]{1,0:T(8,128)(2,1)S(1)} collective-permute-done((bf16[256,256]{1,0:T(8,128)(2,1)S(1)}, bf16[256,256]{1,0:T(8,128)(2,1)S(1)}, u32[]{:S(2)}, u32[]{:S(2)}) %collective-permute-start.5) | collective-permute-done | bytes 131104 | tf_op jit(solution)/shard_map/ppermute | solution.py:216
  18.2 0.4 grad_y.1
  18.6 0.7 %collective-permute-start.6 = (bf16[128,256]{1,0:T(8,128)(2,1)S(1)}, bf16[128,256]{1,0:T(8,128)(2,1)S(1)}, u32[]{:S(2)}, u32[]{:S(2)}) collective-permute-start(bf16[128,256]{1,0:T(8,128)(2,1)S(1)} %get-tuple-element.79), channel_id=1, source_target_pairs={{0,8},{8,16},{16,24},{24,0},{1,9},{9,17},{17,25},{25,1},{2,10},{10... | collective-permute-start | bytes 196616 | tf_op jit(solution)/shard_map/ppermute | solution.py:212
  19.4 1.3 %collective-permute-start.7 = (bf16[128,256]{1,0:T(8,128)(2,1)S(1)}, bf16[128,256]{1,0:T(8,128)(2,1)S(1)}, u32[]{:S(2)}, u32[]{:S(2)}) collective-permute-start(bf16[128,256]{1,0:T(8,128)(2,1)S(1)} %get-tuple-element.80), channel_id=1, source_target_pairs={{0,16},{8,24},{16,0},{24,8},{1,17},{9,25},{17,1},{25,9},{2,18},{10... | collective-permute-start | bytes 196616 | tf_op jit(solution)/shard_map/ppermute | solution.py:212
  20.7 1.8 %collective-permute-start.8 = (bf16[128,256]{1,0:T(8,128)(2,1)S(1)}, bf16[128,256]{1,0:T(8,128)(2,1)S(1)}, u32[]{:S(2)}, u32[]{:S(2)}) collective-permute-start(bf16[128,256]{1,0:T(8,128)(2,1)S(1)} %get-tuple-element.81), channel_id=1, source_target_pairs={{0,24},{8,0},{16,8},{24,16},{1,25},{9,1},{17,9},{25,17},{2,26},{10... | collective-permute-start | bytes 196616 | tf_op jit(solution)/shard_map/ppermute | solution.py:212
  22.5 1.4 %ready.1 = (f32[6,256,256]{2,1,0:T(8,128)S(1)}, f32[3,256,256]{2,1,0:T(8,128)S(1)}, f32[2,256,256]{2,1,0:T(8,128)S(1)}, bf16[4,128,128]{2,1,0:T(8,128)(2,1)S(1)}...) custom-call(bf16[3,256,256]{2,1,0:T(8,128)(2,1)S(1)} %get-tuple-element.62.turned, ...), custom_call_target="tpu_custom_call" | custom-call | bytes 6291456 | tf_op jit(solution)/shard_map/ready/pallas_call | solution.py:234
  23.9 0.9 %collective-permute-done.6.rest_5_.rest_1_ = bf16[128,256]{1,0:T(8,128)(2,1)S(1)} collective-permute-done((bf16[128,256]{1,0:T(8,128)(2,1)S(1)}, bf16[128,256]{1,0:T(8,128)(2,1)S(1)}, u32[]{:S(2)}, u32[]{:S(2)}) %collective-permute-start.6) | collective-permute-done | bytes 65568 | tf_op jit(solution)/shard_map/ppermute | solution.py:212
  24.9 1.1 %collective-permute-done.7.rest_6_.rest_2_ = bf16[128,256]{1,0:T(8,128)(2,1)S(1)} collective-permute-done((bf16[128,256]{1,0:T(8,128)(2,1)S(1)}, bf16[128,256]{1,0:T(8,128)(2,1)S(1)}, u32[]{:S(2)}, u32[]{:S(2)}) %collective-permute-start.7) | collective-permute-done | bytes 65568 | tf_op jit(solution)/shard_map/ppermute | solution.py:212
  25.9 0.0 collective-permute-done.8.rest_7_.rest_3_
  25.9 0.4 weight_grad.1
  26.4 0.1 collective-permute-start.9
  26.4 0.4 mixed_part.1
  26.9 0.6 %collective-permute-start.10 = (bf16[512,256]{1,0:T(8,128)(2,1)S(1)}, bf16[512,256]{1,0:T(8,128)(2,1)S(1)}, u32[]{:S(2)}, u32[]{:S(2)}) collective-permute-start(bf16[512,256]{1,0:T(8,128)(2,1)S(1)} %get-tuple-element.98), channel_id=1, source_target_pairs={{0,2},{2,0},{4,6},{6,4},{1,3},{3,1},{5,7},{7,5},{8,10},{10,8},{12,... | collective-permute-start | bytes 786440 | tf_op jit(solution)/shard_map/ppermute | solution.py:216
  27.5 0.9 %collective-permute-done.9.other = f32[128,1024]{1,0:T(8,128)S(1)} collective-permute-done((f32[128,1024]{1,0:T(8,128)S(1)}, f32[128,1024]{1,0:T(8,128)S(1)}, u32[]{:S(2)}, u32[]{:S(2)}) %collective-permute-start.9) | collective-permute-done | bytes 524320 | tf_op jit(solution)/shard_map/ppermute | solution.py:212
  28.3 0.1 core_sum.1
  28.4 1.5 %collective-permute-start.15 = (bf16[32,1024]{1,0:T(8,128)(2,1)S(1)}, bf16[32,1024]{1,0:T(8,128)(2,1)S(1)}, u32[]{:S(2)}, u32[]{:S(2)}) collective-permute-start(bf16[32,1024]{1,0:T(8,128)(2,1)S(1)} %get-tuple-element.90), channel_id=1, source_target_pairs={{0,8},{8,16},{16,24},{24,0},{1,9},{9,17},{17,25},{25,1},{2,10},{10... | collective-permute-start | bytes 196616 | tf_op jit(solution)/shard_map/ppermute | solution.py:212
  29.9 1.8 %collective-permute-start.16 = (bf16[32,1024]{1,0:T(8,128)(2,1)S(1)}, bf16[32,1024]{1,0:T(8,128)(2,1)S(1)}, u32[]{:S(2)}, u32[]{:S(2)}) collective-permute-start(bf16[32,1024]{1,0:T(8,128)(2,1)S(1)} %get-tuple-element.108), channel_id=1, source_target_pairs={{0,16},{8,24},{16,0},{24,8},{1,17},{9,25},{17,1},{25,9},{2,18},{10... | collective-permute-start | bytes 196616 | tf_op jit(solution)/shard_map/ppermute | solution.py:212
  31.7 0.6 %collective-permute-start.17 = (bf16[32,1024]{1,0:T(8,128)(2,1)S(1)}, bf16[32,1024]{1,0:T(8,128)(2,1)S(1)}, u32[]{:S(2)}, u32[]{:S(2)}) collective-permute-start(bf16[32,1024]{1,0:T(8,128)(2,1)S(1)} %get-tuple-element.109), channel_id=1, source_target_pairs={{0,24},{8,0},{16,8},{24,16},{1,25},{9,1},{17,9},{25,17},{2,26},{10... | collective-permute-start | bytes 196616 | tf_op jit(solution)/shard_map/ppermute | solution.py:212
  32.3 2.2 %backward.1 = (bf16[96,256]{1,0:T(8,128)(2,1)S(1)}, bf16[96,256]{1,0:T(8,128)(2,1)S(1)}, bf16[96,256]{1,0:T(8,128)(2,1)S(1)}, bf16[96,256]{1,0:T(8,128)(2,1)S(1)}, f32[256,256]{1,0:T(8,128)S(1)}) custom-call(bf16[4,256,1024]{2,1,0:T(8,128)(2,1)S(1)} %get-tuple-element.84.toeplitz, f32[256,16]{1,0:T(8,128)S(1)} %get-tuple-element.64.columns, ...), custom_call_target="tpu_custom_call" | custom-call | flops 1073741824 | bytes 6766592 | tf_op jit(solution)/shard_map/backward/pallas_call | solution.py:234
  34.6 1.4 %collective-permute-start.12 = (bf16[96,256]{1,0:T(8,128)(2,1)S(1)}, bf16[96,256]{1,0:T(8,128)(2,1)S(1)}, u32[]{:S(2)}, u32[]{:S(2)}) collective-permute-start(bf16[96,256]{1,0:T(8,128)(2,1)S(1)} %get-tuple-element.103), channel_id=1, source_target_pairs={{0,8},{8,16},{16,24},{24,0},{1,9},{9,17},{17,25},{25,1},{2,10},{10... | collective-permute-start | bytes 147464 | tf_op jit(solution)/shard_map/ppermute | solution.py:212
  36.0 0.0 collective-permute-done.10.come
  36.0 1.1 %collective-permute-start.13 = (bf16[96,256]{1,0:T(8,128)(2,1)S(1)}, bf16[96,256]{1,0:T(8,128)(2,1)S(1)}, u32[]{:S(2)}, u32[]{:S(2)}) collective-permute-start(bf16[96,256]{1,0:T(8,128)(2,1)S(1)} %get-tuple-element.104), channel_id=1, source_target_pairs={{0,16},{8,24},{16,0},{24,8},{1,17},{9,25},{17,1},{25,9},{2,18},{10... | collective-permute-start | bytes 147464 | tf_op jit(solution)/shard_map/ppermute | solution.py:212
  37.2 0.1 collective-permute-done.16.refs_2_
  37.3 2.9 %collective-permute-start.14 = (bf16[96,256]{1,0:T(8,128)(2,1)S(1)}, bf16[96,256]{1,0:T(8,128)(2,1)S(1)}, u32[]{:S(2)}, u32[]{:S(2)}) collective-permute-start(bf16[96,256]{1,0:T(8,128)(2,1)S(1)} %get-tuple-element.105), channel_id=1, source_target_pairs={{0,24},{8,0},{16,8},{24,16},{1,25},{9,1},{17,9},{25,17},{2,26},{10... | collective-permute-start | bytes 147464 | tf_op jit(solution)/shard_map/ppermute | solution.py:212
  40.3 0.0 collective-permute-done.17.refs_3_
  40.3 1.6 %collective-permute-start.11 = (bf16[256,256]{1,0:T(8,128)(2,1)S(1)}, bf16[256,256]{1,0:T(8,128)(2,1)S(1)}, u32[]{:S(2)}, u32[]{:S(2)}) collective-permute-start(bf16[256,256]{1,0:T(8,128)(2,1)S(1)} %get-tuple-element.100), channel_id=1, source_target_pairs={{0,4},{2,6},{4,0},{6,2},{1,5},{3,7},{5,1},{7,3},{8,12},{10,14},{12... | collective-permute-start | bytes 393224 | tf_op jit(solution)/shard_map/ppermute | solution.py:216
  41.9 0.0 collective-permute-done.15.refs_1_
  41.9 0.2 collective-permute-start.21
  42.2 0.0 collective-permute-done.12.refs_1_
  42.2 0.4 collective-permute-start.20
  42.6 0.0 collective-permute-done.13.refs_2_
  42.6 1.7 %collective-permute-start.18 = (bf16[32,1024]{1,0:T(8,128)(2,1)S(1)}, bf16[32,1024]{1,0:T(8,128)(2,1)S(1)}, u32[]{:S(2)}, u32[]{:S(2)}) collective-permute-start(bf16[32,1024]{1,0:T(8,128)(2,1)S(1)} %block_sum.1.refs_0_), channel_id=1, source_target_pairs={{0,8},{8,16},{16,24},{24,0},{1,9},{9,17},{17,25},{25,1},{2,10},{10... | collective-permute-start | bytes 196616 | tf_op jit(solution)/shard_map/ppermute | solution.py:212
  44.3 0.0 collective-permute-done.14.refs_3_
  44.3 0.1 collective-permute-start.19
  44.4 1.3 %grad_out.1 = bf16[3,256,256]{2,1,0:T(8,128)(2,1)} custom-call(f32[256,256]{1,0:T(8,128)S(1)} %get-tuple-element.96.query_part, f32[6,256,256]{2,1,0:T(8,128)S(1)} %get-tuple-element.101.pair_w, f32[3,16,256]{2,1,0:T(8,128)S(1)} %get-tuple-element.106.later, bf16[96,256]{1,0:T(8,128)(2,1)S(1)} %get-tuple-element.102.refs_0_, ...), custom_call_target="tpu_custom_call" | custom-call | bytes 2473984 | tf_op jit(solution)/shard_map/grad_out/pallas_call | solution.py:234
  45.7 0.0 collective-permute-done.19.refs_9_
  45.7 0.5 collective-permute-start.22
  46.2 3.2 %collective-permute-done.18.refs_1_ = bf16[32,1024]{1,0:T(8,128)(2,1)S(1)} collective-permute-done((bf16[32,1024]{1,0:T(8,128)(2,1)S(1)}, bf16[32,1024]{1,0:T(8,128)(2,1)S(1)}, u32[]{:S(2)}, u32[]{:S(2)}) %collective-permute-start.18) | collective-permute-done | bytes 65568 | tf_op jit(solution)/shard_map/ppermute | solution.py:212
  49.4 0.0 collective-permute-done.20.refs_2_
  49.5 0.5 collective-permute-start.24
  50.0 0.1 collective-permute-start.23
  50.0 0.7 %mixed_sum.1 = bf16[256,256]{1,0:T(8,128)(2,1)} custom-call(f32[256,256]{1,0:T(8,128)S(1)} %get-tuple-element.99.own, bf16[256,256]{1,0:T(8,128)(2,1)S(1)} %collective-permute-done.11.come), custom_call_target="tpu_custom_call" | custom-call | bytes 524288 | tf_op jit(solution)/shard_map/mixed_sum/pallas_call | solution.py:234
  50.7 0.1 collective-permute-done.24.refs_6_
  50.9 0.4 collective-permute-done.23.refs_5_
  51.2 1.1 %final.1 = (f32[256,1024]{1,0:T(8,128)}, f32[3,3,256]{2,1,0:T(4,128)}, f32[16,256]{1,0:T(8,128)}) custom-call(bf16[32,1024]{1,0:T(8,128)(2,1)S(1)} %block_sum.1.refs_0_, bf16[32,1024]{1,0:T(8,128)(2,1)S(1)} %collective-permute-done.18.refs_1_, bf16[32,1024]{1,0:T(8,128)(2,1)S(1)} %collective-permute-done.20.refs_2_, ...), custom_call_target="tpu_custom_call" | custom-call | bytes 1664000 | tf_op jit(solution)/shard_map/final/pallas_call | solution.py:234
  (13 shorter events, 0.1 us)
Async XLA Ops:
  0.6 12.0 %collective-permute-start = (bf16[256,256]{1,0:T(8,128)(2,1)}, bf16[256,256]{1,0:T(8,128)(2,1)S(1)}, u32[]{:S(2)}, u32[]{:S(2)}) collective-permute-start(bf16[256,256]{1,0:T(8,128)(2,1)} %bitcast.8), channel_id=1, source_target_pairs={{0,2},{2,0},{4,6},{6,4},{1,3},{3,1},{5,7},{7,5},{8,10},{10,8},{12,... | collective-permute-start | bytes 393224 | tf_op jit(solution)/shard_map/ppermute | solution.py:216
  5.5 10.4 %collective-permute-start.1 = (bf16[160,256]{1,0:T(8,128)(2,1)}, bf16[160,256]{1,0:T(8,128)(2,1)S(1)}, u32[]{:S(2)}, u32[]{:S(2)}) collective-permute-start(bf16[160,256]{1,0:T(8,128)(2,1)} %get-tuple-element.63), channel_id=1, source_target_pairs={{0,8},{8,16},{16,24},{24,0},{1,9},{9,17},{17,25},{25,1},{2,10},{10... | collective-permute-start | bytes 245768 | tf_op jit(solution)/shard_map/ppermute | solution.py:212
  7.1 8.8 %collective-permute-start.2 = (bf16[144,256]{1,0:T(8,128)(2,1)}, bf16[144,256]{1,0:T(8,128)(2,1)S(1)}, u32[]{:S(2)}, u32[]{:S(2)}) collective-permute-start(bf16[144,256]{1,0:T(8,128)(2,1)} %get-tuple-element.66), channel_id=1, source_target_pairs={{0,16},{8,24},{16,0},{24,8},{1,17},{9,25},{17,1},{25,9},{2,18},{10... | collective-permute-start | bytes 221192 | tf_op jit(solution)/shard_map/ppermute | solution.py:212
  9.7 6.2 %collective-permute-start.3 = (bf16[144,256]{1,0:T(8,128)(2,1)}, bf16[144,256]{1,0:T(8,128)(2,1)S(1)}, u32[]{:S(2)}, u32[]{:S(2)}) collective-permute-start(bf16[144,256]{1,0:T(8,128)(2,1)} %get-tuple-element.67), channel_id=1, source_target_pairs={{0,24},{8,0},{16,8},{24,16},{1,25},{9,1},{17,9},{25,17},{2,26},{10... | collective-permute-start | bytes 221192 | tf_op jit(solution)/shard_map/ppermute | solution.py:212
  11.1 6.4 %collective-permute-start.4 = (bf16[256,256]{1,0:T(8,128)(2,1)}, bf16[256,256]{1,0:T(8,128)(2,1)S(1)}, u32[]{:S(2)}, u32[]{:S(2)}) collective-permute-start(bf16[256,256]{1,0:T(8,128)(2,1)} %bitcast.9), channel_id=1, source_target_pairs={{0,4},{2,6},{4,0},{6,2},{1,5},{3,7},{5,1},{7,3},{8,12},{10,14},{12... | collective-permute-start | bytes 393224 | tf_op jit(solution)/shard_map/ppermute | solution.py:216
  12.6 5.6 %collective-permute-start.5 = (bf16[256,256]{1,0:T(8,128)(2,1)S(1)}, bf16[256,256]{1,0:T(8,128)(2,1)S(1)}, u32[]{:S(2)}, u32[]{:S(2)}) collective-permute-start(bf16[256,256]{1,0:T(8,128)(2,1)S(1)} %collective-permute-done.rest_1_), channel_id=1, source_target_pairs={{0,4},{2,6},{4,0},{6,2},{1,5},{3,7},{5,1},{7,3},{8,12},{10,14},{12... | collective-permute-start | bytes 393224 | tf_op jit(solution)/shard_map/ppermute | solution.py:216
  13.1 1.0 %copy-start.1 = (bf16[3,1,256,256]{3,2,1,0:T(8,128)(2,1)S(1)}, bf16[3,1,256,256]{3,2,1,0:T(8,128)(2,1)}, u32[]{:S(2)}) copy-start(bf16[3,1,256,256]{3,2,1,0:T(8,128)(2,1)} %param.6) | copy-start | bytes 1179652
  14.1 0.9 %copy-start.3 = (bf16[144,256]{1,0:T(8,128)(2,1)S(1)}, bf16[144,256]{1,0:T(8,128)(2,1)}, u32[]{:S(2)}) copy-start(bf16[144,256]{1,0:T(8,128)(2,1)} %get-tuple-element.61.chunk) | copy-start | bytes 221188
  15.0 0.7 %copy-start.4 = (f32[3,3,256]{2,1,0:T(4,128)S(1)}, f32[3,3,256]{2,1,0:T(4,128)}, u32[]{:S(2)}) copy-start(f32[3,3,256]{2,1,0:T(4,128)} %short_filter) | copy-start | bytes 27652
  15.9 2.3 %copy-start = (bf16[256,1024]{1,0:T(8,128)(2,1)S(1)}, bf16[256,1024]{1,0:T(8,128)(2,1)}, u32[]{:S(2)}) copy-start(bf16[256,1024]{1,0:T(8,128)(2,1)} %weights.3) | copy-start | bytes 1572868
  16.0 2.3 %copy-start.2 = (bf16[1,256,256]{2,1,0:T(8,128)(2,1)S(1)}, bf16[1,256,256]{2,1,0:T(8,128)(2,1)}, u32[]{:S(2)}) copy-start(bf16[1,256,256]{2,1,0:T(8,128)(2,1)} %param.11) | copy-start | bytes 393220
  18.6 6.2 %collective-permute-start.6 = (bf16[128,256]{1,0:T(8,128)(2,1)S(1)}, bf16[128,256]{1,0:T(8,128)(2,1)S(1)}, u32[]{:S(2)}, u32[]{:S(2)}) collective-permute-start(bf16[128,256]{1,0:T(8,128)(2,1)S(1)} %get-tuple-element.79), channel_id=1, source_target_pairs={{0,8},{8,16},{16,24},{24,0},{1,9},{9,17},{17,25},{25,1},{2,10},{10... | collective-permute-start | bytes 196616 | tf_op jit(solution)/shard_map/ppermute | solution.py:212
  19.4 6.6 %collective-permute-start.7 = (bf16[128,256]{1,0:T(8,128)(2,1)S(1)}, bf16[128,256]{1,0:T(8,128)(2,1)S(1)}, u32[]{:S(2)}, u32[]{:S(2)}) collective-permute-start(bf16[128,256]{1,0:T(8,128)(2,1)S(1)} %get-tuple-element.80), channel_id=1, source_target_pairs={{0,16},{8,24},{16,0},{24,8},{1,17},{9,25},{17,1},{25,9},{2,18},{10... | collective-permute-start | bytes 196616 | tf_op jit(solution)/shard_map/ppermute | solution.py:212
  20.7 5.3 %collective-permute-start.8 = (bf16[128,256]{1,0:T(8,128)(2,1)S(1)}, bf16[128,256]{1,0:T(8,128)(2,1)S(1)}, u32[]{:S(2)}, u32[]{:S(2)}) collective-permute-start(bf16[128,256]{1,0:T(8,128)(2,1)S(1)} %get-tuple-element.81), channel_id=1, source_target_pairs={{0,24},{8,0},{16,8},{24,16},{1,25},{9,1},{17,9},{25,17},{2,26},{10... | collective-permute-start | bytes 196616 | tf_op jit(solution)/shard_map/ppermute | solution.py:212
  26.4 2.0 %collective-permute-start.9 = (f32[128,1024]{1,0:T(8,128)S(1)}, f32[128,1024]{1,0:T(8,128)S(1)}, u32[]{:S(2)}, u32[]{:S(2)}) collective-permute-start(f32[128,1024]{1,0:T(8,128)S(1)} %get-tuple-element.89), channel_id=1, source_target_pairs={{0,1},{1,0},{2,3},{3,2},{4,5},{5,4},{6,7},{7,6},{8,9},{9,8},{10,11... | collective-permute-start | bytes 1572872 | tf_op jit(solution)/shard_map/ppermute | solution.py:212
  26.9 9.2 %collective-permute-start.10 = (bf16[512,256]{1,0:T(8,128)(2,1)S(1)}, bf16[512,256]{1,0:T(8,128)(2,1)S(1)}, u32[]{:S(2)}, u32[]{:S(2)}) collective-permute-start(bf16[512,256]{1,0:T(8,128)(2,1)S(1)} %get-tuple-element.98), channel_id=1, source_target_pairs={{0,2},{2,0},{4,6},{6,4},{1,3},{3,1},{5,7},{7,5},{8,10},{10,8},{12,... | collective-permute-start | bytes 786440 | tf_op jit(solution)/shard_map/ppermute | solution.py:216
  28.4 13.5 %collective-permute-start.15 = (bf16[32,1024]{1,0:T(8,128)(2,1)S(1)}, bf16[32,1024]{1,0:T(8,128)(2,1)S(1)}, u32[]{:S(2)}, u32[]{:S(2)}) collective-permute-start(bf16[32,1024]{1,0:T(8,128)(2,1)S(1)} %get-tuple-element.90), channel_id=1, source_target_pairs={{0,8},{8,16},{16,24},{24,0},{1,9},{9,17},{17,25},{25,1},{2,10},{10... | collective-permute-start | bytes 196616 | tf_op jit(solution)/shard_map/ppermute | solution.py:212
  29.9 7.4 %collective-permute-start.16 = (bf16[32,1024]{1,0:T(8,128)(2,1)S(1)}, bf16[32,1024]{1,0:T(8,128)(2,1)S(1)}, u32[]{:S(2)}, u32[]{:S(2)}) collective-permute-start(bf16[32,1024]{1,0:T(8,128)(2,1)S(1)} %get-tuple-element.108), channel_id=1, source_target_pairs={{0,16},{8,24},{16,0},{24,8},{1,17},{9,25},{17,1},{25,9},{2,18},{10... | collective-permute-start | bytes 196616 | tf_op jit(solution)/shard_map/ppermute | solution.py:212
  31.7 8.6 %collective-permute-start.17 = (bf16[32,1024]{1,0:T(8,128)(2,1)S(1)}, bf16[32,1024]{1,0:T(8,128)(2,1)S(1)}, u32[]{:S(2)}, u32[]{:S(2)}) collective-permute-start(bf16[32,1024]{1,0:T(8,128)(2,1)S(1)} %get-tuple-element.109), channel_id=1, source_target_pairs={{0,24},{8,0},{16,8},{24,16},{1,25},{9,1},{17,9},{25,17},{2,26},{10... | collective-permute-start | bytes 196616 | tf_op jit(solution)/shard_map/ppermute | solution.py:212
  34.6 7.6 %collective-permute-start.12 = (bf16[96,256]{1,0:T(8,128)(2,1)S(1)}, bf16[96,256]{1,0:T(8,128)(2,1)S(1)}, u32[]{:S(2)}, u32[]{:S(2)}) collective-permute-start(bf16[96,256]{1,0:T(8,128)(2,1)S(1)} %get-tuple-element.103), channel_id=1, source_target_pairs={{0,8},{8,16},{16,24},{24,0},{1,9},{9,17},{17,25},{25,1},{2,10},{10... | collective-permute-start | bytes 147464 | tf_op jit(solution)/shard_map/ppermute | solution.py:212
  36.0 6.5 %collective-permute-start.13 = (bf16[96,256]{1,0:T(8,128)(2,1)S(1)}, bf16[96,256]{1,0:T(8,128)(2,1)S(1)}, u32[]{:S(2)}, u32[]{:S(2)}) collective-permute-start(bf16[96,256]{1,0:T(8,128)(2,1)S(1)} %get-tuple-element.104), channel_id=1, source_target_pairs={{0,16},{8,24},{16,0},{24,8},{1,17},{9,25},{17,1},{25,9},{2,18},{10... | collective-permute-start | bytes 147464 | tf_op jit(solution)/shard_map/ppermute | solution.py:212
  37.3 7.0 %collective-permute-start.14 = (bf16[96,256]{1,0:T(8,128)(2,1)S(1)}, bf16[96,256]{1,0:T(8,128)(2,1)S(1)}, u32[]{:S(2)}, u32[]{:S(2)}) collective-permute-start(bf16[96,256]{1,0:T(8,128)(2,1)S(1)} %get-tuple-element.105), channel_id=1, source_target_pairs={{0,24},{8,0},{16,8},{24,16},{1,25},{9,1},{17,9},{25,17},{2,26},{10... | collective-permute-start | bytes 147464 | tf_op jit(solution)/shard_map/ppermute | solution.py:212
  40.3 5.9 %collective-permute-start.11 = (bf16[256,256]{1,0:T(8,128)(2,1)S(1)}, bf16[256,256]{1,0:T(8,128)(2,1)S(1)}, u32[]{:S(2)}, u32[]{:S(2)}) collective-permute-start(bf16[256,256]{1,0:T(8,128)(2,1)S(1)} %get-tuple-element.100), channel_id=1, source_target_pairs={{0,4},{2,6},{4,0},{6,2},{1,5},{3,7},{5,1},{7,3},{8,12},{10,14},{12... | collective-permute-start | bytes 393224 | tf_op jit(solution)/shard_map/ppermute | solution.py:216
  41.9 7.5 %collective-permute-start.21 = (bf16[32,1024]{1,0:T(8,128)(2,1)S(1)}, bf16[32,1024]{1,0:T(8,128)(2,1)S(1)}, u32[]{:S(2)}, u32[]{:S(2)}) collective-permute-start(bf16[32,1024]{1,0:T(8,128)(2,1)S(1)} %block_sum.1.refs_0_), channel_id=1, source_target_pairs={{0,24},{8,0},{16,8},{24,16},{1,25},{9,1},{17,9},{25,17},{2,26},{10... | collective-permute-start | bytes 196616 | tf_op jit(solution)/shard_map/ppermute | solution.py:212
  42.2 7.3 %collective-permute-start.20 = (bf16[32,1024]{1,0:T(8,128)(2,1)S(1)}, bf16[32,1024]{1,0:T(8,128)(2,1)S(1)}, u32[]{:S(2)}, u32[]{:S(2)}) collective-permute-start(bf16[32,1024]{1,0:T(8,128)(2,1)S(1)} %block_sum.1.refs_0_), channel_id=1, source_target_pairs={{0,16},{8,24},{16,0},{24,8},{1,17},{9,25},{17,1},{25,9},{2,18},{10... | collective-permute-start | bytes 196616 | tf_op jit(solution)/shard_map/ppermute | solution.py:212
  42.6 6.9 %collective-permute-start.18 = (bf16[32,1024]{1,0:T(8,128)(2,1)S(1)}, bf16[32,1024]{1,0:T(8,128)(2,1)S(1)}, u32[]{:S(2)}, u32[]{:S(2)}) collective-permute-start(bf16[32,1024]{1,0:T(8,128)(2,1)S(1)} %block_sum.1.refs_0_), channel_id=1, source_target_pairs={{0,8},{8,16},{16,24},{24,0},{1,9},{9,17},{17,25},{25,1},{2,10},{10... | collective-permute-start | bytes 196616 | tf_op jit(solution)/shard_map/ppermute | solution.py:212
  44.3 1.4 %collective-permute-start.19 = (bf16[16,1024]{1,0:T(8,128)(2,1)S(1)}, bf16[16,1024]{1,0:T(8,128)(2,1)S(1)}, u32[]{:S(2)}, u32[]{:S(2)}) collective-permute-start(bf16[16,1024]{1,0:T(8,128)(2,1)S(1)} %get-tuple-element.110.refs_8_), channel_id=1, source_target_pairs={{0,1},{1,0},{2,3},{3,2},{4,5},{5,4},{6,7},{7,6},{8,9},{9,8},{10,11... | collective-permute-start | bytes 98312 | tf_op jit(solution)/shard_map/ppermute | solution.py:212
  45.7 5.0 %collective-permute-start.22 = (bf16[32,1024]{1,0:T(8,128)(2,1)S(1)}, bf16[32,1024]{1,0:T(8,128)(2,1)S(1)}, u32[]{:S(2)}, u32[]{:S(2)}) collective-permute-start(bf16[32,1024]{1,0:T(8,128)(2,1)S(1)} %block_sum.1.refs_0_), channel_id=1, source_target_pairs={{0,1},{1,0},{2,3},{3,2},{4,5},{5,4},{6,7},{7,6},{8,9},{9,8},{10,11... | collective-permute-start | bytes 196616 | tf_op jit(solution)/shard_map/ppermute | solution.py:212
  49.4 1.3 %collective-permute-start.25 = (bf16[32,1024]{1,0:T(8,128)(2,1)S(1)}, bf16[32,1024]{1,0:T(8,128)(2,1)S(1)}, u32[]{:S(2)}, u32[]{:S(2)}) collective-permute-start(bf16[32,1024]{1,0:T(8,128)(2,1)S(1)} %collective-permute-done.21.refs_3_), channel_id=1, source_target_pairs={{0,1},{1,0},{2,3},{3,2},{4,5},{5,4},{6,7},{7,6},{8,9},{9,8},{10,11... | collective-permute-start | bytes 196616 | tf_op jit(solution)/shard_map/ppermute | solution.py:212
  49.5 1.4 %collective-permute-start.24 = (bf16[32,1024]{1,0:T(8,128)(2,1)S(1)}, bf16[32,1024]{1,0:T(8,128)(2,1)S(1)}, u32[]{:S(2)}, u32[]{:S(2)}) collective-permute-start(bf16[32,1024]{1,0:T(8,128)(2,1)S(1)} %collective-permute-done.20.refs_2_), channel_id=1, source_target_pairs={{0,1},{1,0},{2,3},{3,2},{4,5},{5,4},{6,7},{7,6},{8,9},{9,8},{10,11... | collective-permute-start | bytes 196616 | tf_op jit(solution)/shard_map/ppermute | solution.py:212
  50.0 1.3 %collective-permute-start.23 = (bf16[32,1024]{1,0:T(8,128)(2,1)S(1)}, bf16[32,1024]{1,0:T(8,128)(2,1)S(1)}, u32[]{:S(2)}, u32[]{:S(2)}) collective-permute-start(bf16[32,1024]{1,0:T(8,128)(2,1)S(1)} %collective-permute-done.18.refs_1_), channel_id=1, source_target_pairs={{0,1},{1,0},{2,3},{3,2},{4,5},{5,4},{6,7},{7,6},{8,9},{9,8},{10,11... | collective-permute-start | bytes 196616 | tf_op jit(solution)/shard_map/ppermute | solution.py:212

commit v5 on v4

--- a/solution.py
+++ b/solution.py
@@ -246,36 +246,44 @@
     return pl.ds(pl.multiple_of(index * size, size), size)
 
 
-def pack_kernel(devices, reach, *refs):
-    sources, refs = refs[:3], refs[3:]
+def pack_kernel(devices, reach, projected, filter_source, segment_source, *refs):
     outs, refs = refs[:devices], refs[devices:]
-    held, (turned, small, tail, sems) = refs[:3], refs[3:]
+    pair, query, filters, segments, turned, small, tail, sems = refs
+    _, rows, _ = projected.shape
+    sources = (
+        (projected.at[1], pair.at[0]),
+        (projected.at[2], pair.at[1]),
+        (projected.at[0, pl.ds(rows - 16, 16)], query),
+        (filter_source, filters),
+        (segment_source, segments),
+    )
     copies = [
-        pltpu.make_async_copy(sources[n], held[n], sems.at[n]) for n in range(len(sources))
+        pltpu.make_async_copy(source, held, sems.at[n])
+        for n, (source, held) in enumerate(sources)
     ]
     for copy in copies:
         copy.start()
-    projected, filters, segments = held
     me = lax.axis_index("ctx")
-    stacked, rows, width = projected.shape
+    width = pair.shape[2]
     chunk = width // devices
     count = filters.shape[0]
     groups = count // devices
-    for copy in copies:
+    body = pair.shape[0] * chunk
+    small[...] = jnp.zeros_like(small)
+    tail[...] = jnp.zeros_like(tail)
+    for i in range(pair.shape[0]):
+        copies[i].wait()
+        turned[i] = pair[i].T
+    for copy in copies[2:]:
         copy.wait()
-    for i in range(1, stacked):
-        turned[i - 1] = projected[i].T
-    tail[...] = jnp.zeros_like(tail)
-    for i in range(stacked):
-        tail[i * reach : (i + 1) * reach] = projected[i, rows - reach :].astype(f32)
-    small[...] = jnp.zeros_like(small)
+    for i, last in enumerate((query[...], pair[0, rows - 16 :], pair[1, rows - 16 :])):
+        tail[i * reach : (i + 1) * reach] = last.astype(f32)[16 - reach :]
     seg = segments[...]
     small[2 * groups : 2 * groups + 1] = (seg >> 8).astype(f32)
     small[2 * groups + 1 : 2 * groups + 2] = (seg & 255).astype(f32)
-    body = (stacked - 1) * chunk
     for s in range(devices):
         to = lax.rem(me + s, devices)
-        for i in range(stacked - 1):
+        for i in range(pair.shape[0]):
             outs[s][i * chunk : (i + 1) * chunk] = turned[i, block_at(to, chunk)]
         lines = pltpu.roll(filters[...], lax.rem(count - to * groups, count), 0)[0:groups]
         high = lines.astype(bf16).astype(f32)
@@ -730,12 +738,15 @@
         ],
         inputs,
         "pack",
-        [pltpu.VMEM(a.shape, a.dtype) for a in inputs]
-        + [
+        [
+            pltpu.VMEM((stacked - 1, length, width), bf16),
+            pltpu.VMEM((16, width), bf16),
+            pltpu.VMEM(long_filter.shape, f32),
+            pltpu.VMEM(segment_ids.shape, jnp.int32),
             pltpu.VMEM((stacked - 1, width, length), bf16),
             pltpu.VMEM((room, length), f32),
             pltpu.VMEM((room, width), f32),
-            pltpu.SemaphoreType.DMA((len(inputs),)),
+            pltpu.SemaphoreType.DMA((5,)),
         ],
         whole=True,
     )
@@ -767,7 +778,7 @@
             pltpu.VMEM((chunk, span), bf16),
             pltpu.VMEM((groups, length, span), bf16),
         ],
-        flops=9 * 100000000,
+        flops=900_000_000,
     )
     longs, kept = outs[:devices], outs[devices:]
     seg = kept[2]
@@ -854,7 +865,7 @@
         back,
         "small_sum",
         [pltpu.VMEM((devices, 2 * room, width), f32)],
-        flops=2000 * 1000000,
+        flops=2_000_000_000,
     )
     (grad_projected,) = on_core(
         functools.partial(grad_out_kernel, devices, taps),

time: 52.5 us -> 52.5 us (level)
  no operation moved by 1% of the time
where the time goes in v5:
time: 52.5 us; the launch traced here: 52.3 us
  starting transfers between devices  29.6 us (56%)
  Pallas kernels  11.6 us (22%)
  waiting for transfers between devices  7.62 us (15%)
  local copies, waits for them, and re-layouts  2.6 us (5%)
  between operations  0.82 us (2%)
    ppermute x21, starting transfers between devices, rotate(): lax.ppermute(value, axis, [(i, (i + steps) % count) for i in range(count)])  22.4 us
    pallas_call x15, Pallas kernels, on_core(): pl.pallas_call(kernel, out_shape=[jax.ShapeDtypeStruct(shape, kind) for s...  11.6 us
    ppermute x5, starting transfers between devices, swap(): lax.ppermute(value, axis, [(i, i ^ bits) for i in range(lax.axis_size(axi...  7.22 us
    ppermute x21, waiting for transfers between devices, rotate(): lax.ppermute(value, axis, [(i, (i + steps) % count) for i in range(count)])  6.83 us
    unnamed x10, local copies, waits for them, and re-layouts  2.6 us
  transfers between devices with their start and end apart: 26, of which 8 were waited for; matrix products, arithmetic and copies ran while one was open for 0% of the time, Pallas kernels for 19%

profile of v5, /device:TPU:0, one launch (start us, length us, event | category | flops | bytes accessed | tf_op | source)
XLA Modules:
  0.0 52.3 jit_solution(18199605138274801472)
XLA Ops:
  0.6 3.0 %collective-permute-start = (bf16[256,256]{1,0:T(8,128)(2,1)}, bf16[256,256]{1,0:T(8,128)(2,1)S(1)}, u32[]{:S(2)}, u32[]{:S(2)}) collective-permute-start(bf16[256,256]{1,0:T(8,128)(2,1)} %bitcast.8), channel_id=1, source_target_pairs={{0,2},{2,0},{4,6},{6,4},{1,3},{3,1},{5,7},{7,5},{8,10},{10,8},{12,... | collective-permute-start | bytes 393224 | tf_op jit(solution)/shard_map/ppermute | solution.py:216
  3.6 1.9 %pack.1 = (bf16[144,256]{1,0:T(8,128)(2,1)}, bf16[160,256]{1,0:T(8,128)(2,1)}, bf16[144,256]{1,0:T(8,128)(2,1)}, bf16[144,256]{1,0:T(8,128)(2,1)}) custom-call(bf16[3,256,256]{2,1,0:T(8,128)(2,1)} %bitcast.6, f32[16,256]{1,0:T(8,128)} %filter_source.1, s32[1,256]{1,0:T(1,128)} %segment_source.1), custom_call_target="tpu_custom_call" | custom-call | bytes 713728 | tf_op jit(solution)/shard_map/pack/pallas_call | solution.py:234
  5.5 1.6 %collective-permute-start.1 = (bf16[160,256]{1,0:T(8,128)(2,1)}, bf16[160,256]{1,0:T(8,128)(2,1)S(1)}, u32[]{:S(2)}, u32[]{:S(2)}) collective-permute-start(bf16[160,256]{1,0:T(8,128)(2,1)} %get-tuple-element.63), channel_id=1, source_target_pairs={{0,8},{8,16},{16,24},{24,0},{1,9},{9,17},{17,25},{25,1},{2,10},{10... | collective-permute-start | bytes 245768 | tf_op jit(solution)/shard_map/ppermute | solution.py:212
  7.1 2.6 %collective-permute-start.2 = (bf16[144,256]{1,0:T(8,128)(2,1)}, bf16[144,256]{1,0:T(8,128)(2,1)S(1)}, u32[]{:S(2)}, u32[]{:S(2)}) collective-permute-start(bf16[144,256]{1,0:T(8,128)(2,1)} %get-tuple-element.66), channel_id=1, source_target_pairs={{0,16},{8,24},{16,0},{24,8},{1,17},{9,25},{17,1},{25,9},{2,18},{10... | collective-permute-start | bytes 221192 | tf_op jit(solution)/shard_map/ppermute | solution.py:212
  9.7 1.3 %collective-permute-start.3 = (bf16[144,256]{1,0:T(8,128)(2,1)}, bf16[144,256]{1,0:T(8,128)(2,1)S(1)}, u32[]{:S(2)}, u32[]{:S(2)}) collective-permute-start(bf16[144,256]{1,0:T(8,128)(2,1)} %get-tuple-element.67), channel_id=1, source_target_pairs={{0,24},{8,0},{16,8},{24,16},{1,25},{9,1},{17,9},{25,17},{2,26},{10... | collective-permute-start | bytes 221192 | tf_op jit(solution)/shard_map/ppermute | solution.py:212
  11.1 1.5 %collective-permute-start.4 = (bf16[256,256]{1,0:T(8,128)(2,1)}, bf16[256,256]{1,0:T(8,128)(2,1)S(1)}, u32[]{:S(2)}, u32[]{:S(2)}) collective-permute-start(bf16[256,256]{1,0:T(8,128)(2,1)} %bitcast.9), channel_id=1, source_target_pairs={{0,4},{2,6},{4,0},{6,2},{1,5},{3,7},{5,1},{7,3},{8,12},{10,14},{12... | collective-permute-start | bytes 393224 | tf_op jit(solution)/shard_map/ppermute | solution.py:216
  12.6 0.0 collective-permute-done.rest_1_
  12.6 0.5 collective-permute-start.5
  13.1 1.0 %copy-done.1 = bf16[3,1,256,256]{3,2,1,0:T(8,128)(2,1)S(1)} copy-done((bf16[3,1,256,256]{3,2,1,0:T(8,128)(2,1)S(1)}, bf16[3,1,256,256]{3,2,1,0:T(8,128)(2,1)}, u32[]{:S(2)}) %copy-start.1) | copy-done | bytes 393240
  14.1 0.9 %copy-done.3 = bf16[144,256]{1,0:T(8,128)(2,1)S(1)} copy-done((bf16[144,256]{1,0:T(8,128)(2,1)S(1)}, bf16[144,256]{1,0:T(8,128)(2,1)}, u32[]{:S(2)}) %copy-start.3) | copy-done | bytes 73752
  15.0 0.7 %copy-done.4 = f32[3,3,256]{2,1,0:T(4,128)S(1)} copy-done((f32[3,3,256]{2,1,0:T(4,128)S(1)}, f32[3,3,256]{2,1,0:T(4,128)}, u32[]{:S(2)}) %copy-start.4) | copy-done | bytes 9240
  15.7 0.2 prepare.1
  15.9 0.0 collective-permute-done.2.rest_2_
  15.9 0.0 collective-permute-done.3.rest_3_
  15.9 0.0 collective-permute-done.1.rest_1_.previous
  15.9 0.0 copy-start
  15.9 0.0 copy-start.2
  16.0 1.4 %conv.1 = (bf16[64,256]{1,0:T(8,128)(2,1)S(1)}, bf16[64,256]{1,0:T(8,128)(2,1)S(1)}, bf16[64,256]{1,0:T(8,128)(2,1)S(1)}, bf16[64,256]{1,0:T(8,128)(2,1)S(1)}, f...) custom-call(f32[256,16]{1,0:T(8,128)S(1)} %get-tuple-element.64.colu, ...), custom_call_target="tpu_custom_call" | custom-call | flops 900000000 | bytes 3366912 | tf_op jit(solution)/shard_map/conv/pallas_call | solution.py:234
  17.4 0.8 %collective-permute-done.5.rest_3_ = bf16[256,256]{1,0:T(8,128)(2,1)S(1)} collective-permute-done((bf16[256,256]{1,0:T(8,128)(2,1)S(1)}, bf16[256,256]{1,0:T(8,128)(2,1)S(1)}, u32[]{:S(2)}, u32[]{:S(2)}) %collective-permute-start.5) | collective-permute-done | bytes 131104 | tf_op jit(solution)/shard_map/ppermute | solution.py:216
  18.2 0.4 grad_y.1
  18.6 0.7 %collective-permute-start.6 = (bf16[128,256]{1,0:T(8,128)(2,1)S(1)}, bf16[128,256]{1,0:T(8,128)(2,1)S(1)}, u32[]{:S(2)}, u32[]{:S(2)}) collective-permute-start(bf16[128,256]{1,0:T(8,128)(2,1)S(1)} %get-tuple-element.79), channel_id=1, source_target_pairs={{0,8},{8,16},{16,24},{24,0},{1,9},{9,17},{17,25},{25,1},{2,10},{10... | collective-permute-start | bytes 196616 | tf_op jit(solution)/shard_map/ppermute | solution.py:212
  19.4 1.3 %collective-permute-start.7 = (bf16[128,256]{1,0:T(8,128)(2,1)S(1)}, bf16[128,256]{1,0:T(8,128)(2,1)S(1)}, u32[]{:S(2)}, u32[]{:S(2)}) collective-permute-start(bf16[128,256]{1,0:T(8,128)(2,1)S(1)} %get-tuple-element.80), channel_id=1, source_target_pairs={{0,16},{8,24},{16,0},{24,8},{1,17},{9,25},{17,1},{25,9},{2,18},{10... | collective-permute-start | bytes 196616 | tf_op jit(solution)/shard_map/ppermute | solution.py:212
  20.7 1.8 %collective-permute-start.8 = (bf16[128,256]{1,0:T(8,128)(2,1)S(1)}, bf16[128,256]{1,0:T(8,128)(2,1)S(1)}, u32[]{:S(2)}, u32[]{:S(2)}) collective-permute-start(bf16[128,256]{1,0:T(8,128)(2,1)S(1)} %get-tuple-element.81), channel_id=1, source_target_pairs={{0,24},{8,0},{16,8},{24,16},{1,25},{9,1},{17,9},{25,17},{2,26},{10... | collective-permute-start | bytes 196616 | tf_op jit(solution)/shard_map/ppermute | solution.py:212
  22.5 1.4 %ready.1 = (f32[6,256,256]{2,1,0:T(8,128)S(1)}, f32[3,256,256]{2,1,0:T(8,128)S(1)}, f32[2,256,256]{2,1,0:T(8,128)S(1)}, bf16[4,128,128]{2,1,0:T(8,128)(2,1)S(1)}...) custom-call(bf16[3,256,256]{2,1,0:T(8,128)(2,1)S(1)} %get-tuple-element.62.turned, ...), custom_call_target="tpu_custom_call" | custom-call | bytes 6291456 | tf_op jit(solution)/shard_map/ready/pallas_call | solution.py:234
  23.9 0.9 %collective-permute-done.6.rest_5_.rest_1_ = bf16[128,256]{1,0:T(8,128)(2,1)S(1)} collective-permute-done((bf16[128,256]{1,0:T(8,128)(2,1)S(1)}, bf16[128,256]{1,0:T(8,128)(2,1)S(1)}, u32[]{:S(2)}, u32[]{:S(2)}) %collective-permute-start.6) | collective-permute-done | bytes 65568 | tf_op jit(solution)/shard_map/ppermute | solution.py:212
  24.9 1.1 %collective-permute-done.7.rest_6_.rest_2_ = bf16[128,256]{1,0:T(8,128)(2,1)S(1)} collective-permute-done((bf16[128,256]{1,0:T(8,128)(2,1)S(1)}, bf16[128,256]{1,0:T(8,128)(2,1)S(1)}, u32[]{:S(2)}, u32[]{:S(2)}) %collective-permute-start.7) | collective-permute-done | bytes 65568 | tf_op jit(solution)/shard_map/ppermute | solution.py:212
  25.9 0.0 collective-permute-done.8.rest_7_.rest_3_
  25.9 0.4 weight_grad.1
  26.3 0.1 collective-permute-start.9
  26.4 0.4 mixed_part.1
  26.8 0.6 %collective-permute-start.10 = (bf16[512,256]{1,0:T(8,128)(2,1)S(1)}, bf16[512,256]{1,0:T(8,128)(2,1)S(1)}, u32[]{:S(2)}, u32[]{:S(2)}) collective-permute-start(bf16[512,256]{1,0:T(8,128)(2,1)S(1)} %get-tuple-element.98), channel_id=1, source_target_pairs={{0,2},{2,0},{4,6},{6,4},{1,3},{3,1},{5,7},{7,5},{8,10},{10,8},{12,... | collective-permute-start | bytes 786440 | tf_op jit(solution)/shard_map/ppermute | solution.py:216
  27.4 0.9 %collective-permute-done.9.other = f32[128,1024]{1,0:T(8,128)S(1)} collective-permute-done((f32[128,1024]{1,0:T(8,128)S(1)}, f32[128,1024]{1,0:T(8,128)S(1)}, u32[]{:S(2)}, u32[]{:S(2)}) %collective-permute-start.9) | collective-permute-done | bytes 524320 | tf_op jit(solution)/shard_map/ppermute | solution.py:212
  28.3 0.1 core_sum.1
  28.4 1.5 %collective-permute-start.15 = (bf16[32,1024]{1,0:T(8,128)(2,1)S(1)}, bf16[32,1024]{1,0:T(8,128)(2,1)S(1)}, u32[]{:S(2)}, u32[]{:S(2)}) collective-permute-start(bf16[32,1024]{1,0:T(8,128)(2,1)S(1)} %get-tuple-element.90), channel_id=1, source_target_pairs={{0,8},{8,16},{16,24},{24,0},{1,9},{9,17},{17,25},{25,1},{2,10},{10... | collective-permute-start | bytes 196616 | tf_op jit(solution)/shard_map/ppermute | solution.py:212
  29.9 1.8 %collective-permute-start.16 = (bf16[32,1024]{1,0:T(8,128)(2,1)S(1)}, bf16[32,1024]{1,0:T(8,128)(2,1)S(1)}, u32[]{:S(2)}, u32[]{:S(2)}) collective-permute-start(bf16[32,1024]{1,0:T(8,128)(2,1)S(1)} %get-tuple-element.108), channel_id=1, source_target_pairs={{0,16},{8,24},{16,0},{24,8},{1,17},{9,25},{17,1},{25,9},{2,18},{10... | collective-permute-start | bytes 196616 | tf_op jit(solution)/shard_map/ppermute | solution.py:212
  31.7 0.6 %collective-permute-start.17 = (bf16[32,1024]{1,0:T(8,128)(2,1)S(1)}, bf16[32,1024]{1,0:T(8,128)(2,1)S(1)}, u32[]{:S(2)}, u32[]{:S(2)}) collective-permute-start(bf16[32,1024]{1,0:T(8,128)(2,1)S(1)} %get-tuple-element.109), channel_id=1, source_target_pairs={{0,24},{8,0},{16,8},{24,16},{1,25},{9,1},{17,9},{25,17},{2,26},{10... | collective-permute-start | bytes 196616 | tf_op jit(solution)/shard_map/ppermute | solution.py:212
  32.3 2.2 %backward.1 = (bf16[96,256]{1,0:T(8,128)(2,1)S(1)}, bf16[96,256]{1,0:T(8,128)(2,1)S(1)}, bf16[96,256]{1,0:T(8,128)(2,1)S(1)}, bf16[96,256]{1,0:T(8,128)(2,1)S(1)}, f32[256,256]{1,0:T(8,128)S(1)}) custom-call(bf16[4,256,1024]{2,1,0:T(8,128)(2,1)S(1)} %get-tuple-element.84.toeplitz, f32[256,16]{1,0:T(8,128)S(1)} %get-tuple-element.64.columns, ...), custom_call_target="tpu_custom_call" | custom-call | flops 1073741824 | bytes 6766592 | tf_op jit(solution)/shard_map/backward/pallas_call | solution.py:234
  34.6 1.4 %collective-permute-start.12 = (bf16[96,256]{1,0:T(8,128)(2,1)S(1)}, bf16[96,256]{1,0:T(8,128)(2,1)S(1)}, u32[]{:S(2)}, u32[]{:S(2)}) collective-permute-start(bf16[96,256]{1,0:T(8,128)(2,1)S(1)} %get-tuple-element.103), channel_id=1, source_target_pairs={{0,8},{8,16},{16,24},{24,0},{1,9},{9,17},{17,25},{25,1},{2,10},{10... | collective-permute-start | bytes 147464 | tf_op jit(solution)/shard_map/ppermute | solution.py:212
  36.0 0.0 collective-permute-done.10.come
  36.0 1.1 %collective-permute-start.13 = (bf16[96,256]{1,0:T(8,128)(2,1)S(1)}, bf16[96,256]{1,0:T(8,128)(2,1)S(1)}, u32[]{:S(2)}, u32[]{:S(2)}) collective-permute-start(bf16[96,256]{1,0:T(8,128)(2,1)S(1)} %get-tuple-element.104), channel_id=1, source_target_pairs={{0,16},{8,24},{16,0},{24,8},{1,17},{9,25},{17,1},{25,9},{2,18},{10... | collective-permute-start | bytes 147464 | tf_op jit(solution)/shard_map/ppermute | solution.py:212
  37.2 0.1 collective-permute-done.16.refs_2_
  37.3 2.9 %collective-permute-start.14 = (bf16[96,256]{1,0:T(8,128)(2,1)S(1)}, bf16[96,256]{1,0:T(8,128)(2,1)S(1)}, u32[]{:S(2)}, u32[]{:S(2)}) collective-permute-start(bf16[96,256]{1,0:T(8,128)(2,1)S(1)} %get-tuple-element.105), channel_id=1, source_target_pairs={{0,24},{8,0},{16,8},{24,16},{1,25},{9,1},{17,9},{25,17},{2,26},{10... | collective-permute-start | bytes 147464 | tf_op jit(solution)/shard_map/ppermute | solution.py:212
  40.3 0.0 collective-permute-done.17.refs_3_
  40.3 1.6 %collective-permute-start.11 = (bf16[256,256]{1,0:T(8,128)(2,1)S(1)}, bf16[256,256]{1,0:T(8,128)(2,1)S(1)}, u32[]{:S(2)}, u32[]{:S(2)}) collective-permute-start(bf16[256,256]{1,0:T(8,128)(2,1)S(1)} %get-tuple-element.100), channel_id=1, source_target_pairs={{0,4},{2,6},{4,0},{6,2},{1,5},{3,7},{5,1},{7,3},{8,12},{10,14},{12... | collective-permute-start | bytes 393224 | tf_op jit(solution)/shard_map/ppermute | solution.py:216
  41.9 0.0 collective-permute-done.15.refs_1_
  41.9 0.2 collective-permute-start.21
  42.2 0.4 collective-permute-start.20
  42.5 1.7 %collective-permute-start.18 = (bf16[32,1024]{1,0:T(8,128)(2,1)S(1)}, bf16[32,1024]{1,0:T(8,128)(2,1)S(1)}, u32[]{:S(2)}, u32[]{:S(2)}) collective-permute-start(bf16[32,1024]{1,0:T(8,128)(2,1)S(1)} %block_sum.1.refs_0_), channel_id=1, source_target_pairs={{0,8},{8,16},{16,24},{24,0},{1,9},{9,17},{17,25},{25,1},{2,10},{10... | collective-permute-start | bytes 196616 | tf_op jit(solution)/shard_map/ppermute | solution.py:212
  44.3 0.0 collective-permute-done.14.refs_3_
  44.3 0.1 collective-permute-start.19
  44.4 1.3 %grad_out.1 = bf16[3,256,256]{2,1,0:T(8,128)(2,1)} custom-call(f32[256,256]{1,0:T(8,128)S(1)} %get-tuple-element.96.query_part, f32[6,256,256]{2,1,0:T(8,128)S(1)} %get-tuple-element.101.pair_w, f32[3,16,256]{2,1,0:T(8,128)S(1)} %get-tuple-element.106.later, bf16[96,256]{1,0:T(8,128)(2,1)S(1)} %get-tuple-element.102.refs_0_, ...), custom_call_target="tpu_custom_call" | custom-call | bytes 2473984 | tf_op jit(solution)/shard_map/grad_out/pallas_call | solution.py:234
  45.7 0.5 collective-permute-start.22
  46.2 3.2 %collective-permute-done.18.refs_1_ = bf16[32,1024]{1,0:T(8,128)(2,1)S(1)} collective-permute-done((bf16[32,1024]{1,0:T(8,128)(2,1)S(1)}, bf16[32,1024]{1,0:T(8,128)(2,1)S(1)}, u32[]{:S(2)}, u32[]{:S(2)}) %collective-permute-start.18) | collective-permute-done | bytes 65568 | tf_op jit(solution)/shard_map/ppermute | solution.py:212
  49.4 0.0 collective-permute-done.21.refs_3_
  49.4 0.0 collective-permute-start.25
  49.4 0.0 collective-permute-done.20.refs_2_
  49.5 0.5 collective-permute-start.24
  49.9 0.1 collective-permute-start.23
  50.0 0.7 %mixed_sum.1 = bf16[256,256]{1,0:T(8,128)(2,1)} custom-call(f32[256,256]{1,0:T(8,128)S(1)} %get-tuple-element.99.own, bf16[256,256]{1,0:T(8,128)(2,1)S(1)} %collective-permute-done.11.come), custom_call_target="tpu_custom_call" | custom-call | bytes 524288 | tf_op jit(solution)/shard_map/mixed_sum/pallas_call | solution.py:234
  50.7 0.0 collective-permute-done.22.refs_4_
  50.7 0.0 collective-permute-done.25.refs_7_
  50.7 0.1 collective-permute-done.24.refs_6_
  50.8 0.4 collective-permute-done.23.refs_5_
  51.2 1.1 %final.1 = (f32[256,1024]{1,0:T(8,128)}, f32[3,3,256]{2,1,0:T(4,128)}, f32[16,256]{1,0:T(8,128)}) custom-call(bf16[32,1024]{1,0:T(8,128)(2,1)S(1)} %block_sum.1.refs_0_, bf16[32,1024]{1,0:T(8,128)(2,1)S(1)} %collective-permute-done.18.refs_1_, bf16[32,1024]{1,0:T(8,128)(2,1)S(1)} %collective-permute-done.20.refs_2_, ...), custom_call_target="tpu_custom_call" | custom-call | bytes 1664000 | tf_op jit(solution)/shard_map/final/pallas_call | solution.py:234
  (13 shorter events, 0.1 us)
Async XLA Ops:
  0.6 12.0 %collective-permute-start = (bf16[256,256]{1,0:T(8,128)(2,1)}, bf16[256,256]{1,0:T(8,128)(2,1)S(1)}, u32[]{:S(2)}, u32[]{:S(2)}) collective-permute-start(bf16[256,256]{1,0:T(8,128)(2,1)} %bitcast.8), channel_id=1, source_target_pairs={{0,2},{2,0},{4,6},{6,4},{1,3},{3,1},{5,7},{7,5},{8,10},{10,8},{12,... | collective-permute-start | bytes 393224 | tf_op jit(solution)/shard_map/ppermute | solution.py:216
  5.5 10.4 %collective-permute-start.1 = (bf16[160,256]{1,0:T(8,128)(2,1)}, bf16[160,256]{1,0:T(8,128)(2,1)S(1)}, u32[]{:S(2)}, u32[]{:S(2)}) collective-permute-start(bf16[160,256]{1,0:T(8,128)(2,1)} %get-tuple-element.63), channel_id=1, source_target_pairs={{0,8},{8,16},{16,24},{24,0},{1,9},{9,17},{17,25},{25,1},{2,10},{10... | collective-permute-start | bytes 245768 | tf_op jit(solution)/shard_map/ppermute | solution.py:212
  7.1 8.8 %collective-permute-start.2 = (bf16[144,256]{1,0:T(8,128)(2,1)}, bf16[144,256]{1,0:T(8,128)(2,1)S(1)}, u32[]{:S(2)}, u32[]{:S(2)}) collective-permute-start(bf16[144,256]{1,0:T(8,128)(2,1)} %get-tuple-element.66), channel_id=1, source_target_pairs={{0,16},{8,24},{16,0},{24,8},{1,17},{9,25},{17,1},{25,9},{2,18},{10... | collective-permute-start | bytes 221192 | tf_op jit(solution)/shard_map/ppermute | solution.py:212
  9.7 6.2 %collective-permute-start.3 = (bf16[144,256]{1,0:T(8,128)(2,1)}, bf16[144,256]{1,0:T(8,128)(2,1)S(1)}, u32[]{:S(2)}, u32[]{:S(2)}) collective-permute-start(bf16[144,256]{1,0:T(8,128)(2,1)} %get-tuple-element.67), channel_id=1, source_target_pairs={{0,24},{8,0},{16,8},{24,16},{1,25},{9,1},{17,9},{25,17},{2,26},{10... | collective-permute-start | bytes 221192 | tf_op jit(solution)/shard_map/ppermute | solution.py:212
  11.1 6.3 %collective-permute-start.4 = (bf16[256,256]{1,0:T(8,128)(2,1)}, bf16[256,256]{1,0:T(8,128)(2,1)S(1)}, u32[]{:S(2)}, u32[]{:S(2)}) collective-permute-start(bf16[256,256]{1,0:T(8,128)(2,1)} %bitcast.9), channel_id=1, source_target_pairs={{0,4},{2,6},{4,0},{6,2},{1,5},{3,7},{5,1},{7,3},{8,12},{10,14},{12... | collective-permute-start | bytes 393224 | tf_op jit(solution)/shard_map/ppermute | solution.py:216
  12.6 5.6 %collective-permute-start.5 = (bf16[256,256]{1,0:T(8,128)(2,1)S(1)}, bf16[256,256]{1,0:T(8,128)(2,1)S(1)}, u32[]{:S(2)}, u32[]{:S(2)}) collective-permute-start(bf16[256,256]{1,0:T(8,128)(2,1)S(1)} %collective-permute-done.rest_1_), channel_id=1, source_target_pairs={{0,4},{2,6},{4,0},{6,2},{1,5},{3,7},{5,1},{7,3},{8,12},{10,14},{12... | collective-permute-start | bytes 393224 | tf_op jit(solution)/shard_map/ppermute | solution.py:216
  13.1 1.0 %copy-start.1 = (bf16[3,1,256,256]{3,2,1,0:T(8,128)(2,1)S(1)}, bf16[3,1,256,256]{3,2,1,0:T(8,128)(2,1)}, u32[]{:S(2)}) copy-start(bf16[3,1,256,256]{3,2,1,0:T(8,128)(2,1)} %param.6) | copy-start | bytes 1179652
  14.1 0.9 %copy-start.3 = (bf16[144,256]{1,0:T(8,128)(2,1)S(1)}, bf16[144,256]{1,0:T(8,128)(2,1)}, u32[]{:S(2)}) copy-start(bf16[144,256]{1,0:T(8,128)(2,1)} %get-tuple-element.61.chunk) | copy-start | bytes 221188
  15.0 0.7 %copy-start.4 = (f32[3,3,256]{2,1,0:T(4,128)S(1)}, f32[3,3,256]{2,1,0:T(4,128)}, u32[]{:S(2)}) copy-start(f32[3,3,256]{2,1,0:T(4,128)} %short_filter) | copy-start | bytes 27652
  15.9 2.3 %copy-start = (bf16[256,1024]{1,0:T(8,128)(2,1)S(1)}, bf16[256,1024]{1,0:T(8,128)(2,1)}, u32[]{:S(2)}) copy-start(bf16[256,1024]{1,0:T(8,128)(2,1)} %weights.3) | copy-start | bytes 1572868
  15.9 2.3 %copy-start.2 = (bf16[1,256,256]{2,1,0:T(8,128)(2,1)S(1)}, bf16[1,256,256]{2,1,0:T(8,128)(2,1)}, u32[]{:S(2)}) copy-start(bf16[1,256,256]{2,1,0:T(8,128)(2,1)} %param.11) | copy-start | bytes 393220
  18.6 6.2 %collective-permute-start.6 = (bf16[128,256]{1,0:T(8,128)(2,1)S(1)}, bf16[128,256]{1,0:T(8,128)(2,1)S(1)}, u32[]{:S(2)}, u32[]{:S(2)}) collective-permute-start(bf16[128,256]{1,0:T(8,128)(2,1)S(1)} %get-tuple-element.79), channel_id=1, source_target_pairs={{0,8},{8,16},{16,24},{24,0},{1,9},{9,17},{17,25},{25,1},{2,10},{10... | collective-permute-start | bytes 196616 | tf_op jit(solution)/shard_map/ppermute | solution.py:212
  19.4 6.6 %collective-permute-start.7 = (bf16[128,256]{1,0:T(8,128)(2,1)S(1)}, bf16[128,256]{1,0:T(8,128)(2,1)S(1)}, u32[]{:S(2)}, u32[]{:S(2)}) collective-permute-start(bf16[128,256]{1,0:T(8,128)(2,1)S(1)} %get-tuple-element.80), channel_id=1, source_target_pairs={{0,16},{8,24},{16,0},{24,8},{1,17},{9,25},{17,1},{25,9},{2,18},{10... | collective-permute-start | bytes 196616 | tf_op jit(solution)/shard_map/ppermute | solution.py:212
  20.7 5.3 %collective-permute-start.8 = (bf16[128,256]{1,0:T(8,128)(2,1)S(1)}, bf16[128,256]{1,0:T(8,128)(2,1)S(1)}, u32[]{:S(2)}, u32[]{:S(2)}) collective-permute-start(bf16[128,256]{1,0:T(8,128)(2,1)S(1)} %get-tuple-element.81), channel_id=1, source_target_pairs={{0,24},{8,0},{16,8},{24,16},{1,25},{9,1},{17,9},{25,17},{2,26},{10... | collective-permute-start | bytes 196616 | tf_op jit(solution)/shard_map/ppermute | solution.py:212
  26.3 2.0 %collective-permute-start.9 = (f32[128,1024]{1,0:T(8,128)S(1)}, f32[128,1024]{1,0:T(8,128)S(1)}, u32[]{:S(2)}, u32[]{:S(2)}) collective-permute-start(f32[128,1024]{1,0:T(8,128)S(1)} %get-tuple-element.89), channel_id=1, source_target_pairs={{0,1},{1,0},{2,3},{3,2},{4,5},{5,4},{6,7},{7,6},{8,9},{9,8},{10,11... | collective-permute-start | bytes 1572872 | tf_op jit(solution)/shard_map/ppermute | solution.py:212
  26.8 9.2 %collective-permute-start.10 = (bf16[512,256]{1,0:T(8,128)(2,1)S(1)}, bf16[512,256]{1,0:T(8,128)(2,1)S(1)}, u32[]{:S(2)}, u32[]{:S(2)}) collective-permute-start(bf16[512,256]{1,0:T(8,128)(2,1)S(1)} %get-tuple-element.98), channel_id=1, source_target_pairs={{0,2},{2,0},{4,6},{6,4},{1,3},{3,1},{5,7},{7,5},{8,10},{10,8},{12,... | collective-permute-start | bytes 786440 | tf_op jit(solution)/shard_map/ppermute | solution.py:216
  28.4 13.5 %collective-permute-start.15 = (bf16[32,1024]{1,0:T(8,128)(2,1)S(1)}, bf16[32,1024]{1,0:T(8,128)(2,1)S(1)}, u32[]{:S(2)}, u32[]{:S(2)}) collective-permute-start(bf16[32,1024]{1,0:T(8,128)(2,1)S(1)} %get-tuple-element.90), channel_id=1, source_target_pairs={{0,8},{8,16},{16,24},{24,0},{1,9},{9,17},{17,25},{25,1},{2,10},{10... | collective-permute-start | bytes 196616 | tf_op jit(solution)/shard_map/ppermute | solution.py:212
  29.9 7.4 %collective-permute-start.16 = (bf16[32,1024]{1,0:T(8,128)(2,1)S(1)}, bf16[32,1024]{1,0:T(8,128)(2,1)S(1)}, u32[]{:S(2)}, u32[]{:S(2)}) collective-permute-start(bf16[32,1024]{1,0:T(8,128)(2,1)S(1)} %get-tuple-element.108), channel_id=1, source_target_pairs={{0,16},{8,24},{16,0},{24,8},{1,17},{9,25},{17,1},{25,9},{2,18},{10... | collective-permute-start | bytes 196616 | tf_op jit(solution)/shard_map/ppermute | solution.py:212
  31.7 8.6 %collective-permute-start.17 = (bf16[32,1024]{1,0:T(8,128)(2,1)S(1)}, bf16[32,1024]{1,0:T(8,128)(2,1)S(1)}, u32[]{:S(2)}, u32[]{:S(2)}) collective-permute-start(bf16[32,1024]{1,0:T(8,128)(2,1)S(1)} %get-tuple-element.109), channel_id=1, source_target_pairs={{0,24},{8,0},{16,8},{24,16},{1,25},{9,1},{17,9},{25,17},{2,26},{10... | collective-permute-start | bytes 196616 | tf_op jit(solution)/shard_map/ppermute | solution.py:212
  34.6 7.6 %collective-permute-start.12 = (bf16[96,256]{1,0:T(8,128)(2,1)S(1)}, bf16[96,256]{1,0:T(8,128)(2,1)S(1)}, u32[]{:S(2)}, u32[]{:S(2)}) collective-permute-start(bf16[96,256]{1,0:T(8,128)(2,1)S(1)} %get-tuple-element.103), channel_id=1, source_target_pairs={{0,8},{8,16},{16,24},{24,0},{1,9},{9,17},{17,25},{25,1},{2,10},{10... | collective-permute-start | bytes 147464 | tf_op jit(solution)/shard_map/ppermute | solution.py:212
  36.0 6.5 %collective-permute-start.13 = (bf16[96,256]{1,0:T(8,128)(2,1)S(1)}, bf16[96,256]{1,0:T(8,128)(2,1)S(1)}, u32[]{:S(2)}, u32[]{:S(2)}) collective-permute-start(bf16[96,256]{1,0:T(8,128)(2,1)S(1)} %get-tuple-element.104), channel_id=1, source_target_pairs={{0,16},{8,24},{16,0},{24,8},{1,17},{9,25},{17,1},{25,9},{2,18},{10... | collective-permute-start | bytes 147464 | tf_op jit(solution)/shard_map/ppermute | solution.py:212
  37.3 7.0 %collective-permute-start.14 = (bf16[96,256]{1,0:T(8,128)(2,1)S(1)}, bf16[96,256]{1,0:T(8,128)(2,1)S(1)}, u32[]{:S(2)}, u32[]{:S(2)}) collective-permute-start(bf16[96,256]{1,0:T(8,128)(2,1)S(1)} %get-tuple-element.105), channel_id=1, source_target_pairs={{0,24},{8,0},{16,8},{24,16},{1,25},{9,1},{17,9},{25,17},{2,26},{10... | collective-permute-start | bytes 147464 | tf_op jit(solution)/shard_map/ppermute | solution.py:212
  40.3 5.9 %collective-permute-start.11 = (bf16[256,256]{1,0:T(8,128)(2,1)S(1)}, bf16[256,256]{1,0:T(8,128)(2,1)S(1)}, u32[]{:S(2)}, u32[]{:S(2)}) collective-permute-start(bf16[256,256]{1,0:T(8,128)(2,1)S(1)} %get-tuple-element.100), channel_id=1, source_target_pairs={{0,4},{2,6},{4,0},{6,2},{1,5},{3,7},{5,1},{7,3},{8,12},{10,14},{12... | collective-permute-start | bytes 393224 | tf_op jit(solution)/shard_map/ppermute | solution.py:216
  41.9 7.5 %collective-permute-start.21 = (bf16[32,1024]{1,0:T(8,128)(2,1)S(1)}, bf16[32,1024]{1,0:T(8,128)(2,1)S(1)}, u32[]{:S(2)}, u32[]{:S(2)}) collective-permute-start(bf16[32,1024]{1,0:T(8,128)(2,1)S(1)} %block_sum.1.refs_0_), channel_id=1, source_target_pairs={{0,24},{8,0},{16,8},{24,16},{1,25},{9,1},{17,9},{25,17},{2,26},{10... | collective-permute-start | bytes 196616 | tf_op jit(solution)/shard_map/ppermute | solution.py:212
  42.2 7.3 %collective-permute-start.20 = (bf16[32,1024]{1,0:T(8,128)(2,1)S(1)}, bf16[32,1024]{1,0:T(8,128)(2,1)S(1)}, u32[]{:S(2)}, u32[]{:S(2)}) collective-permute-start(bf16[32,1024]{1,0:T(8,128)(2,1)S(1)} %block_sum.1.refs_0_), channel_id=1, source_target_pairs={{0,16},{8,24},{16,0},{24,8},{1,17},{9,25},{17,1},{25,9},{2,18},{10... | collective-permute-start | bytes 196616 | tf_op jit(solution)/shard_map/ppermute | solution.py:212
  42.5 6.9 %collective-permute-start.18 = (bf16[32,1024]{1,0:T(8,128)(2,1)S(1)}, bf16[32,1024]{1,0:T(8,128)(2,1)S(1)}, u32[]{:S(2)}, u32[]{:S(2)}) collective-permute-start(bf16[32,1024]{1,0:T(8,128)(2,1)S(1)} %block_sum.1.refs_0_), channel_id=1, source_target_pairs={{0,8},{8,16},{16,24},{24,0},{1,9},{9,17},{17,25},{25,1},{2,10},{10... | collective-permute-start | bytes 196616 | tf_op jit(solution)/shard_map/ppermute | solution.py:212
  44.3 1.4 %collective-permute-start.19 = (bf16[16,1024]{1,0:T(8,128)(2,1)S(1)}, bf16[16,1024]{1,0:T(8,128)(2,1)S(1)}, u32[]{:S(2)}, u32[]{:S(2)}) collective-permute-start(bf16[16,1024]{1,0:T(8,128)(2,1)S(1)} %get-tuple-element.110.refs_8_), channel_id=1, source_target_pairs={{0,1},{1,0},{2,3},{3,2},{4,5},{5,4},{6,7},{7,6},{8,9},{9,8},{10,11... | collective-permute-start | bytes 98312 | tf_op jit(solution)/shard_map/ppermute | solution.py:212
  45.7 5.0 %collective-permute-start.22 = (bf16[32,1024]{1,0:T(8,128)(2,1)S(1)}, bf16[32,1024]{1,0:T(8,128)(2,1)S(1)}, u32[]{:S(2)}, u32[]{:S(2)}) collective-permute-start(bf16[32,1024]{1,0:T(8,128)(2,1)S(1)} %block_sum.1.refs_0_), channel_id=1, source_target_pairs={{0,1},{1,0},{2,3},{3,2},{4,5},{5,4},{6,7},{7,6},{8,9},{9,8},{10,11... | collective-permute-start | bytes 196616 | tf_op jit(solution)/shard_map/ppermute | solution.py:212
  49.4 1.3 %collective-permute-start.25 = (bf16[32,1024]{1,0:T(8,128)(2,1)S(1)}, bf16[32,1024]{1,0:T(8,128)(2,1)S(1)}, u32[]{:S(2)}, u32[]{:S(2)}) collective-permute-start(bf16[32,1024]{1,0:T(8,128)(2,1)S(1)} %collective-permute-done.21.refs_3_), channel_id=1, source_target_pairs={{0,1},{1,0},{2,3},{3,2},{4,5},{5,4},{6,7},{7,6},{8,9},{9,8},{10,11... | collective-permute-start | bytes 196616 | tf_op jit(solution)/shard_map/ppermute | solution.py:212
  49.5 1.4 %collective-permute-start.24 = (bf16[32,1024]{1,0:T(8,128)(2,1)S(1)}, bf16[32,1024]{1,0:T(8,128)(2,1)S(1)}, u32[]{:S(2)}, u32[]{:S(2)}) collective-permute-start(bf16[32,1024]{1,0:T(8,128)(2,1)S(1)} %collective-permute-done.20.refs_2_), channel_id=1, source_target_pairs={{0,1},{1,0},{2,3},{3,2},{4,5},{5,4},{6,7},{7,6},{8,9},{9,8},{10,11... | collective-permute-start | bytes 196616 | tf_op jit(solution)/shard_map/ppermute | solution.py:212
  49.9 1.3 %collective-permute-start.23 = (bf16[32,1024]{1,0:T(8,128)(2,1)S(1)}, bf16[32,1024]{1,0:T(8,128)(2,1)S(1)}, u32[]{:S(2)}, u32[]{:S(2)}) collective-permute-start(bf16[32,1024]{1,0:T(8,128)(2,1)S(1)} %collective-permute-done.18.refs_1_), channel_id=1, source_target_pairs={{0,1},{1,0},{2,3},{3,2},{4,5},{5,4},{6,7},{7,6},{8,9},{9,8},{10,11... | collective-permute-start | bytes 196616 | tf_op jit(solution)/shard_map/ppermute | solution.py:212

commit v6 on v5

--- a/solution.py
+++ b/solution.py
@@ -440,7 +440,7 @@
         at = block_at(mine ^ s, width)
         full[:, at] = jnp.dot(y, cot, preferred_element_type=f32)
     keep[...] = full[block_at(core, half)]
-    send[...] = full[block_at(1 - core, half)]
+    send[...] = full[block_at(1 - core, half)].astype(send.dtype)
 
 
 def core_sum_kernel(devices, keep, other, *rest):
@@ -817,7 +817,7 @@
             ((width, length), bf16),
             ((width, length), f32),
             ((half, total_cols), f32),
-            ((half, total_cols), f32),
+            ((half, total_cols), bf16),
         ],
         (query_conv, *cots, *pairs),
         "weight_grad",

time: 52.5 us -> 51.9 us (0.989)
  waiting for transfers between devices: 7.62 us -> 6.89 us
    ppermute x21, waiting for transfers between devices: 6.83 us -> 6.1 us  [rotate(): lax.ppermute(value, axis, [(i, (i + steps) % count) for i in range(count)])]
where the time goes in v6:
time: 51.9 us; the launch traced here: 51.6 us
  starting transfers between devices  29.7 us (57%)
  Pallas kernels  11.6 us (22%)
  waiting for transfers between devices  6.89 us (13%)
  local copies, waits for them, and re-layouts  2.6 us (5%)
  between operations  0.83 us (2%)
    ppermute x21, starting transfers between devices, rotate(): lax.ppermute(value, axis, [(i, (i + steps) % count) for i in range(count)])  22.5 us
    pallas_call x15, Pallas kernels, on_core(): pl.pallas_call(kernel, out_shape=[jax.ShapeDtypeStruct(shape, kind) for s...  11.6 us
    ppermute x5, starting transfers between devices, swap(): lax.ppermute(value, axis, [(i, i ^ bits) for i in range(lax.axis_size(axi...  7.21 us
    ppermute x21, waiting for transfers between devices, rotate(): lax.ppermute(value, axis, [(i, (i + steps) % count) for i in range(count)])  6.1 us
    unnamed x10, local copies, waits for them, and re-layouts  2.6 us
  transfers between devices with their start and end apart: 26, of which 8 were waited for; matrix products, arithmetic and copies ran while one was open for 0% of the time, Pallas kernels for 19%

profile of v6, /device:TPU:0, one launch (start us, length us, event | category | flops | bytes accessed | tf_op | source)
XLA Modules:
  0.0 51.6 jit_solution(16777663499197571766)
XLA Ops:
  0.6 3.0 %collective-permute-start = (bf16[256,256]{1,0:T(8,128)(2,1)}, bf16[256,256]{1,0:T(8,128)(2,1)S(1)}, u32[]{:S(2)}, u32[]{:S(2)}) collective-permute-start(bf16[256,256]{1,0:T(8,128)(2,1)} %bitcast.8), channel_id=1, source_target_pairs={{0,2},{2,0},{4,6},{6,4},{1,3},{3,1},{5,7},{7,5},{8,10},{10,8},{12,... | collective-permute-start | bytes 393224 | tf_op jit(solution)/shard_map/ppermute | solution.py:216
  3.6 1.9 %pack.1 = (bf16[144,256]{1,0:T(8,128)(2,1)}, bf16[160,256]{1,0:T(8,128)(2,1)}, bf16[144,256]{1,0:T(8,128)(2,1)}, bf16[144,256]{1,0:T(8,128)(2,1)}) custom-call(bf16[3,256,256]{2,1,0:T(8,128)(2,1)} %bitcast.6, f32[16,256]{1,0:T(8,128)} %filter_source.1, s32[1,256]{1,0:T(1,128)} %segment_source.1), custom_call_target="tpu_custom_call" | custom-call | bytes 713728 | tf_op jit(solution)/shard_map/pack/pallas_call | solution.py:234
  5.5 1.6 %collective-permute-start.1 = (bf16[160,256]{1,0:T(8,128)(2,1)}, bf16[160,256]{1,0:T(8,128)(2,1)S(1)}, u32[]{:S(2)}, u32[]{:S(2)}) collective-permute-start(bf16[160,256]{1,0:T(8,128)(2,1)} %get-tuple-element.63), channel_id=1, source_target_pairs={{0,8},{8,16},{16,24},{24,0},{1,9},{9,17},{17,25},{25,1},{2,10},{10... | collective-permute-start | bytes 245768 | tf_op jit(solution)/shard_map/ppermute | solution.py:212
  7.1 2.6 %collective-permute-start.2 = (bf16[144,256]{1,0:T(8,128)(2,1)}, bf16[144,256]{1,0:T(8,128)(2,1)S(1)}, u32[]{:S(2)}, u32[]{:S(2)}) collective-permute-start(bf16[144,256]{1,0:T(8,128)(2,1)} %get-tuple-element.66), channel_id=1, source_target_pairs={{0,16},{8,24},{16,0},{24,8},{1,17},{9,25},{17,1},{25,9},{2,18},{10... | collective-permute-start | bytes 221192 | tf_op jit(solution)/shard_map/ppermute | solution.py:212
  9.7 1.3 %collective-permute-start.3 = (bf16[144,256]{1,0:T(8,128)(2,1)}, bf16[144,256]{1,0:T(8,128)(2,1)S(1)}, u32[]{:S(2)}, u32[]{:S(2)}) collective-permute-start(bf16[144,256]{1,0:T(8,128)(2,1)} %get-tuple-element.67), channel_id=1, source_target_pairs={{0,24},{8,0},{16,8},{24,16},{1,25},{9,1},{17,9},{25,17},{2,26},{10... | collective-permute-start | bytes 221192 | tf_op jit(solution)/shard_map/ppermute | solution.py:212
  11.1 1.5 %collective-permute-start.4 = (bf16[256,256]{1,0:T(8,128)(2,1)}, bf16[256,256]{1,0:T(8,128)(2,1)S(1)}, u32[]{:S(2)}, u32[]{:S(2)}) collective-permute-start(bf16[256,256]{1,0:T(8,128)(2,1)} %bitcast.9), channel_id=1, source_target_pairs={{0,4},{2,6},{4,0},{6,2},{1,5},{3,7},{5,1},{7,3},{8,12},{10,14},{12... | collective-permute-start | bytes 393224 | tf_op jit(solution)/shard_map/ppermute | solution.py:216
  12.6 0.0 collective-permute-done.rest_1_
  12.6 0.5 collective-permute-start.5
  13.1 1.0 %copy-done.1 = bf16[3,1,256,256]{3,2,1,0:T(8,128)(2,1)S(1)} copy-done((bf16[3,1,256,256]{3,2,1,0:T(8,128)(2,1)S(1)}, bf16[3,1,256,256]{3,2,1,0:T(8,128)(2,1)}, u32[]{:S(2)}) %copy-start.1) | copy-done | bytes 393240
  14.1 0.9 %copy-done.3 = bf16[144,256]{1,0:T(8,128)(2,1)S(1)} copy-done((bf16[144,256]{1,0:T(8,128)(2,1)S(1)}, bf16[144,256]{1,0:T(8,128)(2,1)}, u32[]{:S(2)}) %copy-start.3) | copy-done | bytes 73752
  15.0 0.7 %copy-done.4 = f32[3,3,256]{2,1,0:T(4,128)S(1)} copy-done((f32[3,3,256]{2,1,0:T(4,128)S(1)}, f32[3,3,256]{2,1,0:T(4,128)}, u32[]{:S(2)}) %copy-start.4) | copy-done | bytes 9240
  15.7 0.2 prepare.1
  15.9 0.0 collective-permute-done.2.rest_2_
  15.9 0.0 collective-permute-done.3.rest_3_
  15.9 0.0 collective-permute-done.1.rest_1_.previous
  15.9 0.0 copy-start
  15.9 0.0 copy-start.2
  16.0 1.4 %conv.1 = (bf16[64,256]{1,0:T(8,128)(2,1)S(1)}, bf16[64,256]{1,0:T(8,128)(2,1)S(1)}, bf16[64,256]{1,0:T(8,128)(2,1)S(1)}, bf16[64,256]{1,0:T(8,128)(2,1)S(1)}, f...) custom-call(f32[256,16]{1,0:T(8,128)S(1)} %get-tuple-element.64.colu, ...), custom_call_target="tpu_custom_call" | custom-call | flops 900000000 | bytes 3366912 | tf_op jit(solution)/shard_map/conv/pallas_call | solution.py:234
  17.4 0.0 collective-permute-done.4.rest_2_
  17.4 0.8 %collective-permute-done.5.rest_3_ = bf16[256,256]{1,0:T(8,128)(2,1)S(1)} collective-permute-done((bf16[256,256]{1,0:T(8,128)(2,1)S(1)}, bf16[256,256]{1,0:T(8,128)(2,1)S(1)}, u32[]{:S(2)}, u32[]{:S(2)}) %collective-permute-start.5) | collective-permute-done | bytes 131104 | tf_op jit(solution)/shard_map/ppermute | solution.py:216
  18.2 0.4 grad_y.1
  18.6 0.7 %collective-permute-start.6 = (bf16[128,256]{1,0:T(8,128)(2,1)S(1)}, bf16[128,256]{1,0:T(8,128)(2,1)S(1)}, u32[]{:S(2)}, u32[]{:S(2)}) collective-permute-start(bf16[128,256]{1,0:T(8,128)(2,1)S(1)} %get-tuple-element.79), channel_id=1, source_target_pairs={{0,8},{8,16},{16,24},{24,0},{1,9},{9,17},{17,25},{25,1},{2,10},{10... | collective-permute-start | bytes 196616 | tf_op jit(solution)/shard_map/ppermute | solution.py:212
  19.4 1.3 %collective-permute-start.7 = (bf16[128,256]{1,0:T(8,128)(2,1)S(1)}, bf16[128,256]{1,0:T(8,128)(2,1)S(1)}, u32[]{:S(2)}, u32[]{:S(2)}) collective-permute-start(bf16[128,256]{1,0:T(8,128)(2,1)S(1)} %get-tuple-element.80), channel_id=1, source_target_pairs={{0,16},{8,24},{16,0},{24,8},{1,17},{9,25},{17,1},{25,9},{2,18},{10... | collective-permute-start | bytes 196616 | tf_op jit(solution)/shard_map/ppermute | solution.py:212
  20.7 1.8 %collective-permute-start.8 = (bf16[128,256]{1,0:T(8,128)(2,1)S(1)}, bf16[128,256]{1,0:T(8,128)(2,1)S(1)}, u32[]{:S(2)}, u32[]{:S(2)}) collective-permute-start(bf16[128,256]{1,0:T(8,128)(2,1)S(1)} %get-tuple-element.81), channel_id=1, source_target_pairs={{0,24},{8,0},{16,8},{24,16},{1,25},{9,1},{17,9},{25,17},{2,26},{10... | collective-permute-start | bytes 196616 | tf_op jit(solution)/shard_map/ppermute | solution.py:212
  22.5 1.4 %ready.1 = (f32[6,256,256]{2,1,0:T(8,128)S(1)}, f32[3,256,256]{2,1,0:T(8,128)S(1)}, f32[2,256,256]{2,1,0:T(8,128)S(1)}, bf16[4,128,128]{2,1,0:T(8,128)(2,1)S(1)}...) custom-call(bf16[3,256,256]{2,1,0:T(8,128)(2,1)S(1)} %get-tuple-element.62.turned, ...), custom_call_target="tpu_custom_call" | custom-call | bytes 6291456 | tf_op jit(solution)/shard_map/ready/pallas_call | solution.py:234
  23.9 0.9 %collective-permute-done.6.rest_5_.rest_1_ = bf16[128,256]{1,0:T(8,128)(2,1)S(1)} collective-permute-done((bf16[128,256]{1,0:T(8,128)(2,1)S(1)}, bf16[128,256]{1,0:T(8,128)(2,1)S(1)}, u32[]{:S(2)}, u32[]{:S(2)}) %collective-permute-start.6) | collective-permute-done | bytes 65568 | tf_op jit(solution)/shard_map/ppermute | solution.py:212
  24.9 1.1 %collective-permute-done.7.rest_6_.rest_2_ = bf16[128,256]{1,0:T(8,128)(2,1)S(1)} collective-permute-done((bf16[128,256]{1,0:T(8,128)(2,1)S(1)}, bf16[128,256]{1,0:T(8,128)(2,1)S(1)}, u32[]{:S(2)}, u32[]{:S(2)}) %collective-permute-start.7) | collective-permute-done | bytes 65568 | tf_op jit(solution)/shard_map/ppermute | solution.py:212
  25.9 0.0 collective-permute-done.8.rest_7_.rest_3_
  25.9 0.4 weight_grad.1
  26.3 0.1 collective-permute-start.9
  26.4 0.4 mixed_part.1
  26.8 0.6 %collective-permute-start.10 = (bf16[512,256]{1,0:T(8,128)(2,1)S(1)}, bf16[512,256]{1,0:T(8,128)(2,1)S(1)}, u32[]{:S(2)}, u32[]{:S(2)}) collective-permute-start(bf16[512,256]{1,0:T(8,128)(2,1)S(1)} %get-tuple-element.98), channel_id=1, source_target_pairs={{0,2},{2,0},{4,6},{6,4},{1,3},{3,1},{5,7},{7,5},{8,10},{10,8},{12,... | collective-permute-start | bytes 786440 | tf_op jit(solution)/shard_map/ppermute | solution.py:216
  27.4 0.5 collective-permute-done.9.other
  27.9 0.1 core_sum.1
  28.0 1.5 %collective-permute-start.15 = (bf16[32,1024]{1,0:T(8,128)(2,1)S(1)}, bf16[32,1024]{1,0:T(8,128)(2,1)S(1)}, u32[]{:S(2)}, u32[]{:S(2)}) collective-permute-start(bf16[32,1024]{1,0:T(8,128)(2,1)S(1)} %get-tuple-element.90), channel_id=1, source_target_pairs={{0,8},{8,16},{16,24},{24,0},{1,9},{9,17},{17,25},{25,1},{2,10},{10... | collective-permute-start | bytes 196616 | tf_op jit(solution)/shard_map/ppermute | solution.py:212
  29.5 1.8 %collective-permute-start.16 = (bf16[32,1024]{1,0:T(8,128)(2,1)S(1)}, bf16[32,1024]{1,0:T(8,128)(2,1)S(1)}, u32[]{:S(2)}, u32[]{:S(2)}) collective-permute-start(bf16[32,1024]{1,0:T(8,128)(2,1)S(1)} %get-tuple-element.108), channel_id=1, source_target_pairs={{0,16},{8,24},{16,0},{24,8},{1,17},{9,25},{17,1},{25,9},{2,18},{10... | collective-permute-start | bytes 196616 | tf_op jit(solution)/shard_map/ppermute | solution.py:212
  31.3 0.6 %collective-permute-start.17 = (bf16[32,1024]{1,0:T(8,128)(2,1)S(1)}, bf16[32,1024]{1,0:T(8,128)(2,1)S(1)}, u32[]{:S(2)}, u32[]{:S(2)}) collective-permute-start(bf16[32,1024]{1,0:T(8,128)(2,1)S(1)} %get-tuple-element.109), channel_id=1, source_target_pairs={{0,24},{8,0},{16,8},{24,16},{1,25},{9,1},{17,9},{25,17},{2,26},{10... | collective-permute-start | bytes 196616 | tf_op jit(solution)/shard_map/ppermute | solution.py:212
  31.9 2.2 %backward.1 = (bf16[96,256]{1,0:T(8,128)(2,1)S(1)}, bf16[96,256]{1,0:T(8,128)(2,1)S(1)}, bf16[96,256]{1,0:T(8,128)(2,1)S(1)}, bf16[96,256]{1,0:T(8,128)(2,1)S(1)}, f32[256,256]{1,0:T(8,128)S(1)}) custom-call(bf16[4,256,1024]{2,1,0:T(8,128)(2,1)S(1)} %get-tuple-element.84.toeplitz, f32[256,16]{1,0:T(8,128)S(1)} %get-tuple-element.64.columns, ...), custom_call_target="tpu_custom_call" | custom-call | flops 1073741824 | bytes 6766592 | tf_op jit(solution)/shard_map/backward/pallas_call | solution.py:234
  34.2 1.4 %collective-permute-start.12 = (bf16[96,256]{1,0:T(8,128)(2,1)S(1)}, bf16[96,256]{1,0:T(8,128)(2,1)S(1)}, u32[]{:S(2)}, u32[]{:S(2)}) collective-permute-start(bf16[96,256]{1,0:T(8,128)(2,1)S(1)} %get-tuple-element.103), channel_id=1, source_target_pairs={{0,8},{8,16},{16,24},{24,0},{1,9},{9,17},{17,25},{25,1},{2,10},{10... | collective-permute-start | bytes 147464 | tf_op jit(solution)/shard_map/ppermute | solution.py:212
  35.6 0.0 collective-permute-done.10.come
  35.6 1.1 %collective-permute-start.13 = (bf16[96,256]{1,0:T(8,128)(2,1)S(1)}, bf16[96,256]{1,0:T(8,128)(2,1)S(1)}, u32[]{:S(2)}, u32[]{:S(2)}) collective-permute-start(bf16[96,256]{1,0:T(8,128)(2,1)S(1)} %get-tuple-element.104), channel_id=1, source_target_pairs={{0,16},{8,24},{16,0},{24,8},{1,17},{9,25},{17,1},{25,9},{2,18},{10... | collective-permute-start | bytes 147464 | tf_op jit(solution)/shard_map/ppermute | solution.py:212
  36.8 0.1 collective-permute-done.16.refs_2_
  36.9 2.9 %collective-permute-start.14 = (bf16[96,256]{1,0:T(8,128)(2,1)S(1)}, bf16[96,256]{1,0:T(8,128)(2,1)S(1)}, u32[]{:S(2)}, u32[]{:S(2)}) collective-permute-start(bf16[96,256]{1,0:T(8,128)(2,1)S(1)} %get-tuple-element.105), channel_id=1, source_target_pairs={{0,24},{8,0},{16,8},{24,16},{1,25},{9,1},{17,9},{25,17},{2,26},{10... | collective-permute-start | bytes 147464 | tf_op jit(solution)/shard_map/ppermute | solution.py:212
  39.9 0.0 collective-permute-done.17.refs_3_
  39.9 1.6 %collective-permute-start.11 = (bf16[256,256]{1,0:T(8,128)(2,1)S(1)}, bf16[256,256]{1,0:T(8,128)(2,1)S(1)}, u32[]{:S(2)}, u32[]{:S(2)}) collective-permute-start(bf16[256,256]{1,0:T(8,128)(2,1)S(1)} %get-tuple-element.100), channel_id=1, source_target_pairs={{0,4},{2,6},{4,0},{6,2},{1,5},{3,7},{5,1},{7,3},{8,12},{10,14},{12... | collective-permute-start | bytes 393224 | tf_op jit(solution)/shard_map/ppermute | solution.py:216
  41.5 0.0 collective-permute-done.15.refs_1_
  41.5 0.2 collective-permute-start.21
  41.8 0.0 collective-permute-done.12.refs_1_
  41.8 0.4 collective-permute-start.20
  42.2 0.1 collective-permute-done.13.refs_2_
  42.2 1.9 %collective-permute-start.18 = (bf16[32,1024]{1,0:T(8,128)(2,1)S(1)}, bf16[32,1024]{1,0:T(8,128)(2,1)S(1)}, u32[]{:S(2)}, u32[]{:S(2)}) collective-permute-start(bf16[32,1024]{1,0:T(8,128)(2,1)S(1)} %block_sum.1.refs_0_), channel_id=1, source_target_pairs={{0,8},{8,16},{16,24},{24,0},{1,9},{9,17},{17,25},{25,1},{2,10},{10... | collective-permute-start | bytes 196616 | tf_op jit(solution)/shard_map/ppermute | solution.py:212
  44.1 0.0 collective-permute-done.14.refs_3_
  44.1 0.1 collective-permute-start.19
  44.2 1.3 %grad_out.1 = bf16[3,256,256]{2,1,0:T(8,128)(2,1)} custom-call(f32[256,256]{1,0:T(8,128)S(1)} %get-tuple-element.96.query_part, f32[6,256,256]{2,1,0:T(8,128)S(1)} %get-tuple-element.101.pair_w, f32[3,16,256]{2,1,0:T(8,128)S(1)} %get-tuple-element.106.later, bf16[96,256]{1,0:T(8,128)(2,1)S(1)} %get-tuple-element.102.refs_0_, ...), custom_call_target="tpu_custom_call" | custom-call | bytes 2473984 | tf_op jit(solution)/shard_map/grad_out/pallas_call | solution.py:234
  45.5 0.0 collective-permute-done.19.refs_9_
  45.5 0.5 collective-permute-start.22
  46.0 0.1 collective-permute-start.25
  46.0 3.1 %collective-permute-done.20.refs_2_ = bf16[32,1024]{1,0:T(8,128)(2,1)S(1)} collective-permute-done((bf16[32,1024]{1,0:T(8,128)(2,1)S(1)}, bf16[32,1024]{1,0:T(8,128)(2,1)S(1)}, u32[]{:S(2)}, u32[]{:S(2)}) %collective-permute-start.20) | collective-permute-done | bytes 65568 | tf_op jit(solution)/shard_map/ppermute | solution.py:212
  49.2 0.5 collective-permute-start.23
  49.7 0.7 %mixed_sum.1 = bf16[256,256]{1,0:T(8,128)(2,1)} custom-call(f32[256,256]{1,0:T(8,128)S(1)} %get-tuple-element.99.own, bf16[256,256]{1,0:T(8,128)(2,1)S(1)} %collective-permute-done.11.come), custom_call_target="tpu_custom_call" | custom-call | bytes 524288 | tf_op jit(solution)/shard_map/mixed_sum/pallas_call | solution.py:234
  50.4 0.0 collective-permute-done.22.refs_4_
  50.4 0.1 collective-permute-done.24.refs_6_
  50.4 0.2 collective-permute-done.23.refs_5_
  50.6 1.1 %final.1 = (f32[256,1024]{1,0:T(8,128)}, f32[3,3,256]{2,1,0:T(4,128)}, f32[16,256]{1,0:T(8,128)}) custom-call(bf16[32,1024]{1,0:T(8,128)(2,1)S(1)} %block_sum.1.refs_0_, bf16[32,1024]{1,0:T(8,128)(2,1)S(1)} %collective-permute-done.18.refs_1_, bf16[32,1024]{1,0:T(8,128)(2,1)S(1)} %collective-permute-done.20.refs_2_, ...), custom_call_target="tpu_custom_call" | custom-call | bytes 1664000 | tf_op jit(solution)/shard_map/final/pallas_call | solution.py:234
  (13 shorter events, 0.1 us)
Async XLA Ops:
  0.6 12.0 %collective-permute-start = (bf16[256,256]{1,0:T(8,128)(2,1)}, bf16[256,256]{1,0:T(8,128)(2,1)S(1)}, u32[]{:S(2)}, u32[]{:S(2)}) collective-permute-start(bf16[256,256]{1,0:T(8,128)(2,1)} %bitcast.8), channel_id=1, source_target_pairs={{0,2},{2,0},{4,6},{6,4},{1,3},{3,1},{5,7},{7,5},{8,10},{10,8},{12,... | collective-permute-start | bytes 393224 | tf_op jit(solution)/shard_map/ppermute | solution.py:216
  5.5 10.4 %collective-permute-start.1 = (bf16[160,256]{1,0:T(8,128)(2,1)}, bf16[160,256]{1,0:T(8,128)(2,1)S(1)}, u32[]{:S(2)}, u32[]{:S(2)}) collective-permute-start(bf16[160,256]{1,0:T(8,128)(2,1)} %get-tuple-element.63), channel_id=1, source_target_pairs={{0,8},{8,16},{16,24},{24,0},{1,9},{9,17},{17,25},{25,1},{2,10},{10... | collective-permute-start | bytes 245768 | tf_op jit(solution)/shard_map/ppermute | solution.py:212
  7.1 8.8 %collective-permute-start.2 = (bf16[144,256]{1,0:T(8,128)(2,1)}, bf16[144,256]{1,0:T(8,128)(2,1)S(1)}, u32[]{:S(2)}, u32[]{:S(2)}) collective-permute-start(bf16[144,256]{1,0:T(8,128)(2,1)} %get-tuple-element.66), channel_id=1, source_target_pairs={{0,16},{8,24},{16,0},{24,8},{1,17},{9,25},{17,1},{25,9},{2,18},{10... | collective-permute-start | bytes 221192 | tf_op jit(solution)/shard_map/ppermute | solution.py:212
  9.7 6.2 %collective-permute-start.3 = (bf16[144,256]{1,0:T(8,128)(2,1)}, bf16[144,256]{1,0:T(8,128)(2,1)S(1)}, u32[]{:S(2)}, u32[]{:S(2)}) collective-permute-start(bf16[144,256]{1,0:T(8,128)(2,1)} %get-tuple-element.67), channel_id=1, source_target_pairs={{0,24},{8,0},{16,8},{24,16},{1,25},{9,1},{17,9},{25,17},{2,26},{10... | collective-permute-start | bytes 221192 | tf_op jit(solution)/shard_map/ppermute | solution.py:212
  11.1 6.3 %collective-permute-start.4 = (bf16[256,256]{1,0:T(8,128)(2,1)}, bf16[256,256]{1,0:T(8,128)(2,1)S(1)}, u32[]{:S(2)}, u32[]{:S(2)}) collective-permute-start(bf16[256,256]{1,0:T(8,128)(2,1)} %bitcast.9), channel_id=1, source_target_pairs={{0,4},{2,6},{4,0},{6,2},{1,5},{3,7},{5,1},{7,3},{8,12},{10,14},{12... | collective-permute-start | bytes 393224 | tf_op jit(solution)/shard_map/ppermute | solution.py:216
  12.6 5.6 %collective-permute-start.5 = (bf16[256,256]{1,0:T(8,128)(2,1)S(1)}, bf16[256,256]{1,0:T(8,128)(2,1)S(1)}, u32[]{:S(2)}, u32[]{:S(2)}) collective-permute-start(bf16[256,256]{1,0:T(8,128)(2,1)S(1)} %collective-permute-done.rest_1_), channel_id=1, source_target_pairs={{0,4},{2,6},{4,0},{6,2},{1,5},{3,7},{5,1},{7,3},{8,12},{10,14},{12... | collective-permute-start | bytes 393224 | tf_op jit(solution)/shard_map/ppermute | solution.py:216
  13.1 1.0 %copy-start.1 = (bf16[3,1,256,256]{3,2,1,0:T(8,128)(2,1)S(1)}, bf16[3,1,256,256]{3,2,1,0:T(8,128)(2,1)}, u32[]{:S(2)}) copy-start(bf16[3,1,256,256]{3,2,1,0:T(8,128)(2,1)} %param.6) | copy-start | bytes 1179652
  14.1 0.9 %copy-start.3 = (bf16[144,256]{1,0:T(8,128)(2,1)S(1)}, bf16[144,256]{1,0:T(8,128)(2,1)}, u32[]{:S(2)}) copy-start(bf16[144,256]{1,0:T(8,128)(2,1)} %get-tuple-element.61.chunk) | copy-start | bytes 221188
  15.0 0.7 %copy-start.4 = (f32[3,3,256]{2,1,0:T(4,128)S(1)}, f32[3,3,256]{2,1,0:T(4,128)}, u32[]{:S(2)}) copy-start(f32[3,3,256]{2,1,0:T(4,128)} %short_filter) | copy-start | bytes 27652
  15.9 2.3 %copy-start = (bf16[256,1024]{1,0:T(8,128)(2,1)S(1)}, bf16[256,1024]{1,0:T(8,128)(2,1)}, u32[]{:S(2)}) copy-start(bf16[256,1024]{1,0:T(8,128)(2,1)} %weights.3) | copy-start | bytes 1572868
  15.9 2.3 %copy-start.2 = (bf16[1,256,256]{2,1,0:T(8,128)(2,1)S(1)}, bf16[1,256,256]{2,1,0:T(8,128)(2,1)}, u32[]{:S(2)}) copy-start(bf16[1,256,256]{2,1,0:T(8,128)(2,1)} %param.11) | copy-start | bytes 393220
  18.6 6.2 %collective-permute-start.6 = (bf16[128,256]{1,0:T(8,128)(2,1)S(1)}, bf16[128,256]{1,0:T(8,128)(2,1)S(1)}, u32[]{:S(2)}, u32[]{:S(2)}) collective-permute-start(bf16[128,256]{1,0:T(8,128)(2,1)S(1)} %get-tuple-element.79), channel_id=1, source_target_pairs={{0,8},{8,16},{16,24},{24,0},{1,9},{9,17},{17,25},{25,1},{2,10},{10... | collective-permute-start | bytes 196616 | tf_op jit(solution)/shard_map/ppermute | solution.py:212
  19.4 6.6 %collective-permute-start.7 = (bf16[128,256]{1,0:T(8,128)(2,1)S(1)}, bf16[128,256]{1,0:T(8,128)(2,1)S(1)}, u32[]{:S(2)}, u32[]{:S(2)}) collective-permute-start(bf16[128,256]{1,0:T(8,128)(2,1)S(1)} %get-tuple-element.80), channel_id=1, source_target_pairs={{0,16},{8,24},{16,0},{24,8},{1,17},{9,25},{17,1},{25,9},{2,18},{10... | collective-permute-start | bytes 196616 | tf_op jit(solution)/shard_map/ppermute | solution.py:212
  20.7 5.3 %collective-permute-start.8 = (bf16[128,256]{1,0:T(8,128)(2,1)S(1)}, bf16[128,256]{1,0:T(8,128)(2,1)S(1)}, u32[]{:S(2)}, u32[]{:S(2)}) collective-permute-start(bf16[128,256]{1,0:T(8,128)(2,1)S(1)} %get-tuple-element.81), channel_id=1, source_target_pairs={{0,24},{8,0},{16,8},{24,16},{1,25},{9,1},{17,9},{25,17},{2,26},{10... | collective-permute-start | bytes 196616 | tf_op jit(solution)/shard_map/ppermute | solution.py:212
  26.3 1.6 %collective-permute-start.9 = (bf16[128,1024]{1,0:T(8,128)(2,1)S(1)}, bf16[128,1024]{1,0:T(8,128)(2,1)S(1)}, u32[]{:S(2)}, u32[]{:S(2)}) collective-permute-start(bf16[128,1024]{1,0:T(8,128)(2,1)S(1)} %get-tuple-element.89), channel_id=1, source_target_pairs={{0,1},{1,0},{2,3},{3,2},{4,5},{5,4},{6,7},{7,6},{8,9},{9,8},{10,11... | collective-permute-start | bytes 786440 | tf_op jit(solution)/shard_map/ppermute | solution.py:212
  26.8 8.8 %collective-permute-start.10 = (bf16[512,256]{1,0:T(8,128)(2,1)S(1)}, bf16[512,256]{1,0:T(8,128)(2,1)S(1)}, u32[]{:S(2)}, u32[]{:S(2)}) collective-permute-start(bf16[512,256]{1,0:T(8,128)(2,1)S(1)} %get-tuple-element.98), channel_id=1, source_target_pairs={{0,2},{2,0},{4,6},{6,4},{1,3},{3,1},{5,7},{7,5},{8,10},{10,8},{12,... | collective-permute-start | bytes 786440 | tf_op jit(solution)/shard_map/ppermute | solution.py:216
  28.0 13.5 %collective-permute-start.15 = (bf16[32,1024]{1,0:T(8,128)(2,1)S(1)}, bf16[32,1024]{1,0:T(8,128)(2,1)S(1)}, u32[]{:S(2)}, u32[]{:S(2)}) collective-permute-start(bf16[32,1024]{1,0:T(8,128)(2,1)S(1)} %get-tuple-element.90), channel_id=1, source_target_pairs={{0,8},{8,16},{16,24},{24,0},{1,9},{9,17},{17,25},{25,1},{2,10},{10... | collective-permute-start | bytes 196616 | tf_op jit(solution)/shard_map/ppermute | solution.py:212
  29.5 7.4 %collective-permute-start.16 = (bf16[32,1024]{1,0:T(8,128)(2,1)S(1)}, bf16[32,1024]{1,0:T(8,128)(2,1)S(1)}, u32[]{:S(2)}, u32[]{:S(2)}) collective-permute-start(bf16[32,1024]{1,0:T(8,128)(2,1)S(1)} %get-tuple-element.108), channel_id=1, source_target_pairs={{0,16},{8,24},{16,0},{24,8},{1,17},{9,25},{17,1},{25,9},{2,18},{10... | collective-permute-start | bytes 196616 | tf_op jit(solution)/shard_map/ppermute | solution.py:212
  31.3 8.6 %collective-permute-start.17 = (bf16[32,1024]{1,0:T(8,128)(2,1)S(1)}, bf16[32,1024]{1,0:T(8,128)(2,1)S(1)}, u32[]{:S(2)}, u32[]{:S(2)}) collective-permute-start(bf16[32,1024]{1,0:T(8,128)(2,1)S(1)} %get-tuple-element.109), channel_id=1, source_target_pairs={{0,24},{8,0},{16,8},{24,16},{1,25},{9,1},{17,9},{25,17},{2,26},{10... | collective-permute-start | bytes 196616 | tf_op jit(solution)/shard_map/ppermute | solution.py:212
  34.2 7.6 %collective-permute-start.12 = (bf16[96,256]{1,0:T(8,128)(2,1)S(1)}, bf16[96,256]{1,0:T(8,128)(2,1)S(1)}, u32[]{:S(2)}, u32[]{:S(2)}) collective-permute-start(bf16[96,256]{1,0:T(8,128)(2,1)S(1)} %get-tuple-element.103), channel_id=1, source_target_pairs={{0,8},{8,16},{16,24},{24,0},{1,9},{9,17},{17,25},{25,1},{2,10},{10... | collective-permute-start | bytes 147464 | tf_op jit(solution)/shard_map/ppermute | solution.py:212
  35.6 6.6 %collective-permute-start.13 = (bf16[96,256]{1,0:T(8,128)(2,1)S(1)}, bf16[96,256]{1,0:T(8,128)(2,1)S(1)}, u32[]{:S(2)}, u32[]{:S(2)}) collective-permute-start(bf16[96,256]{1,0:T(8,128)(2,1)S(1)} %get-tuple-element.104), channel_id=1, source_target_pairs={{0,16},{8,24},{16,0},{24,8},{1,17},{9,25},{17,1},{25,9},{2,18},{10... | collective-permute-start | bytes 147464 | tf_op jit(solution)/shard_map/ppermute | solution.py:212
  36.9 7.2 %collective-permute-start.14 = (bf16[96,256]{1,0:T(8,128)(2,1)S(1)}, bf16[96,256]{1,0:T(8,128)(2,1)S(1)}, u32[]{:S(2)}, u32[]{:S(2)}) collective-permute-start(bf16[96,256]{1,0:T(8,128)(2,1)S(1)} %get-tuple-element.105), channel_id=1, source_target_pairs={{0,24},{8,0},{16,8},{24,16},{1,25},{9,1},{17,9},{25,17},{2,26},{10... | collective-permute-start | bytes 147464 | tf_op jit(solution)/shard_map/ppermute | solution.py:212
  39.9 9.3 %collective-permute-start.11 = (bf16[256,256]{1,0:T(8,128)(2,1)S(1)}, bf16[256,256]{1,0:T(8,128)(2,1)S(1)}, u32[]{:S(2)}, u32[]{:S(2)}) collective-permute-start(bf16[256,256]{1,0:T(8,128)(2,1)S(1)} %get-tuple-element.100), channel_id=1, source_target_pairs={{0,4},{2,6},{4,0},{6,2},{1,5},{3,7},{5,1},{7,3},{8,12},{10,14},{12... | collective-permute-start | bytes 393224 | tf_op jit(solution)/shard_map/ppermute | solution.py:216
  41.5 4.4 %collective-permute-start.21 = (bf16[32,1024]{1,0:T(8,128)(2,1)S(1)}, bf16[32,1024]{1,0:T(8,128)(2,1)S(1)}, u32[]{:S(2)}, u32[]{:S(2)}) collective-permute-start(bf16[32,1024]{1,0:T(8,128)(2,1)S(1)} %block_sum.1.refs_0_), channel_id=1, source_target_pairs={{0,24},{8,0},{16,8},{24,16},{1,25},{9,1},{17,9},{25,17},{2,26},{10... | collective-permute-start | bytes 196616 | tf_op jit(solution)/shard_map/ppermute | solution.py:212
  41.8 7.4 %collective-permute-start.20 = (bf16[32,1024]{1,0:T(8,128)(2,1)S(1)}, bf16[32,1024]{1,0:T(8,128)(2,1)S(1)}, u32[]{:S(2)}, u32[]{:S(2)}) collective-permute-start(bf16[32,1024]{1,0:T(8,128)(2,1)S(1)} %block_sum.1.refs_0_), channel_id=1, source_target_pairs={{0,16},{8,24},{16,0},{24,8},{1,17},{9,25},{17,1},{25,9},{2,18},{10... | collective-permute-start | bytes 196616 | tf_op jit(solution)/shard_map/ppermute | solution.py:212
  42.2 6.9 %collective-permute-start.18 = (bf16[32,1024]{1,0:T(8,128)(2,1)S(1)}, bf16[32,1024]{1,0:T(8,128)(2,1)S(1)}, u32[]{:S(2)}, u32[]{:S(2)}) collective-permute-start(bf16[32,1024]{1,0:T(8,128)(2,1)S(1)} %block_sum.1.refs_0_), channel_id=1, source_target_pairs={{0,8},{8,16},{16,24},{24,0},{1,9},{9,17},{17,25},{25,1},{2,10},{10... | collective-permute-start | bytes 196616 | tf_op jit(solution)/shard_map/ppermute | solution.py:212
  44.1 1.4 %collective-permute-start.19 = (bf16[16,1024]{1,0:T(8,128)(2,1)S(1)}, bf16[16,1024]{1,0:T(8,128)(2,1)S(1)}, u32[]{:S(2)}, u32[]{:S(2)}) collective-permute-start(bf16[16,1024]{1,0:T(8,128)(2,1)S(1)} %get-tuple-element.110.refs_8_), channel_id=1, source_target_pairs={{0,1},{1,0},{2,3},{3,2},{4,5},{5,4},{6,7},{7,6},{8,9},{9,8},{10,11... | collective-permute-start | bytes 98312 | tf_op jit(solution)/shard_map/ppermute | solution.py:212
  45.5 4.9 %collective-permute-start.22 = (bf16[32,1024]{1,0:T(8,128)(2,1)S(1)}, bf16[32,1024]{1,0:T(8,128)(2,1)S(1)}, u32[]{:S(2)}, u32[]{:S(2)}) collective-permute-start(bf16[32,1024]{1,0:T(8,128)(2,1)S(1)} %block_sum.1.refs_0_), channel_id=1, source_target_pairs={{0,1},{1,0},{2,3},{3,2},{4,5},{5,4},{6,7},{7,6},{8,9},{9,8},{10,11... | collective-permute-start | bytes 196616 | tf_op jit(solution)/shard_map/ppermute | solution.py:212
  46.0 4.4 %collective-permute-start.25 = (bf16[32,1024]{1,0:T(8,128)(2,1)S(1)}, bf16[32,1024]{1,0:T(8,128)(2,1)S(1)}, u32[]{:S(2)}, u32[]{:S(2)}) collective-permute-start(bf16[32,1024]{1,0:T(8,128)(2,1)S(1)} %collective-permute-done.21.refs_3_), channel_id=1, source_target_pairs={{0,1},{1,0},{2,3},{3,2},{4,5},{5,4},{6,7},{7,6},{8,9},{9,8},{10,11... | collective-permute-start | bytes 196616 | tf_op jit(solution)/shard_map/ppermute | solution.py:212
  49.2 1.3 %collective-permute-start.24 = (bf16[32,1024]{1,0:T(8,128)(2,1)S(1)}, bf16[32,1024]{1,0:T(8,128)(2,1)S(1)}, u32[]{:S(2)}, u32[]{:S(2)}) collective-permute-start(bf16[32,1024]{1,0:T(8,128)(2,1)S(1)} %collective-permute-done.20.refs_2_), channel_id=1, source_target_pairs={{0,1},{1,0},{2,3},{3,2},{4,5},{5,4},{6,7},{7,6},{8,9},{9,8},{10,11... | collective-permute-start | bytes 196616 | tf_op jit(solution)/shard_map/ppermute | solution.py:212
  49.2 1.4 %collective-permute-start.23 = (bf16[32,1024]{1,0:T(8,128)(2,1)S(1)}, bf16[32,1024]{1,0:T(8,128)(2,1)S(1)}, u32[]{:S(2)}, u32[]{:S(2)}) collective-permute-start(bf16[32,1024]{1,0:T(8,128)(2,1)S(1)} %collective-permute-done.18.refs_1_), channel_id=1, source_target_pairs={{0,1},{1,0},{2,3},{3,2},{4,5},{5,4},{6,7},{7,6},{8,9},{9,8},{10,11... | collective-permute-start | bytes 196616 | tf_op jit(solution)/shard_map/ppermute | solution.py:212

commit v7 on v6

--- a/solution.py
+++ b/solution.py
@@ -842,6 +842,7 @@
         "core_sum",
         [pltpu.VMEM((half, total_cols), f32)],
     )
+    first_sums = sums[1]
     parts_out = scatter_chunks(sums, "ctx")
 
     outs = on_core(
@@ -879,11 +880,12 @@
         [((rows, total_cols), bf16)],
         parts_out,
         "block_sum",
+        flops=2_000_000_000,
     )
     own_part, sent_part = on_core(
         mixed_pair_kernel,
         [((length, width), f32), ((length, width), bf16)],
-        (after(kept_part, query_part), swap(sent_part, "tp", 1)),
+        (after(kept_part, query_part), swap(after(sent_part, first_sums), "tp", 1)),
         "mixed_pair",
     )
     come_part = swap(sent_part, "tp", 2)

time: 51.9 us -> 52.1 us (level)
  transfers between devices with their start and end apart: 26 -> 26, of which waited for: 8 -> 7; matrix products, arithmetic and copies ran while one was open for 0% -> 0% of each run, Pallas kernels for 19% -> 19%
where the time goes in v7:
time: 52.1 us; the launch traced here: 51.8 us
  starting transfers between devices  29.9 us (57%)
  Pallas kernels  11.6 us (22%)
  waiting for transfers between devices  6.91 us (13%)
  local copies, waits for them, and re-layouts  2.6 us (5%)
  between operations  0.83 us (2%)
    ppermute x21, starting transfers between devices, rotate(): lax.ppermute(value, axis, [(i, (i + steps) % count) for i in range(count)])  22.8 us
    pallas_call x15, Pallas kernels, on_core(): pl.pallas_call(kernel, out_shape=[jax.ShapeDtypeStruct(shape, kind) for s...  11.6 us
    ppermute x5, starting transfers between devices, swap(): lax.ppermute(value, axis, [(i, i ^ bits) for i in range(lax.axis_size(axi...  7.08 us
    ppermute x21, waiting for transfers between devices, rotate(): lax.ppermute(value, axis, [(i, (i + steps) % count) for i in range(count)])  6.12 us
    unnamed x10, local copies, waits for them, and re-layouts  2.6 us
  transfers between devices with their start and end apart: 26, of which 7 were waited for; matrix products, arithmetic and copies ran while one was open for 0% of the time, Pallas kernels for 19%

profile of v7, /device:TPU:0, one launch (start us, length us, event | category | flops | bytes accessed | tf_op | source)
XLA Modules:
  0.0 51.8 jit_solution(2388782615727856362)
XLA Ops:
  0.6 3.0 %collective-permute-start = (bf16[256,256]{1,0:T(8,128)(2,1)}, bf16[256,256]{1,0:T(8,128)(2,1)S(1)}, u32[]{:S(2)}, u32[]{:S(2)}) collective-permute-start(bf16[256,256]{1,0:T(8,128)(2,1)} %bitcast.8), channel_id=1, source_target_pairs={{0,2},{2,0},{4,6},{6,4},{1,3},{3,1},{5,7},{7,5},{8,10},{10,8},{12,... | collective-permute-start | bytes 393224 | tf_op jit(solution)/shard_map/ppermute | solution.py:216
  3.6 1.9 %pack.1 = (bf16[144,256]{1,0:T(8,128)(2,1)}, bf16[160,256]{1,0:T(8,128)(2,1)}, bf16[144,256]{1,0:T(8,128)(2,1)}, bf16[144,256]{1,0:T(8,128)(2,1)}) custom-call(bf16[3,256,256]{2,1,0:T(8,128)(2,1)} %bitcast.6, f32[16,256]{1,0:T(8,128)} %filter_source.1, s32[1,256]{1,0:T(1,128)} %segment_source.1), custom_call_target="tpu_custom_call" | custom-call | bytes 713728 | tf_op jit(solution)/shard_map/pack/pallas_call | solution.py:234
  5.5 1.6 %collective-permute-start.1 = (bf16[160,256]{1,0:T(8,128)(2,1)}, bf16[160,256]{1,0:T(8,128)(2,1)S(1)}, u32[]{:S(2)}, u32[]{:S(2)}) collective-permute-start(bf16[160,256]{1,0:T(8,128)(2,1)} %get-tuple-element.64), channel_id=1, source_target_pairs={{0,8},{8,16},{16,24},{24,0},{1,9},{9,17},{17,25},{25,1},{2,10},{10... | collective-permute-start | bytes 245768 | tf_op jit(solution)/shard_map/ppermute | solution.py:212
  7.1 2.6 %collective-permute-start.2 = (bf16[144,256]{1,0:T(8,128)(2,1)}, bf16[144,256]{1,0:T(8,128)(2,1)S(1)}, u32[]{:S(2)}, u32[]{:S(2)}) collective-permute-start(bf16[144,256]{1,0:T(8,128)(2,1)} %get-tuple-element.67), channel_id=1, source_target_pairs={{0,16},{8,24},{16,0},{24,8},{1,17},{9,25},{17,1},{25,9},{2,18},{10... | collective-permute-start | bytes 221192 | tf_op jit(solution)/shard_map/ppermute | solution.py:212
  9.7 1.3 %collective-permute-start.3 = (bf16[144,256]{1,0:T(8,128)(2,1)}, bf16[144,256]{1,0:T(8,128)(2,1)S(1)}, u32[]{:S(2)}, u32[]{:S(2)}) collective-permute-start(bf16[144,256]{1,0:T(8,128)(2,1)} %get-tuple-element.68), channel_id=1, source_target_pairs={{0,24},{8,0},{16,8},{24,16},{1,25},{9,1},{17,9},{25,17},{2,26},{10... | collective-permute-start | bytes 221192 | tf_op jit(solution)/shard_map/ppermute | solution.py:212
  11.1 1.5 %collective-permute-start.4 = (bf16[256,256]{1,0:T(8,128)(2,1)}, bf16[256,256]{1,0:T(8,128)(2,1)S(1)}, u32[]{:S(2)}, u32[]{:S(2)}) collective-permute-start(bf16[256,256]{1,0:T(8,128)(2,1)} %bitcast.9), channel_id=1, source_target_pairs={{0,4},{2,6},{4,0},{6,2},{1,5},{3,7},{5,1},{7,3},{8,12},{10,14},{12... | collective-permute-start | bytes 393224 | tf_op jit(solution)/shard_map/ppermute | solution.py:216
  12.6 0.0 collective-permute-done.rest_1_
  12.6 0.5 collective-permute-start.5
  13.1 1.0 %copy-done.1 = bf16[3,1,256,256]{3,2,1,0:T(8,128)(2,1)S(1)} copy-done((bf16[3,1,256,256]{3,2,1,0:T(8,128)(2,1)S(1)}, bf16[3,1,256,256]{3,2,1,0:T(8,128)(2,1)}, u32[]{:S(2)}) %copy-start.1) | copy-done | bytes 393240
  14.1 0.9 %copy-done.3 = bf16[144,256]{1,0:T(8,128)(2,1)S(1)} copy-done((bf16[144,256]{1,0:T(8,128)(2,1)S(1)}, bf16[144,256]{1,0:T(8,128)(2,1)}, u32[]{:S(2)}) %copy-start.3) | copy-done | bytes 73752
  15.0 0.7 %copy-done.4 = f32[3,3,256]{2,1,0:T(4,128)S(1)} copy-done((f32[3,3,256]{2,1,0:T(4,128)S(1)}, f32[3,3,256]{2,1,0:T(4,128)}, u32[]{:S(2)}) %copy-start.4) | copy-done | bytes 9240
  15.7 0.2 prepare.1
  15.9 0.0 collective-permute-done.2.rest_2_
  15.9 0.0 collective-permute-done.3.rest_3_
  15.9 0.0 collective-permute-done.1.rest_1_.previous
  15.9 0.0 copy-start
  15.9 0.0 copy-start.2
  16.0 1.4 %conv.1 = (bf16[64,256]{1,0:T(8,128)(2,1)S(1)}, bf16[64,256]{1,0:T(8,128)(2,1)S(1)}, bf16[64,256]{1,0:T(8,128)(2,1)S(1)}, bf16[64,256]{1,0:T(8,128)(2,1)S(1)}, f...) custom-call(f32[256,16]{1,0:T(8,128)S(1)} %get-tuple-element.65.colu, ...), custom_call_target="tpu_custom_call" | custom-call | flops 900000000 | bytes 3366912 | tf_op jit(solution)/shard_map/conv/pallas_call | solution.py:234
  17.4 0.0 collective-permute-done.4.rest_2_
  17.4 0.8 %collective-permute-done.5.rest_3_ = bf16[256,256]{1,0:T(8,128)(2,1)S(1)} collective-permute-done((bf16[256,256]{1,0:T(8,128)(2,1)S(1)}, bf16[256,256]{1,0:T(8,128)(2,1)S(1)}, u32[]{:S(2)}, u32[]{:S(2)}) %collective-permute-start.5) | collective-permute-done | bytes 131104 | tf_op jit(solution)/shard_map/ppermute | solution.py:216
  18.2 0.4 grad_y.1
  18.6 0.7 %collective-permute-start.6 = (bf16[128,256]{1,0:T(8,128)(2,1)S(1)}, bf16[128,256]{1,0:T(8,128)(2,1)S(1)}, u32[]{:S(2)}, u32[]{:S(2)}) collective-permute-start(bf16[128,256]{1,0:T(8,128)(2,1)S(1)} %get-tuple-element.80), channel_id=1, source_target_pairs={{0,8},{8,16},{16,24},{24,0},{1,9},{9,17},{17,25},{25,1},{2,10},{10... | collective-permute-start | bytes 196616 | tf_op jit(solution)/shard_map/ppermute | solution.py:212
  19.4 1.3 %collective-permute-start.7 = (bf16[128,256]{1,0:T(8,128)(2,1)S(1)}, bf16[128,256]{1,0:T(8,128)(2,1)S(1)}, u32[]{:S(2)}, u32[]{:S(2)}) collective-permute-start(bf16[128,256]{1,0:T(8,128)(2,1)S(1)} %get-tuple-element.81), channel_id=1, source_target_pairs={{0,16},{8,24},{16,0},{24,8},{1,17},{9,25},{17,1},{25,9},{2,18},{10... | collective-permute-start | bytes 196616 | tf_op jit(solution)/shard_map/ppermute | solution.py:212
  20.7 1.8 %collective-permute-start.8 = (bf16[128,256]{1,0:T(8,128)(2,1)S(1)}, bf16[128,256]{1,0:T(8,128)(2,1)S(1)}, u32[]{:S(2)}, u32[]{:S(2)}) collective-permute-start(bf16[128,256]{1,0:T(8,128)(2,1)S(1)} %get-tuple-element.82), channel_id=1, source_target_pairs={{0,24},{8,0},{16,8},{24,16},{1,25},{9,1},{17,9},{25,17},{2,26},{10... | collective-permute-start | bytes 196616 | tf_op jit(solution)/shard_map/ppermute | solution.py:212
  22.5 1.4 %ready.1 = (f32[6,256,256]{2,1,0:T(8,128)S(1)}, f32[3,256,256]{2,1,0:T(8,128)S(1)}, f32[2,256,256]{2,1,0:T(8,128)S(1)}, bf16[4,128,128]{2,1,0:T(8,128)(2,1)S(1)}...) custom-call(bf16[3,256,256]{2,1,0:T(8,128)(2,1)S(1)} %get-tuple-element.63.turned, ...), custom_call_target="tpu_custom_call" | custom-call | bytes 6291456 | tf_op jit(solution)/shard_map/ready/pallas_call | solution.py:234
  23.9 0.9 %collective-permute-done.6.rest_5_.rest_1_ = bf16[128,256]{1,0:T(8,128)(2,1)S(1)} collective-permute-done((bf16[128,256]{1,0:T(8,128)(2,1)S(1)}, bf16[128,256]{1,0:T(8,128)(2,1)S(1)}, u32[]{:S(2)}, u32[]{:S(2)}) %collective-permute-start.6) | collective-permute-done | bytes 65568 | tf_op jit(solution)/shard_map/ppermute | solution.py:212
  24.9 1.1 %collective-permute-done.7.rest_6_.rest_2_ = bf16[128,256]{1,0:T(8,128)(2,1)S(1)} collective-permute-done((bf16[128,256]{1,0:T(8,128)(2,1)S(1)}, bf16[128,256]{1,0:T(8,128)(2,1)S(1)}, u32[]{:S(2)}, u32[]{:S(2)}) %collective-permute-start.7) | collective-permute-done | bytes 65568 | tf_op jit(solution)/shard_map/ppermute | solution.py:212
  25.9 0.0 collective-permute-done.8.rest_7_.rest_3_
  25.9 0.4 weight_grad.1
  26.3 0.1 collective-permute-start.9
  26.4 0.4 mixed_part.1
  26.8 1.1 %collective-permute-done.9.other = bf16[128,1024]{1,0:T(8,128)(2,1)S(1)} collective-permute-done((bf16[128,1024]{1,0:T(8,128)(2,1)S(1)}, bf16[128,1024]{1,0:T(8,128)(2,1)S(1)}, u32[]{:S(2)}, u32[]{:S(2)}) %collective-permute-start.9) | collective-permute-done | bytes 262176 | tf_op jit(solution)/shard_map/ppermute | solution.py:212
  27.9 0.1 core_sum.1
  28.0 1.5 %collective-permute-start.15 = (bf16[32,1024]{1,0:T(8,128)(2,1)S(1)}, bf16[32,1024]{1,0:T(8,128)(2,1)S(1)}, u32[]{:S(2)}, u32[]{:S(2)}) collective-permute-start(bf16[32,1024]{1,0:T(8,128)(2,1)S(1)} %get-tuple-element.91), channel_id=1, source_target_pairs={{0,8},{8,16},{16,24},{24,0},{1,9},{9,17},{17,25},{25,1},{2,10},{10... | collective-permute-start | bytes 196616 | tf_op jit(solution)/shard_map/ppermute | solution.py:212
  29.5 1.8 %collective-permute-start.16 = (bf16[32,1024]{1,0:T(8,128)(2,1)S(1)}, bf16[32,1024]{1,0:T(8,128)(2,1)S(1)}, u32[]{:S(2)}, u32[]{:S(2)}) collective-permute-start(bf16[32,1024]{1,0:T(8,128)(2,1)S(1)} %get-tuple-element.110), channel_id=1, source_target_pairs={{0,16},{8,24},{16,0},{24,8},{1,17},{9,25},{17,1},{25,9},{2,18},{10... | collective-permute-start | bytes 196616 | tf_op jit(solution)/shard_map/ppermute | solution.py:212
  31.3 0.6 %collective-permute-start.17 = (bf16[32,1024]{1,0:T(8,128)(2,1)S(1)}, bf16[32,1024]{1,0:T(8,128)(2,1)S(1)}, u32[]{:S(2)}, u32[]{:S(2)}) collective-permute-start(bf16[32,1024]{1,0:T(8,128)(2,1)S(1)} %get-tuple-element.111), channel_id=1, source_target_pairs={{0,24},{8,0},{16,8},{24,16},{1,25},{9,1},{17,9},{25,17},{2,26},{10... | collective-permute-start | bytes 196616 | tf_op jit(solution)/shard_map/ppermute | solution.py:212
  31.9 0.5 %collective-permute-start.10 = (bf16[512,256]{1,0:T(8,128)(2,1)S(1)}, bf16[512,256]{1,0:T(8,128)(2,1)S(1)}, u32[]{:S(2)}, u32[]{:S(2)}) collective-permute-start(bf16[512,256]{1,0:T(8,128)(2,1)S(1)} %get-tuple-element.100), channel_id=1, source_target_pairs={{0,2},{2,0},{4,6},{6,4},{1,3},{3,1},{5,7},{7,5},{8,10},{10,8},{12,... | collective-permute-start | bytes 786440 | tf_op jit(solution)/shard_map/ppermute | solution.py:216
  32.5 2.2 %backward.1 = (bf16[96,256]{1,0:T(8,128)(2,1)S(1)}, bf16[96,256]{1,0:T(8,128)(2,1)S(1)}, bf16[96,256]{1,0:T(8,128)(2,1)S(1)}, bf16[96,256]{1,0:T(8,128)(2,1)S(1)}, f32[256,256]{1,0:T(8,128)S(1)}) custom-call(bf16[4,256,1024]{2,1,0:T(8,128)(2,1)S(1)} %get-tuple-element.85.toeplitz, f32[256,16]{1,0:T(8,128)S(1)} %get-tuple-element.65.columns, ...), custom_call_target="tpu_custom_call" | custom-call | flops 1073741824 | bytes 6766592 | tf_op jit(solution)/shard_map/backward/pallas_call | solution.py:234
  34.7 1.4 %collective-permute-start.12 = (bf16[96,256]{1,0:T(8,128)(2,1)S(1)}, bf16[96,256]{1,0:T(8,128)(2,1)S(1)}, u32[]{:S(2)}, u32[]{:S(2)}) collective-permute-start(bf16[96,256]{1,0:T(8,128)(2,1)S(1)} %get-tuple-element.105), channel_id=1, source_target_pairs={{0,8},{8,16},{16,24},{24,0},{1,9},{9,17},{17,25},{25,1},{2,10},{10... | collective-permute-start | bytes 147464 | tf_op jit(solution)/shard_map/ppermute | solution.py:212
  36.2 0.7 %collective-permute-done.16.refs_2_ = bf16[32,1024]{1,0:T(8,128)(2,1)S(1)} collective-permute-done((bf16[32,1024]{1,0:T(8,128)(2,1)S(1)}, bf16[32,1024]{1,0:T(8,128)(2,1)S(1)}, u32[]{:S(2)}, u32[]{:S(2)}) %collective-permute-start.16) | collective-permute-done | bytes 65568 | tf_op jit(solution)/shard_map/ppermute | solution.py:212
  36.9 0.4 collective-permute-start.13
  37.3 0.0 collective-permute-done.17.refs_3_
  37.3 2.4 %collective-permute-start.14 = (bf16[96,256]{1,0:T(8,128)(2,1)S(1)}, bf16[96,256]{1,0:T(8,128)(2,1)S(1)}, u32[]{:S(2)}, u32[]{:S(2)}) collective-permute-start(bf16[96,256]{1,0:T(8,128)(2,1)S(1)} %get-tuple-element.107), channel_id=1, source_target_pairs={{0,24},{8,0},{16,8},{24,16},{1,25},{9,1},{17,9},{25,17},{2,26},{10... | collective-permute-start | bytes 147464 | tf_op jit(solution)/shard_map/ppermute | solution.py:212
  39.7 0.0 collective-permute-done.15.refs_1_
  39.8 1.6 %collective-permute-start.21 = (bf16[32,1024]{1,0:T(8,128)(2,1)S(1)}, bf16[32,1024]{1,0:T(8,128)(2,1)S(1)}, u32[]{:S(2)}, u32[]{:S(2)}) collective-permute-start(bf16[32,1024]{1,0:T(8,128)(2,1)S(1)} %block_sum.1.refs_0_), channel_id=1, source_target_pairs={{0,24},{8,0},{16,8},{24,16},{1,25},{9,1},{17,9},{25,17},{2,26},{10... | collective-permute-start | bytes 196616 | tf_op jit(solution)/shard_map/ppermute | solution.py:212
  41.4 0.0 collective-permute-done.10.come
  41.4 0.4 collective-permute-start.20
  41.8 0.0 collective-permute-done.12.refs_1_
  41.9 2.0 %collective-permute-start.18 = (bf16[32,1024]{1,0:T(8,128)(2,1)S(1)}, bf16[32,1024]{1,0:T(8,128)(2,1)S(1)}, u32[]{:S(2)}, u32[]{:S(2)}) collective-permute-start(bf16[32,1024]{1,0:T(8,128)(2,1)S(1)} %block_sum.1.refs_0_), channel_id=1, source_target_pairs={{0,8},{8,16},{16,24},{24,0},{1,9},{9,17},{17,25},{25,1},{2,10},{10... | collective-permute-start | bytes 196616 | tf_op jit(solution)/shard_map/ppermute | solution.py:212
  43.9 0.0 collective-permute-done.13.refs_2_
  43.9 1.5 %collective-permute-start.11 = (bf16[256,256]{1,0:T(8,128)(2,1)S(1)}, bf16[256,256]{1,0:T(8,128)(2,1)S(1)}, u32[]{:S(2)}, u32[]{:S(2)}) collective-permute-start(bf16[256,256]{1,0:T(8,128)(2,1)S(1)} %get-tuple-element.102), channel_id=1, source_target_pairs={{0,4},{2,6},{4,0},{6,2},{1,5},{3,7},{5,1},{7,3},{8,12},{10,14},{12... | collective-permute-start | bytes 393224 | tf_op jit(solution)/shard_map/ppermute | solution.py:216
  45.4 0.0 collective-permute-done.14.refs_3_
  45.4 0.1 collective-permute-start.19
  45.5 1.3 %grad_out.1 = bf16[3,256,256]{2,1,0:T(8,128)(2,1)} custom-call(f32[256,256]{1,0:T(8,128)S(1)} %get-tuple-element.97.query_part, f32[6,256,256]{2,1,0:T(8,128)S(1)} %get-tuple-element.103.pair_w, f32[3,16,256]{2,1,0:T(8,128)S(1)} %get-tuple-element.108.later, bf16[96,256]{1,0:T(8,128)(2,1)S(1)} %get-tuple-element.104.refs_0_, ...), custom_call_target="tpu_custom_call" | custom-call | bytes 2473984 | tf_op jit(solution)/shard_map/grad_out/pallas_call | solution.py:234
  46.8 0.0 collective-permute-done.19.refs_9_
  46.8 0.5 collective-permute-start.22
  47.3 0.0 collective-permute-done.21.refs_3_
  47.3 0.1 collective-permute-start.25
  47.3 2.0 %collective-permute-done.20.refs_2_ = bf16[32,1024]{1,0:T(8,128)(2,1)S(1)} collective-permute-done((bf16[32,1024]{1,0:T(8,128)(2,1)S(1)}, bf16[32,1024]{1,0:T(8,128)(2,1)S(1)}, u32[]{:S(2)}, u32[]{:S(2)}) %collective-permute-start.20) | collective-permute-done | bytes 65568 | tf_op jit(solution)/shard_map/ppermute | solution.py:212
  49.4 0.5 collective-permute-start.23
  49.9 0.7 %mixed_sum.1 = bf16[256,256]{1,0:T(8,128)(2,1)} custom-call(f32[256,256]{1,0:T(8,128)S(1)} %get-tuple-element.101.own, bf16[256,256]{1,0:T(8,128)(2,1)S(1)} %collective-permute-done.11.come), custom_call_target="tpu_custom_call" | custom-call | bytes 524288 | tf_op jit(solution)/shard_map/mixed_sum/pallas_call | solution.py:234
  50.6 0.1 collective-permute-done.24.refs_6_
  50.6 0.2 collective-permute-done.23.refs_5_
  50.8 1.1 %final.1 = (f32[256,1024]{1,0:T(8,128)}, f32[3,3,256]{2,1,0:T(4,128)}, f32[16,256]{1,0:T(8,128)}) custom-call(bf16[32,1024]{1,0:T(8,128)(2,1)S(1)} %block_sum.1.refs_0_, bf16[32,1024]{1,0:T(8,128)(2,1)S(1)} %collective-permute-done.18.refs_1_, bf16[32,1024]{1,0:T(8,128)(2,1)S(1)} %collective-permute-done.20.refs_2_, ...), custom_call_target="tpu_custom_call" | custom-call | bytes 1664000 | tf_op jit(solution)/shard_map/final/pallas_call | solution.py:234
  (13 shorter events, 0.1 us)
Async XLA Ops:
  0.6 12.0 %collective-permute-start = (bf16[256,256]{1,0:T(8,128)(2,1)}, bf16[256,256]{1,0:T(8,128)(2,1)S(1)}, u32[]{:S(2)}, u32[]{:S(2)}) collective-permute-start(bf16[256,256]{1,0:T(8,128)(2,1)} %bitcast.8), channel_id=1, source_target_pairs={{0,2},{2,0},{4,6},{6,4},{1,3},{3,1},{5,7},{7,5},{8,10},{10,8},{12,... | collective-permute-start | bytes 393224 | tf_op jit(solution)/shard_map/ppermute | solution.py:216
  5.5 10.4 %collective-permute-start.1 = (bf16[160,256]{1,0:T(8,128)(2,1)}, bf16[160,256]{1,0:T(8,128)(2,1)S(1)}, u32[]{:S(2)}, u32[]{:S(2)}) collective-permute-start(bf16[160,256]{1,0:T(8,128)(2,1)} %get-tuple-element.64), channel_id=1, source_target_pairs={{0,8},{8,16},{16,24},{24,0},{1,9},{9,17},{17,25},{25,1},{2,10},{10... | collective-permute-start | bytes 245768 | tf_op jit(solution)/shard_map/ppermute | solution.py:212
  7.1 8.8 %collective-permute-start.2 = (bf16[144,256]{1,0:T(8,128)(2,1)}, bf16[144,256]{1,0:T(8,128)(2,1)S(1)}, u32[]{:S(2)}, u32[]{:S(2)}) collective-permute-start(bf16[144,256]{1,0:T(8,128)(2,1)} %get-tuple-element.67), channel_id=1, source_target_pairs={{0,16},{8,24},{16,0},{24,8},{1,17},{9,25},{17,1},{25,9},{2,18},{10... | collective-permute-start | bytes 221192 | tf_op jit(solution)/shard_map/ppermute | solution.py:212
  9.7 6.2 %collective-permute-start.3 = (bf16[144,256]{1,0:T(8,128)(2,1)}, bf16[144,256]{1,0:T(8,128)(2,1)S(1)}, u32[]{:S(2)}, u32[]{:S(2)}) collective-permute-start(bf16[144,256]{1,0:T(8,128)(2,1)} %get-tuple-element.68), channel_id=1, source_target_pairs={{0,24},{8,0},{16,8},{24,16},{1,25},{9,1},{17,9},{25,17},{2,26},{10... | collective-permute-start | bytes 221192 | tf_op jit(solution)/shard_map/ppermute | solution.py:212
  11.1 6.3 %collective-permute-start.4 = (bf16[256,256]{1,0:T(8,128)(2,1)}, bf16[256,256]{1,0:T(8,128)(2,1)S(1)}, u32[]{:S(2)}, u32[]{:S(2)}) collective-permute-start(bf16[256,256]{1,0:T(8,128)(2,1)} %bitcast.9), channel_id=1, source_target_pairs={{0,4},{2,6},{4,0},{6,2},{1,5},{3,7},{5,1},{7,3},{8,12},{10,14},{12... | collective-permute-start | bytes 393224 | tf_op jit(solution)/shard_map/ppermute | solution.py:216
  12.6 5.6 %collective-permute-start.5 = (bf16[256,256]{1,0:T(8,128)(2,1)S(1)}, bf16[256,256]{1,0:T(8,128)(2,1)S(1)}, u32[]{:S(2)}, u32[]{:S(2)}) collective-permute-start(bf16[256,256]{1,0:T(8,128)(2,1)S(1)} %collective-permute-done.rest_1_), channel_id=1, source_target_pairs={{0,4},{2,6},{4,0},{6,2},{1,5},{3,7},{5,1},{7,3},{8,12},{10,14},{12... | collective-permute-start | bytes 393224 | tf_op jit(solution)/shard_map/ppermute | solution.py:216
  13.1 1.0 %copy-start.1 = (bf16[3,1,256,256]{3,2,1,0:T(8,128)(2,1)S(1)}, bf16[3,1,256,256]{3,2,1,0:T(8,128)(2,1)}, u32[]{:S(2)}) copy-start(bf16[3,1,256,256]{3,2,1,0:T(8,128)(2,1)} %param.6) | copy-start | bytes 1179652
  14.1 0.9 %copy-start.3 = (bf16[144,256]{1,0:T(8,128)(2,1)S(1)}, bf16[144,256]{1,0:T(8,128)(2,1)}, u32[]{:S(2)}) copy-start(bf16[144,256]{1,0:T(8,128)(2,1)} %get-tuple-element.62.chunk) | copy-start | bytes 221188
  15.0 0.7 %copy-start.4 = (f32[3,3,256]{2,1,0:T(4,128)S(1)}, f32[3,3,256]{2,1,0:T(4,128)}, u32[]{:S(2)}) copy-start(f32[3,3,256]{2,1,0:T(4,128)} %short_filter) | copy-start | bytes 27652
  15.9 2.3 %copy-start = (bf16[256,1024]{1,0:T(8,128)(2,1)S(1)}, bf16[256,1024]{1,0:T(8,128)(2,1)}, u32[]{:S(2)}) copy-start(bf16[256,1024]{1,0:T(8,128)(2,1)} %weights.3) | copy-start | bytes 1572868
  15.9 2.3 %copy-start.2 = (bf16[1,256,256]{2,1,0:T(8,128)(2,1)S(1)}, bf16[1,256,256]{2,1,0:T(8,128)(2,1)}, u32[]{:S(2)}) copy-start(bf16[1,256,256]{2,1,0:T(8,128)(2,1)} %param.11) | copy-start | bytes 393220
  18.6 6.2 %collective-permute-start.6 = (bf16[128,256]{1,0:T(8,128)(2,1)S(1)}, bf16[128,256]{1,0:T(8,128)(2,1)S(1)}, u32[]{:S(2)}, u32[]{:S(2)}) collective-permute-start(bf16[128,256]{1,0:T(8,128)(2,1)S(1)} %get-tuple-element.80), channel_id=1, source_target_pairs={{0,8},{8,16},{16,24},{24,0},{1,9},{9,17},{17,25},{25,1},{2,10},{10... | collective-permute-start | bytes 196616 | tf_op jit(solution)/shard_map/ppermute | solution.py:212
  19.4 6.6 %collective-permute-start.7 = (bf16[128,256]{1,0:T(8,128)(2,1)S(1)}, bf16[128,256]{1,0:T(8,128)(2,1)S(1)}, u32[]{:S(2)}, u32[]{:S(2)}) collective-permute-start(bf16[128,256]{1,0:T(8,128)(2,1)S(1)} %get-tuple-element.81), channel_id=1, source_target_pairs={{0,16},{8,24},{16,0},{24,8},{1,17},{9,25},{17,1},{25,9},{2,18},{10... | collective-permute-start | bytes 196616 | tf_op jit(solution)/shard_map/ppermute | solution.py:212
  20.7 5.3 %collective-permute-start.8 = (bf16[128,256]{1,0:T(8,128)(2,1)S(1)}, bf16[128,256]{1,0:T(8,128)(2,1)S(1)}, u32[]{:S(2)}, u32[]{:S(2)}) collective-permute-start(bf16[128,256]{1,0:T(8,128)(2,1)S(1)} %get-tuple-element.82), channel_id=1, source_target_pairs={{0,24},{8,0},{16,8},{24,16},{1,25},{9,1},{17,9},{25,17},{2,26},{10... | collective-permute-start | bytes 196616 | tf_op jit(solution)/shard_map/ppermute | solution.py:212
  26.3 1.6 %collective-permute-start.9 = (bf16[128,1024]{1,0:T(8,128)(2,1)S(1)}, bf16[128,1024]{1,0:T(8,128)(2,1)S(1)}, u32[]{:S(2)}, u32[]{:S(2)}) collective-permute-start(bf16[128,1024]{1,0:T(8,128)(2,1)S(1)} %get-tuple-element.90), channel_id=1, source_target_pairs={{0,1},{1,0},{2,3},{3,2},{4,5},{5,4},{6,7},{7,6},{8,9},{9,8},{10,11... | collective-permute-start | bytes 786440 | tf_op jit(solution)/shard_map/ppermute | solution.py:212
  28.0 11.7 %collective-permute-start.15 = (bf16[32,1024]{1,0:T(8,128)(2,1)S(1)}, bf16[32,1024]{1,0:T(8,128)(2,1)S(1)}, u32[]{:S(2)}, u32[]{:S(2)}) collective-permute-start(bf16[32,1024]{1,0:T(8,128)(2,1)S(1)} %get-tuple-element.91), channel_id=1, source_target_pairs={{0,8},{8,16},{16,24},{24,0},{1,9},{9,17},{17,25},{25,1},{2,10},{10... | collective-permute-start | bytes 196616 | tf_op jit(solution)/shard_map/ppermute | solution.py:212
  29.5 7.4 %collective-permute-start.16 = (bf16[32,1024]{1,0:T(8,128)(2,1)S(1)}, bf16[32,1024]{1,0:T(8,128)(2,1)S(1)}, u32[]{:S(2)}, u32[]{:S(2)}) collective-permute-start(bf16[32,1024]{1,0:T(8,128)(2,1)S(1)} %get-tuple-element.110), channel_id=1, source_target_pairs={{0,16},{8,24},{16,0},{24,8},{1,17},{9,25},{17,1},{25,9},{2,18},{10... | collective-permute-start | bytes 196616 | tf_op jit(solution)/shard_map/ppermute | solution.py:212
  31.3 6.0 %collective-permute-start.17 = (bf16[32,1024]{1,0:T(8,128)(2,1)S(1)}, bf16[32,1024]{1,0:T(8,128)(2,1)S(1)}, u32[]{:S(2)}, u32[]{:S(2)}) collective-permute-start(bf16[32,1024]{1,0:T(8,128)(2,1)S(1)} %get-tuple-element.111), channel_id=1, source_target_pairs={{0,24},{8,0},{16,8},{24,16},{1,25},{9,1},{17,9},{25,17},{2,26},{10... | collective-permute-start | bytes 196616 | tf_op jit(solution)/shard_map/ppermute | solution.py:212
  31.9 9.5 %collective-permute-start.10 = (bf16[512,256]{1,0:T(8,128)(2,1)S(1)}, bf16[512,256]{1,0:T(8,128)(2,1)S(1)}, u32[]{:S(2)}, u32[]{:S(2)}) collective-permute-start(bf16[512,256]{1,0:T(8,128)(2,1)S(1)} %get-tuple-element.100), channel_id=1, source_target_pairs={{0,2},{2,0},{4,6},{6,4},{1,3},{3,1},{5,7},{7,5},{8,10},{10,8},{12,... | collective-permute-start | bytes 786440 | tf_op jit(solution)/shard_map/ppermute | solution.py:216
  34.7 7.1 %collective-permute-start.12 = (bf16[96,256]{1,0:T(8,128)(2,1)S(1)}, bf16[96,256]{1,0:T(8,128)(2,1)S(1)}, u32[]{:S(2)}, u32[]{:S(2)}) collective-permute-start(bf16[96,256]{1,0:T(8,128)(2,1)S(1)} %get-tuple-element.105), channel_id=1, source_target_pairs={{0,8},{8,16},{16,24},{24,0},{1,9},{9,17},{17,25},{25,1},{2,10},{10... | collective-permute-start | bytes 147464 | tf_op jit(solution)/shard_map/ppermute | solution.py:212
  36.9 6.9 %collective-permute-start.13 = (bf16[96,256]{1,0:T(8,128)(2,1)S(1)}, bf16[96,256]{1,0:T(8,128)(2,1)S(1)}, u32[]{:S(2)}, u32[]{:S(2)}) collective-permute-start(bf16[96,256]{1,0:T(8,128)(2,1)S(1)} %get-tuple-element.106), channel_id=1, source_target_pairs={{0,16},{8,24},{16,0},{24,8},{1,17},{9,25},{17,1},{25,9},{2,18},{10... | collective-permute-start | bytes 147464 | tf_op jit(solution)/shard_map/ppermute | solution.py:212
  37.3 8.1 %collective-permute-start.14 = (bf16[96,256]{1,0:T(8,128)(2,1)S(1)}, bf16[96,256]{1,0:T(8,128)(2,1)S(1)}, u32[]{:S(2)}, u32[]{:S(2)}) collective-permute-start(bf16[96,256]{1,0:T(8,128)(2,1)S(1)} %get-tuple-element.107), channel_id=1, source_target_pairs={{0,24},{8,0},{16,8},{24,16},{1,25},{9,1},{17,9},{25,17},{2,26},{10... | collective-permute-start | bytes 147464 | tf_op jit(solution)/shard_map/ppermute | solution.py:212
  39.8 7.5 %collective-permute-start.21 = (bf16[32,1024]{1,0:T(8,128)(2,1)S(1)}, bf16[32,1024]{1,0:T(8,128)(2,1)S(1)}, u32[]{:S(2)}, u32[]{:S(2)}) collective-permute-start(bf16[32,1024]{1,0:T(8,128)(2,1)S(1)} %block_sum.1.refs_0_), channel_id=1, source_target_pairs={{0,24},{8,0},{16,8},{24,16},{1,25},{9,1},{17,9},{25,17},{2,26},{10... | collective-permute-start | bytes 196616 | tf_op jit(solution)/shard_map/ppermute | solution.py:212
  41.4 7.9 %collective-permute-start.20 = (bf16[32,1024]{1,0:T(8,128)(2,1)S(1)}, bf16[32,1024]{1,0:T(8,128)(2,1)S(1)}, u32[]{:S(2)}, u32[]{:S(2)}) collective-permute-start(bf16[32,1024]{1,0:T(8,128)(2,1)S(1)} %block_sum.1.refs_0_), channel_id=1, source_target_pairs={{0,16},{8,24},{16,0},{24,8},{1,17},{9,25},{17,1},{25,9},{2,18},{10... | collective-permute-start | bytes 196616 | tf_op jit(solution)/shard_map/ppermute | solution.py:212
  41.9 7.5 %collective-permute-start.18 = (bf16[32,1024]{1,0:T(8,128)(2,1)S(1)}, bf16[32,1024]{1,0:T(8,128)(2,1)S(1)}, u32[]{:S(2)}, u32[]{:S(2)}) collective-permute-start(bf16[32,1024]{1,0:T(8,128)(2,1)S(1)} %block_sum.1.refs_0_), channel_id=1, source_target_pairs={{0,8},{8,16},{16,24},{24,0},{1,9},{9,17},{17,25},{25,1},{2,10},{10... | collective-permute-start | bytes 196616 | tf_op jit(solution)/shard_map/ppermute | solution.py:212
  43.9 5.5 %collective-permute-start.11 = (bf16[256,256]{1,0:T(8,128)(2,1)S(1)}, bf16[256,256]{1,0:T(8,128)(2,1)S(1)}, u32[]{:S(2)}, u32[]{:S(2)}) collective-permute-start(bf16[256,256]{1,0:T(8,128)(2,1)S(1)} %get-tuple-element.102), channel_id=1, source_target_pairs={{0,4},{2,6},{4,0},{6,2},{1,5},{3,7},{5,1},{7,3},{8,12},{10,14},{12... | collective-permute-start | bytes 393224 | tf_op jit(solution)/shard_map/ppermute | solution.py:216
  45.4 1.4 %collective-permute-start.19 = (bf16[16,1024]{1,0:T(8,128)(2,1)S(1)}, bf16[16,1024]{1,0:T(8,128)(2,1)S(1)}, u32[]{:S(2)}, u32[]{:S(2)}) collective-permute-start(bf16[16,1024]{1,0:T(8,128)(2,1)S(1)} %get-tuple-element.112.refs_8_), channel_id=1, source_target_pairs={{0,1},{1,0},{2,3},{3,2},{4,5},{5,4},{6,7},{7,6},{8,9},{9,8},{10,11... | collective-permute-start | bytes 98312 | tf_op jit(solution)/shard_map/ppermute | solution.py:212
  46.8 3.8 %collective-permute-start.22 = (bf16[32,1024]{1,0:T(8,128)(2,1)S(1)}, bf16[32,1024]{1,0:T(8,128)(2,1)S(1)}, u32[]{:S(2)}, u32[]{:S(2)}) collective-permute-start(bf16[32,1024]{1,0:T(8,128)(2,1)S(1)} %block_sum.1.refs_0_), channel_id=1, source_target_pairs={{0,1},{1,0},{2,3},{3,2},{4,5},{5,4},{6,7},{7,6},{8,9},{9,8},{10,11... | collective-permute-start | bytes 196616 | tf_op jit(solution)/shard_map/ppermute | solution.py:212
  47.3 3.3 %collective-permute-start.25 = (bf16[32,1024]{1,0:T(8,128)(2,1)S(1)}, bf16[32,1024]{1,0:T(8,128)(2,1)S(1)}, u32[]{:S(2)}, u32[]{:S(2)}) collective-permute-start(bf16[32,1024]{1,0:T(8,128)(2,1)S(1)} %collective-permute-done.21.refs_3_), channel_id=1, source_target_pairs={{0,1},{1,0},{2,3},{3,2},{4,5},{5,4},{6,7},{7,6},{8,9},{9,8},{10,11... | collective-permute-start | bytes 196616 | tf_op jit(solution)/shard_map/ppermute | solution.py:212
  49.4 1.3 %collective-permute-start.24 = (bf16[32,1024]{1,0:T(8,128)(2,1)S(1)}, bf16[32,1024]{1,0:T(8,128)(2,1)S(1)}, u32[]{:S(2)}, u32[]{:S(2)}) collective-permute-start(bf16[32,1024]{1,0:T(8,128)(2,1)S(1)} %collective-permute-done.20.refs_2_), channel_id=1, source_target_pairs={{0,1},{1,0},{2,3},{3,2},{4,5},{5,4},{6,7},{7,6},{8,9},{9,8},{10,11... | collective-permute-start | bytes 196616 | tf_op jit(solution)/shard_map/ppermute | solution.py:212
  49.4 1.4 %collective-permute-start.23 = (bf16[32,1024]{1,0:T(8,128)(2,1)S(1)}, bf16[32,1024]{1,0:T(8,128)(2,1)S(1)}, u32[]{:S(2)}, u32[]{:S(2)}) collective-permute-start(bf16[32,1024]{1,0:T(8,128)(2,1)S(1)} %collective-permute-done.18.refs_1_), channel_id=1, source_target_pairs={{0,1},{1,0},{2,3},{3,2},{4,5},{5,4},{6,7},{7,6},{8,9},{9,8},{10,11... | collective-permute-start | bytes 196616 | tf_op jit(solution)/shard_map/ppermute | solution.py:212
